TPU v7x, 32 devices: a whole 2x2x4 slice. The times are simulated.
32 devices in a mesh: dp: 8 (over z, x), seq: 4 (over y, core).
Axes of the slice: x: 2, y: 2, z: 4, core: 2. Of those that a mesh axis runs over, the one named last changes fastest.
Arguments:
- inputs: bfloat16 [64, 1024, 512], P('dp', 'seq'), may hold values from -6 to 6
- segments: int32 [64, 1024], P('dp', 'seq'), may hold values from 0 to 6, as said below
- cotangent: bfloat16 [64, 1024, 512], P('dp', 'seq'), may hold values from -6 to 6
- gain_attn: float32 [512], P(('dp', 'seq')), may hold values from 0.1 to 1.9
- w_qkv: float32 [512, 1536], P(('dp', 'seq')), may hold values from -0.25 to 0.25
- w_out: float32 [512, 512], P(('dp', 'seq')), may hold values from -2 to 2
- gain_mix: float32 [512], P(('dp', 'seq')), may hold values from 0.1 to 1.9
- w_control: float32 [4, 512], P(None, ('dp', 'seq')), may hold values from -0.1875 to 0.1875
- w_expand: float32 [4, 512, 2048], P(None, ('dp', 'seq')), may hold values from -4 to 4
- w_shrink: float32 [4, 2048, 512], P(None, ('dp', 'seq')), may hold values from -1.5 to 1.5
Outputs:
- output: bfloat16 [64, 1024, 512], P('dp', 'seq')
- grad_inputs: bfloat16 [64, 1024, 512], P('dp', 'seq')
- grad_gain_attn: float32 [512], P(('dp', 'seq'))
- grad_w_qkv: float32 [512, 1536], P(('dp', 'seq'))
- grad_w_out: float32 [512, 512], P(('dp', 'seq'))
- grad_gain_mix: float32 [512], P(('dp', 'seq'))
- grad_w_control: float32 [4, 512], P(None, ('dp', 'seq'))
- grad_w_expand: float32 [4, 512, 2048], P(None, ('dp', 'seq'))
- grad_w_shrink: float32 [4, 2048, 512], P(None, ('dp', 'seq'))
Inputs may be any that keep to these rules, and one draw needn't show every extreme that they name: `segments`: each row's segment numbers start at 0 and never fall along the row; a document is the run of positions with one number.
All inputs are finite; a program needn't handle non-finite values.
Results may differ from a plain program's by a relative error of at most 0.033.
Values may be sent and summed in bfloat16 or wider, within the bound.
No kernel may reach another device: no remote copies, remote signals or barrier semaphores. Data moves between devices by JAX's collectives and lax.ppermute only.
A program may use at most 256 MiB of HBM per device.

v0:
```python
import math

import jax
import jax.numpy as jnp
from jax import lax
from jax.sharding import PartitionSpec as P

HEADS = 8
GROUP = 32


highest = lax.Precision.HIGHEST
masked_score = -1e30


def layer_norm(values):
    center = values - jnp.mean(values, axis=-1, keepdims=True)
    scaled = lax.rsqrt(jnp.mean(center * center, axis=-1, keepdims=True) + 1e-05)
    return (center * scaled, scaled)


def norm_back(incoming, normed, scaled):
    return scaled * (
        incoming
        - jnp.mean(incoming, axis=-1, keepdims=True)
        - normed * jnp.mean(incoming * normed, axis=-1, keepdims=True)
    )


def gelu_tanh(values):
    return jax.nn.gelu(values, approximate=True)


def key_mask(query_segments, piece_segments, first_query, piece_len):
    query_len = query_segments.shape[1]
    key_places = jnp.arange(piece_len)
    query_places = first_query + jnp.arange(query_len)
    causal = key_places[None, :] <= query_places[:, None]
    same_doc = query_segments[:, :, None] == jnp.transpose(piece_segments)[:, None, :]
    return (causal[None] & same_doc)[:, None]


def mix_forward(group_in, control, expand, shrink):
    total_rows, single, item_count, model_width = group_in.shape
    tokens = group_in.reshape(total_rows // GROUP, GROUP, item_count, model_width)
    logits = jnp.einsum("gtnd,ed->gtne", tokens, control, preferred_element_type=jnp.float32)
    weights = jax.nn.softmax(logits, axis=1)
    mixed_tokens = jnp.einsum(
        "gtne,gtnd->gned", weights.astype(jnp.bfloat16), tokens, preferred_element_type=jnp.float32
    ).astype(jnp.bfloat16)
    hidden_pre = jnp.einsum(
        "gned,edf->gnef", mixed_tokens, expand, preferred_element_type=jnp.float32
    )
    hidden = gelu_tanh(hidden_pre).astype(jnp.bfloat16)
    results = jnp.einsum("gnef,efd->gned", hidden, shrink, preferred_element_type=jnp.float32)
    spread = jnp.sum(weights[..., None] * results[:, None], axis=3)
    spread = spread.reshape(total_rows, single, item_count, model_width).astype(jnp.bfloat16)
    return (spread, tokens, weights, mixed_tokens, hidden_pre, hidden, results)


def mix_backward(group_in, group_grad, control, expand, shrink):
    unused_spread, tokens, weights, mixed_tokens, hidden_pre, hidden, results = mix_forward(
        group_in, control, expand, shrink
    )
    grad_out = group_grad.reshape(tokens.shape).astype(jnp.float32)
    grad_weights = jnp.sum(grad_out[:, :, :, None, :] * results[:, None], axis=-1)
    grad_results = jnp.sum(weights[..., None] * grad_out[:, :, :, None, :], axis=1).astype(
        jnp.bfloat16
    )
    grad_shrink = jnp.einsum(
        "gnef,gned->efd", hidden, grad_results, preferred_element_type=jnp.float32
    )
    grad_hidden = jnp.einsum(
        "gned,efd->gnef", grad_results, shrink, preferred_element_type=jnp.float32
    )
    gelu_pull = jax.vjp(gelu_tanh, hidden_pre)[1]
    grad_pre = gelu_pull(grad_hidden)[0].astype(jnp.bfloat16)
    grad_expand = jnp.einsum(
        "gned,gnef->edf", mixed_tokens, grad_pre, preferred_element_type=jnp.float32
    )
    grad_mixed = jnp.einsum(
        "gnef,edf->gned", grad_pre, expand, preferred_element_type=jnp.float32
    ).astype(jnp.bfloat16)
    grad_weights = grad_weights + jnp.einsum(
        "gned,gtnd->gtne", grad_mixed, tokens, preferred_element_type=jnp.float32
    )
    grad_logits = weights * (grad_weights - jnp.sum(weights * grad_weights, axis=1, keepdims=True))
    token_values = tokens.astype(jnp.float32)
    grad_control = jnp.einsum("gtne,gtnd->ed", grad_logits, token_values, precision=highest)
    grad_tokens = jnp.einsum(
        "gtne,gned->gtnd",
        weights.astype(jnp.bfloat16),
        grad_mixed,
        preferred_element_type=jnp.float32,
    )
    grad_tokens = grad_tokens + jnp.einsum(
        "gtne,ed->gtnd", grad_logits, control.astype(jnp.float32), precision=highest
    )
    return (
        grad_tokens.reshape(group_in.shape).astype(jnp.bfloat16),
        grad_control,
        grad_expand,
        grad_shrink,
    )


def on_device(
    inputs, segments, cotangent, gain_attn, w_qkv, w_out, gain_mix, w_control, w_expand, w_shrink
):
    local_rows, positions, model_width = inputs.shape
    head_size = model_width // HEADS
    score_scale = 1.0 / math.sqrt(head_size)
    dp_count = lax.axis_size("dp")
    slice_len = positions // dp_count
    first_query = lax.axis_index("seq") * positions
    attn_gain, proj_in, proj_out = (
        lax.all_gather(gain_attn.astype(jnp.bfloat16), ("dp", "seq"), axis=0, tiled=True),
        lax.all_gather(w_qkv.astype(jnp.bfloat16), ("dp", "seq"), axis=0, tiled=True),
        lax.all_gather(w_out.astype(jnp.bfloat16), ("dp", "seq"), axis=0, tiled=True),
    )
    hidden_in = inputs.astype(jnp.float32)
    normed_one, scaled_one = layer_norm(hidden_in)
    first_in = (normed_one * attn_gain.astype(jnp.float32)).astype(jnp.bfloat16)
    queries = jnp.einsum(
        "rpd,de->rpe", first_in, proj_in[:, :model_width], preferred_element_type=jnp.float32
    ).astype(jnp.bfloat16)
    key_values = jnp.einsum(
        "rpd,de->pre", first_in, proj_in[:, model_width:], preferred_element_type=jnp.float32
    ).astype(jnp.bfloat16)
    key_segments = jnp.transpose(segments)
    query_heads = queries.reshape(local_rows, positions, HEADS, head_size)
    running_max = jnp.full((local_rows, HEADS, positions), masked_score, jnp.float32)
    piece_kv = lax.all_gather(key_values, "seq", axis=0, tiled=True)
    piece_seg = lax.all_gather(key_segments, "seq", axis=0, tiled=True)
    piece_len = piece_kv.shape[0]
    key_heads = piece_kv[:, :, :model_width].reshape(piece_len, local_rows, HEADS, head_size)
    value_heads = piece_kv[:, :, model_width:].reshape(piece_len, local_rows, HEADS, head_size)
    allowed = key_mask(segments, piece_seg, first_query, piece_len)
    scores = (
        jnp.einsum("rqhd,krhd->rhqk", query_heads, key_heads, preferred_element_type=jnp.float32)
        * score_scale
    )
    scores = jnp.where(allowed, scores, masked_score)
    new_max = jnp.maximum(running_max, jnp.max(scores, axis=-1))
    weights = jnp.where(allowed, jnp.exp(scores - new_max[..., None]), 0.0)
    new_sum = jnp.sum(weights, axis=-1)
    update = jnp.einsum(
        "rhqk,krhd->rqhd",
        weights.astype(jnp.bfloat16),
        value_heads,
        preferred_element_type=jnp.float32,
    )
    attended = update / jnp.transpose(new_sum, (0, 2, 1))[..., None]
    log_total = new_max + jnp.log(new_sum)
    attended_low = attended.reshape(local_rows, positions, model_width).astype(jnp.bfloat16)
    middle = hidden_in + jnp.einsum(
        "rpd,de->rpe", attended_low, proj_out, preferred_element_type=jnp.float32
    )
    mix_gain, control, expand, shrink = (
        lax.all_gather(gain_mix.astype(jnp.bfloat16), ("dp", "seq"), axis=0, tiled=True),
        lax.all_gather(w_control.astype(jnp.bfloat16), ("dp", "seq"), axis=1, tiled=True),
        lax.all_gather(w_expand.astype(jnp.bfloat16), ("dp", "seq"), axis=1, tiled=True),
        lax.all_gather(w_shrink.astype(jnp.bfloat16), ("dp", "seq"), axis=1, tiled=True),
    )
    normed_two, scaled_two = layer_norm(middle)
    second_in = (normed_two * mix_gain.astype(jnp.float32)).astype(jnp.bfloat16)
    group_in = lax.all_to_all(
        second_in.reshape(local_rows, dp_count, slice_len, model_width),
        "dp",
        split_axis=1,
        concat_axis=0,
        tiled=True,
    )
    group_out, group_in = (mix_forward(group_in, control, expand, shrink)[0], group_in)
    returned = lax.all_to_all(group_out, "dp", split_axis=0, concat_axis=1, tiled=True).reshape(
        local_rows, positions, model_width
    )
    output = (middle + returned.astype(jnp.float32)).astype(jnp.bfloat16)
    group_grad = lax.all_to_all(
        cotangent.reshape(local_rows, dp_count, slice_len, model_width),
        "dp",
        split_axis=1,
        concat_axis=0,
        tiled=True,
    )
    mix_gain_back, control_back, expand_back, shrink_back = (
        lax.all_gather(gain_mix.astype(jnp.bfloat16), ("dp", "seq"), axis=0, tiled=True),
        lax.all_gather(w_control.astype(jnp.bfloat16), ("dp", "seq"), axis=1, tiled=True),
        lax.all_gather(w_expand.astype(jnp.bfloat16), ("dp", "seq"), axis=1, tiled=True),
        lax.all_gather(w_shrink.astype(jnp.bfloat16), ("dp", "seq"), axis=1, tiled=True),
    )
    grad_group, grad_control, grad_expand, grad_shrink = mix_backward(
        group_in, group_grad, control_back, expand_back, shrink_back
    )
    grad_second = lax.all_to_all(grad_group, "dp", split_axis=0, concat_axis=1, tiled=True)
    grad_second = grad_second.reshape(local_rows, positions, model_width).astype(jnp.float32)
    grad_mix_gain = jnp.sum(grad_second * normed_two, axis=(0, 1))
    grad_middle = cotangent.astype(jnp.float32) + norm_back(
        grad_second * mix_gain_back.astype(jnp.float32), normed_two, scaled_two
    )
    mix_sums = (
        lax.psum_scatter(grad_mix_gain, ("dp", "seq"), scatter_dimension=0, tiled=True),
        lax.psum_scatter(grad_control, ("dp", "seq"), scatter_dimension=1, tiled=True),
        lax.psum_scatter(grad_expand, ("dp", "seq"), scatter_dimension=1, tiled=True),
        lax.psum_scatter(grad_shrink, ("dp", "seq"), scatter_dimension=1, tiled=True),
    )
    attn_gain_back, proj_in_back, proj_out_back = (
        lax.all_gather(gain_attn.astype(jnp.bfloat16), ("dp", "seq"), axis=0, tiled=True),
        lax.all_gather(w_qkv.astype(jnp.bfloat16), ("dp", "seq"), axis=0, tiled=True),
        lax.all_gather(w_out.astype(jnp.bfloat16), ("dp", "seq"), axis=0, tiled=True),
    )
    grad_attn_out = grad_middle.astype(jnp.bfloat16)
    grad_proj_out = jnp.einsum(
        "rpd,rpe->de", attended_low, grad_attn_out, preferred_element_type=jnp.float32
    )
    grad_attended = jnp.einsum(
        "rpe,de->rpd", grad_attn_out, proj_out_back, preferred_element_type=jnp.float32
    ).astype(jnp.bfloat16)
    grad_heads = grad_attended.reshape(local_rows, positions, HEADS, head_size)
    row_dot = jnp.transpose(jnp.sum(grad_heads.astype(jnp.float32) * attended, axis=-1), (0, 2, 1))
    piece_kv = lax.all_gather(key_values, "seq", axis=0, tiled=True)
    piece_seg = lax.all_gather(key_segments, "seq", axis=0, tiled=True)
    piece_len = piece_kv.shape[0]
    split_piece_len = piece_kv.shape[0]
    key_heads = piece_kv[:, :, :model_width].reshape(split_piece_len, local_rows, HEADS, head_size)
    value_heads = piece_kv[:, :, model_width:].reshape(
        split_piece_len, local_rows, HEADS, head_size
    )
    key_heads, value_heads = (key_heads, value_heads)
    allowed = key_mask(segments, piece_seg, first_query, piece_len)
    scores = (
        jnp.einsum("rqhd,krhd->rhqk", query_heads, key_heads, preferred_element_type=jnp.float32)
        * score_scale
    )
    weights = jnp.where(
        allowed, jnp.exp(jnp.where(allowed, scores, masked_score) - log_total[..., None]), 0.0
    )
    grad_weights = jnp.einsum(
        "rqhd,krhd->rhqk", grad_heads, value_heads, preferred_element_type=jnp.float32
    )
    grad_scores = (weights * (grad_weights - row_dot[..., None])).astype(jnp.bfloat16)
    weights, grad_scores = (weights, grad_scores)
    grad_query = score_scale * jnp.einsum(
        "rhqk,krhd->rqhd", grad_scores, key_heads, preferred_element_type=jnp.float32
    )
    grad_key_piece = score_scale * jnp.einsum(
        "rhqk,rqhd->krhd", grad_scores, query_heads, preferred_element_type=jnp.float32
    )
    grad_value_piece = jnp.einsum(
        "rhqk,rqhd->krhd",
        weights.astype(jnp.bfloat16),
        grad_heads,
        preferred_element_type=jnp.float32,
    )
    key_term = jnp.concatenate(
        [
            grad_key_piece.reshape(piece_len, local_rows, model_width),
            grad_value_piece.reshape(piece_len, local_rows, model_width),
        ],
        axis=2,
    )
    grad_query, grad_keys_all = (grad_query, key_term)
    grad_kv = lax.psum_scatter(grad_keys_all, "seq", scatter_dimension=0, tiled=True).astype(
        jnp.bfloat16
    )
    grad_queries = grad_query.reshape(local_rows, positions, model_width).astype(jnp.bfloat16)
    grad_proj_in = jnp.concatenate(
        [
            jnp.einsum("rpd,rpe->de", first_in, grad_queries, preferred_element_type=jnp.float32),
            jnp.einsum("rpd,pre->de", first_in, grad_kv, preferred_element_type=jnp.float32),
        ],
        axis=1,
    )
    grad_first = jnp.einsum(
        "rpe,de->rpd",
        grad_queries,
        proj_in_back[:, :model_width],
        preferred_element_type=jnp.float32,
    )
    grad_first = grad_first + jnp.einsum(
        "pre,de->rpd", grad_kv, proj_in_back[:, model_width:], preferred_element_type=jnp.float32
    )
    grad_attn_gain = jnp.sum(grad_first * normed_one, axis=(0, 1))
    grad_inputs = grad_middle + norm_back(
        grad_first * attn_gain_back.astype(jnp.float32), normed_one, scaled_one
    )
    attn_sums = (
        lax.psum_scatter(grad_attn_gain, ("dp", "seq"), scatter_dimension=0, tiled=True),
        lax.psum_scatter(grad_proj_in, ("dp", "seq"), scatter_dimension=0, tiled=True),
        lax.psum_scatter(grad_proj_out, ("dp", "seq"), scatter_dimension=0, tiled=True),
    )
    return (
        output,
        grad_inputs.astype(jnp.bfloat16),
        attn_sums[0],
        attn_sums[1],
        attn_sums[2],
        mix_sums[0],
        mix_sums[1],
        mix_sums[2],
        mix_sums[3],
    )


def solution(mesh):
    return jax.shard_map(
        on_device,
        mesh=mesh,
        in_specs=(
            P("dp", "seq", None),
            P("dp", "seq"),
            P("dp", "seq", None),
            P(("dp", "seq")),
            P(("dp", "seq"), None),
            P(("dp", "seq"), None),
            P(("dp", "seq")),
            P(None, ("dp", "seq")),
            P(None, ("dp", "seq"), None),
            P(None, ("dp", "seq"), None),
        ),
        out_specs=(
            P("dp", "seq", None),
            P("dp", "seq", None),
            P(("dp", "seq")),
            P(("dp", "seq"), None),
            P(("dp", "seq"), None),
            P(("dp", "seq")),
            P(None, ("dp", "seq")),
            P(None, ("dp", "seq"), None),
            P(None, ("dp", "seq"), None),
        ),
        check_vma=False,
    )
```

profile of v0, /device:TPU:0, one launch (start us, length us, event | category | flops | bytes accessed | tf_op | source)
XLA Modules:
  0.0 1717.8 jit_solution(8908839166252423727)
XLA Ops:
  10.7 42.0 %all-reduce.5 = (bf16[512]{0:T(512)(128)(2,1)S(1)}, bf16[512]{0:T(512)(128)(2,1)S(1)}) all-reduce(bf16[512]{0:T(512)(128)(2,1)S(1)} %dynamic-update-slice, bf16[512]{0:T(512)(128)(2,1)S(1)} %dynamic-update-slice.1), channel_id=1, replica_groups=mesh['dp'=8,'seq'=4] {'dp','seq'}, use_global_device_ids=true, to_apply=%add | all-reduce | flops 1024 | bytes 4096
  52.7 1.9 convert_reduce_fusion
  54.7 2.4 fusion.31
  57.1 12.1 all-gather.6.cloned.1.call-done
  69.3 5.2 convert_bitcast_fusion.2
  76.3 3.2 copy.181
  79.5 4.4 all-to-all-start.2
  84.7 5.2 all_gather.39
  90.2 66.6 %all_gather.40 = bf16[512,512]{1,0:T(8,128)(2,1)S(1)} all-gather(bf16[16,512]{1,0:T(8,128)(2,1)S(1)} %convert_element_type.210), channel_id=1, replica_groups=mesh['dp'=8,'seq'=4] {'dp','seq'}, dimensions={0}, use_global_device_ids=true | all-gather | bytes 540672 | tf_op jit(solution)/shard_map/all_gather | solution.py:119
  156.7 2.5 compare_and_fusion
  159.3 3.6 convolution_convert_fusion.1
  162.9 4.0 copy.169
  166.8 18.0 %all-gather.8.cloned.1.call-done = bf16[1024,8,1024]{2,0,1:T(8,128)(2,1)} async-done(((bf16[256,8,1024]{2,0,1:T(8,128)(2,1)}), bf16[1024,8,1024]{2,0,1:T(8,128)(2,1)}) %all-gather.8.cloned.1.call-update) | async-done | bytes 16777232 | tf_op jit(solution)/shard_map/all_gather | solution.py:133
  184.9 11.4 fusion.102
  196.3 11.5 copy.170
  207.8 30.3 %fusion.3 = (f32[8,8,256]{2,1,0:T(8,128)S(1)}, f32[8,8,256,1024]{3,2,1,0:T(8,128)}) fusion(pred[8,256,1024]{2,1,0:T(8,128)(4,1)} %compare_and_fusion, bf16[8,256,8,64]{1,3,2,0:T(8,128)(2,1)} %bitcast.185, bf16[1024,8,8,64]{0,3,2,1:T(8,128)(2,1)} %bitcast.178), kind=kOutput, calls=%fused_computation.7 | convolution fusion | flops 2197798912 | bytes 79757312 | tf_op jit(solution)/shard_map/rqhd,krhd->rhqk/dot_general | solution.py:140
  238.1 11.5 copy.168
  249.6 23.3 %fusion = f32[8,8,256]{2,1,0:T(8,128)S(1)} fusion(f32[8,8,256,1024]{3,2,1,0:T(8,128)} %get-tuple-element.28, f32[8,8,256]{2,1,0:T(8,128)S(1)} %broadcast_maximum_fusion, pred[8,256,1024]{2,1,0:T(8,128)(4,1)} %compare_and_fusion), kind=kLoop, calls=%fused_computation.4 | loop fusion | flops 83869696 | bytes 69337088 | tf_op jit(solution)/shard_map/reduce_sum | solution.py:146
  272.9 31.0 %fusion.103 = (bf16[8,256,8,64]{1,3,2,0:T(8,128)(2,1)}, f32[8,256,8,64]{1,3,2,0:T(8,128)}) fusion(f32[8,256,8]{1,2,0:T(8,128)S(1)} %bitcast.208, bf16[1024,8,8,64]{0,3,2,1:T(8,128)(2,1)} %bitcast.199, f32[8,8,256,1024]{3,2,1,0:T(8,128)} %get-tuple-element.28, f32[8,8,256]{2,1,0:T(8,128)S(1)} %broadcast_maximum_fusion, ...), kind=kOutput, calls=%fused_computation.139 | convolution fusion | flops 2233466880 | bytes 84017152 | tf_op jit(solution)/shard_map/rhqk,krhd->rqhd/dot_general | solution.py:147
  303.9 3.0 fusion.104
  310.4 5.4 all-to-all-start
  315.8 90.9 %all-gather = bf16[32,16,4]{1,2,0:T(4,128)(2,1)S(1)} all-gather(bf16[1,16,4]{1,2,0:T(4,128)(2,1)S(1)} %convert_bitcast_fusion.3), channel_id=1, replica_groups=mesh['dp'=8,'seq'=4] {'dp','seq'}, dimensions={0}, use_global_device_ids=true | all-gather | bytes 4224 | tf_op jit(solution)/shard_map/all_gather | solution.py:161
  406.8 4.2 bitcast_convert_fusion
  414.0 6.4 fusion.37
  420.4 5.8 fusion.61
  426.3 7.3 multiply_reduce_fusion
  433.6 2.8 fusion.48
  436.4 2.7 fusion.70
  439.1 2.8 fusion.83
  443.5 3.8 fusion.33
  448.5 56.5 %all_to_all.42 = bf16[64,1,32,512]{3,2,1,0:T(8,128)(2,1)S(1)} all-to-all(bf16[64,1,32,512]{3,2,1,0:T(8,128)(2,1)S(1)} %bitcast.201), channel_id=1, replica_groups=mesh['dp'=8,'seq'=4] {'dp'}, dimensions={0} | all-to-all | bytes 4194304 | tf_op jit(solution)/shard_map/all_to_all | solution.py:195
  505.0 4.3 all-to-all-start.1
  510.0 2.5 copy.192
  513.0 4.9 multiply_reduce_fusion.3
  518.0 39.2 %all-to-all-done.1 = bf16[64,1,32,512]{3,2,1,0:T(8,128)(2,1)} async-done(((bf16[64,1,32,512]{3,2,1,0:T(8,128)(2,1)}), bf16[64,1,32,512]{3,2,1,0:T(8,128)(2,1)}, u32[]{:S(2)}, u32[]{:S(2)}) %all-to-all-start.1) | async-done | bytes 2097184 | tf_op jit(solution)/shard_map/all_to_all | solution.py:175
  557.2 2.3 convert_bitcast_fusion.1
  563.0 3.0 multiply_add_fusion
  566.0 1.9 copy-done.4
  569.2 2.4 copy.194
  571.7 3.9 multiply_reduce_fusion.4
  575.6 31.0 %fusion.4 = f32[8,8,64,1024]{3,2,1,0:T(8,128)} fusion(bf16[8,256,8,64]{1,3,2,0:T(8,128)(2,1)} %bitcast.197, f32[8,8,256,1024]{3,2,1,0:T(8,128)} %get-tuple-element.28, f32[8,8,256]{2,1,0:T(8,128)S(1)} %log_add_fusion, pred[8,256,1024]{2,1,0:T(8,128)(4,1)S(1)} %copy-done.7), kind=kOutput, calls=%fused_computation.9 | convolution fusion | flops 2231369728 | bytes 88145920 | tf_op jit(solution)/shard_map/rhqk,rqhd->krhd/dot_general | solution.py:249
  606.6 45.1 %multiply_convert_fusion = bf16[8,8,256,1024]{3,2,1,0:T(8,128)(2,1)} fusion(f32[8,8,256,1024]{3,2,1,0:T(8,128)} %get-tuple-element.28, f32[8,8,256]{2,1,0:T(8,128)S(1)} %bitcast.210, f32[8,8,256]{2,1,0:T(8,128)S(1)} %log_add_fusion, pred[8,256,1024]{2,1,0:T(8,128)(4,1)S(1)} %copy-done.7, bf16[8,256,8,64]{1,3,2,0:T(8,128)(2,1)} %bitcast.198, ...), kind=kOutput, calls=%fused_computation | convolution fusion | flops 2264924160 | bytes 113377280 | tf_op jit(solution)/shard_map/rqhd,krhd->rhqk/dot_general | solution.py:238
  651.7 16.5 copy.197
  668.3 22.2 %convolution_multiply_fusion = f32[8,8,64,1024]{3,2,1,0:T(8,128)} fusion(bf16[8,256,8,64]{1,3,2,0:T(8,128)(2,1)S(1)} %bitcast.186, bf16[8,8,256,1024]{3,2,1,0:T(8,128)(2,1)} %multiply_convert_fusion), kind=kOutput, calls=%fused_computation.16 | convolution fusion | flops 2151677952 | bytes 52428800 | tf_op jit(solution)/shard_map/rhqk,rqhd->krhd/dot_general | solution.py:246
  690.5 16.4 copy.196
  706.9 23.2 %pad_maximum_fusion = f32[1024,8,1024]{2,0,1:T(8,128)} fusion(f32[1024,8,512]{2,0,1:T(8,128)} %copy.197, f32[1024,8,512]{2,0,1:T(8,128)} %copy.196), kind=kLoop, calls=%fused_computation.8 | loop fusion | flops 8388608 | bytes 67108864 | tf_op jit(solution)/shard_map/concatenate | solution.py:255
  731.7 9.4 convolution_bitcast_fusion.4
  741.2 6.7 convolution_bitcast_fusion.2
  748.0 12.4 convolution_bitcast_fusion.1
  760.4 2.0 copy-done.11
  762.5 10.9 convolution_bitcast_fusion
  773.6 17.6 %multiply_convert_fusion.1 = bf16[8,8,64,256]{3,2,1,0:T(8,128)(2,1)S(1)} fusion(bf16[1024,8,8,64]{0,3,2,1:T(8,128)(2,1)} %bitcast.179, bf16[8,8,256,1024]{3,2,1,0:T(8,128)(2,1)} %multiply_convert_fusion), kind=kOutput, calls=%fused_computation.54 | convolution fusion | flops 2149580800 | bytes 44040192 | tf_op jit(solution)/shard_map/rhqk,krhd->rqhd/dot_general | solution.py:243
  792.6 1.9 convolution_bitcast_fusion.3
  794.5 168.7 %reduce-scatter.9.cloned.1.call-done = f32[256,8,1024]{2,0,1:T(8,128)} async-done(((f32[1024,8,1024]{2,0,1:T(8,128)}), f32[256,8,1024]{2,0,1:T(8,128)}) %reduce-scatter.9.cloned.1.call-update) | async-done | bytes 8388624 | tf_op jit(solution)/shard_map/reduce_scatter | solution.py:263
  963.2 5.9 fusion.56
  971.0 127.7 %reduce-scatter.19.cloned.1.call-done = f32[16,4]{1,0:T(8,128)} async-done(((f32[512,4]{1,0:T(8,128)}), f32[16,4]{1,0:T(8,128)}) %reduce-scatter.19.cloned.1.call-update) | async-done | bytes 272
  1100.1 3.1 fusion.77
  1103.2 8.8 fusion.30
  1112.0 37.0 %all-reduce.4 = (f32[512]{0:T(512)S(1)}, f32[512]{0:T(512)S(1)}) all-reduce(f32[512]{0:T(512)S(1)} %get-tuple-element.11, f32[512]{0:T(512)S(1)} %copy-done.35), channel_id=3, replica_groups=mesh['dp'=8,'seq'=4] {'dp','seq'}, use_global_device_ids=true, to_apply=%region_19.20.clone | all-reduce | flops 1024 | bytes 8192
  1150.1 5.2 fusion.29
  1155.4 77.1 %reduce-scatter.13.cloned.1.call-done = f32[16,512]{1,0:T(8,128)} async-done(((f32[512,512]{1,0:T(8,128)}), f32[16,512]{1,0:T(8,128)}) %reduce-scatter.13.cloned.1.call-update) | async-done | bytes 32784 | tf_op jit(solution)/shard_map/reduce_scatter | solution.py:290
  1232.5 181.9 %reduce-scatter.15.cloned.1.call-done = f32[4,16,2048]{2,1,0:T(8,128)} async-done(((f32[4,512,2048]{2,1,0:T(8,128)}), f32[4,16,2048]{2,1,0:T(8,128)}) %reduce-scatter.15.cloned.1.call-update) | async-done | bytes 524304 | tf_op jit(solution)/shard_map/reduce_scatter | solution.py:204
  1414.4 187.5 %reduce-scatter.17.cloned.1.call-done = f32[4,64,512]{2,1,0:T(8,128)} async-done(((f32[4,2048,512]{2,1,0:T(8,128)}), f32[4,64,512]{2,1,0:T(8,128)}) %reduce-scatter.17.cloned.1.call-update) | async-done | bytes 524304 | tf_op jit(solution)/shard_map/reduce_scatter | solution.py:205
  1601.8 109.0 %reduce-scatter.11.cloned.1.call-done = f32[16,1536]{1,0:T(8,128)} async-done(((f32[512,1536]{1,0:T(8,128)}), f32[16,1536]{1,0:T(8,128)}) %reduce-scatter.11.cloned.1.call-update) | async-done | bytes 98320 | tf_op jit(solution)/shard_map/reduce_scatter | solution.py:289
  (151 shorter events, 29.7 us)
Async XLA Ops:
  7.2 62.1 %copy-start.2 = (bf16[8,256,512]{2,1,0:T(8,128)(2,1)S(1)}, bf16[8,256,512]{2,1,0:T(8,128)(2,1)}, u32[]{:S(2)}) copy-start(bf16[8,256,512]{2,1,0:T(8,128)(2,1)} %param.10) | copy-start | bytes 6291460
  7.2 62.1 %all-gather.6.cloned.1.call-start = ((), (), s32[]{:S(2)}) async-start(), calls=%async_computation.10 | async-start | bytes 1622016 | tf_op jit(solution)/shard_map/all_gather | solution.py:118
  8.9 176.0 %all-gather.8.cloned.1.call-start = ((), (), s32[]{:S(2)}) async-start(), calls=%async_computation.11 | async-start | bytes 20971520 | tf_op jit(solution)/shard_map/all_gather | solution.py:133
  52.7 106.6 %copy-start.31 = (f32[512]{0:T(512)}, f32[512]{0:T(512)S(1)}, u32[]{:S(2)}) copy-start(f32[512]{0:T(512)S(1)} %convert_element_type.201) | copy-start | bytes 6148
  54.7 104.6 %copy-start.27 = (f32[8,256]{1,0:T(8,128)}, f32[8,256]{1,0:T(8,128)S(1)}, u32[]{:S(2)}) copy-start(f32[8,256]{1,0:T(8,128)S(1)} %broadcast_multiply_fusion.4) | copy-start | bytes 24580
  57.1 102.2 %copy-start.29 = (f32[8,256]{1,0:T(8,128)}, f32[8,256]{1,0:T(8,128)S(1)}, u32[]{:S(2)}) copy-start(f32[8,256]{1,0:T(8,128)S(1)} %add_rsqrt_fusion.1) | copy-start | bytes 24580
  74.4 1.0 copy-start.23
  74.5 339.6 %all-gather.10.cloned.1.call-start = ((), (), s32[]{:S(2)}) async-start(), calls=%async_computation.12 | async-start | bytes 8650752 | tf_op jit(solution)/shard_map/all_gather | solution.py:162
  76.2 7.7 copy-start.24
  76.2 8.5 copy-start.33
  76.3 13.9 copy-start.34
  79.5 230.9 %all-to-all-start.2 = ((bf16[8,8,32,512]{3,2,0,1:T(8,128)(2,1)}), bf16[8,8,32,512]{3,2,0,1:T(8,128)(2,1)}, u32[]{:S(2)}, u32[]{:S(2)}) async-start(bf16[8,8,32,512]{3,2,0,1:T(8,128)(2,1)} %copy.181), calls=%async_computation.2 | async-start | bytes 4194304 | tf_op jit(solution)/shard_map/all_to_all | solution.py:179
  83.9 336.5 %all-gather.12.cloned.1.call-start = ((), (), s32[]{:S(2)}) async-start(), calls=%async_computation.13 | async-start | bytes 8650752 | tf_op jit(solution)/shard_map/all_gather | solution.py:163
  306.9 2.0 copy-start
  308.9 7.0 copy-start.36
  310.4 100.6 %all-to-all-start = ((bf16[8,8,32,512]{3,2,0,1:T(8,128)(2,1)}), bf16[8,8,32,512]{3,2,0,1:T(8,128)(2,1)S(1)}, u32[]{:S(2)}, u32[]{:S(2)}) async-start(bf16[8,8,32,512]{3,2,0,1:T(8,128)(2,1)} %copy.172), calls=%async_computation | async-start | bytes 4194304 | tf_op jit(solution)/shard_map/all_to_all | solution.py:167
  411.0 30.8 %copy-start.8 = (bf16[8,8,32,512]{3,2,0,1:T(8,128)(2,1)}, bf16[8,8,32,512]{3,2,0,1:T(8,128)(2,1)S(1)}, u32[]{:S(2)}) copy-start(bf16[8,8,32,512]{3,2,0,1:T(8,128)(2,1)S(1)} %all-to-all-done) | copy-start | bytes 6291460
  414.0 6.4 copy-start.18
  420.4 5.8 copy-start.12
  420.4 13.1 copy-start.13
  426.2 7.3 copy-start.10
  426.2 10.1 slice-start
  433.5 2.8 copy-start.21
  433.6 2.8 slice-start.1
  436.4 2.7 copy-start.16
  443.4 5.1 copy-start.25
  505.0 52.2 %all-to-all-start.1 = ((bf16[64,1,32,512]{3,2,1,0:T(8,128)(2,1)}), bf16[64,1,32,512]{3,2,1,0:T(8,128)(2,1)}, u32[]{:S(2)}, u32[]{:S(2)}) async-start(bf16[64,1,32,512]{3,2,1,0:T(8,128)(2,1)} %bitcast.196), calls=%async_computation.1 | async-start | bytes 4194304 | tf_op jit(solution)/shard_map/all_to_all | solution.py:175
  509.3 453.9 %reduce-scatter.9.cloned.1.call-start = ((), (), s32[]{:S(2)}) async-start(), calls=%async_computation.14 | async-start | bytes 41943040 | tf_op jit(solution)/shard_map/reduce_scatter | solution.py:263
  557.2 3.1 copy-start.14
  559.5 2.2 copy-start.1
  559.5 3.5 copy-start.5
  566.0 1.9 copy-start.4
  571.7 3.9 copy-start.7
  651.7 16.5 copy-start.6
  730.1 1.6 copy-start.9
  730.1 1.6 copy-start.26
  730.1 368.6 %reduce-scatter.19.cloned.1.call-start = ((), (), s32[]{:S(2)}) async-start(), calls=%async_computation.19 | async-start | bytes 270336
  741.1 6.8 copy-start.17
  741.1 6.8 copy-start.19
  741.2 491.3 %reduce-scatter.13.cloned.1.call-start = ((), (), s32[]{:S(2)}) async-start(), calls=%async_computation.16 | async-start | bytes 1081344 | tf_op jit(solution)/shard_map/reduce_scatter | solution.py:290
  747.9 666.5 %reduce-scatter.15.cloned.1.call-start = ((), (), s32[]{:S(2)}) async-start(), calls=%async_computation.17 | async-start | bytes 17301504 | tf_op jit(solution)/shard_map/reduce_scatter | solution.py:204
  760.3 2.1 copy-start.11
  760.3 2.2 copy-start.22
  760.4 841.5 %reduce-scatter.17.cloned.1.call-start = ((), (), s32[]{:S(2)}) async-start(), calls=%async_computation.18 | async-start | bytes 17301504 | tf_op jit(solution)/shard_map/reduce_scatter | solution.py:205
  773.4 19.2 %copy-start.3 = (bf16[8,256,512]{2,1,0:T(8,128)(2,1)S(1)}, bf16[8,256,512]{2,1,0:T(8,128)(2,1)}, u32[]{:S(2)}) copy-start(bf16[8,256,512]{2,1,0:T(8,128)(2,1)} %param.10) | copy-start | bytes 6291460
  773.4 19.2 %copy-start.28 = (f32[8,256]{1,0:T(8,128)S(1)}, f32[8,256]{1,0:T(8,128)}, u32[]{:S(2)}) copy-start(f32[8,256]{1,0:T(8,128)} %copy-done.27) | copy-start | bytes 24580
  773.4 19.1 %copy-start.30 = (f32[8,256]{1,0:T(8,128)S(1)}, f32[8,256]{1,0:T(8,128)}, u32[]{:S(2)}) copy-start(f32[8,256]{1,0:T(8,128)} %copy-done.29) | copy-start | bytes 24580
  773.4 19.1 %copy-start.32 = (f32[512]{0:T(512)S(1)}, f32[512]{0:T(512)}, u32[]{:S(2)}) copy-start(f32[512]{0:T(512)} %copy-done.31) | copy-start | bytes 6148
  773.4 937.4 %reduce-scatter.11.cloned.1.call-start = ((), (), s32[]{:S(2)}) async-start(), calls=%async_computation.15 | async-start | bytes 3244032 | tf_op jit(solution)/shard_map/reduce_scatter | solution.py:289
  791.2 1.3 copy-start.15
  1100.1 3.1 copy-start.20
  1103.2 8.8 copy-start.35
Sparse Core Ops, SparseCore 0:
  11.5 57.7 all-gather.5
  74.6 110.2 all-gather.7
  188.4 77.3 all-gather.9
  269.2 109.0 all-gather.11
  730.2 232.9 reduce-scatter.8
  965.3 133.3 reduce-scatter.18
  1101.7 130.7 reduce-scatter.12
  1235.4 178.9 reduce-scatter.14
  1417.2 184.5 reduce-scatter.16
  1607.7 103.0 reduce-scatter.10
where the time goes:
time: 1720 us
  waiting for transfers between devices  921 us (54%)
  blocking collectives  298 us (17%)
  matrix products  277 us (16%)
  local copies, waits for them, and re-layouts  97 us (6%)
  other arithmetic  93.7 us (5%)
    reduce_scatter x1, waiting for transfers between devices, on_device(): lax.psum_scatter(grad_shrink, ('dp', 'seq'), scatter_dimension=1, tiled=T...  187 us
    reduce_scatter x1, waiting for transfers between devices, on_device(): lax.psum_scatter(grad_expand, ('dp', 'seq'), scatter_dimension=1, tiled=T...  182 us
    reduce_scatter x1, waiting for transfers between devices, on_device(): lax.psum_scatter(grad_keys_all, 'seq', scatter_dimension=0, tiled=True)  169 us
    unnamed x11, waiting for transfers between devices  128 us
    reduce_scatter x1, waiting for transfers between devices, on_device(): lax.psum_scatter(grad_proj_in, ('dp', 'seq'), scatter_dimension=0, tiled=...  109 us
    all_gather x1, blocking collectives, on_device(): lax.all_gather(w_control.astype(jnp.bfloat16), ('dp', 'seq'), axis=1, til...  90.9 us
    unnamed x2, blocking collectives  79 us
    reduce_scatter x1, waiting for transfers between devices, on_device(): lax.psum_scatter(grad_proj_out, ('dp', 'seq'), scatter_dimension=0, tiled...  77.1 us
  transfers between devices with their start and end apart: 13, of which 9 were waited for; matrix products, arithmetic and copies ran while one was open for 15% of the time, Pallas kernels for 0%

commit v1 on v0

v1 whole, which is shorter than its diff:
```python
import functools
import math

import jax
import jax.numpy as jnp
from jax import lax
from jax.experimental import pallas as pl
from jax.experimental.pallas import tpu as pltpu
from jax.sharding import Mesh
from jax.sharding import PartitionSpec as P

HEADS = 8
GROUP = 32
BLOCK = 256
LANES = 128
VMEM_LIMIT = 60 * 1024 * 1024

LOG2E = math.log2(math.e)
LN2 = math.log(2.0)
BIG = 1e30

bf16 = jnp.bfloat16
f32 = jnp.float32

NN = (((1,), (0,)), ((), ()))
NT = (((1,), (1,)), ((), ()))
TN = (((0,), (0,)), ((), ()))


def dot(a, b, dims=NN):
    return lax.dot_general(a, b, dims, preferred_element_type=f32)


def normalize(values):
    center = values - jnp.mean(values, axis=-1, keepdims=True)
    scaled = lax.rsqrt(jnp.mean(center * center, axis=-1, keepdims=True) + 1e-05)
    return center * scaled, scaled


def norm_back(incoming, normed, scaled):
    return scaled * (
        incoming
        - jnp.mean(incoming, axis=-1, keepdims=True)
        - normed * jnp.mean(incoming * normed, axis=-1, keepdims=True)
    )


def split3(value):
    high = value.astype(bf16).astype(f32)
    rest = value - high
    mid = rest.astype(bf16).astype(f32)
    low = (rest - mid).astype(bf16).astype(f32)
    return high, mid, low


def partner(value, axis, size, mask):
    return lax.ppermute(value, axis, [(i, i ^ mask) for i in range(size)])


def swap_slots(slots, axis):
    size = len(slots)
    return [slots[0]] + [partner(slots[j], axis, size, j) for j in range(1, size)]


def natural(slots, me):
    out = list(slots)
    bit = 1
    while bit < len(out):
        flip = (me & bit) != 0
        out = [jnp.where(flip, out[k ^ bit], out[k]) for k in range(len(out))]
        bit *= 2
    return out


def bits_of(sizes):
    bits = []
    for axis, size in sizes:
        mask = size // 2
        while mask:
            bits.append((axis, size, mask))
            mask //= 2
    return bits


def gather_rows(value, sizes):
    tail = value.shape
    depth = 0
    for axis, size, mask in bits_of(sizes):
        other = partner(value, axis, size, mask)
        high = (lax.axis_index(axis) & mask) != 0
        first, second = jnp.where(high, other, value), jnp.where(high, value, other)
        value = jnp.stack([first, second], axis=depth)
        depth += 1
    return value.reshape((-1,) + tail[1:])


def scatter_rows(value, sizes):
    bits = bits_of(sizes)
    rows = value.shape[0] >> len(bits)
    value = value.reshape((2,) * len(bits) + (rows,) + value.shape[1:])
    for depth in reversed(range(len(bits))):
        axis, size, mask = bits[depth]
        high = ((lax.axis_index(axis) & mask) != 0).astype(jnp.int32)
        keep = lax.dynamic_index_in_dim(value, high, depth, keepdims=False)
        send = lax.dynamic_index_in_dim(value, 1 - high, depth, keepdims=False)
        value = keep.astype(f32) + partner(send.astype(bf16), axis, size, mask).astype(f32)
    return value


def call(kernel, name, grid, in_specs, outs, scratch, args, flops, bytes_accessed):
    return pl.pallas_call(
        kernel,
        grid_spec=pltpu.PrefetchScalarGridSpec(
            num_scalar_prefetch=1,
            grid=grid,
            in_specs=in_specs,
            out_specs=[spec for spec, _, _ in outs],
            scratch_shapes=[pltpu.VMEM(shape, dtype) for shape, dtype in scratch],
        ),
        out_shape=[jax.ShapeDtypeStruct(shape, dtype) for _, shape, dtype in outs],
        compiler_params=pltpu.CompilerParams(vmem_limit_bytes=VMEM_LIMIT),
        cost_estimate=pl.CostEstimate(
            flops=flops, bytes_accessed=bytes_accessed, transcendentals=0
        ),
        name=name,
    )(*args)


def per_row(*shape):
    return pl.BlockSpec((1,) + shape, lambda r, me: (r,) + (0,) * len(shape))


def whole(*shape):
    return pl.BlockSpec(shape, lambda r, me: (0,) * len(shape))


def causal_bias():
    key = lax.broadcasted_iota(jnp.int32, (BLOCK, BLOCK), 0)
    query = lax.broadcasted_iota(jnp.int32, (BLOCK, BLOCK), 1)
    return jnp.where(key <= query, 0.0, -BIG).astype(f32)


def key_features(segment_row, length):
    row = lax.broadcasted_iota(jnp.int32, (LANES, length), 0)
    marks = (row == segment_row) | ((row >= 7) & (row < 10))
    return jnp.where(marks, 1.0, 0.0).astype(f32).T.astype(bf16)


def query_features(segment_row, length):
    row = lax.broadcasted_iota(jnp.int32, (16, length), 0)
    return jnp.where((row < 7) & (row != segment_row), -BIG, 0.0).astype(f32)


def padded_head(head, features, odd):
    blank = jnp.zeros_like(head)
    rest = jnp.zeros((LANES - 16, head.shape[1]), bf16)
    both = [blank, head] if odd else [head, blank]
    return jnp.concatenate(both + [features, rest], axis=0)


def attend_kernel(slot_count, *refs):
    me_ref = refs[0]
    x_refs = refs[1 : 1 + slot_count]
    seg_ref, gain_ref, w_ref = refs[1 + slot_count : 4 + slot_count]
    rest = refs[4 + slot_count :]
    att_refs = rest[:slot_count]
    qt_ref, k_ref, v_ref, q_ref, ot_ref, lse_ref = rest[slot_count : slot_count + 6]
    w_t, k_aux, q_aux, v_t, causal = rest[slot_count + 6 :]
    width = w_ref.shape[0]
    piece = x_refs[0].shape[1]
    length = piece * slot_count
    me = me_ref[0]
    score_scale = LOG2E / math.sqrt(width // HEADS)

    @pl.when(pl.program_id(0) == 0)
    def _():
        w_t[:width] = w_ref[:, :width].T
        w_t[width:] = w_ref[:, 2 * width :].T
        causal[...] = causal_bias()

    segment_row = seg_ref[0]
    q_aux[...] = query_features(segment_row, length)
    k_aux[...] = key_features(segment_row, length)
    gain = gain_ref[...]
    for j in range(slot_count):
        place = pl.ds(pl.multiple_of((me ^ j) * piece, piece), piece)
        normed, _ = normalize(x_refs[j][0].astype(f32))
        first_in = (normed * gain).astype(bf16)
        projected = dot(first_in, w_ref[...])
        q_ref[0, place] = (projected[:, :width] * score_scale).astype(bf16)
        k_ref[0, place] = projected[:, width : 2 * width].astype(bf16)
        v_ref[0, place] = projected[:, 2 * width :].astype(bf16)
        turned = dot(w_t[...], first_in, NT)
        qt_ref[0, :, place] = (turned[:width] * score_scale).astype(bf16)
        v_t[:, place] = turned[width:].astype(bf16)

    def head_pair(pair, carry):
        base = pl.multiple_of(pair * LANES, LANES)
        for odd in range(2):
            rows = pl.ds(pl.multiple_of(pair * LANES + odd * 64, 64), 64)
            for qb in range(length // BLOCK):
                queries = pl.ds(qb * BLOCK, BLOCK)
                feats = q_aux[:, queries].astype(bf16)
                query = padded_head(qt_ref[0, rows, queries], feats, odd)
                scores = []
                for kb in range(qb + 1):
                    keys = pl.ds(kb * BLOCK, BLOCK)
                    key = jnp.concatenate([k_ref[0, keys, pl.ds(base, LANES)], k_aux[keys]], axis=1)
                    score = dot(key, query)
                    scores.append(score + causal[...] if kb == qb else score)
                top = functools.reduce(
                    jnp.maximum, [jnp.max(score, axis=0, keepdims=True) for score in scores]
                )
                total = jnp.zeros((1, BLOCK), f32)
                out = jnp.zeros((64, BLOCK), f32)
                for kb in range(qb + 1):
                    prob = jnp.exp2(scores[kb] - top)
                    total = total + jnp.sum(prob, axis=0, keepdims=True)
                    out = out + dot(v_t[rows, pl.ds(kb * BLOCK, BLOCK)], prob.astype(bf16))
                ot_ref[0, rows, queries] = (out / total).astype(bf16)
                lse_ref[0, pl.ds(pair * 2 + odd, 1), queries] = top + jnp.log2(total)
        return carry

    lax.fori_loop(0, HEADS // 2, head_pair, 0)
    for j in range(slot_count):
        place = pl.ds(pl.multiple_of((me ^ j) * piece, piece), piece)
        att_refs[j][0] = ot_ref[0, :, place].T


def attend(me, x_slots, segment_rows, gain, w_qkv):
    slot_count = len(x_slots)
    rows, piece, width = x_slots[0].shape
    length = piece * slot_count
    outs = [(per_row(piece, width), (rows, piece, width), bf16)] * slot_count + [
        (per_row(width, length), (rows, width, length), bf16),
        (per_row(length, width), (rows, length, width), bf16),
        (per_row(length, width), (rows, length, width), bf16),
        (per_row(length, width), (rows, length, width), bf16),
        (per_row(width, length), (rows, width, length), bf16),
        (per_row(HEADS, length), (rows, HEADS, length), f32),
    ]
    result = call(
        functools.partial(attend_kernel, slot_count),
        "attend",
        (rows,),
        [per_row(piece, width)] * slot_count
        + [per_row(1, length), whole(1, width), whole(width, 3 * width)],
        outs,
        [
            ((2 * width, width), bf16),
            ((length, LANES), bf16),
            ((16, length), f32),
            ((width, length), bf16),
            ((BLOCK, BLOCK), f32),
        ],
        (me, *x_slots, segment_rows, gain, w_qkv),
        rows * length * width * 12000,
        rows * length * width * 16,
    )
    return result[:slot_count], result[slot_count:]


def attend_back_kernel(slot_count, *refs):
    me_ref = refs[0]
    x_refs = refs[1 : 1 + slot_count]
    do_refs = refs[1 + slot_count : 1 + 2 * slot_count]
    rest = refs[1 + 2 * slot_count :]
    seg_ref, gain_ref, w_ref, qt_ref, k_ref, v_ref, q_ref, ot_ref, lse_ref = rest[:9]
    gf_refs = rest[9 : 9 + slot_count]
    dw_ref = rest[9 + slot_count]
    (k_aux, q_aux, v_aux, causal, do, first_t, work_t, k_t, grads, prob, grad_score, delta) = rest[
        10 + slot_count :
    ]
    width = w_ref.shape[0]
    piece = x_refs[0].shape[1]
    length = piece * slot_count
    me = me_ref[0]
    row_id = pl.program_id(0)
    score_scale = 1.0 / math.sqrt(width // HEADS)

    @pl.when(row_id == 0)
    def _():
        causal[...] = causal_bias()
        lane = lax.broadcasted_iota(jnp.int32, (length, LANES), 1)
        v_aux[...] = jnp.where(lane < 3, 1.0, 0.0).astype(bf16)

    segment_row = seg_ref[0]
    q_aux[...] = query_features(segment_row, length)
    k_aux[...] = key_features(segment_row, length)
    gain = gain_ref[...]
    for j in range(slot_count):
        place = pl.ds(pl.multiple_of((me ^ j) * piece, piece), piece)
        normed, _ = normalize(x_refs[j][0].astype(f32))
        first_t[:, place] = (normed * gain).astype(bf16).T
        do[place] = do_refs[j][0]
        turned = do_refs[j][0].T
        work_t[:, place] = turned
        k_t[:, place] = k_ref[0, place].T
        product = turned.astype(f32) * ot_ref[0, :, place].astype(f32)
        delta[:, place] = jnp.sum(product.reshape(HEADS, width // HEADS, piece), axis=1)
    lane = lax.broadcasted_iota(jnp.int32, (1, LANES), 1)
    feature = lax.broadcasted_iota(jnp.int32, (16, BLOCK), 0)
    blocks = length // BLOCK

    def head_pair(pair, carry):
        base = pl.multiple_of(pair * LANES, LANES)
        for odd in range(2):
            rows = pl.ds(pl.multiple_of(pair * LANES + odd * 64, 64), 64)
            head = pl.ds(pair * 2 + odd, 1)
            for qb in range(blocks):
                queries = pl.ds(qb * BLOCK, BLOCK)
                a, b, c = split3(lse_ref[0, head, queries])
                feats = jnp.where(feature == 7, -a, q_aux[:, queries])
                feats = jnp.where(feature == 8, -b, jnp.where(feature == 9, -c, feats))
                query = padded_head(qt_ref[0, rows, queries], feats.astype(bf16), odd)
                a, b, c = split3(delta[head, queries])
                feats = jnp.where(feature == 0, -a, jnp.where(feature == 1, -b, 0.0))
                feats = jnp.where(feature == 2, -c, feats)
                grad = padded_head(work_t[rows, queries], feats.astype(bf16), odd)
                held = pl.ds(odd * length + qb * BLOCK, BLOCK)
                for kb in range(qb + 1):
                    keys = pl.ds(kb * BLOCK, BLOCK)
                    key = jnp.concatenate([k_ref[0, keys, pl.ds(base, LANES)], k_aux[keys]], axis=1)
                    score = dot(key, query)
                    if kb == qb:
                        score = score + causal[...]
                    value = jnp.concatenate(
                        [v_ref[0, keys, pl.ds(base, LANES)], v_aux[keys]], axis=1
                    )
                    grad_prob = dot(value, grad)
                    weight = jnp.exp2(score)
                    prob[keys, held] = weight.astype(bf16)
                    grad_score[keys, held] = (weight * grad_prob).astype(bf16)
                end = (qb + 1) * BLOCK
                grad_q = dot(k_t[rows, 0:end], grad_score[0:end, held])
                work_t[rows, queries] = (grad_q * score_scale).astype(bf16)
        for kb in range(blocks):
            keys = pl.ds(kb * BLOCK, BLOCK)
            later = pl.ds(kb * BLOCK, length - kb * BLOCK)
            grad_v = jnp.zeros((BLOCK, LANES), f32)
            grad_k = jnp.zeros((BLOCK, LANES), f32)
            for odd in range(2):
                mine = (lane >= 64) if odd else (lane < 64)
                held = pl.ds(odd * length + kb * BLOCK, length - kb * BLOCK)
                zero = jnp.zeros((), bf16)
                grad = jnp.where(mine, do[later, pl.ds(base, LANES)], zero)
                query = jnp.where(mine, q_ref[0, later, pl.ds(base, LANES)], zero)
                grad_v = grad_v + dot(prob[keys, held], grad)
                grad_k = grad_k + dot(grad_score[keys, held], query)
            grads[keys, pl.ds(pl.multiple_of(width + pair * LANES, LANES), LANES)] = (
                grad_k * LN2
            ).astype(bf16)
            grads[keys, pl.ds(pl.multiple_of(2 * width + pair * LANES, LANES), LANES)] = (
                grad_v.astype(bf16)
            )
        return carry

    lax.fori_loop(0, HEADS // 2, head_pair, 0)
    for j in range(slot_count):
        place = pl.ds(pl.multiple_of((me ^ j) * piece, piece), piece)
        grads[place, :width] = work_t[:, place].T
        gf_refs[j][0] = dot(grads[place], w_ref[...], NT).astype(bf16)
    update = dot(first_t[...], grads[...])

    @pl.when(row_id == 0)
    def _():
        dw_ref[...] = update

    @pl.when(row_id > 0)
    def _():
        dw_ref[...] += update


def attend_back(me, x_slots, do_slots, segment_rows, gain, w_qkv, saved):
    slot_count = len(x_slots)
    rows, piece, width = x_slots[0].shape
    length = piece * slot_count
    outs = [(per_row(piece, width), (rows, piece, width), bf16)] * slot_count + [
        (whole(width, 3 * width), (width, 3 * width), f32)
    ]
    result = call(
        functools.partial(attend_back_kernel, slot_count),
        "attend_back",
        (rows,),
        [per_row(piece, width)] * (2 * slot_count)
        + [per_row(1, length), whole(1, width), whole(width, 3 * width)]
        + [
            per_row(width, length),
            per_row(length, width),
            per_row(length, width),
            per_row(length, width),
            per_row(width, length),
            per_row(HEADS, length),
        ],
        outs,
        [
            ((length, LANES), bf16),
            ((16, length), f32),
            ((length, LANES), bf16),
            ((BLOCK, BLOCK), f32),
            ((length, width), bf16),
            ((width, length), bf16),
            ((width, length), bf16),
            ((width, length), bf16),
            ((length, 3 * width), bf16),
            ((length, 2 * length), bf16),
            ((length, 2 * length), bf16),
            ((HEADS, length), f32),
        ],
        (me, *x_slots, *do_slots, segment_rows, gain, w_qkv, *saved),
        rows * length * width * 20000,
        rows * length * width * 16,
    )
    return result[:slot_count], result[slot_count]


def middle_of(att_refs, inputs_ref, w_out, me):
    rows, piece, width = att_refs[0].shape
    attended = jnp.concatenate([ref[...] for ref in att_refs], axis=0)
    attended = attended.reshape(-1, width)
    origin = jnp.concatenate(
        [inputs_ref[pl.ds((me ^ j) * rows, rows)] for j in range(len(att_refs))], axis=0
    ).reshape(-1, width)
    return attended, origin.astype(f32) + dot(attended, w_out)


def diagonal(piece):
    place = lax.broadcasted_iota(jnp.int32, (piece, LANES), 0)
    lane = lax.broadcasted_iota(jnp.int32, (piece, LANES), 1)
    return place == lane % piece, lane // piece, lane


def mix_kernel(slot_count, experts, *refs):
    me_ref = refs[0]
    att_refs = refs[1 : 1 + slot_count]
    inputs_ref, cot_ref, w_out_ref, gain_ref, control_ref = refs[1 + slot_count : 6 + slot_count]
    rest = refs[6 + slot_count :]
    pay_refs = rest[:experts]
    second_ref, middle_ref = rest[experts:]
    rows, piece, width = att_refs[0].shape
    tokens = rows * slot_count
    me = me_ref[0]
    _, middle = middle_of(att_refs, inputs_ref, w_out_ref[...], me)
    normed, _ = normalize(middle)
    second = (normed * gain_ref[...]).astype(bf16)
    second_ref[...] = second.reshape(tokens, piece, width)
    middle_ref[...] = middle.reshape(tokens, piece, width)
    grad = jnp.concatenate(
        [cot_ref[pl.ds((me ^ j) * rows, rows)] for j in range(slot_count)], axis=0
    ).reshape(-1, width)
    logits = dot(second, control_ref[...], NT).reshape(tokens, piece, LANES)
    top = jnp.max(logits, axis=0)
    weights = jnp.exp(logits - top)
    total = jnp.sum(weights, axis=0)
    log_total = top + jnp.log(total)
    own, _, lane = diagonal(piece)
    weights = jnp.where(own, weights * (1.0 / total), 0.0)
    spread_out = weights.reshape(-1, LANES).astype(bf16)
    mixed = dot(spread_out, second, TN).astype(bf16)
    grad_results = dot(spread_out, grad, TN).astype(bf16)
    a, b, c = split3(log_total)
    for e in range(experts):
        mine = slice(e * piece, (e + 1) * piece)
        first = slice(e * piece, e * piece + 1)
        stats = jnp.where(lane == 0, a[:, first], jnp.where(lane == 1, b[:, first], c[:, first]))
        pay_refs[e][:, :width] = mixed[mine]
        pay_refs[e][:, width : 2 * width] = grad_results[mine]
        pay_refs[e][:, 2 * width :] = stats.astype(bf16)


def mix(me, att_slots, inputs, cotangent, w_out, gain, control, experts):
    slot_count = len(att_slots)
    rows, positions, width = att_slots[0].shape
    tokens = rows * slot_count
    piece = LANES // experts
    span = pl.BlockSpec((tokens, piece, width), lambda b, me: (0, b, 0))
    pay = (
        pl.BlockSpec((piece, 2 * width + LANES), lambda b, me: (b, 0)),
        (positions, 2 * width + LANES),
        bf16,
    )
    result = call(
        functools.partial(mix_kernel, slot_count, experts),
        "mix",
        (positions // piece,),
        [pl.BlockSpec((rows, piece, width), lambda b, me: (0, b, 0))] * slot_count
        + [span, span, whole(width, width), whole(1, width), whole(LANES, width)],
        [pay] * experts
        + [
            (span, (tokens, positions, width), bf16),
            (span, (tokens, positions, width), f32),
        ],
        [],
        (me, *att_slots, inputs, cotangent, w_out, gain, control),
        tokens * positions * width * 4000,
        tokens * positions * width * 14,
    )
    return result[:experts], result[experts], result[experts + 1]


def expert_kernel(slot_count, *refs):
    pay_refs = refs[1 : 1 + slot_count]
    expand_ref, shrink_ref = refs[1 + slot_count : 3 + slot_count]
    back_ref, grad_expand_ref, grad_shrink_ref = refs[3 + slot_count : 6 + slot_count]
    mixed_acc, grad_acc, mixed_low, grad_low, result_acc, back_acc, stat = refs[6 + slot_count :]
    width = expand_ref.shape[0]
    step = pl.program_id(0)

    @pl.when(step == 0)
    def _():
        logs = []
        for j in range(slot_count):
            stats = pay_refs[j][:, 2 * width :].astype(f32)
            logs.append(stats[:, 0:1] + stats[:, 1:2] + stats[:, 2:3])
        top = functools.reduce(jnp.maximum, logs)
        total = functools.reduce(jnp.add, [jnp.exp(log - top) for log in logs])
        log_total = top + jnp.log(total)
        mixed, grad = 0.0, 0.0
        for j in range(slot_count):
            share = jnp.exp(logs[j] - log_total)
            mixed = mixed + share * pay_refs[j][:, :width].astype(f32)
            grad = grad + share * pay_refs[j][:, width : 2 * width].astype(f32)
        mixed_acc[...] = mixed
        grad_acc[...] = grad
        mixed_low[...] = mixed.astype(bf16)
        grad_low[...] = grad.astype(bf16)
        result_acc[...] = jnp.zeros_like(result_acc)
        back_acc[...] = jnp.zeros_like(back_acc)
        stat[...] = jnp.broadcast_to(log_total, stat.shape)

    mixed, grad = mixed_low[...], grad_low[...]
    expand, shrink = expand_ref[...], shrink_ref[...]
    value = dot(mixed, expand)
    coeff = math.sqrt(2.0 / math.pi)
    square = value * value
    turn = jnp.tanh(coeff * (value + 0.044715 * (square * value)))
    half = 0.5 * (1.0 + turn)
    hidden = (value * half).astype(bf16)
    slope = half + (0.5 * coeff) * value * (1.0 - turn * turn) * (1.0 + (3 * 0.044715) * square)
    result_acc[...] += dot(hidden, shrink)
    grad_pre = (dot(grad, shrink, NT) * slope).astype(bf16)
    back_acc[...] += dot(grad_pre, expand, NT)
    grad_expand_ref[...] = dot(mixed, grad_pre, TN).astype(bf16)
    grad_shrink_ref[...] = dot(hidden, grad, TN).astype(bf16)

    @pl.when(step == pl.num_programs(0) - 1)
    def _():
        results = result_acc[...].astype(bf16)
        back = back_acc[...].astype(bf16)
        back_ref[:, :width] = results
        back_ref[:, width : 2 * width] = back
        inner = jnp.sum(
            results.astype(f32) * grad_acc[...] + back.astype(f32) * mixed_acc[...],
            axis=-1,
            keepdims=True,
        )
        lane = lax.broadcasted_iota(jnp.int32, stat.shape, 1)
        a, b, c = split3(stat[...])
        d, e, f = split3(inner)
        stats = jnp.where(lane == 0, a, jnp.where(lane == 1, b, c))
        stats = jnp.where(lane < 3, stats, jnp.where(lane == 3, d, jnp.where(lane == 4, e, f)))
        back_ref[:, 2 * width :] = stats.astype(bf16)


def expert(me, pay_slots, expand, shrink):
    slot_count = len(pay_slots)
    groups, packed = pay_slots[0].shape
    width, hidden = expand.shape
    chunk = 512
    acc = ((groups, width), f32)
    low = ((groups, width), bf16)
    columns = pl.BlockSpec((width, chunk), lambda f, me: (0, f))
    lines = pl.BlockSpec((chunk, width), lambda f, me: (f, 0))
    return call(
        functools.partial(expert_kernel, slot_count),
        "expert",
        (hidden // chunk,),
        [whole(groups, packed)] * slot_count + [columns, lines],
        [
            (whole(groups, packed), (groups, packed), bf16),
            (columns, (width, hidden), bf16),
            (lines, (hidden, width), bf16),
        ],
        [acc, acc, low, low, acc, acc, ((groups, LANES), f32)],
        (me, *pay_slots, expand, shrink),
        groups * width * hidden * 24,
        width * hidden * 8,
    )


def unmix_kernel(slot_count, experts, *refs):
    me_ref = refs[0]
    ret_refs = refs[1 : 1 + experts]
    att_refs = refs[1 + experts : 1 + experts + slot_count]
    rest = refs[1 + experts + slot_count :]
    second_ref, middle_ref, cot_ref, w_out_ref, gain_ref, control_ref = rest[:6]
    out_ref, grad_middle_ref = rest[6:8]
    back_refs = rest[8 : 8 + slot_count]
    grad_out_ref, grad_control_ref, grad_gain_ref = rest[8 + slot_count :]
    rows, piece, width = att_refs[0].shape
    tokens = rows * slot_count
    me = me_ref[0]

    @pl.when(pl.program_id(0) == 0)
    def _():
        grad_out_ref[...] = jnp.zeros_like(grad_out_ref)
        grad_control_ref[...] = jnp.zeros_like(grad_control_ref)
        grad_gain_ref[...] = jnp.zeros_like(grad_gain_ref)

    second = second_ref[...].reshape(-1, width)
    middle = middle_ref[...].reshape(-1, width)
    cot = jnp.concatenate(
        [cot_ref[pl.ds((me ^ j) * rows, rows)] for j in range(slot_count)], axis=0
    ).reshape(-1, width)
    own, group, _ = diagonal(piece)
    log_total = jnp.zeros((piece, LANES), f32)
    inner = jnp.zeros((piece, LANES), f32)
    for e in range(experts):
        stats = ret_refs[e][:, 2 * width :].astype(f32)
        mine = group == e
        log_total = jnp.where(mine, stats[:, 0:1] + stats[:, 1:2] + stats[:, 2:3], log_total)
        inner = jnp.where(mine, stats[:, 3:4] + stats[:, 4:5] + stats[:, 5:6], inner)
    results = jnp.concatenate([ref[:, :width] for ref in ret_refs], axis=0)
    back = jnp.concatenate([ref[:, width : 2 * width] for ref in ret_refs], axis=0)
    control = control_ref[...]
    logits = dot(second, control, NT).reshape(tokens, piece, LANES)
    weights = jnp.where(own, jnp.exp(logits - log_total), 0.0)
    low = weights.reshape(-1, LANES).astype(bf16)
    output = (middle + dot(low, results).astype(bf16).astype(f32)).astype(bf16)
    grad_weights = (dot(cot, results, NT) + dot(second, back, NT)).reshape(tokens, piece, LANES)
    grad_logits = (weights * (grad_weights - inner)).reshape(-1, LANES).astype(bf16)
    grad_second = dot(low, back) + dot(grad_logits, control)
    grad_second = grad_second.astype(bf16).astype(f32)
    grad_control_ref[...] += dot(grad_logits, second, TN)
    normed, scaled = normalize(middle)
    product = (grad_second * normed).reshape(-1, 8, width)
    grad_gain_ref[...] += jnp.sum(product, axis=0)
    grad_middle = cot.astype(f32) + norm_back(grad_second * gain_ref[...], normed, scaled)
    grad_middle = grad_middle.astype(bf16)
    grad_attended = dot(grad_middle, w_out_ref[...], NT).astype(bf16)
    output = output.reshape(tokens, piece, width)
    grad_attended = grad_attended.reshape(tokens, piece, width)
    grad_middle_ref[...] = grad_middle.reshape(tokens, piece, width)
    for j in range(slot_count):
        mine = slice(j * rows, (j + 1) * rows)
        out_ref[pl.ds((me ^ j) * rows, rows)] = output[mine]
        back_refs[j][...] = grad_attended[mine]
    attended = jnp.concatenate([ref[...] for ref in att_refs], axis=0).reshape(-1, width)
    grad_out_ref[...] += dot(attended, grad_middle, TN)


def unmix(me, ret_slots, att_slots, second, middle, cotangent, w_out, gain, control):
    slot_count, experts = len(att_slots), len(ret_slots)
    rows, positions, width = att_slots[0].shape
    tokens = rows * slot_count
    piece = LANES // experts
    span = pl.BlockSpec((tokens, piece, width), lambda b, me: (0, b, 0))
    part = pl.BlockSpec((rows, piece, width), lambda b, me: (0, b, 0))
    result = call(
        functools.partial(unmix_kernel, slot_count, experts),
        "unmix",
        (positions // piece,),
        [pl.BlockSpec((piece, 2 * width + LANES), lambda b, me: (b, 0))] * experts
        + [part] * slot_count
        + [span, span, span, whole(width, width), whole(1, width), whole(LANES, width)],
        [
            (span, (tokens, positions, width), bf16),
            (span, (tokens, positions, width), bf16),
        ]
        + [(part, (rows, positions, width), bf16)] * slot_count
        + [
            (whole(width, width), (width, width), f32),
            (whole(LANES, width), (LANES, width), f32),
            (whole(8, width), (8, width), f32),
        ],
        [],
        (me, *ret_slots, *att_slots, second, middle, cotangent, w_out, gain, control),
        tokens * positions * width * 6000,
        tokens * positions * width * 20,
    )
    output, grad_middle = result[:2]
    return output, grad_middle, result[2 : 2 + slot_count], result[2 + slot_count :]


def finish_kernel(slot_count, *refs):
    me_ref = refs[0]
    gf_refs = refs[1 : 1 + slot_count]
    inputs_ref, grad_middle_ref, gain_ref, out_ref = refs[1 + slot_count :]
    rows = gf_refs[0].shape[0]
    me = me_ref[0]
    for j in range(slot_count):
        place = pl.ds((me ^ j) * rows, rows)
        normed, scaled = normalize(inputs_ref[place].astype(f32))
        grad = norm_back(gf_refs[j][...].astype(f32) * gain_ref[...], normed, scaled)
        grad = grad + grad_middle_ref[j * rows : (j + 1) * rows].astype(f32)
        out_ref[place] = grad.astype(bf16)


def finish(me, gf_slots, inputs, grad_middle, gain):
    slot_count = len(gf_slots)
    rows, positions, width = gf_slots[0].shape
    tokens = rows * slot_count
    piece = 64
    span = pl.BlockSpec((tokens, piece, width), lambda b, me: (0, b, 0))
    part = pl.BlockSpec((rows, piece, width), lambda b, me: (0, b, 0))
    return call(
        functools.partial(finish_kernel, slot_count),
        "finish",
        (positions // piece,),
        [part] * slot_count + [span, span, whole(1, width)],
        [(span, (tokens, positions, width), bf16)],
        [],
        (me, *gf_slots, inputs, grad_middle, gain),
        tokens * positions * width * 40,
        tokens * positions * width * 8,
    )[0]


def on_device(
    sizes,
    inputs,
    segments,
    cotangent,
    gain_attn,
    w_qkv,
    w_out,
    gain_mix,
    w_control,
    w_expand,
    w_shrink,
):
    groups, members, slots = sizes
    local_rows, positions, width = inputs.shape
    experts = w_expand.shape[0]
    rows = local_rows // slots
    place = (("gq", groups), ("gi", members), ("seq", slots))
    owners = (("gq", groups), ("seq", slots))
    seq_me = lax.axis_index("seq")
    member = lax.axis_index("gi")
    me = seq_me.astype(jnp.int32).reshape(1)

    def row_parts(array):
        return [
            lax.dynamic_slice_in_dim(array, (seq_me ^ j) * rows, rows, axis=0) for j in range(slots)
        ]

    x_slots = swap_slots(row_parts(inputs), "seq")
    segment_rows = jnp.concatenate(natural(swap_slots(row_parts(segments), "seq"), seq_me), axis=1)
    segment_rows = segment_rows[:, None, :]

    small = jnp.concatenate([gain_attn[None], gain_mix[None], w_control], axis=0)
    small = jnp.pad(jnp.transpose(small), ((0, 0), (0, LANES - 2 - experts)))
    packed = jnp.concatenate([w_qkv, w_out, small], axis=1).astype(bf16)
    packed = gather_rows(packed, place)
    proj_in, proj_out = packed[:, : 3 * width], packed[:, 3 * width : 4 * width]
    vectors = jnp.transpose(packed[:, 4 * width :])
    gain_one = vectors[0:1].astype(f32)
    gain_two = vectors[1:2].astype(f32)
    control = natural([vectors[2 + e : 3 + e] for e in range(experts)], member)
    control = jnp.concatenate(
        [jnp.broadcast_to(c, (LANES // experts, width)) for c in control], axis=0
    )

    def to_owner(array):
        array = array.astype(bf16)
        parts = [lax.dynamic_index_in_dim(array, member ^ j, 0, keepdims=False) for j in range(members)]
        array = jnp.stack(natural(swap_slots(parts, "gi"), member))
        array = lax.all_gather(array, ("gq", "seq"), axis=0)
        array = array.reshape((groups, slots) + array.shape[1:])
        array = jnp.swapaxes(array, 1, 2)
        return array.reshape(-1, array.shape[-1])

    expand, shrink = to_owner(w_expand), to_owner(w_shrink)

    att_slots, saved = attend(me, x_slots, segment_rows, gain_one, proj_in)
    att_slots = swap_slots(att_slots, "seq")
    pay_slots, second, middle = mix(
        me, att_slots, inputs, cotangent, proj_out, gain_two, control, experts
    )
    pay_slots = swap_slots(pay_slots, "gi")
    back, grad_expand, grad_shrink = expert(me, pay_slots, expand, shrink)
    ret_slots = swap_slots([back] * members, "gi")
    output, grad_middle, do_slots, sums = unmix(
        me, ret_slots, att_slots, second, middle, cotangent, proj_out, gain_two, control
    )
    grad_out, grad_control, grad_gain = sums

    do_slots = swap_slots(do_slots, "seq")
    gf_slots, grad_in = attend_back(me, x_slots, do_slots, segment_rows, gain_one, proj_in, saved)
    gf_slots = swap_slots(gf_slots, "seq")
    grad_inputs = finish(me, gf_slots, inputs, grad_middle, gain_one)

    def to_places(array):
        lines = array.shape[0] // (groups * members * slots)
        array = array.reshape(groups, members, slots, lines, array.shape[1])
        array = jnp.swapaxes(array, 1, 2).reshape(groups * slots, members, lines, array.shape[-1])
        array = lax.psum_scatter(array, ("gq", "seq"), scatter_dimension=0, tiled=True)[0]
        parts = [lax.dynamic_index_in_dim(array, member ^ j, 0, keepdims=False) for j in range(members)]
        return jnp.stack(natural(swap_slots(parts, "gi"), member)).astype(f32)

    grad_control = grad_control.reshape(experts, LANES // experts, width).sum(axis=1)
    grad_control = jnp.concatenate(
        natural([grad_control[e : e + 1] for e in range(experts)], member), axis=0
    )
    small = jnp.concatenate([grad_gain.sum(axis=0, keepdims=True), grad_control], axis=0)
    small = jnp.pad(jnp.transpose(small), ((0, 0), (0, LANES - 1 - experts)))
    grad_out = scatter_rows(jnp.concatenate([grad_out, small], axis=1), place)
    small = jnp.transpose(grad_out[:, width:])
    grad_in = scatter_rows(grad_in, place)
    weighted = jnp.sum(grad_in * w_qkv.astype(bf16).astype(f32), axis=1)
    return (
        output,
        grad_inputs,
        weighted / gain_attn.astype(bf16).astype(f32),
        grad_in,
        grad_out[:, :width],
        small[0],
        small[1 : 1 + experts],
        to_places(grad_expand),
        to_places(grad_shrink),
    )


def solution(mesh):
    dp_count, seq_count = mesh.shape["dp"], mesh.shape["seq"]

    def run(inputs, *args):
        members = GROUP * dp_count // inputs.shape[0]
        sizes = (dp_count // members, members, seq_count)
        fine = Mesh(mesh.devices.reshape(sizes), ("gq", "gi", "seq"))
        dp, both = ("gq", "gi"), ("gq", "gi", "seq")
        return jax.shard_map(
            functools.partial(on_device, sizes),
            mesh=fine,
            in_specs=(
                P(dp, "seq", None),
                P(dp, "seq"),
                P(dp, "seq", None),
                P(both),
                P(both, None),
                P(both, None),
                P(both),
                P(None, both),
                P(None, both, None),
                P(None, both, None),
            ),
            out_specs=(
                P(dp, "seq", None),
                P(dp, "seq", None),
                P(both),
                P(both, None),
                P(both, None),
                P(both),
                P(None, both),
                P(None, both, None),
                P(None, both, None),
            ),
            check_vma=False,
        )(inputs, *args)

    return run
```

time: 1720 us -> 420 us (0.24)
  waiting for transfers between devices: 921 us -> 161 us
  blocking collectives: 298 us -> 0 us
  matrix products: 277 us -> 0 us
  Pallas kernels: 0 us -> 132 us
  other arithmetic: 93.7 us -> 22.1 us
  local copies, waits for them, and re-layouts: 97 us -> 26.9 us
  starting transfers between devices: 15.1 us -> 61.9 us
    reduce_scatter x5 -> x2, waiting for transfers between devices: 724 us -> 15.7 us  [to_places(): lax.psum_scatter(array, ('gq', 'seq'), scatter_dimension=0, tiled=True)[0]]
    dot_general x27 -> x0, matrix products: 277 us -> none  [the longest x1 45.1 us: on_device(): jnp.einsum('rqhd,krhd->rhqk', grad_heads, value_heads, preferred_element_...]
    all_gather x3 -> x0, blocking collectives: 163 us -> none  [the longest x1 90.9 us: on_device(): lax.all_gather(w_control.astype(jnp.bfloat16), ('dp', 'seq'), axis=1, til...]
    ppermute x0 -> x48, waiting for transfers between devices: none -> 145 us  [partner(): return lax.ppermute(value, axis, [(i, i ^ mask) for i in range(size)])]
    pallas_call x0 -> x6, Pallas kernels: none -> 132 us  [call(): pl.pallas_call(kernel, grid_spec=pltpu.PrefetchScalarGridSpec(num_scalar_...]
    unnamed x11 -> x4, waiting for transfers between devices: 128 us -> 0.07 us
    unnamed x2 -> x0, blocking collectives: 79 us -> none
    ppermute x0 -> x48, starting transfers between devices: none -> 61.7 us  [partner(): return lax.ppermute(value, axis, [(i, i ^ mask) for i in range(size)])]
  transfers between devices with their start and end apart: 13 -> 52, of which waited for: 9 -> 27; matrix products, arithmetic and copies ran while one was open for 15% -> 8% of each run, Pallas kernels for 0% -> 25%
where the time goes in v1:
time: 420 us; the launch traced here: 418 us
  waiting for transfers between devices  161 us (38%)
  Pallas kernels  132 us (31%)
  starting transfers between devices  61.9 us (15%)
  local copies, waits for them, and re-layouts  26.9 us (6%)
  other arithmetic  22.1 us (5%)
  between operations  14.2 us (3%)
    ppermute x48, waiting for transfers between devices, partner(): return lax.ppermute(value, axis, [(i, i ^ mask) for i in range(size)])  145 us
    pallas_call x6, Pallas kernels, call(): pl.pallas_call(kernel, grid_spec=pltpu.PrefetchScalarGridSpec(num_scalar_...  132 us
    ppermute x48, starting transfers between devices, partner(): return lax.ppermute(value, axis, [(i, i ^ mask) for i in range(size)])  61.7 us
    reduce_scatter x2, waiting for transfers between devices, to_places(): lax.psum_scatter(array, ('gq', 'seq'), scatter_dimension=0, tiled=True)[0]  15.7 us
  transfers between devices with their start and end apart: 52, of which 27 were waited for; matrix products, arithmetic and copies ran while one was open for 8% of the time, Pallas kernels for 25%

profile of v1, /device:TPU:0, one launch (start us, length us, event | category | flops | bytes accessed | tf_op | source)
XLA Modules:
  0.0 418.3 jit_solution(472213488529181304)
XLA Ops:
  10.4 4.1 collective-permute-start.6
  14.5 1.1 convert_element_type.143
  15.6 2.7 collective-permute-done.6
  19.0 2.6 collective-permute-start.17
  22.6 2.2 collective-permute-done.7
  27.9 3.6 collective-permute-done.8
  31.6 1.6 collective-permute-start.9
  33.2 12.6 %collective-permute-done.9 = bf16[2,2,2,16,2176]{4,3,2,1,0:T(8,128)(2,1)S(1)} collective-permute-done((bf16[2,2,2,16,2176]{4,3,2,1,0:T(8,128)(2,1)S(1)}, bf16[2,2,2,16,2176]{4,3,2,1,0:T(8,128)(2,1)S(1)}, u32[]{:S(2)}, u32[]{:S(2)}) %collective-permute-start.9) | collective-permute-done | bytes 557088 | tf_op jit(solution)/shard_map/ppermute | solution.py:57
  45.9 1.1 pad_maximum_fusion.1
  47.1 1.7 collective-permute-start.3
  49.3 1.4 constant_dynamic-slice_fusion.6
  51.2 3.3 collective-permute-start.20
  54.8 1.4 collective-permute-start.22
  57.1 1.7 collective-permute-start.1
  60.2 1.5 select_bitcast_fusion.1
  62.0 1.3 slice.70.refs_7_.refs_11_
  64.0 8.2 %collective-permute-done.1.refs_3_ = bf16[2,256,512]{2,1,0:T(8,128)(2,1)S(1)} collective-permute-done((bf16[2,256,512]{2,1,0:T(8,128)(2,1)}, bf16[2,256,512]{2,1,0:T(8,128)(2,1)S(1)}, u32[]{:S(2)}, u32[]{:S(2)}) %collective-permute-start.1) | collective-permute-done | bytes 524320 | tf_op jit(solution)/shard_map/ppermute | solution.py:57
  72.2 11.8 %collective-permute-done.2.refs_4_ = bf16[2,256,512]{2,1,0:T(8,128)(2,1)} collective-permute-done((bf16[2,256,512]{2,1,0:T(8,128)(2,1)}, bf16[2,256,512]{2,1,0:T(8,128)(2,1)}, u32[]{:S(2)}, u32[]{:S(2)}) %collective-permute-start.2) | collective-permute-done | bytes 524320 | tf_op jit(solution)/shard_map/ppermute | solution.py:57
  84.0 35.6 %attend.1 = (bf16[2,256,512]{2,1,0:T(8,128)(2,1)}, bf16[2,256,512]{2,1,0:T(8,128)(2,1)}, bf16[2,256,512]{2,1,0:T(8,128)(2,1)}, bf16[2,256,512]{2,1,0:T(8,128)(2,...) custom-call(s32[1]{0:T(128)} %bitcast.refs_0_, ...), custom_call_target="tpu_custom_call" | custom-call | flops 12582912000 | bytes 16777216 | tf_op jit(solution)/shard_map/attend/pallas_call | solution.py:111
  120.3 1.7 collective-permute-start.12
  123.5 11.7 %collective-permute-done.12.refs_3_.refs_7_ = bf16[2,256,512]{2,1,0:T(8,128)(2,1)S(1)} collective-permute-done((bf16[2,256,512]{2,1,0:T(8,128)(2,1)}, bf16[2,256,512]{2,1,0:T(8,128)(2,1)S(1)}, u32[]{:S(2)}, u32[]{:S(2)}) %collective-permute-start.12) | collective-permute-done | bytes 524320 | tf_op jit(solution)/shard_map/ppermute | solution.py:57
  135.3 9.7 %collective-permute-done.13.refs_4_.refs_8_ = bf16[2,256,512]{2,1,0:T(8,128)(2,1)S(1)} collective-permute-done((bf16[2,256,512]{2,1,0:T(8,128)(2,1)}, bf16[2,256,512]{2,1,0:T(8,128)(2,1)S(1)}, u32[]{:S(2)}, u32[]{:S(2)}) %collective-permute-start.13) | collective-permute-done | bytes 524320 | tf_op jit(solution)/shard_map/ppermute | solution.py:57
  145.8 12.3 %mix.1 = (bf16[256,1152]{1,0:T(8,128)(2,1)}, bf16[256,1152]{1,0:T(8,128)(2,1)}, bf16[256,1152]{1,0:T(8,128)(2,1)}, bf16[256,1152]{1,0:T(8,128)(2,1)}, bf16[8,256...) custom-call(s32[1]{0:T(128)} %bitcast.refs_0_, bf16[2,256,512]{2,1,0:T(8,128)(2,1)} %get-tuple-element.42.refs_1_.refs_5_, ...), custom_call_target="tpu_custom_call" | custom-call | flops 4194304000 | bytes 14680064 | tf_op jit(solution)/shard_map/mix/pallas_call | solution.py:111
  158.1 1.1 collective-permute-start.14
  159.2 3.0 collective-permute-start.15
  162.7 3.2 copy.93
  165.8 3.1 copy.94
  168.9 5.1 %collective-permute-done.14.refs_2_ = bf16[256,1152]{1,0:T(8,128)(2,1)S(1)} collective-permute-done((bf16[256,1152]{1,0:T(8,128)(2,1)}, bf16[256,1152]{1,0:T(8,128)(2,1)S(1)}, u32[]{:S(2)}, u32[]{:S(2)}) %collective-permute-start.14) | collective-permute-done | bytes 589856 | tf_op jit(solution)/shard_map/ppermute | solution.py:57
  174.0 2.4 collective-permute-done.15.refs_3_
  176.5 12.9 %collective-permute-done.16.refs_4_ = bf16[256,1152]{1,0:T(8,128)(2,1)S(1)} collective-permute-done((bf16[256,1152]{1,0:T(8,128)(2,1)}, bf16[256,1152]{1,0:T(8,128)(2,1)S(1)}, u32[]{:S(2)}, u32[]{:S(2)}) %collective-permute-start.16) | collective-permute-done | bytes 589856 | tf_op jit(solution)/shard_map/ppermute | solution.py:57
  190.2 9.7 %expert.1 = (bf16[256,1152]{1,0:T(8,128)(2,1)}, bf16[512,2048]{1,0:T(8,128)(2,1)}, bf16[2048,512]{1,0:T(8,128)(2,1)}) custom-call(s32[1]{0:T(128)} %bitcast.refs_0_, bf16[256,1152]{1,0:T(8,128)(2,1)} %get-tuple-element.46.refs_1_, bf16[256,1152]{1,0:T(8,128)(2,1)} %copy-done.12, bf16[256,1152]{1,0:T(8,128)(2,1)} %copy-done.13, bf16[256,1152]{1,0:T(8,128)(2,1)} %copy-done.14, ...), custom_call_target="tpu_custom_call" | custom-call | flops 6442450944 | bytes 8388608 | tf_op jit(solution)/shard_map/expert/pallas_call | solution.py:111
  200.7 1.8 collective-permute-start.24
  202.5 1.0 collective-permute-start.25
  203.4 12.1 %collective-permute-done.23.refs_2_ = bf16[256,1152]{1,0:T(8,128)(2,1)S(1)} collective-permute-done((bf16[256,1152]{1,0:T(8,128)(2,1)}, bf16[256,1152]{1,0:T(8,128)(2,1)S(1)}, u32[]{:S(2)}, u32[]{:S(2)}) %collective-permute-start.23) | collective-permute-done | bytes 589856 | tf_op jit(solution)/shard_map/ppermute | solution.py:57
  215.5 1.7 collective-permute-done.24.refs_3_
  217.2 11.8 %collective-permute-done.25.refs_4_ = bf16[256,1152]{1,0:T(8,128)(2,1)S(1)} collective-permute-done((bf16[256,1152]{1,0:T(8,128)(2,1)}, bf16[256,1152]{1,0:T(8,128)(2,1)S(1)}, u32[]{:S(2)}, u32[]{:S(2)}) %collective-permute-start.25) | collective-permute-done | bytes 589856 | tf_op jit(solution)/shard_map/ppermute | solution.py:57
  229.8 16.7 %unmix.1 = (bf16[8,256,512]{2,1,0:T(8,128)(2,1)}, bf16[8,256,512]{2,1,0:T(8,128)(2,1)}, bf16[2,256,512]{2,1,0:T(8,128)(2,1)}, bf16[2,256,512]{2,1,0:T(8,128)(2,1...) custom-call(s32[1]{0:T(128)} %bitcast.refs_0_, ...), custom_call_target="tpu_custom_call" | custom-call | flops 6291456000 | bytes 20971520 | tf_op jit(solution)/shard_map/unmix/pallas_call | solution.py:111
  246.5 1.0 bitcast_reduce_fusion
  249.1 1.5 select_maximum_fusion
  252.0 1.5 collective-permute-start.27
  253.5 1.5 copy.100
  255.1 1.0 bitcast_add_fusion.2
  256.2 1.4 collective-permute-start.38
  257.6 9.5 %collective-permute-done.27.refs_7_ = bf16[2,256,512]{2,1,0:T(8,128)(2,1)} collective-permute-done((bf16[2,256,512]{2,1,0:T(8,128)(2,1)}, bf16[2,256,512]{2,1,0:T(8,128)(2,1)}, u32[]{:S(2)}, u32[]{:S(2)}) %collective-permute-start.27) | collective-permute-done | bytes 524320 | tf_op jit(solution)/shard_map/ppermute | solution.py:57
  267.1 10.3 %collective-permute-done.28.refs_8_ = bf16[2,256,512]{2,1,0:T(8,128)(2,1)} collective-permute-done((bf16[2,256,512]{2,1,0:T(8,128)(2,1)}, bf16[2,256,512]{2,1,0:T(8,128)(2,1)}, u32[]{:S(2)}, u32[]{:S(2)}) %collective-permute-start.28) | collective-permute-done | bytes 524320 | tf_op jit(solution)/shard_map/ppermute | solution.py:57
  277.4 51.9 %attend_back.1 = (bf16[2,256,512]{2,1,0:T(8,128)(2,1)}, bf16[2,256,512]{2,1,0:T(8,128)(2,1)}, bf16[2,256,512]{2,1,0:T(8,128)(2,1)}, bf16[2,256,512]{2,1,0:T(8,128)(2,1)}, f32[512,1536]{1,0:T(8,128)}) custom-call(s32[1]{0:T(128)} %bitcast.refs_0_, bf16[2,256,512]{2,1,0:T(8,128)(2,1)} %get-tuple-element.131.refs_1_, bf16[2,256,512]{2,1,0:T(8,128)(2,1)} %copy-done.15, ...), custom_call_target="tpu_custom_call" | custom-call | flops 20971520000 | bytes 16777216 | tf_op jit(solution)/shard_map/attend_back/pallas_call | solution.py:111
  329.3 1.5 fusion
  332.5 3.8 collective-permute-done.39
  336.3 1.7 bitcast_add_fusion
  338.7 1.5 collective-permute-start.33
  340.3 1.6 collective-permute-start.40
  341.8 3.2 copy.99
  345.7 1.2 collective-permute-start.31
  347.0 9.0 %collective-permute-start.41 = (bf16[16,640]{1,0:T(8,128)(2,1)S(1)}, bf16[16,640]{1,0:T(8,128)(2,1)S(1)}, u32[]{:S(2)}, u32[]{:S(2)}) collective-permute-start(bf16[16,640]{1,0:T(8,128)(2,1)S(1)} %fusion.11), channel_id=1, source_target_pairs={{0,16},{16,0},{1,17},{17,1},{2,18},{18,2},{3,19},{19,3},{4,20},{20... | collective-permute-start | bytes 61448 | tf_op jit(solution)/shard_map/ppermute | solution.py:57
  356.1 1.1 bitcast_add_fusion.1
  357.2 1.6 collective-permute-start.34
  358.8 5.4 %collective-permute-done.34 = bf16[2,2,16,1536]{3,2,0,1:T(8,128)(2,1)S(1)} collective-permute-done((bf16[2,2,16,1536]{3,2,0,1:T(8,128)(2,1)S(1)}, bf16[2,2,16,1536]{3,2,0,1:T(8,128)(2,1)S(1)}, u32[]{:S(2)}, u32[]{:S(2)}) %collective-permute-start.34) | collective-permute-done | bytes 196640 | tf_op jit(solution)/shard_map/ppermute | solution.py:57
  364.8 4.1 collective-permute-done.35
  369.0 2.0 collective-permute-start.36
  374.1 6.2 %finish.1 = bf16[8,256,512]{2,1,0:T(8,128)(2,1)} custom-call(s32[1]{0:T(128)} %bitcast.refs_0_, bf16[2,256,512]{2,1,0:T(8,128)(2,1)} %get-tuple-element.64.refs_1_, bf16[2,256,512]{2,1,0:T(8,128)(2,1)} %copy-done.2, bf16[2,256,512]{2,1,0:T(8,128)(2,1)} %copy-done.3, bf16[2,256,512]{2,1,0:T(8,128)(2,1)} %copy-done.4, bf16[8,256,512]{2,1,0:T(8,128)(2,1)} %refs_5_.3, ...), custom_call_target="tpu_custom_call" | custom-call | flops 41943040 | bytes 8388608 | tf_op jit(solution)/shard_map/finish/pallas_call | solution.py:111
  382.5 3.4 collective-permute-start.45
  386.6 15.7 %reduce-scatter.3.cloned.1.call-done = bf16[1,4,16,2048]{3,2,1,0:T(8,128)(2,1)} async-done(((bf16[8,4,16,2048]{3,2,1,0:T(8,128)(2,1)}), bf16[1,4,16,2048]{3,2,1,0:T(8,128)(2,1)}) %reduce-scatter.3.cloned.1.call-update) | async-done | bytes 262160 | tf_op jit(solution)/shard_map/reduce_scatter | solution.py:797
  403.2 2.3 collective-permute-start.42
  408.7 1.1 collective-permute-done.43
  (172 shorter events, 37.6 us)
Async XLA Ops:
  7.2 155.5 %all-gather.5.cloned.1.call-start = ((), (), s32[]{:S(2)}) async-start(), calls=%async_computation.4 | async-start | bytes 2359296 | tf_op jit(solution)/shard_map/all_gather | solution.py:768
  10.4 7.9 %collective-permute-start.6 = (bf16[16,2176]{1,0:T(8,128)(2,1)S(1)}, bf16[16,2176]{1,0:T(8,128)(2,1)S(1)}, u32[]{:S(2)}, u32[]{:S(2)}) collective-permute-start(bf16[16,2176]{1,0:T(8,128)(2,1)S(1)} %fusion.8), channel_id=1, source_target_pairs={{0,16},{16,0},{1,17},{17,1},{2,18},{18,2},{3,19},{19,3},{4,20},{20... | collective-permute-start | bytes 208904 | tf_op jit(solution)/shard_map/ppermute | solution.py:57
  18.3 6.5 %collective-permute-start.7 = (bf16[2,16,2176]{2,1,0:T(8,128)(2,1)S(1)}, bf16[2,16,2176]{2,1,0:T(8,128)(2,1)S(1)}, u32[]{:S(2)}, u32[]{:S(2)}) collective-permute-start(bf16[2,16,2176]{2,1,0:T(8,128)(2,1)S(1)} %pad_maximum_fusion.6), channel_id=1, source_target_pairs={{0,8},{4,12},{8,0},{12,4},{1,9},{5,13},{9,1},{13,5},{2,10},{6,14},... | collective-permute-start | bytes 417800 | tf_op jit(solution)/shard_map/ppermute | solution.py:57
  19.0 6.6 %collective-permute-start.17 = (bf16[16,2048]{1,0:T(8,128)(2,1)S(1)}, bf16[16,2048]{1,0:T(8,128)(2,1)S(1)}, u32[]{:S(2)}, u32[]{:S(2)}) collective-permute-start(bf16[16,2048]{1,0:T(8,128)(2,1)S(1)} %get-tuple-element.165), channel_id=1, source_target_pairs={{0,12},{4,8},{8,4},{12,0},{1,13},{5,9},{9,5},{13,1},{2,14},{6,10},... | collective-permute-start | bytes 196616 | tf_op jit(solution)/shard_map/ppermute | solution.py:57
  21.6 4.6 %collective-permute-start.18 = (bf16[16,2048]{1,0:T(8,128)(2,1)S(1)}, bf16[16,2048]{1,0:T(8,128)(2,1)S(1)}, u32[]{:S(2)}, u32[]{:S(2)}) collective-permute-start(bf16[16,2048]{1,0:T(8,128)(2,1)S(1)} %get-tuple-element.164), channel_id=1, source_target_pairs={{0,8},{4,12},{8,0},{12,4},{1,9},{5,13},{9,1},{13,5},{2,10},{6,14},... | collective-permute-start | bytes 196616 | tf_op jit(solution)/shard_map/ppermute | solution.py:57
  22.0 5.0 %collective-permute-start.19 = (bf16[16,2048]{1,0:T(8,128)(2,1)S(1)}, bf16[16,2048]{1,0:T(8,128)(2,1)S(1)}, u32[]{:S(2)}, u32[]{:S(2)}) collective-permute-start(bf16[16,2048]{1,0:T(8,128)(2,1)S(1)} %get-tuple-element.163), channel_id=1, source_target_pairs={{0,4},{4,0},{8,12},{12,8},{1,5},{5,1},{9,13},{13,9},{2,6},{6,2},{1... | collective-permute-start | bytes 196616 | tf_op jit(solution)/shard_map/ppermute | solution.py:57
  24.9 6.6 %collective-permute-start.8 = (bf16[2,2,16,2176]{3,2,1,0:T(8,128)(2,1)S(1)}, bf16[2,2,16,2176]{3,2,1,0:T(8,128)(2,1)S(1)}, u32[]{:S(2)}, u32[]{:S(2)}) collective-permute-start(bf16[2,2,16,2176]{3,2,1,0:T(8,128)(2,1)S(1)} %pad_maximum_fusion.3), channel_id=1, source_target_pairs={{0,4},{4,0},{8,12},{12,8},{1,5},{5,1},{9,13},{13,9},{2,6},{6,2},{1... | collective-permute-start | bytes 835592 | tf_op jit(solution)/shard_map/ppermute | solution.py:57
  27.8 138.0 %all-gather.7.cloned.1.call-start = ((), (), s32[]{:S(2)}) async-start(), calls=%async_computation.5 | async-start | bytes 2359296 | tf_op jit(solution)/shard_map/all_gather | solution.py:768
  31.6 14.2 %collective-permute-start.9 = (bf16[2,2,2,16,2176]{4,3,2,1,0:T(8,128)(2,1)S(1)}, bf16[2,2,2,16,2176]{4,3,2,1,0:T(8,128)(2,1)S(1)}, u32[]{:S(2)}, u32[]{:S(2)}) collective-permute-start(bf16[2,2,2,16,2176]{4,3,2,1,0:T(8,128)(2,1)S(1)} %pad_maximum_fusion.2), channel_id=1, source_target_pairs={{0,2},{1,3},{2,0},{3,1},{4,6},{5,7},{6,4},{7,5},{8,10},{9,11},{10,... | collective-permute-start | bytes 1671176 | tf_op jit(solution)/shard_map/ppermute | solution.py:57
  45.9 3.3 copy-start
  47.0 13.1 %collective-permute-start.10 = (bf16[2,2,2,2,16,2176]{5,4,3,2,1,0:T(8,128)(2,1)}, bf16[2,2,2,2,16,2176]{5,4,3,2,1,0:T(8,128)(2,1)}, u32[]{:S(2)}, u32[]{:S(2)}) collective-permute-start(bf16[2,2,2,2,16,2176]{5,4,3,2,1,0:T(8,128)(2,1)} %pad_maximum_fusion.1), channel_id=1, source_target_pairs={{0,1},{1,0},{2,3},{3,2},{4,5},{5,4},{6,7},{7,6},{8,9},{9,8},{10,11... | collective-permute-start | bytes 3342344 | tf_op jit(solution)/shard_map/ppermute | solution.py:57
  47.1 4.2 collective-permute-start.3
  48.8 5.8 %collective-permute-start.4 = (s32[2,256]{1,0:T(2,128)S(1)}, s32[2,256]{1,0:T(2,128)S(1)}, u32[]{:S(2)}, u32[]{:S(2)}) collective-permute-start(s32[2,256]{1,0:T(2,128)S(1)} %get-tuple-element.179), channel_id=1, source_target_pairs={{0,2},{1,3},{2,0},{3,1},{4,6},{5,7},{6,4},{7,5},{8,10},{9,11},{10,... | collective-permute-start | bytes 6152 | tf_op jit(solution)/shard_map/ppermute | solution.py:57
  49.3 5.5 %collective-permute-start.5 = (s32[2,256]{1,0:T(2,128)S(1)}, s32[2,256]{1,0:T(2,128)S(1)}, u32[]{:S(2)}, u32[]{:S(2)}) collective-permute-start(s32[2,256]{1,0:T(2,128)S(1)} %get-tuple-element.178), channel_id=1, source_target_pairs={{0,1},{1,0},{2,3},{3,2},{4,5},{5,4},{6,7},{7,6},{8,9},{9,8},{10,11... | collective-permute-start | bytes 6152 | tf_op jit(solution)/shard_map/ppermute | solution.py:57
  50.6 13.3 %collective-permute-start = (bf16[2,256,512]{2,1,0:T(8,128)(2,1)}, bf16[2,256,512]{2,1,0:T(8,128)(2,1)S(1)}, u32[]{:S(2)}, u32[]{:S(2)}) collective-permute-start(bf16[2,256,512]{2,1,0:T(8,128)(2,1)} %get-tuple-element.130), channel_id=1, source_target_pairs={{0,1},{1,0},{2,3},{3,2},{4,5},{5,4},{6,7},{7,6},{8,9},{9,8},{10,11... | collective-permute-start | bytes 1572872 | tf_op jit(solution)/shard_map/ppermute | solution.py:57
  51.2 5.9 %collective-permute-start.20 = (bf16[64,512]{1,0:T(8,128)(2,1)S(1)}, bf16[64,512]{1,0:T(8,128)(2,1)S(1)}, u32[]{:S(2)}, u32[]{:S(2)}) collective-permute-start(bf16[64,512]{1,0:T(8,128)(2,1)S(1)} %get-tuple-element.162), channel_id=1, source_target_pairs={{0,12},{4,8},{8,4},{12,0},{1,13},{5,9},{9,5},{13,1},{2,14},{6,10},... | collective-permute-start | bytes 196616 | tf_op jit(solution)/shard_map/ppermute | solution.py:57
  54.6 4.3 %collective-permute-start.21 = (bf16[64,512]{1,0:T(8,128)(2,1)S(1)}, bf16[64,512]{1,0:T(8,128)(2,1)S(1)}, u32[]{:S(2)}, u32[]{:S(2)}) collective-permute-start(bf16[64,512]{1,0:T(8,128)(2,1)S(1)} %get-tuple-element.161), channel_id=1, source_target_pairs={{0,8},{4,12},{8,0},{12,4},{1,9},{5,13},{9,1},{13,5},{2,10},{6,14},... | collective-permute-start | bytes 196616 | tf_op jit(solution)/shard_map/ppermute | solution.py:57
  54.8 4.5 %collective-permute-start.22 = (bf16[64,512]{1,0:T(8,128)(2,1)S(1)}, bf16[64,512]{1,0:T(8,128)(2,1)S(1)}, u32[]{:S(2)}, u32[]{:S(2)}) collective-permute-start(bf16[64,512]{1,0:T(8,128)(2,1)S(1)} %get-tuple-element.160), channel_id=1, source_target_pairs={{0,4},{4,0},{8,12},{12,8},{1,5},{5,1},{9,13},{13,9},{2,6},{6,2},{1... | collective-permute-start | bytes 196616 | tf_op jit(solution)/shard_map/ppermute | solution.py:57
  57.1 15.1 %collective-permute-start.1 = (bf16[2,256,512]{2,1,0:T(8,128)(2,1)}, bf16[2,256,512]{2,1,0:T(8,128)(2,1)S(1)}, u32[]{:S(2)}, u32[]{:S(2)}) collective-permute-start(bf16[2,256,512]{2,1,0:T(8,128)(2,1)} %get-tuple-element.129), channel_id=1, source_target_pairs={{0,2},{1,3},{2,0},{3,1},{4,6},{5,7},{6,4},{7,5},{8,10},{9,11},{10,... | collective-permute-start | bytes 1572872 | tf_op jit(solution)/shard_map/ppermute | solution.py:57
  58.8 25.2 %collective-permute-start.2 = (bf16[2,256,512]{2,1,0:T(8,128)(2,1)}, bf16[2,256,512]{2,1,0:T(8,128)(2,1)}, u32[]{:S(2)}, u32[]{:S(2)}) collective-permute-start(bf16[2,256,512]{2,1,0:T(8,128)(2,1)} %get-tuple-element.128), channel_id=1, source_target_pairs={{0,3},{1,2},{2,1},{3,0},{4,7},{5,6},{6,5},{7,4},{8,11},{9,10},{10,... | collective-permute-start | bytes 1572872 | tf_op jit(solution)/shard_map/ppermute | solution.py:57
  60.1 321.5 %reduce-scatter.5.cloned.1.call-start = ((), (), s32[]{:S(2)}) async-start(), calls=%async_computation.3 | async-start | bytes 2359296 | tf_op jit(solution)/shard_map/reduce_scatter | solution.py:797
  64.0 20.0 %copy-start.15 = (bf16[2,256,512]{2,1,0:T(8,128)(2,1)}, bf16[2,256,512]{2,1,0:T(8,128)(2,1)S(1)}, u32[]{:S(2)}) copy-start(bf16[2,256,512]{2,1,0:T(8,128)(2,1)S(1)} %collective-permute-done.refs_2_) | copy-start | bytes 1572868
  72.2 11.8 %copy-start.16 = (bf16[2,256,512]{2,1,0:T(8,128)(2,1)}, bf16[2,256,512]{2,1,0:T(8,128)(2,1)S(1)}, u32[]{:S(2)}) copy-start(bf16[2,256,512]{2,1,0:T(8,128)(2,1)S(1)} %collective-permute-done.1.refs_3_) | copy-start | bytes 1572868
  119.6 3.9 collective-permute-start.11
  120.3 15.0 %collective-permute-start.12 = (bf16[2,256,512]{2,1,0:T(8,128)(2,1)}, bf16[2,256,512]{2,1,0:T(8,128)(2,1)S(1)}, u32[]{:S(2)}, u32[]{:S(2)}) collective-permute-start(bf16[2,256,512]{2,1,0:T(8,128)(2,1)} %get-tuple-element.44), channel_id=1, source_target_pairs={{0,2},{1,3},{2,0},{3,1},{4,6},{5,7},{6,4},{7,5},{8,10},{9,11},{10,... | collective-permute-start | bytes 1572872 | tf_op jit(solution)/shard_map/ppermute | solution.py:57
  122.0 23.0 %collective-permute-start.13 = (bf16[2,256,512]{2,1,0:T(8,128)(2,1)}, bf16[2,256,512]{2,1,0:T(8,128)(2,1)S(1)}, u32[]{:S(2)}, u32[]{:S(2)}) collective-permute-start(bf16[2,256,512]{2,1,0:T(8,128)(2,1)} %get-tuple-element.45), channel_id=1, source_target_pairs={{0,3},{1,2},{2,1},{3,0},{4,7},{5,6},{6,5},{7,4},{8,11},{9,10},{10,... | collective-permute-start | bytes 1572872 | tf_op jit(solution)/shard_map/ppermute | solution.py:57
  123.5 21.5 %copy-start.17 = (bf16[2,256,512]{2,1,0:T(8,128)(2,1)}, bf16[2,256,512]{2,1,0:T(8,128)(2,1)S(1)}, u32[]{:S(2)}) copy-start(bf16[2,256,512]{2,1,0:T(8,128)(2,1)S(1)} %collective-permute-done.11.refs_2_.refs_6_) | copy-start | bytes 1572868
  135.3 9.7 %copy-start.18 = (bf16[2,256,512]{2,1,0:T(8,128)(2,1)}, bf16[2,256,512]{2,1,0:T(8,128)(2,1)S(1)}, u32[]{:S(2)}) copy-start(bf16[2,256,512]{2,1,0:T(8,128)(2,1)S(1)} %collective-permute-done.12.refs_3_.refs_7_) | copy-start | bytes 1572868
  158.1 16.0 %collective-permute-start.14 = (bf16[256,1152]{1,0:T(8,128)(2,1)}, bf16[256,1152]{1,0:T(8,128)(2,1)S(1)}, u32[]{:S(2)}, u32[]{:S(2)}) collective-permute-start(bf16[256,1152]{1,0:T(8,128)(2,1)} %get-tuple-element.47), channel_id=1, source_target_pairs={{0,4},{4,0},{8,12},{12,8},{1,5},{5,1},{9,13},{13,9},{2,6},{6,2},{1... | collective-permute-start | bytes 1769480 | tf_op jit(solution)/shard_map/ppermute | solution.py:57
  159.2 17.3 %collective-permute-start.15 = (bf16[256,1152]{1,0:T(8,128)(2,1)}, bf16[256,1152]{1,0:T(8,128)(2,1)S(1)}, u32[]{:S(2)}, u32[]{:S(2)}) collective-permute-start(bf16[256,1152]{1,0:T(8,128)(2,1)} %get-tuple-element.48), channel_id=1, source_target_pairs={{0,8},{4,12},{8,0},{12,4},{1,9},{5,13},{9,1},{13,5},{2,10},{6,14},... | collective-permute-start | bytes 1769480 | tf_op jit(solution)/shard_map/ppermute | solution.py:57
  162.2 27.2 %collective-permute-start.16 = (bf16[256,1152]{1,0:T(8,128)(2,1)}, bf16[256,1152]{1,0:T(8,128)(2,1)S(1)}, u32[]{:S(2)}, u32[]{:S(2)}) collective-permute-start(bf16[256,1152]{1,0:T(8,128)(2,1)} %get-tuple-element.49), channel_id=1, source_target_pairs={{0,12},{4,8},{8,4},{12,0},{1,13},{5,9},{9,5},{13,1},{2,14},{6,10},... | collective-permute-start | bytes 1769480 | tf_op jit(solution)/shard_map/ppermute | solution.py:57
  174.0 15.3 %copy-start.12 = (bf16[256,1152]{1,0:T(8,128)(2,1)}, bf16[256,1152]{1,0:T(8,128)(2,1)S(1)}, u32[]{:S(2)}) copy-start(bf16[256,1152]{1,0:T(8,128)(2,1)S(1)} %collective-permute-done.14.refs_2_) | copy-start | bytes 1769476
  176.5 12.9 %copy-start.13 = (bf16[256,1152]{1,0:T(8,128)(2,1)}, bf16[256,1152]{1,0:T(8,128)(2,1)S(1)}, u32[]{:S(2)}) copy-start(bf16[256,1152]{1,0:T(8,128)(2,1)S(1)} %collective-permute-done.15.refs_3_) | copy-start | bytes 1769476
  200.0 15.6 %collective-permute-start.23 = (bf16[256,1152]{1,0:T(8,128)(2,1)}, bf16[256,1152]{1,0:T(8,128)(2,1)S(1)}, u32[]{:S(2)}, u32[]{:S(2)}) collective-permute-start(bf16[256,1152]{1,0:T(8,128)(2,1)} %get-tuple-element.50.refs_1_), channel_id=1, source_target_pairs={{0,4},{4,0},{8,12},{12,8},{1,5},{5,1},{9,13},{13,9},{2,6},{6,2},{1... | collective-permute-start | bytes 1769480 | tf_op jit(solution)/shard_map/ppermute | solution.py:57
  200.7 16.5 %collective-permute-start.24 = (bf16[256,1152]{1,0:T(8,128)(2,1)}, bf16[256,1152]{1,0:T(8,128)(2,1)S(1)}, u32[]{:S(2)}, u32[]{:S(2)}) collective-permute-start(bf16[256,1152]{1,0:T(8,128)(2,1)} %get-tuple-element.50.refs_1_), channel_id=1, source_target_pairs={{0,8},{4,12},{8,0},{12,4},{1,9},{5,13},{9,1},{13,5},{2,10},{6,14},... | collective-permute-start | bytes 1769480 | tf_op jit(solution)/shard_map/ppermute | solution.py:57
  202.5 26.5 %collective-permute-start.25 = (bf16[256,1152]{1,0:T(8,128)(2,1)}, bf16[256,1152]{1,0:T(8,128)(2,1)S(1)}, u32[]{:S(2)}, u32[]{:S(2)}) collective-permute-start(bf16[256,1152]{1,0:T(8,128)(2,1)} %get-tuple-element.50.refs_1_), channel_id=1, source_target_pairs={{0,12},{4,8},{8,4},{12,0},{1,13},{5,9},{9,5},{13,1},{2,14},{6,10},... | collective-permute-start | bytes 1769480 | tf_op jit(solution)/shard_map/ppermute | solution.py:57
  215.5 13.5 %copy-start.9 = (bf16[256,1152]{1,0:T(8,128)(2,1)}, bf16[256,1152]{1,0:T(8,128)(2,1)S(1)}, u32[]{:S(2)}) copy-start(bf16[256,1152]{1,0:T(8,128)(2,1)S(1)} %collective-permute-done.23.refs_2_) | copy-start | bytes 1769476
  217.2 11.8 %copy-start.10 = (bf16[256,1152]{1,0:T(8,128)(2,1)}, bf16[256,1152]{1,0:T(8,128)(2,1)S(1)}, u32[]{:S(2)}) copy-start(bf16[256,1152]{1,0:T(8,128)(2,1)S(1)} %collective-permute-done.24.refs_3_) | copy-start | bytes 1769476
  249.1 4.4 %copy-start.1 = (bf16[2048,512]{1,0:T(8,128)(2,1)S(1)}, bf16[2048,512]{1,0:T(8,128)(2,1)}, u32[]{:S(2)}) copy-start(bf16[2048,512]{1,0:T(8,128)(2,1)} %get-tuple-element.74) | copy-start | bytes 6291460
  251.4 3.6 collective-permute-start.37
  251.4 6.2 %collective-permute-start.26 = (bf16[2,256,512]{2,1,0:T(8,128)(2,1)}, bf16[2,256,512]{2,1,0:T(8,128)(2,1)}, u32[]{:S(2)}, u32[]{:S(2)}) collective-permute-start(bf16[2,256,512]{2,1,0:T(8,128)(2,1)} %get-tuple-element.55), channel_id=1, source_target_pairs={{0,1},{1,0},{2,3},{3,2},{4,5},{5,4},{6,7},{7,6},{8,9},{9,8},{10,11... | collective-permute-start | bytes 1572872 | tf_op jit(solution)/shard_map/ppermute | solution.py:57
  252.0 15.1 %collective-permute-start.27 = (bf16[2,256,512]{2,1,0:T(8,128)(2,1)}, bf16[2,256,512]{2,1,0:T(8,128)(2,1)}, u32[]{:S(2)}, u32[]{:S(2)}) collective-permute-start(bf16[2,256,512]{2,1,0:T(8,128)(2,1)} %get-tuple-element.56), channel_id=1, source_target_pairs={{0,2},{1,3},{2,0},{3,1},{4,6},{5,7},{6,4},{7,5},{8,10},{9,11},{10,... | collective-permute-start | bytes 1572872 | tf_op jit(solution)/shard_map/ppermute | solution.py:57
  253.5 23.9 %collective-permute-start.28 = (bf16[2,256,512]{2,1,0:T(8,128)(2,1)}, bf16[2,256,512]{2,1,0:T(8,128)(2,1)}, u32[]{:S(2)}, u32[]{:S(2)}) collective-permute-start(bf16[2,256,512]{2,1,0:T(8,128)(2,1)} %get-tuple-element.57), channel_id=1, source_target_pairs={{0,3},{1,2},{2,1},{3,0},{4,7},{5,6},{6,5},{7,4},{8,11},{9,10},{10,... | collective-permute-start | bytes 1572872 | tf_op jit(solution)/shard_map/ppermute | solution.py:57
  255.0 147.2 %reduce-scatter.3.cloned.1.call-start = ((), (), s32[]{:S(2)}) async-start(), calls=%async_computation.2 | async-start | bytes 2359296 | tf_op jit(solution)/shard_map/reduce_scatter | solution.py:797
  256.2 75.5 %collective-permute-start.38 = (bf16[2,2,2,16,640]{4,3,2,1,0:T(8,128)(2,1)S(1)}, bf16[2,2,2,16,640]{4,3,2,1,0:T(8,128)(2,1)S(1)}, u32[]{:S(2)}, u32[]{:S(2)}) collective-permute-start(bf16[2,2,2,16,640]{4,3,2,1,0:T(8,128)(2,1)S(1)} %fusion.4), channel_id=1, source_target_pairs={{0,2},{1,3},{2,0},{3,1},{4,6},{5,7},{6,4},{7,5},{8,10},{9,11},{10,... | collective-permute-start | bytes 491528 | tf_op jit(solution)/shard_map/ppermute | solution.py:57
  330.8 5.5 %collective-permute-start.32 = (bf16[2,2,2,2,16,1536]{5,4,0,1,2,3:T(8,128)(2,1)S(1)}, bf16[2,2,2,2,16,1536]{5,4,0,1,2,3:T(8,128)(2,1)S(1)}, u32[]{:S(2)}, u32[]{:S(2)}) collective-permute-start(bf16[2,2,2,2,16,1536]{5,4,0,1,2,3:T(8,128)(2,1)S(1)} %fusion), channel_id=1, source_target_pairs={{0,1},{1,0},{2,3},{3,2},{4,5},{5,4},{6,7},{7,6},{8,9},{9,8},{10,11... | collective-permute-start | bytes 2359304 | tf_op jit(solution)/shard_map/ppermute | solution.py:57
  331.8 4.5 %collective-permute-start.39 = (bf16[2,2,16,640]{3,2,1,0:T(8,128)(2,1)S(1)}, bf16[2,2,16,640]{3,2,1,0:T(8,128)(2,1)S(1)}, u32[]{:S(2)}, u32[]{:S(2)}) collective-permute-start(bf16[2,2,16,640]{3,2,1,0:T(8,128)(2,1)S(1)} %fusion.7), channel_id=1, source_target_pairs={{0,4},{4,0},{8,12},{12,8},{1,5},{5,1},{9,13},{13,9},{2,6},{6,2},{1... | collective-permute-start | bytes 245768 | tf_op jit(solution)/shard_map/ppermute | solution.py:57
  338.7 17.3 %collective-permute-start.33 = (bf16[2,2,2,16,1536]{4,3,0,1,2:T(8,128)(2,1)}, bf16[2,2,2,16,1536]{4,3,0,1,2:T(8,128)(2,1)}, u32[]{:S(2)}, u32[]{:S(2)}) collective-permute-start(bf16[2,2,2,16,1536]{4,3,0,1,2:T(8,128)(2,1)} %fusion.1), channel_id=1, source_target_pairs={{0,2},{1,3},{2,0},{3,1},{4,6},{5,7},{6,4},{7,5},{8,10},{9,11},{10,... | collective-permute-start | bytes 1179656 | tf_op jit(solution)/shard_map/ppermute | solution.py:57
  340.3 6.7 %collective-permute-start.40 = (bf16[2,16,640]{2,1,0:T(8,128)(2,1)S(1)}, bf16[2,16,640]{2,1,0:T(8,128)(2,1)S(1)}, u32[]{:S(2)}, u32[]{:S(2)}) collective-permute-start(bf16[2,16,640]{2,1,0:T(8,128)(2,1)S(1)} %fusion.10), channel_id=1, source_target_pairs={{0,8},{4,12},{8,0},{12,4},{1,9},{5,13},{9,1},{13,5},{2,10},{6,14},... | collective-permute-start | bytes 122888 | tf_op jit(solution)/shard_map/ppermute | solution.py:57
  345.0 27.9 %collective-permute-start.29 = (bf16[2,256,512]{2,1,0:T(8,128)(2,1)}, bf16[2,256,512]{2,1,0:T(8,128)(2,1)S(1)}, u32[]{:S(2)}, u32[]{:S(2)}) collective-permute-start(bf16[2,256,512]{2,1,0:T(8,128)(2,1)} %get-tuple-element.65), channel_id=1, source_target_pairs={{0,1},{1,0},{2,3},{3,2},{4,5},{5,4},{6,7},{7,6},{8,9},{9,8},{10,11... | collective-permute-start | bytes 1572872 | tf_op jit(solution)/shard_map/ppermute | solution.py:57
  345.1 27.8 %collective-permute-start.30 = (bf16[2,256,512]{2,1,0:T(8,128)(2,1)}, bf16[2,256,512]{2,1,0:T(8,128)(2,1)S(1)}, u32[]{:S(2)}, u32[]{:S(2)}) collective-permute-start(bf16[2,256,512]{2,1,0:T(8,128)(2,1)} %get-tuple-element.66), channel_id=1, source_target_pairs={{0,2},{1,3},{2,0},{3,1},{4,6},{5,7},{6,4},{7,5},{8,10},{9,11},{10,... | collective-permute-start | bytes 1572872 | tf_op jit(solution)/shard_map/ppermute | solution.py:57
  345.7 27.2 %collective-permute-start.31 = (bf16[2,256,512]{2,1,0:T(8,128)(2,1)}, bf16[2,256,512]{2,1,0:T(8,128)(2,1)S(1)}, u32[]{:S(2)}, u32[]{:S(2)}) collective-permute-start(bf16[2,256,512]{2,1,0:T(8,128)(2,1)} %get-tuple-element.67), channel_id=1, source_target_pairs={{0,3},{1,2},{2,1},{3,0},{4,7},{5,6},{6,5},{7,4},{8,11},{9,10},{10,... | collective-permute-start | bytes 1572872 | tf_op jit(solution)/shard_map/ppermute | solution.py:57
  347.0 11.7 %collective-permute-start.41 = (bf16[16,640]{1,0:T(8,128)(2,1)S(1)}, bf16[16,640]{1,0:T(8,128)(2,1)S(1)}, u32[]{:S(2)}, u32[]{:S(2)}) collective-permute-start(bf16[16,640]{1,0:T(8,128)(2,1)S(1)} %fusion.11), channel_id=1, source_target_pairs={{0,16},{16,0},{1,17},{17,1},{2,18},{18,2},{3,19},{19,3},{4,20},{20... | collective-permute-start | bytes 61448 | tf_op jit(solution)/shard_map/ppermute | solution.py:57
  357.2 6.9 %collective-permute-start.34 = (bf16[2,2,16,1536]{3,2,0,1:T(8,128)(2,1)S(1)}, bf16[2,2,16,1536]{3,2,0,1:T(8,128)(2,1)S(1)}, u32[]{:S(2)}, u32[]{:S(2)}) collective-permute-start(bf16[2,2,16,1536]{3,2,0,1:T(8,128)(2,1)S(1)} %fusion.3), channel_id=1, source_target_pairs={{0,4},{4,0},{8,12},{12,8},{1,5},{5,1},{9,13},{13,9},{2,6},{6,2},{1... | collective-permute-start | bytes 589832 | tf_op jit(solution)/shard_map/ppermute | solution.py:57
  364.2 4.7 %collective-permute-start.35 = (bf16[2,16,1536]{2,1,0:T(8,128)(2,1)S(1)}, bf16[2,16,1536]{2,1,0:T(8,128)(2,1)S(1)}, u32[]{:S(2)}, u32[]{:S(2)}) collective-permute-start(bf16[2,16,1536]{2,1,0:T(8,128)(2,1)S(1)} %fusion.6), channel_id=1, source_target_pairs={{0,8},{4,12},{8,0},{12,4},{1,9},{5,13},{9,1},{13,5},{2,10},{6,14},... | collective-permute-start | bytes 294920 | tf_op jit(solution)/shard_map/ppermute | solution.py:57
  369.0 11.4 %collective-permute-start.36 = (bf16[16,1536]{1,0:T(8,128)(2,1)S(1)}, bf16[16,1536]{1,0:T(8,128)(2,1)S(1)}, u32[]{:S(2)}, u32[]{:S(2)}) collective-permute-start(bf16[16,1536]{1,0:T(8,128)(2,1)S(1)} %fusion.9), channel_id=1, source_target_pairs={{0,16},{16,0},{1,17},{17,1},{2,18},{18,2},{3,19},{19,3},{4,20},{20... | collective-permute-start | bytes 147464 | tf_op jit(solution)/shard_map/ppermute | solution.py:57
  374.1 6.2 %copy-start.6 = (f32[16,1536]{1,0:T(8,128)S(1)}, f32[16,1536]{1,0:T(8,128)}, u32[]{:S(2)}) copy-start(f32[16,1536]{1,0:T(8,128)} %param.14) | copy-start | bytes 294916
  374.1 7.0 %copy-start.8 = (f32[16]{0:T(128)S(1)}, f32[16]{0:T(128)}, u32[]{:S(2)}) copy-start(f32[16]{0:T(128)} %param.13) | copy-start | bytes 196
  382.5 23.3 %collective-permute-start.45 = (bf16[64,512]{1,0:T(8,128)(2,1)S(1)}, bf16[64,512]{1,0:T(8,128)(2,1)S(1)}, u32[]{:S(2)}, u32[]{:S(2)}) collective-permute-start(bf16[64,512]{1,0:T(8,128)(2,1)S(1)} %get-tuple-element.156), channel_id=1, source_target_pairs={{0,12},{4,8},{8,4},{12,0},{1,13},{5,9},{9,5},{13,1},{2,14},{6,10},... | collective-permute-start | bytes 196616 | tf_op jit(solution)/shard_map/ppermute | solution.py:57
  385.9 20.8 %collective-permute-start.46 = (bf16[64,512]{1,0:T(8,128)(2,1)S(1)}, bf16[64,512]{1,0:T(8,128)(2,1)S(1)}, u32[]{:S(2)}, u32[]{:S(2)}) collective-permute-start(bf16[64,512]{1,0:T(8,128)(2,1)S(1)} %get-tuple-element.155), channel_id=1, source_target_pairs={{0,8},{4,12},{8,0},{12,4},{1,9},{5,13},{9,1},{13,5},{2,10},{6,14},... | collective-permute-start | bytes 196616 | tf_op jit(solution)/shard_map/ppermute | solution.py:57
  385.9 20.8 %collective-permute-start.47 = (bf16[64,512]{1,0:T(8,128)(2,1)S(1)}, bf16[64,512]{1,0:T(8,128)(2,1)S(1)}, u32[]{:S(2)}, u32[]{:S(2)}) collective-permute-start(bf16[64,512]{1,0:T(8,128)(2,1)S(1)} %get-tuple-element.154), channel_id=1, source_target_pairs={{0,4},{4,0},{8,12},{12,8},{1,5},{5,1},{9,13},{13,9},{2,6},{6,2},{1... | collective-permute-start | bytes 196616 | tf_op jit(solution)/shard_map/ppermute | solution.py:57
  403.2 5.5 %collective-permute-start.42 = (bf16[16,2048]{1,0:T(8,128)(2,1)S(1)}, bf16[16,2048]{1,0:T(8,128)(2,1)S(1)}, u32[]{:S(2)}, u32[]{:S(2)}) collective-permute-start(bf16[16,2048]{1,0:T(8,128)(2,1)S(1)} %get-tuple-element.159), channel_id=1, source_target_pairs={{0,12},{4,8},{8,4},{12,0},{1,13},{5,9},{9,5},{13,1},{2,14},{6,10},... | collective-permute-start | bytes 196616 | tf_op jit(solution)/shard_map/ppermute | solution.py:57
  405.5 4.3 %collective-permute-start.43 = (bf16[16,2048]{1,0:T(8,128)(2,1)S(1)}, bf16[16,2048]{1,0:T(8,128)(2,1)S(1)}, u32[]{:S(2)}, u32[]{:S(2)}) collective-permute-start(bf16[16,2048]{1,0:T(8,128)(2,1)S(1)} %get-tuple-element.158), channel_id=1, source_target_pairs={{0,8},{4,12},{8,0},{12,4},{1,9},{5,13},{9,1},{13,5},{2,10},{6,14},... | collective-permute-start | bytes 196616 | tf_op jit(solution)/shard_map/ppermute | solution.py:57
  405.8 4.3 %collective-permute-start.44 = (bf16[16,2048]{1,0:T(8,128)(2,1)S(1)}, bf16[16,2048]{1,0:T(8,128)(2,1)S(1)}, u32[]{:S(2)}, u32[]{:S(2)}) collective-permute-start(bf16[16,2048]{1,0:T(8,128)(2,1)S(1)} %get-tuple-element.157), channel_id=1, source_target_pairs={{0,4},{4,0},{8,12},{12,8},{1,5},{5,1},{9,13},{13,9},{2,6},{6,2},{1... | collective-permute-start | bytes 196616 | tf_op jit(solution)/shard_map/ppermute | solution.py:57
  (8 other events, 8.4 us)
Sparse Core Ops, SparseCore 0:
  28.0 37.6 all-gather.4
  67.6 36.6 all-gather.6
  255.2 58.3 reduce-scatter.4
  345.2 57.0 reduce-scatter.2

commit v2 on v1

v2 whole, which is shorter than its diff:
```python
import functools
import math

import jax
import jax.numpy as jnp
from jax import lax
from jax.experimental import pallas as pl
from jax.experimental.pallas import tpu as pltpu
from jax.sharding import Mesh
from jax.sharding import PartitionSpec as P

HEADS = 8
GROUP = 32
BLOCK = 256
LANES = 128
MARKS = 16
VMEM_LIMIT = 60 * 1024 * 1024

LOG2E = math.log2(math.e)
LN2 = math.log(2.0)
BIG = 1e30

bf16 = jnp.bfloat16
f32 = jnp.float32

NN = (((1,), (0,)), ((), ()))
NT = (((1,), (1,)), ((), ()))
TN = (((0,), (0,)), ((), ()))


def dot(a, b, dims=NN):
    return lax.dot_general(a, b, dims, preferred_element_type=f32)


def normalize(values):
    center = values - jnp.mean(values, axis=-1, keepdims=True)
    scaled = lax.rsqrt(jnp.mean(center * center, axis=-1, keepdims=True) + 1e-05)
    return center * scaled, scaled


def norm_back(incoming, normed, scaled):
    return scaled * (
        incoming
        - jnp.mean(incoming, axis=-1, keepdims=True)
        - normed * jnp.mean(incoming * normed, axis=-1, keepdims=True)
    )


def split3(value):
    high = value.astype(bf16).astype(f32)
    rest = value - high
    mid = rest.astype(bf16).astype(f32)
    low = (rest - mid).astype(bf16).astype(f32)
    return high, mid, low


def partner(value, axis, size, mask):
    return lax.ppermute(value, axis, [(i, i ^ mask) for i in range(size)])


def swap_slots(slots, axis):
    size = len(slots)
    return [slots[0]] + [partner(slots[j], axis, size, j) for j in range(1, size)]


def natural(slots, me):
    out = list(slots)
    bit = 1
    while bit < len(out):
        flip = (me & bit) != 0
        out = [jnp.where(flip, out[k ^ bit], out[k]) for k in range(len(out))]
        bit *= 2
    return out


def bits_of(sizes):
    bits = []
    for axis, size in sizes:
        mask = size // 2
        while mask:
            bits.append((axis, size, mask))
            mask //= 2
    return bits


def named(bit):
    axis, _, mask = bit
    return "core" if axis == "seq" and mask == 1 else axis


class Steps:
    def __init__(self, value, sizes, order):
        self.order = [bit for axis in order for bit in reversed(bits_of(sizes)) if named(bit) == axis]
        self.value = value

    def steps(self, axis):
        while self.order and named(self.order[0]) == axis:
            self.step(self.order.pop(0))
        return self

    def finish(self):
        while self.order:
            self.step(self.order.pop(0))
        return self.value


class Doubling(Steps):
    def __init__(self, value, sizes, order, inner=0):
        super().__init__(value, sizes, order)
        self.inner = inner
        self.place = bits_of(sizes)
        self.have = []

    def step(self, bit):
        axis, size, mask = bit
        depth = sum(self.place.index(other) < self.place.index(bit) for other in self.have)
        depth += self.inner if axis == "seq" else 0
        other = partner(self.value, axis, size, mask)
        high = (lax.axis_index(axis) & mask) != 0
        first = jnp.where(high, other, self.value)
        second = jnp.where(high, self.value, other)
        self.value = jnp.stack([first, second], axis=depth)
        self.have.append(bit)

    def at_once(self, axis):
        bits = [bit for bit in self.place if bit[0] == axis]
        self.order = [bit for bit in self.order if bit[0] != axis]
        depth = sum(self.place.index(other) < self.place.index(bits[0]) for other in self.have)
        depth += self.inner if axis == "seq" else 0
        slots = natural(swap_slots([self.value] * 2 ** len(bits), axis), lax.axis_index(axis))
        shape = self.value.shape
        value = jnp.stack(slots, axis=depth)
        self.value = value.reshape(shape[:depth] + (2,) * len(bits) + shape[depth:])
        self.have += bits


class Halving(Steps):
    def __init__(self, value, sizes, order, inner=0):
        super().__init__(value, sizes, order)
        self.left = [bit for bit in bits_of(sizes) if bit in self.order]
        self.inner = inner

    def step(self, bit):
        depth = self.left.index(bit)
        self.left.pop(depth)
        axis, size, mask = bit
        depth += self.inner if axis == "seq" else 0
        high = ((lax.axis_index(axis) & mask) != 0).astype(jnp.int32)
        keep = lax.dynamic_index_in_dim(self.value, high, depth, keepdims=False)
        send = lax.dynamic_index_in_dim(self.value, 1 - high, depth, keepdims=False)
        other = partner(send.astype(bf16), axis, size, mask)
        self.value = keep.astype(f32) + other.astype(f32)


hold = lax.optimization_barrier


def together(values, *sums):
    values, held = lax.optimization_barrier((values, [item.value for item in sums]))
    for item, value in zip(sums, held):
        item.value = value
    return values


def call(kernel, name, grid, in_specs, outs, scratch, args, micros, aliases=None):
    return pl.pallas_call(
        kernel,
        grid_spec=pltpu.PrefetchScalarGridSpec(
            num_scalar_prefetch=1,
            grid=grid,
            in_specs=in_specs,
            out_specs=[spec for spec, _, _ in outs],
            scratch_shapes=[pltpu.VMEM(shape, dtype) for shape, dtype in scratch],
        ),
        out_shape=[jax.ShapeDtypeStruct(shape, dtype) for _, shape, dtype in outs],
        input_output_aliases=aliases or {},
        compiler_params=pltpu.CompilerParams(vmem_limit_bytes=VMEM_LIMIT),
        cost_estimate=pl.CostEstimate(
            flops=int(micros * 1e9), bytes_accessed=1 << 20, transcendentals=0
        ),
        name=name,
    )(*args)


def per_row(*shape):
    return pl.BlockSpec((1,) + shape, lambda r, me: (r,) + (0,) * len(shape))


def whole(*shape):
    return pl.BlockSpec(shape, lambda r, me: (0,) * len(shape))


def by_core(me, pairs):
    odd = me % 2 == 1
    first, second = pairs[:, 0], pairs[:, 1]
    return jnp.where(odd, second, first), jnp.where(odd, first, second)


def causal_bias(step=LANES):
    rows = LANES + step * (BLOCK // LANES - 1)
    key = lax.broadcasted_iota(jnp.int32, (rows, BLOCK), 0)
    query = lax.broadcasted_iota(jnp.int32, (rows, BLOCK), 1)
    query = query + (query // LANES) * (step - LANES)
    return jnp.where(key <= query, 0.0, -BIG).astype(f32)


def key_features(segment_row, length):
    row = lax.broadcasted_iota(jnp.int32, (LANES, length), 0)
    marks = (row == segment_row) | ((row >= 7) & (row < 10))
    return jnp.where(marks, 1.0, 0.0).astype(f32).T.astype(bf16)


def query_features(segment_row, length):
    row = lax.broadcasted_iota(jnp.int32, (16, length), 0)
    return jnp.where((row < 7) & (row != segment_row), -BIG, 0.0).astype(f32)


def padded_head(head, features, odd):
    blank = jnp.zeros_like(head)
    rest = jnp.zeros((LANES - 16, head.shape[1]), bf16)
    both = [blank, head] if odd else [head, blank]
    return jnp.concatenate(both + [features, rest], axis=0)


def attend_queries(part, parts, slots, me, seg_ref, q_t, k_ref, v_t, att_refs, ot_ref, lse_ref, aux):
    k_aux, q_aux, causal = aux
    length = k_ref.shape[1]
    piece = length // slots
    some = piece // parts
    step = piece if parts > 1 else LANES
    segment_row = seg_ref[0]
    q_aux[...] = query_features(segment_row, length)
    k_aux[...] = key_features(segment_row, length)
    blocks = slots * some // BLOCK
    count = BLOCK // some if parts > 1 else 1

    def head_pair(pair, carry):
        base = pl.multiple_of(pair * LANES, LANES)
        for odd in range(2):
            rows = pl.ds(pl.multiple_of(pair * LANES + odd * 64, 64), 64)
            for block in range(blocks):
                if parts > 1:
                    first = block * count * piece + part * some
                    places = [pl.ds(first + i * piece, some) for i in range(count)]
                else:
                    first = block * BLOCK
                    places = [pl.ds(first, BLOCK)]
                feats = jnp.concatenate([q_aux[:, p] for p in places], axis=1).astype(bf16)
                head = jnp.concatenate([q_t[0, rows, p] for p in places], axis=1)
                query = padded_head(head, feats, odd)
                chunks = [(k, min(BLOCK, first - k)) for k in range(0, first, BLOCK)]
                chunks.append((first, causal.shape[0]))
                scores = []
                for start, size in chunks:
                    keys = pl.ds(start, size)
                    key = jnp.concatenate([k_ref[0, keys, pl.ds(base, LANES)], k_aux[keys]], axis=1)
                    score = dot(key, query)
                    scores.append(score + causal[...] if start == first else score)
                top = functools.reduce(
                    jnp.maximum, [jnp.max(score, axis=0, keepdims=True) for score in scores]
                )
                total = jnp.zeros((1, BLOCK), f32)
                out = jnp.zeros((64, BLOCK), f32)
                for (start, size), score in zip(chunks, scores):
                    prob = jnp.exp2(score - top)
                    total = total + jnp.sum(prob, axis=0, keepdims=True)
                    out = out + dot(v_t[0, rows, pl.ds(start, size)], prob.astype(bf16))
                held = pl.ds(block * BLOCK, BLOCK)
                ot_ref[0, rows, held] = (out / total).astype(bf16)
                lse_ref[0, pl.ds(pair * 2 + odd, 1), held] = top + jnp.log2(total)
        return carry

    lax.fori_loop(0, HEADS // 2, head_pair, 0)
    for j in range(slots):
        place = pl.ds(pl.multiple_of((me ^ j) * some, some), some)
        att_refs[j][0] = ot_ref[0, :, place].T


def attend_first_kernel(parts, slots, old, *refs):
    me_ref = refs[0]
    x_refs = refs[1 : 1 + slots]
    gain_ref, w_ref = refs[1 + slots : 3 + slots]
    rest = refs[3 + slots + old :]
    att_refs = rest[:slots]
    seg_ref, qt_ref, k_ref, v_ref, q_ref, vt_ref, ot_ref, lse_ref = rest[slots : slots + 8]
    w_t, *aux = rest[slots + 8 :]
    width = w_ref.shape[0]
    piece = x_refs[0].shape[1] - MARKS
    me = me_ref[0]
    score_scale = LOG2E / math.sqrt(width // HEADS)

    w_t[:width] = w_ref[:, :width].T
    w_t[width:] = w_ref[:, 2 * width :].T
    aux[2][...] = causal_bias(piece if parts > 1 else LANES)
    gain = gain_ref[...]
    for j in range(slots):
        place = pl.ds(pl.multiple_of((me ^ j) * piece, piece), piece)
        marks = x_refs[j][0, piece:].astype(f32)
        seg_ref[0, :, place] = marks[0:1, :piece].astype(jnp.int32)
        normed, _ = normalize(x_refs[j][0, :piece].astype(f32))
        first_in = (normed * gain).astype(bf16)
        projected = dot(first_in, w_ref[...])
        q_ref[0, place] = (projected[:, :width] * score_scale).astype(bf16)
        k_ref[0, place] = projected[:, width : 2 * width].astype(bf16)
        v_ref[0, place] = projected[:, 2 * width :].astype(bf16)
        turned = dot(w_t[...], first_in, NT)
        qt_ref[0, :, place] = (turned[:width] * score_scale).astype(bf16)
        vt_ref[0, :, place] = turned[width:].astype(bf16)
    attend_queries(
        0, parts, slots, me, seg_ref, qt_ref, k_ref, vt_ref, att_refs, ot_ref, lse_ref, aux
    )


def attend_next_kernel(part, parts, slots, *refs):
    me_ref, seg_ref, qt_ref, k_ref, vt_ref = refs[:5]
    att_refs = refs[5 : 5 + slots]
    ot_ref, lse_ref, *aux = refs[5 + slots :]

    @pl.when(pl.program_id(0) == 0)
    def _():
        aux[2][...] = causal_bias(k_ref.shape[1] // slots if parts > 1 else LANES)

    attend_queries(
        part, parts, slots, me_ref[0], seg_ref, qt_ref, k_ref, vt_ref, att_refs, ot_ref, lse_ref, aux
    )


def attend_outs(rows, slots, some, width):
    return [(per_row(some, width), (rows, some, width), bf16)] * slots, [
        (per_row(width, slots * some), (rows, width, slots * some), bf16),
        (per_row(HEADS, slots * some), (rows, HEADS, slots * some), f32),
    ]


def attend_scratch(length, piece, parts):
    span = LANES + (piece if parts > 1 else LANES) * (BLOCK // LANES - 1)
    return [((length, LANES), bf16), ((16, length), f32), ((span, BLOCK), f32)]


def attend_first(me, row, rows, x_slots, gain, w_qkv, parts, old):
    slots = len(x_slots)
    _, packed, width = x_slots[0].shape
    piece = packed - MARKS
    length = piece * slots

    def this(*shape):
        return pl.BlockSpec((1,) + shape, lambda r, me: (row,) + (0,) * len(shape))

    some = piece // parts
    turned = (this(width, length), (rows, width, length), bf16)
    plain = (this(length, width), (rows, length, width), bf16)
    outs = (
        [(this(some, width), (rows, some, width), bf16)] * slots
        + [(this(1, length), (rows, 1, length), jnp.int32)]
        + [turned, plain, plain, plain, turned]
        + [
            (this(width, slots * some), (rows, width, slots * some), bf16),
            (this(HEADS, slots * some), (rows, HEADS, slots * some), f32),
        ]
    )
    result = call(
        functools.partial(attend_first_kernel, parts, slots, len(old)),
        "attend_first",
        (1,),
        [per_row(packed, width)] * slots
        + [whole(1, width), whole(width, 3 * width)]
        + [pl.BlockSpec(memory_space=pl.ANY)] * len(old),
        outs,
        [((2 * width, width), bf16)] + attend_scratch(length, piece, parts),
        (me, *x_slots, gain, w_qkv, *old),
        12,
        {3 + slots + i: i for i in range(len(old))},
    )
    return result


def attend_next(me, part, parts, projected, slots):
    segment_rows, q_t, k, _, _, v_t = projected
    rows, length, width = k.shape
    piece = length // slots
    att, more = attend_outs(rows, slots, piece // parts, width)
    result = call(
        functools.partial(attend_next_kernel, part, parts, slots),
        "attend_next",
        (rows,),
        [
            per_row(1, length),
            per_row(width, length),
            per_row(length, width),
            per_row(width, length),
        ],
        att + more,
        attend_scratch(length, piece, parts),
        (me, segment_rows, q_t, k, v_t),
        28 / parts,
    )
    return result[:slots], result[slots:]


def attend_back_kernel(row, last, parts, slot_count, *refs):
    me_ref = refs[0]
    x_refs = refs[1 : 1 + slot_count]
    rest = refs[1 + slot_count :]
    do_refs, rest = rest[: parts * slot_count], rest[parts * slot_count :]
    seg_ref, gain_ref, w_ref, qt_ref, k_ref, v_ref, q_ref = rest[:7]
    ot_refs, lse_refs = rest[7 : 7 + parts], rest[7 + parts : 7 + 2 * parts]
    rest = rest[7 + 2 * parts :]
    if row:
        before_ref, rest = rest[0], rest[1:]
    gf_refs, rest = rest[:slot_count], rest[slot_count:]
    dw_refs, rest = rest[: 1 + last], rest[1 + last :]
    (
        k_aux, q_aux, v_aux, causal, do, first_t, work_t, k_t, grads, prob, grad_score, delta, lse
    ) = rest
    width = w_ref.shape[0]
    piece = x_refs[0].shape[1] - MARKS
    some = piece // parts
    length = piece * slot_count
    me = me_ref[0]
    score_scale = 1.0 / math.sqrt(width // HEADS)
    causal[...] = causal_bias()
    lane = lax.broadcasted_iota(jnp.int32, (length, LANES), 1)
    v_aux[...] = jnp.where(lane < 3, 1.0, 0.0).astype(bf16)
    for part in range(parts):
        for i in range(slot_count):
            held = pl.ds(i * some, some)
            lse[:, pl.ds(i * piece + part * some, some)] = lse_refs[part][0, :, held]

    segment_row = seg_ref[0]
    q_aux[...] = query_features(segment_row, length)
    k_aux[...] = key_features(segment_row, length)
    gain = gain_ref[...]
    for j in range(slot_count):
        place = pl.ds(pl.multiple_of((me ^ j) * piece, piece), piece)
        normed, _ = normalize(x_refs[j][0, :piece].astype(f32))
        first_t[:, place] = (normed * gain).astype(bf16).T
        k_t[:, place] = k_ref[0, place].T
        for part in range(parts):
            start = (me ^ j) * piece + part * some
            place = pl.ds(pl.multiple_of(start, some), some)
            held = pl.ds(pl.multiple_of((me ^ j) * some, some), some)
            grad = do_refs[part * slot_count + j][0]
            do[place] = grad
            turned = grad.T
            work_t[:, place] = turned
            product = turned.astype(f32) * ot_refs[part][0, :, held].astype(f32)
            delta[:, place] = jnp.sum(product.reshape(HEADS, width // HEADS, some), axis=1)
    lane = lax.broadcasted_iota(jnp.int32, (1, LANES), 1)
    feature = lax.broadcasted_iota(jnp.int32, (16, BLOCK), 0)
    blocks = length // BLOCK

    def head_pair(pair, carry):
        base = pl.multiple_of(pair * LANES, LANES)
        for odd in range(2):
            rows = pl.ds(pl.multiple_of(pair * LANES + odd * 64, 64), 64)
            head = pl.ds(pair * 2 + odd, 1)
            for qb in range(blocks):
                queries = pl.ds(qb * BLOCK, BLOCK)
                a, b, c = split3(lse[head, queries])
                feats = jnp.where(feature == 7, -a, q_aux[:, queries])
                feats = jnp.where(feature == 8, -b, jnp.where(feature == 9, -c, feats))
                query = padded_head(qt_ref[0, rows, queries], feats.astype(bf16), odd)
                a, b, c = split3(delta[head, queries])
                feats = jnp.where(feature == 0, -a, jnp.where(feature == 1, -b, 0.0))
                feats = jnp.where(feature == 2, -c, feats)
                grad = padded_head(work_t[rows, queries], feats.astype(bf16), odd)
                held = pl.ds(odd * length + qb * BLOCK, BLOCK)
                for kb in range(qb + 1):
                    keys = pl.ds(kb * BLOCK, BLOCK)
                    key = jnp.concatenate([k_ref[0, keys, pl.ds(base, LANES)], k_aux[keys]], axis=1)
                    score = dot(key, query)
                    if kb == qb:
                        score = score + causal[...]
                    value = jnp.concatenate(
                        [v_ref[0, keys, pl.ds(base, LANES)], v_aux[keys]], axis=1
                    )
                    grad_prob = dot(value, grad)
                    weight = jnp.exp2(score)
                    prob[keys, held] = weight.astype(bf16)
                    grad_score[keys, held] = (weight * grad_prob).astype(bf16)
                end = (qb + 1) * BLOCK
                grad_q = dot(k_t[rows, 0:end], grad_score[0:end, held])
                work_t[rows, queries] = (grad_q * score_scale).astype(bf16)
        for kb in range(blocks):
            keys = pl.ds(kb * BLOCK, BLOCK)
            later = pl.ds(kb * BLOCK, length - kb * BLOCK)
            grad_v = jnp.zeros((BLOCK, LANES), f32)
            grad_k = jnp.zeros((BLOCK, LANES), f32)
            for odd in range(2):
                mine = (lane >= 64) if odd else (lane < 64)
                held = pl.ds(odd * length + kb * BLOCK, length - kb * BLOCK)
                zero = jnp.zeros((), bf16)
                grad = jnp.where(mine, do[later, pl.ds(base, LANES)], zero)
                query = jnp.where(mine, q_ref[0, later, pl.ds(base, LANES)], zero)
                grad_v = grad_v + dot(prob[keys, held], grad)
                grad_k = grad_k + dot(grad_score[keys, held], query)
            grads[keys, pl.ds(pl.multiple_of(width + pair * LANES, LANES), LANES)] = (
                grad_k * LN2
            ).astype(bf16)
            grads[keys, pl.ds(pl.multiple_of(2 * width + pair * LANES, LANES), LANES)] = (
                grad_v.astype(bf16)
            )
        return carry

    lax.fori_loop(0, HEADS // 2, head_pair, 0)
    for j in range(slot_count):
        place = pl.ds(pl.multiple_of((me ^ j) * piece, piece), piece)
        grads[place, :width] = work_t[:, place].T
        gf_refs[j][0] = dot(grads[place], w_ref[...], NT).astype(bf16)
    update = dot(first_t[...], grads[...])
    if row:
        update = before_ref[...] + update
    if last:
        keep, send = by_core(me, update.reshape(-1, 2, *dw_refs[0].shape[1:]))
        dw_refs[0][...] = keep
        dw_refs[1][...] = send.astype(bf16)
    else:
        dw_refs[0][...] = update


def attend_back(me, row, rows, shards, x_slots, do_parts, gain, w_qkv, projected, kept, before):
    slot_count, parts = len(x_slots), len(do_parts)
    _, packed, width = x_slots[0].shape
    piece = packed - MARKS
    length = piece * slot_count
    some = piece // parts
    last = row == rows - 1

    def this(*shape):
        return pl.BlockSpec((1,) + shape, lambda r, me: (row,) + (0,) * len(shape))

    half = (shards // 2, width // shards, 3 * width)
    outs = [(per_row(piece, width), (1, piece, width), bf16)] * slot_count
    if last:
        outs += [(whole(*half), half, f32), (whole(*half), half, bf16)]
    else:
        outs += [(whole(width, 3 * width), (width, 3 * width), f32)]
    segment_rows, q_t, k, v, q, _ = projected
    result = call(
        functools.partial(attend_back_kernel, row, last, parts, slot_count),
        "attend_back",
        (1,),
        [per_row(packed, width)] * slot_count
        + [this(some, width)] * (parts * slot_count)
        + [this(1, length), whole(1, width), whole(width, 3 * width)]
        + [this(width, length)]
        + [this(length, width)] * 3
        + [this(width, some * slot_count)] * parts
        + [this(HEADS, some * slot_count)] * parts
        + ([whole(width, 3 * width)] if row else []),
        outs,
        [
            ((length, LANES), bf16),
            ((16, length), f32),
            ((length, LANES), bf16),
            ((BLOCK, BLOCK), f32),
            ((length, width), bf16),
            ((width, length), bf16),
            ((width, length), bf16),
            ((width, length), bf16),
            ((length, 3 * width), bf16),
            ((length, 2 * length), bf16),
            ((length, 2 * length), bf16),
            ((HEADS, length), f32),
            ((HEADS, length), f32),
        ],
        (
            me,
            *x_slots,
            *[do for part in do_parts for do in part],
            segment_rows,
            gain,
            w_qkv,
            q_t,
            k,
            v,
            q,
            *[o for o, _ in kept],
            *[l for _, l in kept],
            *([before] if row else []),
        ),
        28,
    )
    return result[:slot_count], result[slot_count:]


def middle_of(att_refs, inputs_ref, w_out, me):
    rows, piece, width = att_refs[0].shape
    attended = jnp.concatenate([ref[...] for ref in att_refs], axis=0)
    attended = attended.reshape(-1, width)
    origin = jnp.concatenate(
        [inputs_ref[pl.ds((me ^ j) * rows, rows)] for j in range(len(att_refs))], axis=0
    ).reshape(-1, width)
    return attended, origin.astype(f32) + dot(attended, w_out)


def diagonal(piece):
    place = lax.broadcasted_iota(jnp.int32, (piece, LANES), 0)
    lane = lax.broadcasted_iota(jnp.int32, (piece, LANES), 1)
    return place == lane % piece, lane // piece, lane


def mix_kernel(slot_count, experts, *refs):
    me_ref = refs[0]
    att_refs = refs[1 : 1 + slot_count]
    inputs_ref, cot_ref, w_out_ref, gain_ref, control_ref = refs[1 + slot_count : 6 + slot_count]
    rest = refs[6 + slot_count :]
    pay_refs = rest[:experts]
    second_ref, middle_ref = rest[experts:]
    rows, piece, width = att_refs[0].shape
    tokens = rows * slot_count
    me = me_ref[0]
    _, middle = middle_of(att_refs, inputs_ref, w_out_ref[...], me)
    normed, _ = normalize(middle)
    second = (normed * gain_ref[...]).astype(bf16)
    second_ref[...] = second.reshape(tokens, piece, width)
    middle_ref[...] = middle.reshape(tokens, piece, width)
    grad = jnp.concatenate(
        [cot_ref[pl.ds((me ^ j) * rows, rows)] for j in range(slot_count)], axis=0
    ).reshape(-1, width)
    logits = dot(second, control_ref[...], NT).reshape(tokens, piece, LANES)
    top = jnp.max(logits, axis=0)
    weights = jnp.exp(logits - top)
    total = jnp.sum(weights, axis=0)
    log_total = top + jnp.log(total)
    own, _, lane = diagonal(piece)
    weights = jnp.where(own, weights * (1.0 / total), 0.0)
    spread_out = weights.reshape(-1, LANES).astype(bf16)
    mixed = dot(spread_out, second, TN).astype(bf16)
    grad_results = dot(spread_out, grad, TN).astype(bf16)
    a, b, c = split3(log_total)
    for e in range(experts):
        mine = slice(e * piece, (e + 1) * piece)
        first = slice(e * piece, e * piece + 1)
        stats = jnp.where(lane == 0, a[:, first], jnp.where(lane == 1, b[:, first], c[:, first]))
        pay_refs[e][:, :width] = mixed[mine]
        pay_refs[e][:, width : 2 * width] = grad_results[mine]
        pay_refs[e][:, 2 * width :] = stats.astype(bf16)


def mix(me, part, att_slots, inputs, cotangent, w_out, gain, control, experts):
    slot_count = len(att_slots)
    rows, positions, width = att_slots[0].shape
    tokens = rows * slot_count
    piece = LANES // experts
    steps = positions // piece
    span = pl.BlockSpec((tokens, piece, width), lambda b, me: (0, b, 0))
    shifted = pl.BlockSpec((tokens, piece, width), lambda b, me: (0, part * steps + b, 0))
    pay = (
        pl.BlockSpec((piece, 2 * width + LANES), lambda b, me: (b, 0)),
        (positions, 2 * width + LANES),
        bf16,
    )
    result = call(
        functools.partial(mix_kernel, slot_count, experts),
        "mix",
        (steps,),
        [pl.BlockSpec((rows, piece, width), lambda b, me: (0, b, 0))] * slot_count
        + [shifted, shifted, whole(width, width), whole(1, width), whole(LANES, width)],
        [pay] * experts
        + [
            (span, (tokens, positions, width), bf16),
            (span, (tokens, positions, width), f32),
        ],
        [],
        (me, *att_slots, inputs, cotangent, w_out, gain, control),
        positions * 12 / 256,
    )
    return result[:experts], result[experts], result[experts + 1]


def expert_kernel(part, parts, tiled, slot_count, *refs):
    me_ref = refs[0]
    pay_refs = refs[1 : 1 + slot_count]
    rest = refs[1 + slot_count :]
    count = 4 if tiled else 2
    weight_refs, rest = rest[:count], rest[count:]
    expand_ref = weight_refs[0]
    last = part == parts - 1
    earlier, rest = rest[: 4 * part], rest[4 * part :]
    if last:
        back_ref, keep_ref, send_ref = rest[:3]
        mixed_acc, grad_acc, result_acc, back_acc, stat, *more, mixed_low, grad_low = rest[3:]
    else:
        back_ref, mixed_low, grad_low, hidden_ref, pre_ref = rest[:5]
        mixed_acc, grad_acc, result_acc, back_acc, stat, *more = rest[5:]
    me = me_ref[0]
    width = expand_ref.shape[-1]
    step = pl.program_id(0)

    @pl.when(step == 0)
    def _():
        logs = []
        for j in range(slot_count):
            stats = pay_refs[j][:, 2 * width :].astype(f32)
            logs.append(stats[:, 0:1] + stats[:, 1:2] + stats[:, 2:3])
        top = functools.reduce(jnp.maximum, logs)
        total = functools.reduce(jnp.add, [jnp.exp(log - top) for log in logs])
        log_total = top + jnp.log(total)
        mixed, grad = 0.0, 0.0
        for j in range(slot_count):
            share = jnp.exp(logs[j] - log_total)
            mixed = mixed + share * pay_refs[j][:, :width].astype(f32)
            grad = grad + share * pay_refs[j][:, width : 2 * width].astype(f32)
        mixed_acc[...] = mixed
        grad_acc[...] = grad
        mixed_low[...] = mixed.astype(bf16)
        grad_low[...] = grad.astype(bf16)
        result_acc[...] = jnp.zeros_like(result_acc)
        back_acc[...] = jnp.zeros_like(back_acc)
        stat[...] = jnp.broadcast_to(log_total, stat.shape)

    mixed, grad = mixed_low[...], grad_low[...]
    if tiled:
        for i in range(2):
            own, other = weight_refs[2 * i][...], weight_refs[2 * i + 1][...]
            odd = me % 2 == 1
            more[i][:, 0] = jnp.where(odd, other, own)
            more[i][:, 1] = jnp.where(odd, own, other)
        expand, shrink = [ref[...].reshape(-1, width) for ref in more]
    else:
        expand, shrink = [ref[...].reshape(-1, width) for ref in weight_refs]
    value = dot(mixed, expand)
    coeff = math.sqrt(2.0 / math.pi)
    square = value * value
    turn = jnp.tanh(coeff * (value + 0.044715 * (square * value)))
    half = 0.5 * (1.0 + turn)
    hidden = (value * half).astype(bf16)
    slope = half + (0.5 * coeff) * value * (1.0 - turn * turn) * (1.0 + (3 * 0.044715) * square)
    result_acc[...] += dot(hidden, shrink)
    grad_pre = (dot(grad, shrink, NT) * slope).astype(bf16)
    back_acc[...] += dot(grad_pre, expand, NT)
    if last:
        sets = [earlier[4 * i : 4 * i + 4] for i in range(part)]
        mixed = jnp.concatenate([m[...] for m, _, _, _ in sets] + [mixed], axis=0)
        grad = jnp.concatenate([g[...] for _, g, _, _ in sets] + [grad], axis=0)
        hidden = jnp.concatenate([h[...] for _, _, h, _ in sets] + [hidden], axis=0)
        grad_pre = jnp.concatenate([p[...] for _, _, _, p in sets] + [grad_pre], axis=0)
        grad_expand = dot(mixed, grad_pre, TN).astype(bf16)
        grad_shrink = dot(hidden, grad, TN).astype(bf16)
        if tiled:
            shards = 2 * keep_ref.shape[0]
            lines = width // shards
            both = keep_ref.shape[1]
            keep, send = by_core(me, grad_expand.reshape(shards // 2, 2, lines, width))
            place = pl.ds(pl.multiple_of(step * lines, lines), lines)
            keep_ref[:, place] = keep
            send_ref[:, place] = send
            count = 2 * width // both // 2
            keep, send = by_core(me, grad_shrink.reshape(count, 2, both // 2, width))
            place = pl.ds(step * count, count)
            keep_ref[place, both // 2 :] = keep
            send_ref[place, both // 2 :] = send
        else:
            keep_ref[...] = grad_expand.reshape(keep_ref.shape)
            send_ref[...] = grad_shrink.reshape(send_ref.shape)
    else:
        hidden_ref[...] = hidden
        pre_ref[...] = grad_pre

    @pl.when(step == pl.num_programs(0) - 1)
    def _():
        results = result_acc[...].astype(bf16)
        back = back_acc[...].astype(bf16)
        back_ref[:, :width] = results
        back_ref[:, width : 2 * width] = back
        inner = jnp.sum(
            results.astype(f32) * grad_acc[...] + back.astype(f32) * mixed_acc[...],
            axis=-1,
            keepdims=True,
        )
        lane = lax.broadcasted_iota(jnp.int32, stat.shape, 1)
        a, b, c = split3(stat[...])
        d, e, f = split3(inner)
        stats = jnp.where(lane == 0, a, jnp.where(lane == 1, b, c))
        stats = jnp.where(lane < 3, stats, jnp.where(lane == 3, d, jnp.where(lane == 4, e, f)))
        back_ref[:, 2 * width :] = stats.astype(bf16)


def pack_expert(expand, shrink):
    experts, lines, hidden = expand.shape
    width = shrink.shape[-1]
    expand = expand.reshape(experts, lines, hidden // width, width)
    expand = jnp.swapaxes(expand, 1, 2).reshape(experts, -1, width)
    return jnp.concatenate([expand, shrink], axis=1)


def unpack_expert(packed, lines):
    experts, both, width = packed.shape
    expand = packed[:, : both // 2].reshape(experts, -1, lines, width)
    expand = jnp.swapaxes(expand, 1, 2).reshape(experts, lines, -1)
    return expand, packed[:, both // 2 :]


def expert(me, core, part, parts, pay_slots, halves, earlier):
    slot_count = len(pay_slots)
    groups, packed = pay_slots[0].shape
    shards = 2 * halves[0][0].shape[0]
    tail, width = halves[0][0].shape[1:]
    hidden = shards * tail
    chunks = hidden // width
    lines = width // shards
    acc = ((groups, width), f32)
    low = ((groups, width), bf16)
    tiled = lines % 16 == 0
    group = shards // chunks // 2
    if tiled:
        columns = pl.BlockSpec((shards // 2, lines, width), lambda f, me: (0, f, 0))
        lower = pl.BlockSpec((group, tail, width), lambda f, me: (f, 0, 0))
        weights = [*halves[0], *halves[1]]
        specs = [columns, columns, lower, lower]
        built = [((shards // 2, 2, lines, width), bf16), ((group, 2, tail, width), bf16)]
        both = (shards // 2, 2 * tail, width)
        grads = [(whole(*both), both, bf16)] * 2
    else:
        odd = core == 1
        weights = [
            jnp.stack([jnp.where(odd, b, a), jnp.where(odd, a, b)], axis=1) for a, b in halves
        ]
        expand = weights[0].reshape(shards, chunks, lines, width)
        expand = jnp.swapaxes(expand, 0, 1).reshape(chunks, width, width)
        weights = [expand, weights[1].reshape(chunks, width, width)]
        specs = [pl.BlockSpec((1, width, width), lambda f, me: (f, 0, 0))] * 2
        built = []
        grads = [(specs[0], (chunks, width, width), bf16)] * 2
    token = whole(groups, width)
    inner = pl.BlockSpec((groups, width), lambda f, me: (0, f))
    last = part == parts - 1
    outs = [(whole(groups, packed), (groups, packed), bf16)]
    scratch = [acc, acc, acc, acc, ((groups, LANES), f32)] + built
    if last:
        outs += grads
        scratch += [low, low]
    else:
        outs += [(token, (groups, width), bf16)] * 2 + [(inner, (groups, hidden), bf16)] * 2
    result = call(
        functools.partial(expert_kernel, part, parts, tiled, slot_count),
        "expert",
        (chunks,),
        [whole(groups, packed)] * slot_count + specs + [token, token, inner, inner] * part,
        outs,
        scratch,
        (me, *pay_slots, *weights, *earlier),
        7,
    )
    more = list(result[1:])
    if last and not tiled:
        grad = jnp.swapaxes(more[0].reshape(chunks, shards, lines, width), 0, 1)
        more = [grad.reshape(shards, tail, width), more[1].reshape(shards, tail, width)]
        more = jnp.concatenate(more, axis=1).reshape(shards // 2, 2, 2 * tail, width)
        odd = core == 1
        more = [
            jnp.where(odd, more[:, 1], more[:, 0]),
            jnp.where(odd, more[:, 0], more[:, 1]),
        ]
    return result[0], more


def unmix_kernel(slot_count, experts, part, *refs):
    me_ref = refs[0]
    ret_refs = refs[1 : 1 + experts]
    att_refs = refs[1 + experts : 1 + experts + slot_count]
    rest = refs[1 + experts + slot_count :]
    second_ref, middle_ref, cot_ref, w_out_ref, gain_ref, control_ref = rest[:6]
    rest = rest[6:]
    if part:
        old_out_ref, old_control_ref, old_gain_ref = rest[2:5]
        rest = rest[5:]
    out_ref, grad_middle_ref = rest[:2]
    back_refs = rest[2 : 2 + slot_count]
    grad_out_ref, grad_control_ref, grad_gain_ref = rest[2 + slot_count :]
    rows, piece, width = att_refs[0].shape
    tokens = rows * slot_count
    me = me_ref[0]

    @pl.when(pl.program_id(0) == 0)
    def _():
        if part:
            grad_out_ref[...] = old_out_ref[...]
            grad_control_ref[...] = old_control_ref[...]
            grad_gain_ref[...] = old_gain_ref[...]
        else:
            grad_out_ref[...] = jnp.zeros_like(grad_out_ref)
            grad_control_ref[...] = jnp.zeros_like(grad_control_ref)
            grad_gain_ref[...] = jnp.zeros_like(grad_gain_ref)

    second = second_ref[...].reshape(-1, width)
    middle = middle_ref[...].reshape(-1, width)
    cot = jnp.concatenate(
        [cot_ref[pl.ds((me ^ j) * rows, rows)] for j in range(slot_count)], axis=0
    ).reshape(-1, width)
    own, group, _ = diagonal(piece)
    log_total = jnp.zeros((piece, LANES), f32)
    inner = jnp.zeros((piece, LANES), f32)
    for e in range(experts):
        stats = ret_refs[e][:, 2 * width :].astype(f32)
        mine = group == e
        log_total = jnp.where(mine, stats[:, 0:1] + stats[:, 1:2] + stats[:, 2:3], log_total)
        inner = jnp.where(mine, stats[:, 3:4] + stats[:, 4:5] + stats[:, 5:6], inner)
    results = jnp.concatenate([ref[:, :width] for ref in ret_refs], axis=0)
    back = jnp.concatenate([ref[:, width : 2 * width] for ref in ret_refs], axis=0)
    control = control_ref[...]
    logits = dot(second, control, NT).reshape(tokens, piece, LANES)
    weights = jnp.where(own, jnp.exp(logits - log_total), 0.0)
    low = weights.reshape(-1, LANES).astype(bf16)
    output = (middle + dot(low, results).astype(bf16).astype(f32)).astype(bf16)
    grad_weights = (dot(cot, results, NT) + dot(second, back, NT)).reshape(tokens, piece, LANES)
    grad_logits = (weights * (grad_weights - inner)).reshape(-1, LANES).astype(bf16)
    grad_second = dot(low, back) + dot(grad_logits, control)
    grad_second = grad_second.astype(bf16).astype(f32)
    grad_control_ref[...] += dot(grad_logits, second, TN)
    normed, scaled = normalize(middle)
    product = (grad_second * normed).reshape(-1, 8, width)
    grad_gain_ref[...] += jnp.sum(product, axis=0)
    grad_middle = cot.astype(f32) + norm_back(grad_second * gain_ref[...], normed, scaled)
    grad_middle = grad_middle.astype(bf16)
    grad_attended = dot(grad_middle, w_out_ref[...], NT).astype(bf16)
    output = output.reshape(tokens, piece, width)
    grad_attended = grad_attended.reshape(tokens, piece, width)
    grad_middle_ref[...] = grad_middle.reshape(tokens, piece, width)
    for j in range(slot_count):
        mine = slice(j * rows, (j + 1) * rows)
        out_ref[pl.ds((me ^ j) * rows, rows)] = output[mine]
        back_refs[j][...] = grad_attended[mine]
    attended = jnp.concatenate([ref[...] for ref in att_refs], axis=0).reshape(-1, width)
    grad_out_ref[...] += dot(attended, grad_middle, TN)


def unmix(me, part, ret_slots, att_slots, second, middle, cotangent, w_out, gain, control, before):
    slot_count, experts = len(att_slots), len(ret_slots)
    rows, positions, width = att_slots[0].shape
    tokens = rows * slot_count
    piece = LANES // experts
    steps = positions // piece
    span = pl.BlockSpec((tokens, piece, width), lambda b, me: (0, b, 0))
    shifted = pl.BlockSpec((tokens, piece, width), lambda b, me: (0, part * steps + b, 0))
    slot = pl.BlockSpec((rows, piece, width), lambda b, me: (0, b, 0))
    full = (shifted, cotangent.shape, bf16)
    sums = [
        (whole(width, width), (width, width), f32),
        (whole(LANES, width), (LANES, width), f32),
        (whole(8, width), (8, width), f32),
    ]
    count = 1 + experts + slot_count + 6
    result = call(
        functools.partial(unmix_kernel, slot_count, experts, part),
        "unmix",
        (steps,),
        [pl.BlockSpec((piece, 2 * width + LANES), lambda b, me: (b, 0))] * experts
        + [slot] * slot_count
        + [span, span, shifted, whole(width, width), whole(1, width), whole(LANES, width)]
        + ([pl.BlockSpec(memory_space=pl.ANY)] * 2 + [spec for spec, _, _ in sums] if part else []),
        [full, full] + [(slot, (rows, positions, width), bf16)] * slot_count + sums,
        [],
        (me, *ret_slots, *att_slots, second, middle, cotangent, w_out, gain, control, *before),
        positions * 17 / 256,
        {count: 0, count + 1: 1} if part else None,
    )
    do_slots = result[2 : 2 + slot_count]
    return do_slots, result[:2] + result[2 + slot_count :]


def finish_kernel(slot_count, row_count, *refs):
    me_ref = refs[0]
    gf_refs = refs[1 : 1 + slot_count * row_count]
    inputs_ref, grad_middle_ref, gain_ref, out_ref = refs[1 + slot_count * row_count :]
    me = me_ref[0]
    for j in range(slot_count):
        for row in range(row_count):
            place = (me ^ j) * row_count + row
            normed, scaled = normalize(inputs_ref[place].astype(f32))
            incoming = gf_refs[row * slot_count + j][0].astype(f32) * gain_ref[...]
            grad = norm_back(incoming, normed, scaled)
            grad = grad + grad_middle_ref[j * row_count + row].astype(f32)
            out_ref[place] = grad.astype(bf16)


def finish(me, gf_rows, inputs, grad_middle, gain):
    slot_count, row_count = len(gf_rows[0]), len(gf_rows)
    tokens, positions, width = inputs.shape
    piece = 64
    span = pl.BlockSpec((tokens, piece, width), lambda b, me: (0, b, 0))
    slot = pl.BlockSpec((1, piece, width), lambda b, me: (0, b, 0))
    return call(
        functools.partial(finish_kernel, slot_count, row_count),
        "finish",
        (positions // piece,),
        [slot] * (slot_count * row_count) + [span, span, whole(1, width)],
        [(span, (tokens, positions, width), bf16)],
        [],
        (me, *[gf for row in gf_rows for gf in row], inputs, grad_middle, gain),
        6,
    )[0]


def on_device(
    sizes,
    inputs,
    segments,
    cotangent,
    gain_attn,
    w_qkv,
    w_out,
    gain_mix,
    w_control,
    w_expand,
    w_shrink,
):
    groups, members, slots = sizes
    local_rows, positions, width = inputs.shape
    experts = w_expand.shape[0]
    rows = local_rows // slots
    place = (("gq", groups), ("gi", members), ("seq", slots))
    owners = (("gq", groups), ("seq", slots))
    seq_me = lax.axis_index("seq")
    member = lax.axis_index("gi")
    me = seq_me.astype(jnp.int32).reshape(1)

    parts = 2 if positions % BLOCK == 0 else 1

    def row_parts(array):
        return [
            lax.dynamic_slice_in_dim(array, (seq_me ^ j) * rows, rows, axis=0) for j in range(slots)
        ]

    marks = segments.astype(bf16)[:, None, :]
    marks = jnp.pad(marks, ((0, 0), (0, MARKS - 1), (0, width - positions)))
    x_parts = row_parts(jnp.concatenate([inputs, marks], axis=1))
    x_parts = [[x[row : row + 1] for x in x_parts] for row in range(rows)]
    x_rows = [swap_slots(x_parts[0], "seq")]

    small = jnp.concatenate([gain_attn[None], gain_mix[None], w_control], axis=0)
    small = jnp.pad(jnp.transpose(small), ((0, 0), (0, LANES - 2 - experts)))
    packed = jnp.concatenate([w_qkv, w_out, small], axis=1).astype(bf16)
    packed = Doubling(packed, place, ("gq", "seq", "core"))
    packed.at_once("gi")
    packed.steps("gq")

    def member_parts(array):
        return [
            lax.dynamic_index_in_dim(array, member ^ j, 0, keepdims=False) for j in range(members)
        ]

    weights = member_parts(pack_expert(w_expand.astype(bf16), w_shrink.astype(bf16)))
    weights = jnp.stack(natural(swap_slots(weights, "gi"), member))
    x_rows[0], x_parts, packed.value, weights = hold(
        (x_rows[0], x_parts, packed.value, weights)
    )
    tail = weights.shape[1] // 2
    halves = [
        Doubling(half, owners, ("gq", "seq"), 1) for half in (weights[:, :tail], weights[:, tail:])
    ]
    halves[0].steps("gq")
    halves[1].value = together(halves[1].value, halves[0])
    halves[1].steps("gq")
    packed.steps("seq").steps("core")
    x_rows[0], x_parts = together((x_rows[0], x_parts), packed, *halves)
    packed = packed.value.reshape(width, -1)
    proj_in, proj_out = packed[:, : 3 * width], packed[:, 3 * width : 4 * width]
    vectors = jnp.transpose(packed[:, 4 * width :])
    gain_one = vectors[0:1].astype(f32)
    gain_two = vectors[1:2].astype(f32)
    control = natural([vectors[2 + e : 3 + e] for e in range(experts)], member)
    control = jnp.concatenate(
        [jnp.broadcast_to(c, (LANES // experts, width)) for c in control], axis=0
    )

    old = []
    for row in range(rows):
        old = attend_first(me, row, rows, x_rows[row], gain_one, proj_in, parts, old)
        if row + 1 < rows:
            x_rows.append(swap_slots(x_parts[row + 1], "seq"))
            old, x_rows[row + 1] = together((old, x_rows[row + 1]), halves[0])
        if row == max(0, rows - 2):
            halves[0].steps("seq")
        if row == rows - 1:
            old = together(old, *halves)
    halves[1].steps("seq")
    att, projected, kept = old[:slots], old[slots : slots + 6], old[slots + 6 :]
    att_parts, kept = [swap_slots(att, "seq")], [kept]
    for part in range(1, parts):
        att, more = attend_next(me, part, parts, projected, slots)
        att, att_parts[-1] = hold((att, att_parts[-1]))
        att_parts.append(swap_slots(att, "seq"))
        kept.append(more)
    pay_parts, second_parts, middle_parts = [], [], []
    for part in range(parts):
        pay, second, middle = mix(
            me, part, att_parts[part], inputs, cotangent, proj_out, gain_two, control, experts
        )
        if part == 0:
            pay, second, middle = together((pay, second, middle), halves[1])
            halves = [half.value.reshape(-1, *half.value.shape[-2:]) for half in halves]
            halves = [(half, partner(half, "seq", slots, 1)) for half in halves]
        pay_parts.append(swap_slots(pay, "gi"))
        second_parts.append(second)
        middle_parts.append(middle)
    ret_parts, earlier = [], []
    for part in range(parts):
        back, more = expert(me, seq_me % 2, part, parts, pay_parts[part], halves, earlier)
        earlier = earlier + list(more)
        if part + 1 < parts:
            pay_parts[part + 1], back = hold((pay_parts[part + 1], back))
        elif part:
            back, more, ret_parts = hold((back, more, ret_parts))
        ret_parts.append(swap_slots([back] * members, "gi"))

    keep, send = more
    bits = [2] * len(bits_of((("gq", groups),)))
    bits += [members] + [2] * (len(bits_of((("seq", slots),))) - 1)
    total = keep.astype(f32) + partner(send, "seq", slots, 1).astype(f32)
    sum_expert = Halving(total.reshape(*bits, *total.shape[1:]), owners, ("seq", "gq"), 1)
    do_parts, before = [], []
    for part in range(parts):
        do, before = unmix(
            me,
            part,
            ret_parts[part],
            att_parts[part],
            second_parts[part],
            middle_parts[part],
            cotangent,
            proj_out,
            gain_two,
            control,
            before,
        )
        do, before = together((do, before), sum_expert)
        if part == 0:
            sum_expert.steps("seq")
        do_parts.append(swap_slots(do, "seq"))
    output, grad_middle, grad_out, grad_control, grad_gain = before
    grad_control = grad_control.reshape(experts, LANES // experts, width).sum(axis=1)
    grad_control = jnp.concatenate(
        natural([grad_control[e : e + 1] for e in range(experts)], member), axis=0
    )
    small = jnp.concatenate([grad_gain.sum(axis=0, keepdims=True), grad_control], axis=0)
    small = jnp.pad(jnp.transpose(small), ((0, 0), (0, LANES - 1 - experts)))
    every_bit = [2] * len(bits_of(place))
    grad_out = jnp.concatenate([grad_out, small], axis=1)
    sum_out = Halving(grad_out.reshape(*every_bit, -1, width + LANES), place, ("core",))
    sum_out.left = bits_of(place)
    sum_out.steps("core")
    do_parts = together(do_parts, sum_out, sum_expert)
    sum_expert.steps("gq")

    gf_rows, grad_in = [], None
    for row in range(rows):
        gf_slots, grad_in = attend_back(
            me,
            row,
            rows,
            groups * members * slots,
            x_rows[row],
            do_parts,
            gain_one,
            proj_in,
            projected,
            kept,
            grad_in,
        )
        grad_in = grad_in[0] if row < rows - 1 else grad_in
        if row == 0:
            gf_slots, grad_in = together((gf_slots, grad_in), sum_expert)
            columns = swap_slots(
                [p if j == 0 else p.astype(bf16) for j, p in enumerate(member_parts(sum_expert.value))],
                "gi",
            )
        if row == rows - 1:
            gf_slots, grad_in, columns, gf_rows = hold((gf_slots, grad_in, columns, gf_rows))
        gf_rows.append(swap_slots(gf_slots, "seq"))
    columns = jnp.stack([c.astype(f32) for c in natural(columns, member)])
    grad_expand, grad_shrink = unpack_expert(columns, width // (groups * members * slots))
    keep, send = grad_in
    total = keep + partner(send, "seq", slots, 1).astype(f32)
    total = total.reshape(*every_bit[1:], *total.shape[1:])
    total = jnp.concatenate([total, sum_out.value], axis=-1)
    sum_in = Halving(total, place, ("gi", "gq", "seq"))
    sum_in.step(sum_in.order.pop(0))
    gf_rows[-1] = together(gf_rows[-1], sum_in)
    sum_in.steps("gi")
    grad_inputs = finish(me, gf_rows, inputs, grad_middle, gain_one)
    grad_inputs = together(grad_inputs, sum_in)
    total = sum_in.finish()
    grad_in, grad_out = total[:, : 3 * width], total[:, 3 * width :]
    small = jnp.transpose(grad_out[:, width:])
    weighted = jnp.sum(grad_in * w_qkv.astype(bf16).astype(f32), axis=1)
    return (
        output,
        grad_inputs,
        weighted / gain_attn.astype(bf16).astype(f32),
        grad_in,
        grad_out[:, :width],
        small[0],
        small[1 : 1 + experts],
        grad_expand,
        grad_shrink,
    )


def solution(mesh):
    dp_count, seq_count = mesh.shape["dp"], mesh.shape["seq"]

    def run(inputs, *args):
        members = GROUP * dp_count // inputs.shape[0]
        sizes = (dp_count // members, members, seq_count)
        fine = Mesh(mesh.devices.reshape(sizes), ("gq", "gi", "seq"))
        dp, both = ("gq", "gi"), ("gq", "gi", "seq")
        return jax.shard_map(
            functools.partial(on_device, sizes),
            mesh=fine,
            in_specs=(
                P(dp, "seq", None),
                P(dp, "seq"),
                P(dp, "seq", None),
                P(both),
                P(both, None),
                P(both, None),
                P(both),
                P(None, both),
                P(None, both, None),
                P(None, both, None),
            ),
            out_specs=(
                P(dp, "seq", None),
                P(dp, "seq", None),
                P(both),
                P(both, None),
                P(both, None),
                P(both),
                P(None, both),
                P(None, both, None),
                P(None, both, None),
            ),
            check_vma=False,
        )(inputs, *args)

    return run
```

time: 420 us -> 390 us (0.929); the launches traced: 418 us -> 384 us
  waiting for transfers between devices: 161 us -> 122 us
  Pallas kernels: 132 us -> 159 us
  between operations: 14.2 us -> 2.1 us
  starting transfers between devices: 61.9 us -> 56.5 us
  local copies, waits for them, and re-layouts: 26.9 us -> 21.6 us
    pallas_call x6 -> x12, Pallas kernels: 132 us -> 159 us  [call(): pl.pallas_call(kernel, grid_spec=pltpu.PrefetchScalarGridSpec(num_scalar_...]
    ppermute x48 -> x63, waiting for transfers between devices: 145 us -> 122 us  [partner(): return lax.ppermute(value, axis, [(i, i ^ mask) for i in range(size)])]
    reduce_scatter x2 -> x0, waiting for transfers between devices: 15.7 us -> none  [to_places(): lax.psum_scatter(array, ('gq', 'seq'), scatter_dimension=0, tiled=True)[0]]
    reshape x4 -> x2, local copies, waits for them, and re-layouts: 11 us -> 0.85 us  [the longest x1 0.83 us: unpack_expert(): expand = jnp.swapaxes(expand, 1, 2).reshape(experts, lines, -1)]
    unnamed x44 -> x108, local copies, waits for them, and re-layouts: 5.33 us -> 12.8 us
    ppermute x48 -> x63, starting transfers between devices: 61.7 us -> 56.5 us  [partner(): return lax.ppermute(value, axis, [(i, i ^ mask) for i in range(size)])]
    add x9, other arithmetic: 3.91 us -> 8.81 us  [the longest x7 4.87 us: step(): self.value = keep.astype(f32) + other.astype(f32)]
  transfers between devices with their start and end apart: 52 -> 63, of which waited for: 27 -> 22; matrix products, arithmetic and copies ran while one was open for 8% -> 4% of each run, Pallas kernels for 25% -> 41%
where the time goes in v2:
time: 390 us; the launch traced here: 384 us
  Pallas kernels  159 us (41%)
  waiting for transfers between devices  122 us (31%)
  starting transfers between devices  56.5 us (14%)
  other arithmetic  22.5 us (6%)
  local copies, waits for them, and re-layouts  21.6 us (6%)
    pallas_call x12, Pallas kernels, call(): pl.pallas_call(kernel, grid_spec=pltpu.PrefetchScalarGridSpec(num_scalar_...  159 us
    ppermute x63, waiting for transfers between devices, partner(): return lax.ppermute(value, axis, [(i, i ^ mask) for i in range(size)])  122 us
    ppermute x63, starting transfers between devices, partner(): return lax.ppermute(value, axis, [(i, i ^ mask) for i in range(size)])  56.5 us
    unnamed x108, local copies, waits for them, and re-layouts  12.8 us
  transfers between devices with their start and end apart: 63, of which 22 were waited for; matrix products, arithmetic and copies ran while one was open for 4% of the time, Pallas kernels for 41%

profile of v2, /device:TPU:0, one launch (start us, length us, event | category | flops | bytes accessed | tf_op | source)
XLA Modules:
  0.0 383.9 jit_solution(18391615035825967846)
XLA Ops:
  4.6 4.0 %collective-permute-start.3 = (bf16[16,2176]{1,0:T(8,128)(2,1)}, bf16[16,2176]{1,0:T(8,128)(2,1)S(1)}, u32[]{:S(2)}, u32[]{:S(2)}) collective-permute-start(bf16[16,2176]{1,0:T(8,128)(2,1)} %fusion.30), channel_id=1, source_target_pairs={{0,12},{4,8},{8,4},{12,0},{1,13},{5,9},{9,5},{13,1},{2,14},{6,10},... | collective-permute-start | bytes 208904 | tf_op jit(solution)/shard_map/ppermute | solution.py:58
  11.3 3.0 collective-permute-start.7
  15.7 1.1 constant_dynamic-slice_fusion.4
  17.0 1.9 collective-permute-start.1
  19.9 2.6 collective-permute-start.6
  22.7 12.9 %collective-permute-done.6 = bf16[2,2,16,2176]{3,2,1,0:T(8,128)(2,1)S(1)} collective-permute-done((bf16[2,2,16,2176]{3,2,1,0:T(8,128)(2,1)S(1)}, bf16[2,2,16,2176]{3,2,1,0:T(8,128)(2,1)S(1)}, u32[]{:S(2)}, u32[]{:S(2)}) %collective-permute-start.6) | collective-permute-done | bytes 278560 | tf_op jit(solution)/shard_map/ppermute | solution.py:58
  37.9 12.9 %collective-permute-done.10 = bf16[2,2,2,16,2176]{4,3,2,1,0:T(8,128)(2,1)S(1)} collective-permute-done((bf16[2,2,2,16,2176]{4,3,2,1,0:T(8,128)(2,1)S(1)}, bf16[2,2,2,16,2176]{4,3,2,1,0:T(8,128)(2,1)S(1)}, u32[]{:S(2)}, u32[]{:S(2)}) %collective-permute-start.10) | collective-permute-done | bytes 557088 | tf_op jit(solution)/shard_map/ppermute | solution.py:58
  52.2 15.2 %collective-permute-done.13 = bf16[4,64,512]{2,1,0:T(8,128)(2,1)S(1)} collective-permute-done((bf16[4,64,512]{2,1,0:T(8,128)(2,1)S(1)}, bf16[4,64,512]{2,1,0:T(8,128)(2,1)S(1)}, u32[]{:S(2)}, u32[]{:S(2)}) %collective-permute-start.13) | collective-permute-done | bytes 262176 | tf_op jit(solution)/shard_map/ppermute | solution.py:58
  68.3 1.3 slice.125.refs_6_.refs_15_
  70.8 1.3 collective-permute-start.16
  72.2 14.2 %attend_first.2 = (bf16[2,128,512]{2,1,0:T(8,128)(2,1)}, bf16[2,128,512]{2,1,0:T(8,128)(2,1)}, bf16[2,128,512]{2,1,0:T(8,128)(2,1)}, bf16[2,128,512]{2,1,0:T(8,1...) custom-call(s32[1]{0:T(128)} %bitcast.refs_0_, ...), custom_call_target="tpu_custom_call" | custom-call | flops 12000000000 | bytes 1048576 | tf_op jit(solution)/shard_map/attend_first/pallas_call | solution.py:166
  89.2 13.6 %attend_first.3 = (bf16[2,128,512]{2,1,0:T(8,128)(2,1)}, bf16[2,128,512]{2,1,0:T(8,128)(2,1)}, bf16[2,128,512]{2,1,0:T(8,128)(2,1)}, bf16[2,128,512]{2,1,0:T(8,1...) custom-call(s32[1]{0:T(128)} %bitcast.refs_0_, ...), custom_call_target="tpu_custom_call", output_to_operand_aliasing={{0}: (7, {}), {1}: (8, {}), {2}: (9, {}), {3}: (10, {}), {4... | custom-call | flops 12000000000 | bytes 1048576 | tf_op jit(solution)/shard_map/attend_first/pallas_call | solution.py:166
  103.0 1.6 collective-permute-start.27
  105.1 1.3 collective-permute-start.20
  106.9 16.5 %attend_next.1 = (bf16[2,128,512]{2,1,0:T(8,128)(2,1)}, bf16[2,128,512]{2,1,0:T(8,128)(2,1)}, bf16[2,128,512]{2,1,0:T(8,128)(2,1)}, bf16[2,128,512]{2,1,0:T(8,12...) custom-call(s32[1]{0:T(128)} %bitcast.refs_0_, s32[2,1,1024]{2,1,0:T(1,128)} %get-tuple-element.290.refs_1_.refs_13_, ...), custom_call_target="tpu_custom_call" | custom-call | flops 14000000000 | bytes 1048576 | tf_op jit(solution)/shard_map/attend_next/pallas_call | solution.py:166
  123.5 3.8 collective-permute-done.20.refs_4_.refs_8_
  127.9 7.1 %mix.3 = (bf16[128,1152]{1,0:T(8,128)(2,1)}, bf16[128,1152]{1,0:T(8,128)(2,1)}, bf16[128,1152]{1,0:T(8,128)(2,1)}, bf16[128,1152]{1,0:T(8,128)(2,1)}, bf16[8,128...) custom-call(s32[1]{0:T(128)} %bitcast.refs_0_, bf16[2,128,512]{2,1,0:T(8,128)(2,1)} %get-tuple-element.310.refs_1_.refs_5_, ...), custom_call_target="tpu_custom_call" | custom-call | flops 6000000000 | bytes 1048576 | tf_op jit(solution)/shard_map/mix/pallas_call | solution.py:166
  136.8 1.5 collective-permute-start.22
  138.9 2.1 collective-permute-start.28
  140.9 5.0 %collective-permute-done.22.refs_3_.refs_7_ = bf16[2,128,512]{2,1,0:T(8,128)(2,1)S(1)} collective-permute-done((bf16[2,128,512]{2,1,0:T(8,128)(2,1)S(1)}, bf16[2,128,512]{2,1,0:T(8,128)(2,1)S(1)}, u32[]{:S(2)}, u32[]{:S(2)}) %collective-permute-start.22) | collective-permute-done | bytes 262176 | tf_op jit(solution)/shard_map/ppermute | solution.py:58
  146.0 3.8 %collective-permute-done.23.refs_4_.refs_8_ = bf16[2,128,512]{2,1,0:T(8,128)(2,1)S(1)} collective-permute-done((bf16[2,128,512]{2,1,0:T(8,128)(2,1)S(1)}, bf16[2,128,512]{2,1,0:T(8,128)(2,1)S(1)}, u32[]{:S(2)}, u32[]{:S(2)}) %collective-permute-start.23) | collective-permute-done | bytes 262176 | tf_op jit(solution)/shard_map/ppermute | solution.py:58
  150.6 7.2 %mix.2 = (bf16[128,1152]{1,0:T(8,128)(2,1)}, bf16[128,1152]{1,0:T(8,128)(2,1)}, bf16[128,1152]{1,0:T(8,128)(2,1)}, bf16[128,1152]{1,0:T(8,128)(2,1)}, bf16[8,128...) custom-call(s32[1]{0:T(128)} %bitcast.refs_0_, bf16[2,128,512]{2,1,0:T(8,128)(2,1)} %get-tuple-element.302.refs_1_.refs_5_, ...), custom_call_target="tpu_custom_call" | custom-call | flops 6000000000 | bytes 1048576 | tf_op jit(solution)/shard_map/mix/pallas_call | solution.py:166
  157.8 2.1 collective-permute-start.24
  159.9 1.5 collective-permute-start.25
  161.4 1.4 collective-permute-start.26
  163.9 7.3 %expert.2 = (bf16[128,1152]{1,0:T(8,128)(2,1)}, bf16[128,512]{1,0:T(8,128)(2,1)}, bf16[128,512]{1,0:T(8,128)(2,1)}, bf16[128,2048]{1,0:T(8,128)(2,1)}, bf16[128,2048]{1,0:T(8,128)(2,1)}) custom-call(s32[1]{0:T(128)} %bitcast.refs_0_, bf16[128,1152]{1,0:T(8,128)(2,1)} %get-tuple-element.321.refs_1_, bf16[128,1152]{1,0:T(8,128)(2,1)} %collective-permute-done.28.refs_2_, ...), custom_call_target="tpu_custom_call" | custom-call | flops 7000000000 | bytes 1048576 | tf_op jit(solution)/shard_map/expert/pallas_call | solution.py:166
  171.2 5.9 %collective-permute-done.26.refs_4_ = bf16[128,1152]{1,0:T(8,128)(2,1)S(1)} collective-permute-done((bf16[128,1152]{1,0:T(8,128)(2,1)}, bf16[128,1152]{1,0:T(8,128)(2,1)S(1)}, u32[]{:S(2)}, u32[]{:S(2)}) %collective-permute-start.26) | collective-permute-done | bytes 294944 | tf_op jit(solution)/shard_map/ppermute | solution.py:58
  178.4 1.5 collective-permute-start.34
  179.9 1.4 collective-permute-start.35
  181.3 9.3 %expert.3 = (bf16[128,1152]{1,0:T(8,128)(2,1)}, bf16[16,128,512]{2,1,0:T(8,128)(2,1)}, bf16[16,128,512]{2,1,0:T(8,128)(2,1)}) custom-call(s32[1]{0:T(128)} %bitcast.refs_0_, bf16[128,1152]{1,0:T(8,128)(2,1)} %get-tuple-element.328.refs_1_, bf16[128,1152]{1,0:T(8,128)(2,1)} %copy-done.26, bf16[128,1152]{1,0:T(8,128)(2,1)} %copy-done.27, ...), custom_call_target="tpu_custom_call" | custom-call | flops 7000000000 | bytes 1048576 | tf_op jit(solution)/shard_map/expert/pallas_call | solution.py:166
  190.6 3.8 collective-permute-done.35.refs_4_
  195.0 1.5 collective-permute-start.37
  196.6 1.4 collective-permute-start.38
  197.9 9.9 %unmix.2 = (bf16[8,256,512]{2,1,0:T(8,128)(2,1)}, bf16[8,256,512]{2,1,0:T(8,128)(2,1)}, bf16[2,128,512]{2,1,0:T(8,128)(2,1)}, bf16[2,128,512]{2,1,0:T(8,128)(2,1...) custom-call(s32[1]{0:T(128)} %bitcast.refs_0_, ...), custom_call_target="tpu_custom_call" | custom-call | flops 8499999744 | bytes 1048576 | tf_op jit(solution)/shard_map/unmix/pallas_call | solution.py:166
  207.9 2.3 convert_add_fusion
  210.2 2.0 copy-done
  212.3 1.5 collective-permute-start.40
  214.8 10.3 %unmix.3 = (bf16[8,256,512]{2,1,0:T(8,128)(2,1)}, bf16[8,256,512]{2,1,0:T(8,128)(2,1)}, bf16[2,128,512]{2,1,0:T(8,128)(2,1)}, bf16[2,128,512]{2,1,0:T(8,128)(2,1...) custom-call(s32[1]{0:T(128)} %bitcast.refs_0_, ...), custom_call_target="tpu_custom_call", output_to_operand_aliasing={{0}: (15, {}), {1}: (16, {})} | custom-call | flops 8499999744 | bytes 1048576 | tf_op jit(solution)/shard_map/unmix/pallas_call | solution.py:166
  225.1 12.1 %collective-permute-done.40 = bf16[2,4,128,512]{3,2,1,0:T(8,128)(2,1)} collective-permute-done((bf16[2,4,128,512]{3,2,1,0:T(8,128)(2,1)S(1)}, bf16[2,4,128,512]{3,2,1,0:T(8,128)(2,1)}, u32[]{:S(2)}, u32[]{:S(2)}) %collective-permute-start.40) | collective-permute-done | bytes 1048608 | tf_op jit(solution)/shard_map/ppermute | solution.py:58
  237.2 2.3 bitcast_add_fusion
  239.8 1.3 select_maximum_fusion
  242.8 1.5 collective-permute-start.42
  245.0 1.5 collective-permute-start.45
  246.7 1.1 bitcast_add_fusion.2
  247.9 4.4 %collective-permute-done.42.refs_7_ = bf16[2,128,512]{2,1,0:T(8,128)(2,1)} collective-permute-done((bf16[2,128,512]{2,1,0:T(8,128)(2,1)}, bf16[2,128,512]{2,1,0:T(8,128)(2,1)}, u32[]{:S(2)}, u32[]{:S(2)}) %collective-permute-start.42) | collective-permute-done | bytes 262176 | tf_op jit(solution)/shard_map/ppermute | solution.py:58
  252.3 4.5 %collective-permute-done.43.refs_8_ = bf16[2,128,512]{2,1,0:T(8,128)(2,1)} collective-permute-done((bf16[2,128,512]{2,1,0:T(8,128)(2,1)S(1)}, bf16[2,128,512]{2,1,0:T(8,128)(2,1)}, u32[]{:S(2)}, u32[]{:S(2)}) %collective-permute-start.43) | collective-permute-done | bytes 262176 | tf_op jit(solution)/shard_map/ppermute | solution.py:58
  256.8 6.7 %collective-permute-done.45.refs_11_ = bf16[2,128,512]{2,1,0:T(8,128)(2,1)} collective-permute-done((bf16[2,128,512]{2,1,0:T(8,128)(2,1)}, bf16[2,128,512]{2,1,0:T(8,128)(2,1)}, u32[]{:S(2)}, u32[]{:S(2)}) %collective-permute-start.45) | collective-permute-done | bytes 262176 | tf_op jit(solution)/shard_map/ppermute | solution.py:58
  263.5 3.9 %collective-permute-done.46.refs_12_ = bf16[2,128,512]{2,1,0:T(8,128)(2,1)} collective-permute-done((bf16[2,128,512]{2,1,0:T(8,128)(2,1)}, bf16[2,128,512]{2,1,0:T(8,128)(2,1)}, u32[]{:S(2)}, u32[]{:S(2)}) %collective-permute-start.46) | collective-permute-done | bytes 262176 | tf_op jit(solution)/shard_map/ppermute | solution.py:58
  267.5 1.4 collective-permute-start.48
  268.9 28.6 %attend_back.2 = (bf16[1,256,512]{2,1,0:T(8,128)(2,1)}, bf16[1,256,512]{2,1,0:T(8,128)(2,1)}, bf16[1,256,512]{2,1,0:T(8,128)(2,1)}, bf16[1,256,512]{2,1,0:T(8,128)(2,1)}, f32[512,1536]{1,0:T(8,128)}) custom-call(s32[1]{0:T(128)} %bitcast.refs_0_, bf16[1,272,512]{2,1,0:T(8,128)(2,1)} %get-tuple-element.238.refs_1_, bf16[1,272,512]{2,1,0:T(8,128)(2,1)} %copy-done.29, ...), custom_call_target="tpu_custom_call" | custom-call | flops 28000000000 | bytes 1048576 | tf_op jit(solution)/shard_map/attend_back/pallas_call | solution.py:166
  299.8 2.4 collective-permute-start.51
  302.2 1.4 collective-permute-start.53
  305.3 29.2 %attend_back.3 = (bf16[1,256,512]{2,1,0:T(8,128)(2,1)}, bf16[1,256,512]{2,1,0:T(8,128)(2,1)}, bf16[1,256,512]{2,1,0:T(8,128)(2,1)}, bf16[1,256,512]{2,1,0:T(8,12...) custom-call(s32[1]{0:T(128)} %bitcast.refs_0_, bf16[1,272,512]{2,1,0:T(8,128)(2,1)} %get-tuple-element.260.refs_1_, ...), custom_call_target="tpu_custom_call" | custom-call | flops 28000000000 | bytes 1048576 | tf_op jit(solution)/shard_map/attend_back/pallas_call | solution.py:166
  334.6 1.7 dynamic-slice_bitcast_fusion
  337.8 2.1 collective-permute-done.58
  339.9 1.6 convert_add_fusion.1
  342.9 1.2 collective-permute-start.57
  344.2 12.5 %collective-permute-done.59 = bf16[2,2,2,16,2176]{4,3,2,1,0:T(8,128)(2,1)} collective-permute-done((bf16[2,2,2,16,2176]{4,3,2,1,0:T(8,128)(2,1)S(1)}, bf16[2,2,2,16,2176]{4,3,2,1,0:T(8,128)(2,1)}, u32[]{:S(2)}, u32[]{:S(2)}) %collective-permute-start.59) | collective-permute-done | bytes 557088 | tf_op jit(solution)/shard_map/ppermute | solution.py:58
  356.7 1.1 fusion.7
  359.9 6.1 %finish.1 = bf16[8,256,512]{2,1,0:T(8,128)(2,1)} custom-call(s32[1]{0:T(128)} %bitcast.refs_0_, bf16[1,256,512]{2,1,0:T(8,128)(2,1)} %get-tuple-element.420.refs_1_, bf16[1,256,512]{2,1,0:T(8,128)(2,1)} %copy-done.41, bf16[1,256,512]{2,1,0:T(8,128)(2,1)} %copy-done.43, bf16[1,256,512]{2,1,0:T(8,128)(2,1)} %copy-done.44, ...), custom_call_target="tpu_custom_call" | custom-call | flops 6000000000 | bytes 1048576 | tf_op jit(solution)/shard_map/finish/pallas_call | solution.py:166
  366.0 1.5 collective-permute-done.60
  367.5 1.7 collective-permute-start.61
  369.4 6.3 %collective-permute-done.61 = bf16[2,16,2176]{2,1,0:T(8,128)(2,1)S(1)} collective-permute-done((bf16[2,16,2176]{2,1,0:T(8,128)(2,1)S(1)}, bf16[2,16,2176]{2,1,0:T(8,128)(2,1)S(1)}, u32[]{:S(2)}, u32[]{:S(2)}) %collective-permute-start.61) | collective-permute-done | bytes 139296 | tf_op jit(solution)/shard_map/ppermute | solution.py:58
  378.1 2.0 collective-permute-done.62
  (261 shorter events, 44.3 us)
Async XLA Ops:
  4.6 12.2 %collective-permute-start.3 = (bf16[16,2176]{1,0:T(8,128)(2,1)}, bf16[16,2176]{1,0:T(8,128)(2,1)S(1)}, u32[]{:S(2)}, u32[]{:S(2)}) collective-permute-start(bf16[16,2176]{1,0:T(8,128)(2,1)} %fusion.30), channel_id=1, source_target_pairs={{0,12},{4,8},{8,4},{12,0},{1,13},{5,9},{9,5},{13,1},{2,14},{6,10},... | collective-permute-start | bytes 208904 | tf_op jit(solution)/shard_map/ppermute | solution.py:58
  8.5 8.5 %collective-permute-start.4 = (bf16[16,2176]{1,0:T(8,128)(2,1)}, bf16[16,2176]{1,0:T(8,128)(2,1)S(1)}, u32[]{:S(2)}, u32[]{:S(2)}) collective-permute-start(bf16[16,2176]{1,0:T(8,128)(2,1)} %fusion.30), channel_id=1, source_target_pairs={{0,8},{4,12},{8,0},{12,4},{1,9},{5,13},{9,1},{13,5},{2,10},{6,14},... | collective-permute-start | bytes 208904 | tf_op jit(solution)/shard_map/ppermute | solution.py:58
  9.0 8.0 %collective-permute-start.5 = (bf16[16,2176]{1,0:T(8,128)(2,1)}, bf16[16,2176]{1,0:T(8,128)(2,1)S(1)}, u32[]{:S(2)}, u32[]{:S(2)}) collective-permute-start(bf16[16,2176]{1,0:T(8,128)(2,1)} %fusion.30), channel_id=1, source_target_pairs={{0,4},{4,0},{8,12},{12,8},{1,5},{5,1},{9,13},{13,9},{2,6},{6,2},{1... | collective-permute-start | bytes 208904 | tf_op jit(solution)/shard_map/ppermute | solution.py:58
  11.3 7.7 %collective-permute-start.7 = (bf16[128,512]{1,0:T(8,128)(2,1)S(1)}, bf16[128,512]{1,0:T(8,128)(2,1)S(1)}, u32[]{:S(2)}, u32[]{:S(2)}) collective-permute-start(bf16[128,512]{1,0:T(8,128)(2,1)S(1)} %get-tuple-element.532), channel_id=1, source_target_pairs={{0,12},{4,8},{8,4},{12,0},{1,13},{5,9},{9,5},{13,1},{2,14},{6,10},... | collective-permute-start | bytes 393224 | tf_op jit(solution)/shard_map/ppermute | solution.py:58
  14.3 5.6 %collective-permute-start.8 = (bf16[128,512]{1,0:T(8,128)(2,1)S(1)}, bf16[128,512]{1,0:T(8,128)(2,1)S(1)}, u32[]{:S(2)}, u32[]{:S(2)}) collective-permute-start(bf16[128,512]{1,0:T(8,128)(2,1)S(1)} %get-tuple-element.533), channel_id=1, source_target_pairs={{0,8},{4,12},{8,0},{12,4},{1,9},{5,13},{9,1},{13,5},{2,10},{6,14},... | collective-permute-start | bytes 393224 | tf_op jit(solution)/shard_map/ppermute | solution.py:58
  16.8 5.7 %collective-permute-start.9 = (bf16[128,512]{1,0:T(8,128)(2,1)S(1)}, bf16[128,512]{1,0:T(8,128)(2,1)S(1)}, u32[]{:S(2)}, u32[]{:S(2)}) collective-permute-start(bf16[128,512]{1,0:T(8,128)(2,1)S(1)} %get-tuple-element.531), channel_id=1, source_target_pairs={{0,4},{4,0},{8,12},{12,8},{1,5},{5,1},{9,13},{13,9},{2,6},{6,2},{1... | collective-permute-start | bytes 393224 | tf_op jit(solution)/shard_map/ppermute | solution.py:58
  17.0 18.8 %collective-permute-start = (bf16[1,272,512]{2,1,0:T(8,128)(2,1)S(1)}, bf16[1,272,512]{2,1,0:T(8,128)(2,1)S(1)}, u32[]{:S(2)}, u32[]{:S(2)}) collective-permute-start(bf16[1,272,512]{2,1,0:T(8,128)(2,1)S(1)} %get-tuple-element.501), channel_id=1, source_target_pairs={{0,1},{1,0},{2,3},{3,2},{4,5},{5,4},{6,7},{7,6},{8,9},{9,8},{10,11... | collective-permute-start | bytes 835592 | tf_op jit(solution)/shard_map/ppermute | solution.py:58
  17.0 18.8 %collective-permute-start.1 = (bf16[1,272,512]{2,1,0:T(8,128)(2,1)S(1)}, bf16[1,272,512]{2,1,0:T(8,128)(2,1)S(1)}, u32[]{:S(2)}, u32[]{:S(2)}) collective-permute-start(bf16[1,272,512]{2,1,0:T(8,128)(2,1)S(1)} %get-tuple-element.500), channel_id=1, source_target_pairs={{0,2},{1,3},{2,0},{3,1},{4,6},{5,7},{6,4},{7,5},{8,10},{9,11},{10,... | collective-permute-start | bytes 835592 | tf_op jit(solution)/shard_map/ppermute | solution.py:58
  19.1 16.8 %collective-permute-start.2 = (bf16[1,272,512]{2,1,0:T(8,128)(2,1)S(1)}, bf16[1,272,512]{2,1,0:T(8,128)(2,1)S(1)}, u32[]{:S(2)}, u32[]{:S(2)}) collective-permute-start(bf16[1,272,512]{2,1,0:T(8,128)(2,1)S(1)} %get-tuple-element.499), channel_id=1, source_target_pairs={{0,3},{1,2},{2,1},{3,0},{4,7},{5,6},{6,5},{7,4},{8,11},{9,10},{10,... | collective-permute-start | bytes 835592 | tf_op jit(solution)/shard_map/ppermute | solution.py:58
  19.9 15.7 %collective-permute-start.6 = (bf16[2,2,16,2176]{3,2,1,0:T(8,128)(2,1)S(1)}, bf16[2,2,16,2176]{3,2,1,0:T(8,128)(2,1)S(1)}, u32[]{:S(2)}, u32[]{:S(2)}) collective-permute-start(bf16[2,2,16,2176]{3,2,1,0:T(8,128)(2,1)S(1)} %bitcast.156), channel_id=1, source_target_pairs={{0,16},{16,0},{1,17},{17,1},{2,18},{18,2},{3,19},{19,3},{4,20},{20... | collective-permute-start | bytes 835592 | tf_op jit(solution)/shard_map/ppermute | solution.py:58
  36.8 14.0 %collective-permute-start.10 = (bf16[2,2,2,16,2176]{4,3,2,1,0:T(8,128)(2,1)S(1)}, bf16[2,2,2,16,2176]{4,3,2,1,0:T(8,128)(2,1)S(1)}, u32[]{:S(2)}, u32[]{:S(2)}) collective-permute-start(bf16[2,2,2,16,2176]{4,3,2,1,0:T(8,128)(2,1)S(1)} %pad_maximum_fusion.5), channel_id=1, source_target_pairs={{0,2},{1,3},{2,0},{3,1},{4,6},{5,7},{6,4},{7,5},{8,10},{9,11},{10,... | collective-permute-start | bytes 1671176 | tf_op jit(solution)/shard_map/ppermute | solution.py:58
  37.8 14.2 %collective-permute-start.12 = (bf16[4,64,512]{2,1,0:T(8,128)(2,1)S(1)}, bf16[4,64,512]{2,1,0:T(8,128)(2,1)S(1)}, u32[]{:S(2)}, u32[]{:S(2)}) collective-permute-start(bf16[4,64,512]{2,1,0:T(8,128)(2,1)S(1)} %slice.102), channel_id=1, source_target_pairs={{0,16},{16,0},{1,17},{17,1},{2,18},{18,2},{3,19},{19,3},{4,20},{20... | collective-permute-start | bytes 786440 | tf_op jit(solution)/shard_map/ppermute | solution.py:58
  52.0 15.5 %collective-permute-start.11 = (bf16[2,2,2,2,16,2176]{5,4,2,1,0,3:T(8,128)(2,1)}, bf16[2,2,2,2,16,2176]{5,4,2,1,0,3:T(8,128)(2,1)S(1)}, u32[]{:S(2)}, u32[]{:S(2)}) collective-permute-start(bf16[2,2,2,2,16,2176]{5,4,2,1,0,3:T(8,128)(2,1)} %pad_maximum_fusion.1), channel_id=1, source_target_pairs={{0,1},{1,0},{2,3},{3,2},{4,5},{5,4},{6,7},{7,6},{8,9},{9,8},{10,11... | collective-permute-start | bytes 3342344 | tf_op jit(solution)/shard_map/ppermute | solution.py:58
  52.2 15.3 %collective-permute-start.13 = (bf16[4,64,512]{2,1,0:T(8,128)(2,1)S(1)}, bf16[4,64,512]{2,1,0:T(8,128)(2,1)S(1)}, u32[]{:S(2)}, u32[]{:S(2)}) collective-permute-start(bf16[4,64,512]{2,1,0:T(8,128)(2,1)S(1)} %get-tuple-element.237), channel_id=1, source_target_pairs={{0,16},{16,0},{1,17},{17,1},{2,18},{18,2},{3,19},{19,3},{4,20},{20... | collective-permute-start | bytes 786440 | tf_op jit(solution)/shard_map/ppermute | solution.py:58
  70.3 17.6 %collective-permute-start.14 = (bf16[1,272,512]{2,1,0:T(8,128)(2,1)}, bf16[1,272,512]{2,1,0:T(8,128)(2,1)S(1)}, u32[]{:S(2)}, u32[]{:S(2)}) collective-permute-start(bf16[1,272,512]{2,1,0:T(8,128)(2,1)} %get-tuple-element.256), channel_id=1, source_target_pairs={{0,1},{1,0},{2,3},{3,2},{4,5},{5,4},{6,7},{7,6},{8,9},{9,8},{10,11... | collective-permute-start | bytes 835592 | tf_op jit(solution)/shard_map/ppermute | solution.py:58
  70.3 17.6 %collective-permute-start.15 = (bf16[1,272,512]{2,1,0:T(8,128)(2,1)}, bf16[1,272,512]{2,1,0:T(8,128)(2,1)S(1)}, u32[]{:S(2)}, u32[]{:S(2)}) collective-permute-start(bf16[1,272,512]{2,1,0:T(8,128)(2,1)} %get-tuple-element.257), channel_id=1, source_target_pairs={{0,2},{1,3},{2,0},{3,1},{4,6},{5,7},{6,4},{7,5},{8,10},{9,11},{10,... | collective-permute-start | bytes 835592 | tf_op jit(solution)/shard_map/ppermute | solution.py:58
  70.8 17.1 %collective-permute-start.16 = (bf16[1,272,512]{2,1,0:T(8,128)(2,1)}, bf16[1,272,512]{2,1,0:T(8,128)(2,1)}, u32[]{:S(2)}, u32[]{:S(2)}) collective-permute-start(bf16[1,272,512]{2,1,0:T(8,128)(2,1)} %get-tuple-element.258), channel_id=1, source_target_pairs={{0,3},{1,2},{2,1},{3,0},{4,7},{5,6},{6,5},{7,4},{8,11},{9,10},{10,... | collective-permute-start | bytes 835592 | tf_op jit(solution)/shard_map/ppermute | solution.py:58
  88.7 14.1 %collective-permute-start.17 = (bf16[2,4,64,512]{3,2,1,0:T(8,128)(2,1)S(1)}, bf16[2,4,64,512]{3,2,1,0:T(8,128)(2,1)S(1)}, u32[]{:S(2)}, u32[]{:S(2)}) collective-permute-start(bf16[2,4,64,512]{3,2,1,0:T(8,128)(2,1)S(1)} %pad_maximum_fusion.7), channel_id=1, source_target_pairs={{0,2},{1,3},{2,0},{3,1},{4,6},{5,7},{6,4},{7,5},{8,10},{9,11},{10,... | collective-permute-start | bytes 1572872 | tf_op jit(solution)/shard_map/ppermute | solution.py:58
  103.0 32.1 %collective-permute-start.27 = (bf16[2,4,64,512]{3,2,1,0:T(8,128)(2,1)S(1)}, bf16[2,4,64,512]{3,2,1,0:T(8,128)(2,1)S(1)}, u32[]{:S(2)}, u32[]{:S(2)}) collective-permute-start(bf16[2,4,64,512]{3,2,1,0:T(8,128)(2,1)S(1)} %pad_maximum_fusion.8), channel_id=1, source_target_pairs={{0,2},{1,3},{2,0},{3,1},{4,6},{5,7},{6,4},{7,5},{8,10},{9,11},{10,... | collective-permute-start | bytes 1572872 | tf_op jit(solution)/shard_map/ppermute | solution.py:58
  104.6 18.8 %collective-permute-start.18 = (bf16[2,128,512]{2,1,0:T(8,128)(2,1)}, bf16[2,128,512]{2,1,0:T(8,128)(2,1)S(1)}, u32[]{:S(2)}, u32[]{:S(2)}) collective-permute-start(bf16[2,128,512]{2,1,0:T(8,128)(2,1)} %get-tuple-element.299), channel_id=1, source_target_pairs={{0,1},{1,0},{2,3},{3,2},{4,5},{5,4},{6,7},{7,6},{8,9},{9,8},{10,11... | collective-permute-start | bytes 786440 | tf_op jit(solution)/shard_map/ppermute | solution.py:58
  104.6 18.9 %collective-permute-start.19 = (bf16[2,128,512]{2,1,0:T(8,128)(2,1)}, bf16[2,128,512]{2,1,0:T(8,128)(2,1)S(1)}, u32[]{:S(2)}, u32[]{:S(2)}) collective-permute-start(bf16[2,128,512]{2,1,0:T(8,128)(2,1)} %get-tuple-element.300), channel_id=1, source_target_pairs={{0,2},{1,3},{2,0},{3,1},{4,6},{5,7},{6,4},{7,5},{8,10},{9,11},{10,... | collective-permute-start | bytes 786440 | tf_op jit(solution)/shard_map/ppermute | solution.py:58
  105.1 22.2 %collective-permute-start.20 = (bf16[2,128,512]{2,1,0:T(8,128)(2,1)}, bf16[2,128,512]{2,1,0:T(8,128)(2,1)S(1)}, u32[]{:S(2)}, u32[]{:S(2)}) collective-permute-start(bf16[2,128,512]{2,1,0:T(8,128)(2,1)} %get-tuple-element.301), channel_id=1, source_target_pairs={{0,3},{1,2},{2,1},{3,0},{4,7},{5,6},{6,5},{7,4},{8,11},{9,10},{10,... | collective-permute-start | bytes 786440 | tf_op jit(solution)/shard_map/ppermute | solution.py:58
  106.5 56.4 %collective-permute-start.31 = (bf16[16,64,512]{2,1,0:T(8,128)(2,1)S(1)}, bf16[16,64,512]{2,1,0:T(8,128)(2,1)S(1)}, u32[]{:S(2)}, u32[]{:S(2)}) collective-permute-start(bf16[16,64,512]{2,1,0:T(8,128)(2,1)S(1)} %bitcast.159), channel_id=1, source_target_pairs={{0,1},{1,0},{2,3},{3,2},{4,5},{5,4},{6,7},{7,6},{8,9},{9,8},{10,11... | collective-permute-start | bytes 3145736 | tf_op jit(solution)/shard_map/ppermute | solution.py:58
  135.4 22.3 %copy-start.6 = (bf16[2,4,2,64,512]{4,3,2,1,0:T(8,128)(2,1)}, bf16[2,4,2,64,512]{4,3,2,1,0:T(8,128)(2,1)S(1)}, u32[]{:S(2)}) copy-start(bf16[2,4,2,64,512]{4,3,2,1,0:T(8,128)(2,1)S(1)} %copy.121) | copy-start | bytes 3145732
  135.5 27.4 %collective-permute-start.32 = (bf16[16,64,512]{2,1,0:T(8,128)(2,1)S(1)}, bf16[16,64,512]{2,1,0:T(8,128)(2,1)}, u32[]{:S(2)}, u32[]{:S(2)}) collective-permute-start(bf16[16,64,512]{2,1,0:T(8,128)(2,1)S(1)} %bitcast.162), channel_id=1, source_target_pairs={{0,1},{1,0},{2,3},{3,2},{4,5},{5,4},{6,7},{7,6},{8,9},{9,8},{10,11... | collective-permute-start | bytes 3145736 | tf_op jit(solution)/shard_map/ppermute | solution.py:58
  136.2 2.7 collective-permute-start.21
  136.8 9.2 %collective-permute-start.22 = (bf16[2,128,512]{2,1,0:T(8,128)(2,1)S(1)}, bf16[2,128,512]{2,1,0:T(8,128)(2,1)S(1)}, u32[]{:S(2)}, u32[]{:S(2)}) collective-permute-start(bf16[2,128,512]{2,1,0:T(8,128)(2,1)S(1)} %copy-done.47), channel_id=1, source_target_pairs={{0,2},{1,3},{2,0},{3,1},{4,6},{5,7},{6,4},{7,5},{8,10},{9,11},{10,... | collective-permute-start | bytes 786440 | tf_op jit(solution)/shard_map/ppermute | solution.py:58
  138.3 11.5 %collective-permute-start.23 = (bf16[2,128,512]{2,1,0:T(8,128)(2,1)S(1)}, bf16[2,128,512]{2,1,0:T(8,128)(2,1)S(1)}, u32[]{:S(2)}, u32[]{:S(2)}) collective-permute-start(bf16[2,128,512]{2,1,0:T(8,128)(2,1)S(1)} %copy-done.46), channel_id=1, source_target_pairs={{0,3},{1,2},{2,1},{3,0},{4,7},{5,6},{6,5},{7,4},{8,11},{9,10},{10,... | collective-permute-start | bytes 786440 | tf_op jit(solution)/shard_map/ppermute | solution.py:58
  138.9 18.9 %collective-permute-start.28 = (bf16[128,1152]{1,0:T(8,128)(2,1)S(1)}, bf16[128,1152]{1,0:T(8,128)(2,1)}, u32[]{:S(2)}, u32[]{:S(2)}) collective-permute-start(bf16[128,1152]{1,0:T(8,128)(2,1)S(1)} %copy-done.25), channel_id=1, source_target_pairs={{0,4},{4,0},{8,12},{12,8},{1,5},{5,1},{9,13},{13,9},{2,6},{6,2},{1... | collective-permute-start | bytes 884744 | tf_op jit(solution)/shard_map/ppermute | solution.py:58
  146.0 13.9 %collective-permute-start.29 = (bf16[128,1152]{1,0:T(8,128)(2,1)S(1)}, bf16[128,1152]{1,0:T(8,128)(2,1)}, u32[]{:S(2)}, u32[]{:S(2)}) collective-permute-start(bf16[128,1152]{1,0:T(8,128)(2,1)S(1)} %copy-done.22), channel_id=1, source_target_pairs={{0,8},{4,12},{8,0},{12,4},{1,9},{5,13},{9,1},{13,5},{2,10},{6,14},... | collective-permute-start | bytes 884744 | tf_op jit(solution)/shard_map/ppermute | solution.py:58
  150.6 10.9 %collective-permute-start.30 = (bf16[128,1152]{1,0:T(8,128)(2,1)S(1)}, bf16[128,1152]{1,0:T(8,128)(2,1)}, u32[]{:S(2)}, u32[]{:S(2)}) collective-permute-start(bf16[128,1152]{1,0:T(8,128)(2,1)S(1)} %copy-done.19), channel_id=1, source_target_pairs={{0,12},{4,8},{8,4},{12,0},{1,13},{5,9},{9,5},{13,1},{2,14},{6,10},... | collective-permute-start | bytes 884744 | tf_op jit(solution)/shard_map/ppermute | solution.py:58
  157.8 13.4 %collective-permute-start.24 = (bf16[128,1152]{1,0:T(8,128)(2,1)}, bf16[128,1152]{1,0:T(8,128)(2,1)S(1)}, u32[]{:S(2)}, u32[]{:S(2)}) collective-permute-start(bf16[128,1152]{1,0:T(8,128)(2,1)} %get-tuple-element.307), channel_id=1, source_target_pairs={{0,4},{4,0},{8,12},{12,8},{1,5},{5,1},{9,13},{13,9},{2,6},{6,2},{1... | collective-permute-start | bytes 884744 | tf_op jit(solution)/shard_map/ppermute | solution.py:58
  159.9 11.3 %collective-permute-start.25 = (bf16[128,1152]{1,0:T(8,128)(2,1)}, bf16[128,1152]{1,0:T(8,128)(2,1)S(1)}, u32[]{:S(2)}, u32[]{:S(2)}) collective-permute-start(bf16[128,1152]{1,0:T(8,128)(2,1)} %get-tuple-element.308), channel_id=1, source_target_pairs={{0,8},{4,12},{8,0},{12,4},{1,9},{5,13},{9,1},{13,5},{2,10},{6,14},... | collective-permute-start | bytes 884744 | tf_op jit(solution)/shard_map/ppermute | solution.py:58
  161.4 15.6 %collective-permute-start.26 = (bf16[128,1152]{1,0:T(8,128)(2,1)}, bf16[128,1152]{1,0:T(8,128)(2,1)S(1)}, u32[]{:S(2)}, u32[]{:S(2)}) collective-permute-start(bf16[128,1152]{1,0:T(8,128)(2,1)} %get-tuple-element.309), channel_id=1, source_target_pairs={{0,12},{4,8},{8,4},{12,0},{1,13},{5,9},{9,5},{13,1},{2,14},{6,10},... | collective-permute-start | bytes 884744 | tf_op jit(solution)/shard_map/ppermute | solution.py:58
  177.8 12.7 %collective-permute-start.33 = (bf16[128,1152]{1,0:T(8,128)(2,1)}, bf16[128,1152]{1,0:T(8,128)(2,1)S(1)}, u32[]{:S(2)}, u32[]{:S(2)}) collective-permute-start(bf16[128,1152]{1,0:T(8,128)(2,1)} %get-tuple-element.343.refs_1_), channel_id=1, source_target_pairs={{0,4},{4,0},{8,12},{12,8},{1,5},{5,1},{9,13},{13,9},{2,6},{6,2},{1... | collective-permute-start | bytes 884744 | tf_op jit(solution)/shard_map/ppermute | solution.py:58
  178.4 12.2 %collective-permute-start.34 = (bf16[128,1152]{1,0:T(8,128)(2,1)}, bf16[128,1152]{1,0:T(8,128)(2,1)S(1)}, u32[]{:S(2)}, u32[]{:S(2)}) collective-permute-start(bf16[128,1152]{1,0:T(8,128)(2,1)} %get-tuple-element.343.refs_1_), channel_id=1, source_target_pairs={{0,8},{4,12},{8,0},{12,4},{1,9},{5,13},{9,1},{13,5},{2,10},{6,14},... | collective-permute-start | bytes 884744 | tf_op jit(solution)/shard_map/ppermute | solution.py:58
  179.9 14.5 %collective-permute-start.35 = (bf16[128,1152]{1,0:T(8,128)(2,1)}, bf16[128,1152]{1,0:T(8,128)(2,1)S(1)}, u32[]{:S(2)}, u32[]{:S(2)}) collective-permute-start(bf16[128,1152]{1,0:T(8,128)(2,1)} %get-tuple-element.343.refs_1_), channel_id=1, source_target_pairs={{0,12},{4,8},{8,4},{12,0},{1,13},{5,9},{9,5},{13,1},{2,14},{6,10},... | collective-permute-start | bytes 884744 | tf_op jit(solution)/shard_map/ppermute | solution.py:58
  194.4 13.5 %collective-permute-start.39 = (bf16[16,128,512]{2,1,0:T(8,128)(2,1)}, bf16[16,128,512]{2,1,0:T(8,128)(2,1)}, u32[]{:S(2)}, u32[]{:S(2)}) collective-permute-start(bf16[16,128,512]{2,1,0:T(8,128)(2,1)} %get-tuple-element.359), channel_id=1, source_target_pairs={{0,1},{1,0},{2,3},{3,2},{4,5},{5,4},{6,7},{7,6},{8,9},{9,8},{10,11... | collective-permute-start | bytes 6291464 | tf_op jit(solution)/shard_map/ppermute | solution.py:58
  194.4 19.5 %collective-permute-start.36 = (bf16[128,1152]{1,0:T(8,128)(2,1)}, bf16[128,1152]{1,0:T(8,128)(2,1)S(1)}, u32[]{:S(2)}, u32[]{:S(2)}) collective-permute-start(bf16[128,1152]{1,0:T(8,128)(2,1)} %get-tuple-element.340.refs_1_), channel_id=1, source_target_pairs={{0,4},{4,0},{8,12},{12,8},{1,5},{5,1},{9,13},{13,9},{2,6},{6,2},{1... | collective-permute-start | bytes 884744 | tf_op jit(solution)/shard_map/ppermute | solution.py:58
  195.0 18.9 %collective-permute-start.37 = (bf16[128,1152]{1,0:T(8,128)(2,1)}, bf16[128,1152]{1,0:T(8,128)(2,1)S(1)}, u32[]{:S(2)}, u32[]{:S(2)}) collective-permute-start(bf16[128,1152]{1,0:T(8,128)(2,1)} %get-tuple-element.340.refs_1_), channel_id=1, source_target_pairs={{0,8},{4,12},{8,0},{12,4},{1,9},{5,13},{9,1},{13,5},{2,10},{6,14},... | collective-permute-start | bytes 884744 | tf_op jit(solution)/shard_map/ppermute | solution.py:58
  196.6 17.3 %collective-permute-start.38 = (bf16[128,1152]{1,0:T(8,128)(2,1)}, bf16[128,1152]{1,0:T(8,128)(2,1)S(1)}, u32[]{:S(2)}, u32[]{:S(2)}) collective-permute-start(bf16[128,1152]{1,0:T(8,128)(2,1)} %get-tuple-element.340.refs_1_), channel_id=1, source_target_pairs={{0,12},{4,8},{8,4},{12,0},{1,13},{5,9},{9,5},{13,1},{2,14},{6,10},... | collective-permute-start | bytes 884744 | tf_op jit(solution)/shard_map/ppermute | solution.py:58
  212.3 24.9 %collective-permute-start.40 = (bf16[2,4,128,512]{3,2,1,0:T(8,128)(2,1)S(1)}, bf16[2,4,128,512]{3,2,1,0:T(8,128)(2,1)}, u32[]{:S(2)}, u32[]{:S(2)}) collective-permute-start(bf16[2,4,128,512]{3,2,1,0:T(8,128)(2,1)S(1)} %fusion.8), channel_id=1, source_target_pairs={{0,2},{1,3},{2,0},{3,1},{4,6},{5,7},{6,4},{7,5},{8,10},{9,11},{10,... | collective-permute-start | bytes 3145736 | tf_op jit(solution)/shard_map/ppermute | solution.py:58
  242.2 4.2 %collective-permute-start.47 = (bf16[2,2,2,2,16,640]{5,4,3,2,1,0:T(8,128)(2,1)S(1)}, bf16[2,2,2,2,16,640]{5,4,3,2,1,0:T(8,128)(2,1)S(1)}, u32[]{:S(2)}, u32[]{:S(2)}) collective-permute-start(bf16[2,2,2,2,16,640]{5,4,3,2,1,0:T(8,128)(2,1)S(1)} %fusion.11), channel_id=1, source_target_pairs={{0,1},{1,0},{2,3},{3,2},{4,5},{5,4},{6,7},{7,6},{8,9},{9,8},{10,11... | collective-permute-start | bytes 983048 | tf_op jit(solution)/shard_map/ppermute | solution.py:58
  242.3 2.6 collective-permute-start.41
  242.8 9.5 %collective-permute-start.42 = (bf16[2,128,512]{2,1,0:T(8,128)(2,1)}, bf16[2,128,512]{2,1,0:T(8,128)(2,1)}, u32[]{:S(2)}, u32[]{:S(2)}) collective-permute-start(bf16[2,128,512]{2,1,0:T(8,128)(2,1)} %get-tuple-element.378), channel_id=1, source_target_pairs={{0,2},{1,3},{2,0},{3,1},{4,6},{5,7},{6,4},{7,5},{8,10},{9,11},{10,... | collective-permute-start | bytes 786440 | tf_op jit(solution)/shard_map/ppermute | solution.py:58
  244.3 12.5 %collective-permute-start.43 = (bf16[2,128,512]{2,1,0:T(8,128)(2,1)S(1)}, bf16[2,128,512]{2,1,0:T(8,128)(2,1)}, u32[]{:S(2)}, u32[]{:S(2)}) collective-permute-start(bf16[2,128,512]{2,1,0:T(8,128)(2,1)S(1)} %copy-done.40), channel_id=1, source_target_pairs={{0,3},{1,2},{2,1},{3,0},{4,7},{5,6},{6,5},{7,4},{8,11},{9,10},{10,... | collective-permute-start | bytes 786440 | tf_op jit(solution)/shard_map/ppermute | solution.py:58
  244.3 12.5 %collective-permute-start.44 = (bf16[2,128,512]{2,1,0:T(8,128)(2,1)}, bf16[2,128,512]{2,1,0:T(8,128)(2,1)}, u32[]{:S(2)}, u32[]{:S(2)}) collective-permute-start(bf16[2,128,512]{2,1,0:T(8,128)(2,1)} %get-tuple-element.381), channel_id=1, source_target_pairs={{0,1},{1,0},{2,3},{3,2},{4,5},{5,4},{6,7},{7,6},{8,9},{9,8},{10,11... | collective-permute-start | bytes 786440 | tf_op jit(solution)/shard_map/ppermute | solution.py:58
  245.0 18.6 %collective-permute-start.45 = (bf16[2,128,512]{2,1,0:T(8,128)(2,1)}, bf16[2,128,512]{2,1,0:T(8,128)(2,1)}, u32[]{:S(2)}, u32[]{:S(2)}) collective-permute-start(bf16[2,128,512]{2,1,0:T(8,128)(2,1)} %get-tuple-element.382), channel_id=1, source_target_pairs={{0,2},{1,3},{2,0},{3,1},{4,6},{5,7},{6,4},{7,5},{8,10},{9,11},{10,... | collective-permute-start | bytes 786440 | tf_op jit(solution)/shard_map/ppermute | solution.py:58
  246.4 21.0 %collective-permute-start.46 = (bf16[2,128,512]{2,1,0:T(8,128)(2,1)}, bf16[2,128,512]{2,1,0:T(8,128)(2,1)}, u32[]{:S(2)}, u32[]{:S(2)}) collective-permute-start(bf16[2,128,512]{2,1,0:T(8,128)(2,1)} %get-tuple-element.383), channel_id=1, source_target_pairs={{0,3},{1,2},{2,1},{3,0},{4,7},{5,6},{6,5},{7,4},{8,11},{9,10},{10,... | collective-permute-start | bytes 786440 | tf_op jit(solution)/shard_map/ppermute | solution.py:58
  267.5 30.0 %collective-permute-start.48 = (bf16[4,128,512]{2,1,0:T(8,128)(2,1)S(1)}, bf16[4,128,512]{2,1,0:T(8,128)(2,1)S(1)}, u32[]{:S(2)}, u32[]{:S(2)}) collective-permute-start(bf16[4,128,512]{2,1,0:T(8,128)(2,1)S(1)} %fusion.10), channel_id=1, source_target_pairs={{0,16},{16,0},{1,17},{17,1},{2,18},{18,2},{3,19},{19,3},{4,20},{20... | collective-permute-start | bytes 1572872 | tf_op jit(solution)/shard_map/ppermute | solution.py:58
  298.7 5.9 %collective-permute-start.49 = (bf16[128,512]{1,0:T(8,128)(2,1)S(1)}, bf16[128,512]{1,0:T(8,128)(2,1)S(1)}, u32[]{:S(2)}, u32[]{:S(2)}) collective-permute-start(bf16[128,512]{1,0:T(8,128)(2,1)S(1)} %get-tuple-element.512), channel_id=1, source_target_pairs={{0,4},{4,0},{8,12},{12,8},{1,5},{5,1},{9,13},{13,9},{2,6},{6,2},{1... | collective-permute-start | bytes 393224 | tf_op jit(solution)/shard_map/ppermute | solution.py:58
  299.3 36.9 %collective-permute-start.50 = (bf16[128,512]{1,0:T(8,128)(2,1)S(1)}, bf16[128,512]{1,0:T(8,128)(2,1)S(1)}, u32[]{:S(2)}, u32[]{:S(2)}) collective-permute-start(bf16[128,512]{1,0:T(8,128)(2,1)S(1)} %get-tuple-element.511), channel_id=1, source_target_pairs={{0,8},{4,12},{8,0},{12,4},{1,9},{5,13},{9,1},{13,5},{2,10},{6,14},... | collective-permute-start | bytes 393224 | tf_op jit(solution)/shard_map/ppermute | solution.py:58
  299.8 36.4 %collective-permute-start.51 = (bf16[128,512]{1,0:T(8,128)(2,1)S(1)}, bf16[128,512]{1,0:T(8,128)(2,1)S(1)}, u32[]{:S(2)}, u32[]{:S(2)}) collective-permute-start(bf16[128,512]{1,0:T(8,128)(2,1)S(1)} %get-tuple-element.510), channel_id=1, source_target_pairs={{0,12},{4,8},{8,4},{12,0},{1,13},{5,9},{9,5},{13,1},{2,14},{6,10},... | collective-permute-start | bytes 393224 | tf_op jit(solution)/shard_map/ppermute | solution.py:58
  302.2 34.0 %collective-permute-start.52 = (bf16[1,256,512]{2,1,0:T(8,128)(2,1)}, bf16[1,256,512]{2,1,0:T(8,128)(2,1)S(1)}, u32[]{:S(2)}, u32[]{:S(2)}) collective-permute-start(bf16[1,256,512]{2,1,0:T(8,128)(2,1)} %get-tuple-element.417), channel_id=1, source_target_pairs={{0,1},{1,0},{2,3},{3,2},{4,5},{5,4},{6,7},{7,6},{8,9},{9,8},{10,11... | collective-permute-start | bytes 786440 | tf_op jit(solution)/shard_map/ppermute | solution.py:58
  302.2 34.0 %collective-permute-start.53 = (bf16[1,256,512]{2,1,0:T(8,128)(2,1)}, bf16[1,256,512]{2,1,0:T(8,128)(2,1)S(1)}, u32[]{:S(2)}, u32[]{:S(2)}) collective-permute-start(bf16[1,256,512]{2,1,0:T(8,128)(2,1)} %get-tuple-element.418), channel_id=1, source_target_pairs={{0,2},{1,3},{2,0},{3,1},{4,6},{5,7},{6,4},{7,5},{8,10},{9,11},{10,... | collective-permute-start | bytes 786440 | tf_op jit(solution)/shard_map/ppermute | solution.py:58
  304.6 31.7 %collective-permute-start.54 = (bf16[1,256,512]{2,1,0:T(8,128)(2,1)}, bf16[1,256,512]{2,1,0:T(8,128)(2,1)S(1)}, u32[]{:S(2)}, u32[]{:S(2)}) collective-permute-start(bf16[1,256,512]{2,1,0:T(8,128)(2,1)} %get-tuple-element.419), channel_id=1, source_target_pairs={{0,3},{1,2},{2,1},{3,0},{4,7},{5,6},{6,5},{7,4},{8,11},{9,10},{10,... | collective-permute-start | bytes 786440 | tf_op jit(solution)/shard_map/ppermute | solution.py:58
  336.9 3.0 collective-permute-start.58
  341.6 15.1 %collective-permute-start.59 = (bf16[2,2,2,16,2176]{4,3,2,1,0:T(8,128)(2,1)S(1)}, bf16[2,2,2,16,2176]{4,3,2,1,0:T(8,128)(2,1)}, u32[]{:S(2)}, u32[]{:S(2)}) collective-permute-start(bf16[2,2,2,16,2176]{4,3,2,1,0:T(8,128)(2,1)S(1)} %fusion.9), channel_id=1, source_target_pairs={{0,4},{4,0},{8,12},{12,8},{1,5},{5,1},{9,13},{13,9},{2,6},{6,2},{1... | collective-permute-start | bytes 1671176 | tf_op jit(solution)/shard_map/ppermute | solution.py:58
  342.3 15.6 %collective-permute-start.55 = (bf16[1,256,512]{2,1,0:T(8,128)(2,1)}, bf16[1,256,512]{2,1,0:T(8,128)(2,1)S(1)}, u32[]{:S(2)}, u32[]{:S(2)}) collective-permute-start(bf16[1,256,512]{2,1,0:T(8,128)(2,1)} %get-tuple-element.425), channel_id=1, source_target_pairs={{0,1},{1,0},{2,3},{3,2},{4,5},{5,4},{6,7},{7,6},{8,9},{9,8},{10,11... | collective-permute-start | bytes 786440 | tf_op jit(solution)/shard_map/ppermute | solution.py:58
  342.4 15.5 %collective-permute-start.56 = (bf16[1,256,512]{2,1,0:T(8,128)(2,1)}, bf16[1,256,512]{2,1,0:T(8,128)(2,1)S(1)}, u32[]{:S(2)}, u32[]{:S(2)}) collective-permute-start(bf16[1,256,512]{2,1,0:T(8,128)(2,1)} %get-tuple-element.426), channel_id=1, source_target_pairs={{0,2},{1,3},{2,0},{3,1},{4,6},{5,7},{6,4},{7,5},{8,10},{9,11},{10,... | collective-permute-start | bytes 786440 | tf_op jit(solution)/shard_map/ppermute | solution.py:58
  342.9 15.0 %collective-permute-start.57 = (bf16[1,256,512]{2,1,0:T(8,128)(2,1)}, bf16[1,256,512]{2,1,0:T(8,128)(2,1)S(1)}, u32[]{:S(2)}, u32[]{:S(2)}) collective-permute-start(bf16[1,256,512]{2,1,0:T(8,128)(2,1)} %get-tuple-element.427), channel_id=1, source_target_pairs={{0,3},{1,2},{2,1},{3,0},{4,7},{5,6},{6,5},{7,4},{8,11},{9,10},{10,... | collective-permute-start | bytes 786440 | tf_op jit(solution)/shard_map/ppermute | solution.py:58
  359.3 8.1 %collective-permute-start.60 = (bf16[2,2,16,2176]{3,2,1,0:T(8,128)(2,1)S(1)}, bf16[2,2,16,2176]{3,2,1,0:T(8,128)(2,1)S(1)}, u32[]{:S(2)}, u32[]{:S(2)}) collective-permute-start(bf16[2,2,16,2176]{3,2,1,0:T(8,128)(2,1)S(1)} %fusion.12), channel_id=1, source_target_pairs={{0,8},{4,12},{8,0},{12,4},{1,9},{5,13},{9,1},{13,5},{2,10},{6,14},... | collective-permute-start | bytes 835592 | tf_op jit(solution)/shard_map/ppermute | solution.py:58
  367.5 8.2 %collective-permute-start.61 = (bf16[2,16,2176]{2,1,0:T(8,128)(2,1)S(1)}, bf16[2,16,2176]{2,1,0:T(8,128)(2,1)S(1)}, u32[]{:S(2)}, u32[]{:S(2)}) collective-permute-start(bf16[2,16,2176]{2,1,0:T(8,128)(2,1)S(1)} %fusion.17), channel_id=1, source_target_pairs={{0,16},{16,0},{1,17},{17,1},{2,18},{18,2},{3,19},{19,3},{4,20},{20... | collective-permute-start | bytes 417800 | tf_op jit(solution)/shard_map/ppermute | solution.py:58
  375.8 4.4 %collective-permute-start.62 = (bf16[16,2176]{1,0:T(8,128)(2,1)S(1)}, bf16[16,2176]{1,0:T(8,128)(2,1)S(1)}, u32[]{:S(2)}, u32[]{:S(2)}) collective-permute-start(bf16[16,2176]{1,0:T(8,128)(2,1)S(1)} %fusion.31), channel_id=1, source_target_pairs={{0,2},{1,3},{2,0},{3,1},{4,6},{5,7},{6,4},{7,5},{8,10},{9,11},{10,... | collective-permute-start | bytes 208904 | tf_op jit(solution)/shard_map/ppermute | solution.py:58
  (51 other events, 238.2 us)

commit v3 on v2

--- a/solution.py
+++ b/solution.py
@@ -137,10 +137,12 @@
 class Halving(Steps):
     def __init__(self, value, sizes, order, inner=0):
         super().__init__(value, sizes, order)
+        self.sizes = sizes
         self.left = [bit for bit in bits_of(sizes) if bit in self.order]
         self.inner = inner
 
-    def step(self, bit):
+    def prepare(self):
+        bit = self.order.pop(0)
         depth = self.left.index(bit)
         self.left.pop(depth)
         axis, size, mask = bit
@@ -148,8 +150,54 @@
         high = ((lax.axis_index(axis) & mask) != 0).astype(jnp.int32)
         keep = lax.dynamic_index_in_dim(self.value, high, depth, keepdims=False)
         send = lax.dynamic_index_in_dim(self.value, 1 - high, depth, keepdims=False)
-        other = partner(send.astype(bf16), axis, size, mask)
-        self.value = keep.astype(f32) + other.astype(f32)
+        self.value = (keep, send.astype(bf16))
+        self.link = bit
+
+    def exchange(self):
+        axis, size, mask = self.link
+        keep, send = self.value
+        self.value = (keep, partner(send, axis, size, mask))
+
+    def combine(self):
+        self.value = functools.reduce(jnp.add, [part.astype(f32) for part in self.value])
+
+    def step(self, bit):
+        self.order.insert(0, bit)
+        self.prepare()
+        self.exchange()
+        self.combine()
+
+    def at_once(self, axes):
+        bits = [bit for bit in self.left if bit[0] in axes]
+        self.order = [bit for bit in self.order if bit not in bits]
+        depth = self.left.index(bits[0])
+        if self.inner or bits != self.left[depth : depth + len(bits)]:
+            raise NotImplementedError
+        self.left = [bit for bit in self.left if bit not in bits]
+        shape = self.value.shape
+        value = self.value.reshape(shape[:depth] + (2 ** len(bits),) + shape[depth + len(bits) :])
+        place, names = 0, []
+        for axis, size, mask in bits:
+            place = 2 * place + ((lax.axis_index(axis) & mask) != 0).astype(jnp.int32)
+            if axis not in names:
+                names.append(axis)
+        total = [lax.dynamic_index_in_dim(value, place, depth, keepdims=False)]
+        sizes = [size for axis, size in self.sizes if axis in names]
+        for j in range(1, 2 ** len(bits)):
+            piece = lax.dynamic_index_in_dim(value, place ^ j, depth, keepdims=False)
+            masks = {axis: 0 for axis in names}
+            for i, (axis, _, mask) in enumerate(bits):
+                if j >> (len(bits) - 1 - i) & 1:
+                    masks[axis] |= mask
+            pairs = []
+            for source in range(math.prod(sizes)):
+                target, rest, unit = 0, source, 1
+                for axis, size in reversed(list(zip(names, sizes))):
+                    target += ((rest % size) ^ masks[axis]) * unit
+                    rest, unit = rest // size, unit * size
+                pairs.append((source, target))
+            total.append(lax.ppermute(piece.astype(bf16), tuple(names), pairs))
+        self.value = total
 
 
 hold = lax.optimization_barrier
@@ -188,6 +236,10 @@
 
 def whole(*shape):
     return pl.BlockSpec(shape, lambda r, me: (0,) * len(shape))
+
+
+def fourth(width):
+    return pl.BlockSpec((width, width), lambda b, me: (0, 3))
 
 
 def by_core(me, pairs):
@@ -279,7 +331,7 @@
 def attend_first_kernel(parts, slots, old, *refs):
     me_ref = refs[0]
     x_refs = refs[1 : 1 + slots]
-    gain_ref, w_ref = refs[1 + slots : 3 + slots]
+    vector_ref, w_ref = refs[1 + slots : 3 + slots]
     rest = refs[3 + slots + old :]
     att_refs = rest[:slots]
     seg_ref, qt_ref, k_ref, v_ref, q_ref, vt_ref, ot_ref, lse_ref = rest[slots : slots + 8]
@@ -292,7 +344,7 @@
     w_t[:width] = w_ref[:, :width].T
     w_t[width:] = w_ref[:, 2 * width :].T
     aux[2][...] = causal_bias(piece if parts > 1 else LANES)
-    gain = gain_ref[...]
+    gain = vector_ref[...].astype(f32).T[0:1]
     for j in range(slots):
         place = pl.ds(pl.multiple_of((me ^ j) * piece, piece), piece)
         marks = x_refs[j][0, piece:].astype(f32)
@@ -337,7 +389,7 @@
     return [((length, LANES), bf16), ((16, length), f32), ((span, BLOCK), f32)]
 
 
-def attend_first(me, row, rows, x_slots, gain, w_qkv, parts, old):
+def attend_first(me, row, rows, x_slots, weights, parts, old):
     slots = len(x_slots)
     _, packed, width = x_slots[0].shape
     piece = packed - MARKS
@@ -363,11 +415,14 @@
         "attend_first",
         (1,),
         [per_row(packed, width)] * slots
-        + [whole(1, width), whole(width, 3 * width)]
+        + [
+            pl.BlockSpec((width, LANES), lambda r, me: (0, 4 * width // LANES)),
+            whole(width, 3 * width),
+        ]
         + [pl.BlockSpec(memory_space=pl.ANY)] * len(old),
         outs,
         [((2 * width, width), bf16)] + attend_scratch(length, piece, parts),
-        (me, *x_slots, gain, w_qkv, *old),
+        (me, *x_slots, weights, weights, *old),
         12,
         {3 + slots + i: i for i in range(len(old))},
     )
@@ -656,7 +711,7 @@
         "mix",
         (steps,),
         [pl.BlockSpec((rows, piece, width), lambda b, me: (0, b, 0))] * slot_count
-        + [shifted, shifted, whole(width, width), whole(1, width), whole(LANES, width)],
+        + [shifted, shifted, fourth(width), whole(1, width), whole(LANES, width)],
         [pay] * experts
         + [
             (span, (tokens, positions, width), bf16),
@@ -856,7 +911,7 @@
     return result[0], more
 
 
-def unmix_kernel(slot_count, experts, part, *refs):
+def unmix_kernel(slot_count, experts, part, last, *refs):
     me_ref = refs[0]
     ret_refs = refs[1 : 1 + experts]
     att_refs = refs[1 + experts : 1 + experts + slot_count]
@@ -868,7 +923,11 @@
         rest = rest[5:]
     out_ref, grad_middle_ref = rest[:2]
     back_refs = rest[2 : 2 + slot_count]
-    grad_out_ref, grad_control_ref, grad_gain_ref = rest[2 + slot_count :]
+    rest = rest[2 + slot_count :]
+    if last:
+        keep_ref, send_ref, grad_out_ref, grad_control_ref, grad_gain_ref, small = rest
+    else:
+        grad_out_ref, grad_control_ref, grad_gain_ref = rest
     rows, piece, width = att_refs[0].shape
     tokens = rows * slot_count
     me = me_ref[0]
@@ -925,8 +984,29 @@
     attended = jnp.concatenate([ref[...] for ref in att_refs], axis=0).reshape(-1, width)
     grad_out_ref[...] += dot(attended, grad_middle, TN)
 
-
-def unmix(me, part, ret_slots, att_slots, second, middle, cotangent, w_out, gain, control, before):
+    if last:
+
+        @pl.when(pl.program_id(0) == pl.num_programs(0) - 1)
+        def _():
+            small[...] = jnp.zeros_like(small)
+            small[0:1] = jnp.sum(grad_gain_ref[...], axis=0, keepdims=True)
+            for e in range(experts):
+                total = grad_control_ref[e * piece : (e + 1) * piece]
+                place = pl.ds(1 + (me_ref[1] ^ e), 1)
+                small[place] = jnp.sum(total, axis=0, keepdims=True)
+            blocks, lines = keep_ref.shape[:2]
+            for columns, value in (
+                (slice(0, width), grad_out_ref[...]),
+                (slice(width, width + LANES), small[...].T),
+            ):
+                keep, send = by_core(me, value.reshape(blocks, 2, lines, -1))
+                keep_ref[:, :, columns] = keep
+                send_ref[:, :, columns] = send.astype(bf16)
+
+
+def unmix(
+    me, part, last, shards, ret_slots, att_slots, second, middle, cotangent, w_out, gain, control, before
+):
     slot_count, experts = len(att_slots), len(ret_slots)
     rows, positions, width = att_slots[0].shape
     tokens = rows * slot_count
@@ -942,16 +1022,22 @@
         (whole(8, width), (8, width), f32),
     ]
     count = 1 + experts + slot_count + 6
+    scratch = []
+    made = sums
+    if last:
+        half = (shards // 2, width // shards, width + LANES)
+        made = [(whole(*half), half, f32), (whole(*half), half, bf16)]
+        scratch = [(shape, dtype) for _, shape, dtype in sums] + [((LANES, width), f32)]
     result = call(
-        functools.partial(unmix_kernel, slot_count, experts, part),
+        functools.partial(unmix_kernel, slot_count, experts, part, last),
         "unmix",
         (steps,),
         [pl.BlockSpec((piece, 2 * width + LANES), lambda b, me: (b, 0))] * experts
         + [slot] * slot_count
-        + [span, span, shifted, whole(width, width), whole(1, width), whole(LANES, width)]
+        + [span, span, shifted, fourth(width), whole(1, width), whole(LANES, width)]
         + ([pl.BlockSpec(memory_space=pl.ANY)] * 2 + [spec for spec, _, _ in sums] if part else []),
-        [full, full] + [(slot, (rows, positions, width), bf16)] * slot_count + sums,
-        [],
+        [full, full] + [(slot, (rows, positions, width), bf16)] * slot_count + made,
+        scratch,
         (me, *ret_slots, *att_slots, second, middle, cotangent, w_out, gain, control, *before),
         positions * 17 / 256,
         {count: 0, count + 1: 1} if part else None,
@@ -1014,7 +1100,7 @@
     owners = (("gq", groups), ("seq", slots))
     seq_me = lax.axis_index("seq")
     member = lax.axis_index("gi")
-    me = seq_me.astype(jnp.int32).reshape(1)
+    me = jnp.stack([seq_me, member]).astype(jnp.int32)
 
     parts = 2 if positions % BLOCK == 0 else 1
 
@@ -1027,36 +1113,53 @@
     marks = jnp.pad(marks, ((0, 0), (0, MARKS - 1), (0, width - positions)))
     x_parts = row_parts(jnp.concatenate([inputs, marks], axis=1))
     x_parts = [[x[row : row + 1] for x in x_parts] for row in range(rows)]
-    x_rows = [swap_slots(x_parts[0], "seq")]
+    x_rows = [[x_parts[0][0]]]
+
+    def send_some(slots_of, done, first, last):
+        for j in range(first, last):
+            done.append(partner(slots_of[j], "seq", slots, j))
 
     small = jnp.concatenate([gain_attn[None], gain_mix[None], w_control], axis=0)
     small = jnp.pad(jnp.transpose(small), ((0, 0), (0, LANES - 2 - experts)))
     packed = jnp.concatenate([w_qkv, w_out, small], axis=1).astype(bf16)
-    packed = Doubling(packed, place, ("gq", "seq", "core"))
-    packed.at_once("gi")
-    packed.steps("gq")
+    packed = Doubling(packed, place, ("seq", "gq", "core"))
+    send_some(x_parts[0], x_rows[0], 1, slots // 2 + 1)
+    packed.steps("seq")
+    x_rows, x_parts, w_expand, w_shrink = together((x_rows, x_parts, w_expand, w_shrink), packed)
 
     def member_parts(array):
         return [
             lax.dynamic_index_in_dim(array, member ^ j, 0, keepdims=False) for j in range(members)
         ]
 
+    send_some(x_parts[0], x_rows[0], slots // 2 + 1, slots)
     weights = member_parts(pack_expert(w_expand.astype(bf16), w_shrink.astype(bf16)))
-    weights = jnp.stack(natural(swap_slots(weights, "gi"), member))
-    x_rows[0], x_parts, packed.value, weights = hold(
-        (x_rows[0], x_parts, packed.value, weights)
-    )
+    weights = swap_slots(weights, "gi")
+    packed.steps("gq")
+    x_rows, x_parts, weights = together((x_rows, x_parts, weights), packed)
+    packed.at_once("gi")
+    weights = jnp.stack(natural(weights, member))
+    x_rows, x_parts, weights = together((x_rows, x_parts, weights), packed)
+    packed.steps("core")
+    x_rows, x_parts, weights = together((x_rows, x_parts, weights), packed)
     tail = weights.shape[1] // 2
     halves = [
         Doubling(half, owners, ("gq", "seq"), 1) for half in (weights[:, :tail], weights[:, tail:])
     ]
     halves[0].steps("gq")
-    halves[1].value = together(halves[1].value, halves[0])
-    halves[1].steps("gq")
-    packed.steps("seq").steps("core")
-    x_rows[0], x_parts = together((x_rows[0], x_parts), packed, *halves)
     packed = packed.value.reshape(width, -1)
-    proj_in, proj_out = packed[:, : 3 * width], packed[:, 3 * width : 4 * width]
+
+    old = []
+    for row in range(rows):
+        old = attend_first(me, row, rows, x_rows[row], packed, parts, old)
+        if row + 1 < rows:
+            x_rows.append(swap_slots(x_parts[row + 1], "seq"))
+            old, x_rows[row + 1] = together((old, x_rows[row + 1]), *halves)
+        if row == max(0, rows - 2):
+            halves[0].steps("seq")
+            halves[1].steps("gq")
+        if row == rows - 1:
+            old = together(old, *halves)
     vectors = jnp.transpose(packed[:, 4 * width :])
     gain_one = vectors[0:1].astype(f32)
     gain_two = vectors[1:2].astype(f32)
@@ -1064,85 +1167,79 @@
     control = jnp.concatenate(
         [jnp.broadcast_to(c, (LANES // experts, width)) for c in control], axis=0
     )
-
-    old = []
-    for row in range(rows):
-        old = attend_first(me, row, rows, x_rows[row], gain_one, proj_in, parts, old)
-        if row + 1 < rows:
-            x_rows.append(swap_slots(x_parts[row + 1], "seq"))
-            old, x_rows[row + 1] = together((old, x_rows[row + 1]), halves[0])
-        if row == max(0, rows - 2):
-            halves[0].steps("seq")
-        if row == rows - 1:
-            old = together(old, *halves)
-    halves[1].steps("seq")
     att, projected, kept = old[:slots], old[slots : slots + 6], old[slots + 6 :]
     att_parts, kept = [swap_slots(att, "seq")], [kept]
     for part in range(1, parts):
         att, more = attend_next(me, part, parts, projected, slots)
-        att, att_parts[-1] = hold((att, att_parts[-1]))
+        more, att_parts[-1], gain_one, gain_two, control = hold(
+            (more, att_parts[-1], gain_one, gain_two, control)
+        )
         att_parts.append(swap_slots(att, "seq"))
         kept.append(more)
     pay_parts, second_parts, middle_parts = [], [], []
     for part in range(parts):
         pay, second, middle = mix(
-            me, part, att_parts[part], inputs, cotangent, proj_out, gain_two, control, experts
+            me, part, att_parts[part], inputs, cotangent, packed, gain_two, control, experts
         )
+        if part + 1 < parts:
+            pay, second, middle, att_parts[part + 1] = together(
+                (pay, second, middle, att_parts[part + 1]), halves[1]
+            )
         if part == 0:
-            pay, second, middle = together((pay, second, middle), halves[1])
-            halves = [half.value.reshape(-1, *half.value.shape[-2:]) for half in halves]
-            halves = [(half, partner(half, "seq", slots, 1)) for half in halves]
+            halves[1].steps("seq")
+        if part == parts - 1:
+            pay, second, middle, pay_parts = together((pay, second, middle, pay_parts), halves[1])
         pay_parts.append(swap_slots(pay, "gi"))
         second_parts.append(second)
         middle_parts.append(middle)
+    halves = [half.value.reshape(-1, *half.value.shape[-2:]) for half in halves]
+    halves = [(half, partner(half, "seq", slots, 1)) for half in halves]
     ret_parts, earlier = [], []
     for part in range(parts):
         back, more = expert(me, seq_me % 2, part, parts, pay_parts[part], halves, earlier)
         earlier = earlier + list(more)
         if part + 1 < parts:
-            pay_parts[part + 1], back = hold((pay_parts[part + 1], back))
+            pay_parts[part + 1][1], back = hold((pay_parts[part + 1][1], back))
         elif part:
             back, more, ret_parts = hold((back, more, ret_parts))
         ret_parts.append(swap_slots([back] * members, "gi"))
 
-    keep, send = more
+    kept_grad, send = more
+    received = partner(send, "seq", slots, 1)
     bits = [2] * len(bits_of((("gq", groups),)))
     bits += [members] + [2] * (len(bits_of((("seq", slots),))) - 1)
-    total = keep.astype(f32) + partner(send, "seq", slots, 1).astype(f32)
-    sum_expert = Halving(total.reshape(*bits, *total.shape[1:]), owners, ("seq", "gq"), 1)
+
+    def to_bits(keep, other):
+        return (keep.astype(f32) + other.astype(f32)).reshape(*bits, *keep.shape[1:])
+
     do_parts, before = [], []
     for part in range(parts):
+        last = part == parts - 1
+        if last:
+            sum_expert = Halving(to_bits(kept_grad, received), owners, ("seq", "gq"), 1)
+            sum_expert.prepare()
+            ret_parts[part], before = together((ret_parts[part], before), sum_expert)
         do, before = unmix(
             me,
             part,
+            last,
+            groups * members * slots,
             ret_parts[part],
             att_parts[part],
             second_parts[part],
             middle_parts[part],
             cotangent,
-            proj_out,
+            packed,
             gain_two,
             control,
             before,
         )
-        do, before = together((do, before), sum_expert)
-        if part == 0:
-            sum_expert.steps("seq")
         do_parts.append(swap_slots(do, "seq"))
-    output, grad_middle, grad_out, grad_control, grad_gain = before
-    grad_control = grad_control.reshape(experts, LANES // experts, width).sum(axis=1)
-    grad_control = jnp.concatenate(
-        natural([grad_control[e : e + 1] for e in range(experts)], member), axis=0
-    )
-    small = jnp.concatenate([grad_gain.sum(axis=0, keepdims=True), grad_control], axis=0)
-    small = jnp.pad(jnp.transpose(small), ((0, 0), (0, LANES - 1 - experts)))
+    output, grad_middle, keep_out, send_out = before
     every_bit = [2] * len(bits_of(place))
-    grad_out = jnp.concatenate([grad_out, small], axis=1)
-    sum_out = Halving(grad_out.reshape(*every_bit, -1, width + LANES), place, ("core",))
-    sum_out.left = bits_of(place)
-    sum_out.steps("core")
-    do_parts = together(do_parts, sum_out, sum_expert)
-    sum_expert.steps("gq")
+    do_parts, send_out = together((do_parts, send_out), sum_expert)
+    sum_expert.exchange()
+    received_out = partner(send_out, "seq", slots, 1)
 
     gf_rows, grad_in = [], None
     for row in range(rows):
@@ -1154,33 +1251,48 @@
             x_rows[row],
             do_parts,
             gain_one,
-            proj_in,
+            packed,
             projected,
             kept,
             grad_in,
         )
         grad_in = grad_in[0] if row < rows - 1 else grad_in
         if row == 0:
+            gf_slots, grad_in, received_out = together((gf_slots, grad_in, received_out), sum_expert)
+            sum_expert.combine()
+            while sum_expert.order[0][0] == "seq":
+                sum_expert.step(sum_expert.order.pop(0))
+            sum_expert.prepare()
             gf_slots, grad_in = together((gf_slots, grad_in), sum_expert)
-            columns = swap_slots(
-                [p if j == 0 else p.astype(bf16) for j, p in enumerate(member_parts(sum_expert.value))],
-                "gi",
-            )
-        if row == rows - 1:
-            gf_slots, grad_in, columns, gf_rows = hold((gf_slots, grad_in, columns, gf_rows))
-        gf_rows.append(swap_slots(gf_slots, "seq"))
-    columns = jnp.stack([c.astype(f32) for c in natural(columns, member)])
+            sum_expert.exchange()
+        if row:
+            gf_slots, grad_in, gf_rows = together((gf_slots, grad_in, gf_rows), sum_expert)
+        if row < rows - 1:
+            gf_rows.append(swap_slots(gf_slots, "seq"))
+    gf_rows.append([gf_slots[0]])
+    send_some(gf_slots, gf_rows[-1], 1, slots // 2 + 1)
+    keep, send = grad_in
+    received = partner(send, "seq", slots, 1)
+    gf_rows, gf_slots, received = hold((gf_rows, gf_slots, received))
+    send_some(gf_slots, gf_rows[-1], slots // 2 + 1, slots)
+    total = keep + received.astype(f32)
+    total = jnp.concatenate([total, keep_out + received_out.astype(f32)], axis=-1)
+    total = total.reshape(*every_bit[1:], *total.shape[1:])
+    sum_in = Halving(total, place, ("gi", "gq", "seq"))
+    sum_in.at_once(("gi",))
+    gf_rows = together(gf_rows, sum_in, sum_expert)
+    sum_in.combine()
+    sum_in.at_once(("gq", "seq"))
+    sum_expert.combine()
+    sums = sum_expert.finish()
+    columns = [p if j == 0 else p.astype(bf16) for j, p in enumerate(member_parts(sums))]
+    columns = swap_slots(columns, "gi")
+    grad_inputs = finish(me, gf_rows, inputs, grad_middle, gain_one)
+    grad_inputs, columns = together((grad_inputs, columns), sum_in)
+    sum_in.combine()
+    columns = natural(columns, member)
+    columns = jnp.stack([c.astype(f32) for c in columns])
     grad_expand, grad_shrink = unpack_expert(columns, width // (groups * members * slots))
-    keep, send = grad_in
-    total = keep + partner(send, "seq", slots, 1).astype(f32)
-    total = total.reshape(*every_bit[1:], *total.shape[1:])
-    total = jnp.concatenate([total, sum_out.value], axis=-1)
-    sum_in = Halving(total, place, ("gi", "gq", "seq"))
-    sum_in.step(sum_in.order.pop(0))
-    gf_rows[-1] = together(gf_rows[-1], sum_in)
-    sum_in.steps("gi")
-    grad_inputs = finish(me, gf_rows, inputs, grad_middle, gain_one)
-    grad_inputs = together(grad_inputs, sum_in)
     total = sum_in.finish()
     grad_in, grad_out = total[:, : 3 * width], total[:, 3 * width :]
     small = jnp.transpose(grad_out[:, width:])

time: 390 us -> 342 us (0.88)
  waiting for transfers between devices: 122 us -> 77.3 us
  Pallas kernels: 159 us -> 168 us
  other arithmetic: 22.5 us -> 15 us
  local copies, waits for them, and re-layouts: 21.6 us -> 14.6 us
    ppermute x63 -> x59, waiting for transfers between devices: 122 us -> 68.8 us  [partner(): return lax.ppermute(value, axis, [(i, i ^ mask) for i in range(size)])]
    ppermute x0 -> x6, waiting for transfers between devices: none -> 8.54 us  [at_once(): total.append(lax.ppermute(piece.astype(bf16), tuple(names), pairs))]
    pallas_call x12, Pallas kernels: 159 us -> 168 us  [call(): pl.pallas_call(kernel, grid_spec=pltpu.PrefetchScalarGridSpec(num_scalar_...]
    ppermute x0 -> x6, starting transfers between devices: none -> 8.07 us  [at_once(): total.append(lax.ppermute(piece.astype(bf16), tuple(names), pairs))]
    ppermute x63 -> x59, starting transfers between devices: 56.5 us -> 52 us  [partner(): return lax.ppermute(value, axis, [(i, i ^ mask) for i in range(size)])]
    add x9 -> x7, other arithmetic: 8.81 us -> 4.35 us  [the longest x1 2.29 us: to_bits(): keep.astype(f32) + other.astype(f32)]
    unnamed x108 -> x93, local copies, waits for them, and re-layouts: 12.8 us -> 8.43 us
  transfers between devices with their start and end apart: 63 -> 65, of which waited for: 22 -> 21; matrix products, arithmetic and copies ran while one was open for 4% -> 3% of each run, Pallas kernels for 41% -> 50%
where the time goes in v3:
time: 342 us; the launch traced here: 336 us
  Pallas kernels  168 us (49%)
  waiting for transfers between devices  77.3 us (23%)
  starting transfers between devices  60 us (18%)
  other arithmetic  15 us (4%)
  local copies, waits for them, and re-layouts  14.6 us (4%)
    pallas_call x12, Pallas kernels, call(): pl.pallas_call(kernel, grid_spec=pltpu.PrefetchScalarGridSpec(num_scalar_...  168 us
    ppermute x59, waiting for transfers between devices, partner(): return lax.ppermute(value, axis, [(i, i ^ mask) for i in range(size)])  68.8 us
    ppermute x59, starting transfers between devices, partner(): return lax.ppermute(value, axis, [(i, i ^ mask) for i in range(size)])  52 us
    ppermute x6, waiting for transfers between devices, at_once(): total.append(lax.ppermute(piece.astype(bf16), tuple(names), pairs))  8.54 us
    unnamed x93, local copies, waits for them, and re-layouts  8.43 us
    ppermute x6, starting transfers between devices, at_once(): total.append(lax.ppermute(piece.astype(bf16), tuple(names), pairs))  8.07 us
  transfers between devices with their start and end apart: 65, of which 21 were waited for; matrix products, arithmetic and copies ran while one was open for 3% of the time, Pallas kernels for 50%

profile of v3, /device:TPU:0, one launch (start us, length us, event | category | flops | bytes accessed | tf_op | source)
XLA Modules:
  0.0 336.4 jit_solution(10079035123215922649)
XLA Ops:
  3.8 3.0 collective-permute-start.2
  7.5 1.8 fusion.1
  10.4 1.5 collective-permute-done.refs_2_
  11.9 7.5 %collective-permute-done.1.refs_3_ = bf16[1,272,512]{2,1,0:T(8,128)(2,1)S(1)} collective-permute-done((bf16[1,272,512]{2,1,0:T(8,128)(2,1)S(1)}, bf16[1,272,512]{2,1,0:T(8,128)(2,1)S(1)}, u32[]{:S(2)}, u32[]{:S(2)}) %collective-permute-start.1) | collective-permute-done | bytes 278560 | tf_op jit(solution)/shard_map/ppermute | solution.py:58
  19.4 2.6 collective-permute-start.7
  22.1 1.6 collective-permute-start.4
  23.7 1.6 collective-permute-start.5
  25.7 3.0 collective-permute-done.7
  28.8 2.4 collective-permute-done.5
  31.1 1.8 collective-permute-done.6
  33.7 1.5 collective-permute-start.10
  35.2 1.5 collective-permute-start.8
  37.3 10.1 %collective-permute-done.10 = bf16[2,2,16,2176]{3,2,1,0:T(8,128)(2,1)S(1)} collective-permute-done((bf16[2,2,16,2176]{3,2,1,0:T(8,128)(2,1)S(1)}, bf16[2,2,16,2176]{3,2,1,0:T(8,128)(2,1)S(1)}, u32[]{:S(2)}, u32[]{:S(2)}) %collective-permute-start.10) | collective-permute-done | bytes 278560 | tf_op jit(solution)/shard_map/ppermute | solution.py:58
  47.4 1.2 collective-permute-done.9
  49.7 2.1 collective-permute-done.11
  52.5 1.4 copy-done
  54.3 2.3 collective-permute-start.13
  56.7 15.0 %attend_first.2 = (bf16[2,128,512]{2,1,0:T(8,128)(2,1)}, bf16[2,128,512]{2,1,0:T(8,128)(2,1)}, bf16[2,128,512]{2,1,0:T(8,128)(2,1)}, bf16[2,128,512]{2,1,0:T(8,1...) custom-call(s32[2]{0:T(128)} %pad_add_fusion.refs_0_, ...), custom_call_target="tpu_custom_call" | custom-call | flops 12000000000 | bytes 1048576 | tf_op jit(solution)/shard_map/attend_first/pallas_call | solution.py:214
  73.2 2.8 collective-permute-start.17
  76.0 1.7 collective-permute-start.16
  77.7 14.3 %attend_first.3 = (bf16[2,128,512]{2,1,0:T(8,128)(2,1)}, bf16[2,128,512]{2,1,0:T(8,128)(2,1)}, bf16[2,128,512]{2,1,0:T(8,128)(2,1)}, bf16[2,128,512]{2,1,0:T(8,1...) custom-call(s32[2]{0:T(128)} %pad_add_fusion.refs_0_, ...), custom_call_target="tpu_custom_call", output_to_operand_aliasing={{0}: (7, {}), {1}: (8, {}), {2}: (9, {}), {3}: (10, {}), {4... | custom-call | flops 12000000000 | bytes 1048576 | tf_op jit(solution)/shard_map/attend_first/pallas_call | solution.py:214
  93.4 1.5 collective-permute-start.20
  94.9 17.2 %attend_next.1 = (bf16[2,128,512]{2,1,0:T(8,128)(2,1)}, bf16[2,128,512]{2,1,0:T(8,128)(2,1)}, bf16[2,128,512]{2,1,0:T(8,128)(2,1)}, bf16[2,128,512]{2,1,0:T(8,12...) custom-call(s32[2]{0:T(128)} %pad_add_fusion.refs_0_, s32[2,1,1024]{2,1,0:T(1,128)} %get-tuple-element.370.refs_1_.refs_13_, ...), custom_call_target="tpu_custom_call" | custom-call | flops 14000000000 | bytes 1048576 | tf_op jit(solution)/shard_map/attend_next/pallas_call | solution.py:214
  112.9 1.3 collective-permute-start.23
  114.9 7.9 %mix.2 = (bf16[128,1152]{1,0:T(8,128)(2,1)}, bf16[128,1152]{1,0:T(8,128)(2,1)}, bf16[128,1152]{1,0:T(8,128)(2,1)}, bf16[128,1152]{1,0:T(8,128)(2,1)}, bf16[8,128...) custom-call(s32[2]{0:T(128)} %pad_add_fusion.refs_0_, bf16[2,128,512]{2,1,0:T(8,128)(2,1)} %get-tuple-element.380.refs_1_.refs_5_, ...), custom_call_target="tpu_custom_call" | custom-call | flops 6000000000 | bytes 1048576 | tf_op jit(solution)/shard_map/mix/pallas_call | solution.py:214
  122.8 3.2 collective-permute-done.23.refs_4_.refs_8_
  127.0 1.5 collective-permute-start.24
  128.5 1.6 collective-permute-start.25
  130.5 7.8 %mix.3 = (bf16[128,1152]{1,0:T(8,128)(2,1)}, bf16[128,1152]{1,0:T(8,128)(2,1)}, bf16[128,1152]{1,0:T(8,128)(2,1)}, bf16[128,1152]{1,0:T(8,128)(2,1)}, bf16[8,128...) custom-call(s32[2]{0:T(128)} %pad_add_fusion.refs_0_, bf16[2,128,512]{2,1,0:T(8,128)(2,1)} %get-tuple-element.397.refs_1_.refs_5_, ...), custom_call_target="tpu_custom_call" | custom-call | flops 6000000000 | bytes 1048576 | tf_op jit(solution)/shard_map/mix/pallas_call | solution.py:214
  138.4 2.7 collective-permute-done.27
  141.3 2.7 collective-permute-done.26.refs_4_
  144.2 1.6 collective-permute-start.28
  145.8 1.6 collective-permute-start.31
  148.7 7.9 %expert.2 = (bf16[128,1152]{1,0:T(8,128)(2,1)}, bf16[128,512]{1,0:T(8,128)(2,1)}, bf16[128,512]{1,0:T(8,128)(2,1)}, bf16[128,2048]{1,0:T(8,128)(2,1)}, bf16[128,2048]{1,0:T(8,128)(2,1)}) custom-call(s32[2]{0:T(128)} %pad_add_fusion.refs_0_, bf16[128,1152]{1,0:T(8,128)(2,1)} %get-tuple-element.414.refs_1_, bf16[128,1152]{1,0:T(8,128)(2,1)} %copy-done.22, ...), custom_call_target="tpu_custom_call" | custom-call | flops 7000000000 | bytes 1048576 | tf_op jit(solution)/shard_map/expert/pallas_call | solution.py:214
  156.7 1.6 collective-permute-start.33
  158.2 1.6 collective-permute-start.34
  160.2 1.8 collective-permute-done.32.refs_4_
  162.0 10.0 %expert.3 = (bf16[128,1152]{1,0:T(8,128)(2,1)}, bf16[16,128,512]{2,1,0:T(8,128)(2,1)}, bf16[16,128,512]{2,1,0:T(8,128)(2,1)}) custom-call(s32[2]{0:T(128)} %pad_add_fusion.refs_0_, bf16[128,1152]{1,0:T(8,128)(2,1)} %get-tuple-element.412.refs_1_, bf16[128,1152]{1,0:T(8,128)(2,1)} %collective-permute-done.28.refs_2_, ...), custom_call_target="tpu_custom_call" | custom-call | flops 7000000000 | bytes 1048576 | tf_op jit(solution)/shard_map/expert/pallas_call | solution.py:214
  172.0 1.7 collective-permute-done.35.refs_4_
  173.8 1.6 collective-permute-start.36
  175.3 1.6 collective-permute-start.37
  177.3 10.4 %unmix.2 = (bf16[8,256,512]{2,1,0:T(8,128)(2,1)}, bf16[8,256,512]{2,1,0:T(8,128)(2,1)}, bf16[2,128,512]{2,1,0:T(8,128)(2,1)}, bf16[2,128,512]{2,1,0:T(8,128)(2,1...) custom-call(s32[2]{0:T(128)} %pad_add_fusion.refs_0_, ...), custom_call_target="tpu_custom_call" | custom-call | flops 8499999744 | bytes 1048576 | tf_op jit(solution)/shard_map/unmix/pallas_call | solution.py:214
  187.9 1.8 collective-permute-start.41
  189.6 2.3 convert_add_fusion
  191.9 1.1 fusion.2
  194.3 11.1 %unmix.3 = (bf16[8,256,512]{2,1,0:T(8,128)(2,1)}, bf16[8,256,512]{2,1,0:T(8,128)(2,1)}, bf16[2,128,512]{2,1,0:T(8,128)(2,1)}, bf16[2,128,512]{2,1,0:T(8,128)(2,1...) custom-call(s32[2]{0:T(128)} %pad_add_fusion.refs_0_, ...), custom_call_target="tpu_custom_call", output_to_operand_aliasing={{0}: (15, {}), {1}: (16, {})} | custom-call | flops 8499999744 | bytes 1048576 | tf_op jit(solution)/shard_map/unmix/pallas_call | solution.py:214
  205.8 1.7 collective-permute-start.44
  207.5 7.6 %collective-permute-done.44.refs_11_ = bf16[2,128,512]{2,1,0:T(8,128)(2,1)S(1)} collective-permute-done((bf16[2,128,512]{2,1,0:T(8,128)(2,1)}, bf16[2,128,512]{2,1,0:T(8,128)(2,1)S(1)}, u32[]{:S(2)}, u32[]{:S(2)}) %collective-permute-start.44) | collective-permute-done | bytes 262176 | tf_op jit(solution)/shard_map/ppermute | solution.py:58
  215.1 4.1 %collective-permute-done.45.refs_12_ = bf16[2,128,512]{2,1,0:T(8,128)(2,1)S(1)} collective-permute-done((bf16[2,128,512]{2,1,0:T(8,128)(2,1)}, bf16[2,128,512]{2,1,0:T(8,128)(2,1)S(1)}, u32[]{:S(2)}, u32[]{:S(2)}) %collective-permute-start.45) | collective-permute-done | bytes 262176 | tf_op jit(solution)/shard_map/ppermute | solution.py:58
  220.0 1.6 collective-permute-start.47
  221.9 29.1 %attend_back.2 = (bf16[1,256,512]{2,1,0:T(8,128)(2,1)}, bf16[1,256,512]{2,1,0:T(8,128)(2,1)}, bf16[1,256,512]{2,1,0:T(8,128)(2,1)}, bf16[1,256,512]{2,1,0:T(8,128)(2,1)}, f32[512,1536]{1,0:T(8,128)}) custom-call(s32[2]{0:T(128)} %pad_add_fusion.refs_0_, bf16[1,272,512]{2,1,0:T(8,128)(2,1)} %get-tuple-element.318.refs_1_, bf16[1,272,512]{2,1,0:T(8,128)(2,1)} %copy-done.23, ...), custom_call_target="tpu_custom_call" | custom-call | flops 28000000000 | bytes 1048576 | tf_op jit(solution)/shard_map/attend_back/pallas_call | solution.py:214
  254.1 30.0 %attend_back.3 = (bf16[1,256,512]{2,1,0:T(8,128)(2,1)}, bf16[1,256,512]{2,1,0:T(8,128)(2,1)}, bf16[1,256,512]{2,1,0:T(8,128)(2,1)}, bf16[1,256,512]{2,1,0:T(8,12...) custom-call(s32[2]{0:T(128)} %pad_add_fusion.refs_0_, bf16[1,272,512]{2,1,0:T(8,128)(2,1)} %get-tuple-element.340.refs_1_, ...), custom_call_target="tpu_custom_call" | custom-call | flops 28000000000 | bytes 1048576 | tf_op jit(solution)/shard_map/attend_back/pallas_call | solution.py:214
  286.2 1.2 convert_add_fusion.4
  287.8 6.4 %collective-permute-done.53.refs_7_ = bf16[1,256,512]{2,1,0:T(8,128)(2,1)S(1)} collective-permute-done((bf16[1,256,512]{2,1,0:T(8,128)(2,1)}, bf16[1,256,512]{2,1,0:T(8,128)(2,1)S(1)}, u32[]{:S(2)}, u32[]{:S(2)}) %collective-permute-start.53) | collective-permute-done | bytes 262176 | tf_op jit(solution)/shard_map/ppermute | solution.py:58
  295.5 1.6 collective-permute-start.56
  297.1 1.6 collective-permute-start.57
  299.1 7.8 %collective-permute-done.55.refs_8_ = bf16[1,256,512]{2,1,0:T(8,128)(2,1)S(1)} collective-permute-done((bf16[1,256,512]{2,1,0:T(8,128)(2,1)S(1)}, bf16[1,256,512]{2,1,0:T(8,128)(2,1)S(1)}, u32[]{:S(2)}, u32[]{:S(2)}) %collective-permute-start.55) | collective-permute-done | bytes 262176 | tf_op jit(solution)/shard_map/ppermute | solution.py:58
  306.9 3.9 %collective-permute-done.58 = bf16[2,2,16,2176]{3,2,1,0:T(8,128)(2,1)S(1)} collective-permute-done((bf16[2,2,16,2176]{3,2,1,0:T(8,128)(2,1)S(1)}, bf16[2,2,16,2176]{3,2,1,0:T(8,128)(2,1)S(1)}, u32[]{:S(2)}, u32[]{:S(2)}) %collective-permute-start.58) | collective-permute-done | bytes 278560 | tf_op jit(solution)/shard_map/ppermute | solution.py:199
  311.7 2.3 collective-permute-start.63
  314.2 1.6 collective-permute-start.59
  315.8 1.6 collective-permute-start.60
  317.8 6.9 %finish.1 = bf16[8,256,512]{2,1,0:T(8,128)(2,1)} custom-call(s32[2]{0:T(128)} %pad_add_fusion.refs_0_, bf16[1,256,512]{2,1,0:T(8,128)(2,1)} %get-tuple-element.535.refs_1_, bf16[1,256,512]{2,1,0:T(8,128)(2,1)} %copy-done.32, bf16[1,256,512]{2,1,0:T(8,128)(2,1)} %collective-permute-done.49.refs_3_, bf16[1,256,512]{2,1,0:T(8,128)(2,1)} %collective-permute-done.50.refs_4_, ...), custom_call_target="tpu_custom_call" | custom-call | flops 6000000000 | bytes 1048576 | tf_op jit(solution)/shard_map/finish/pallas_call | solution.py:214
  324.7 1.5 collective-permute-start.64
  326.2 4.7 %collective-permute-done.64 = bf16[16,2176]{1,0:T(8,128)(2,1)S(1)} collective-permute-done((bf16[16,2176]{1,0:T(8,128)(2,1)S(1)}, bf16[16,2176]{1,0:T(8,128)(2,1)S(1)}, u32[]{:S(2)}, u32[]{:S(2)}) %collective-permute-start.64) | collective-permute-done | bytes 69664 | tf_op jit(solution)/shard_map/ppermute | solution.py:199
  (243 shorter events, 34.1 us)
Async XLA Ops:
  3.8 6.6 %collective-permute-start.2 = (bf16[16,2176]{1,0:T(8,128)(2,1)S(1)}, bf16[16,2176]{1,0:T(8,128)(2,1)S(1)}, u32[]{:S(2)}, u32[]{:S(2)}) collective-permute-start(bf16[16,2176]{1,0:T(8,128)(2,1)S(1)} %fusion.23), channel_id=1, source_target_pairs={{0,2},{1,3},{2,0},{3,1},{4,6},{5,7},{6,4},{7,5},{8,10},{9,11},{10,... | collective-permute-start | bytes 208904 | tf_op jit(solution)/shard_map/ppermute | solution.py:58
  10.3 9.1 %collective-permute-start.1 = (bf16[1,272,512]{2,1,0:T(8,128)(2,1)S(1)}, bf16[1,272,512]{2,1,0:T(8,128)(2,1)S(1)}, u32[]{:S(2)}, u32[]{:S(2)}) collective-permute-start(bf16[1,272,512]{2,1,0:T(8,128)(2,1)S(1)} %get-tuple-element.617), channel_id=1, source_target_pairs={{0,2},{1,3},{2,0},{3,1},{4,6},{5,7},{6,4},{7,5},{8,10},{9,11},{10,... | collective-permute-start | bytes 835592 | tf_op jit(solution)/shard_map/ppermute | solution.py:58
  19.4 9.3 %collective-permute-start.7 = (bf16[2,16,2176]{2,1,0:T(8,128)(2,1)S(1)}, bf16[2,16,2176]{2,1,0:T(8,128)(2,1)S(1)}, u32[]{:S(2)}, u32[]{:S(2)}) collective-permute-start(bf16[2,16,2176]{2,1,0:T(8,128)(2,1)S(1)} %pad_maximum_fusion.10), channel_id=1, source_target_pairs={{0,16},{16,0},{1,17},{17,1},{2,18},{18,2},{3,19},{19,3},{4,20},{20... | collective-permute-start | bytes 417800 | tf_op jit(solution)/shard_map/ppermute | solution.py:58
  22.1 6.6 %collective-permute-start.4 = (bf16[128,512]{1,0:T(8,128)(2,1)S(1)}, bf16[128,512]{1,0:T(8,128)(2,1)S(1)}, u32[]{:S(2)}, u32[]{:S(2)}) collective-permute-start(bf16[128,512]{1,0:T(8,128)(2,1)S(1)} %get-tuple-element.654), channel_id=1, source_target_pairs={{0,4},{4,0},{8,12},{12,8},{1,5},{5,1},{9,13},{13,9},{2,6},{6,2},{1... | collective-permute-start | bytes 393224 | tf_op jit(solution)/shard_map/ppermute | solution.py:58
  23.7 7.4 %collective-permute-start.5 = (bf16[128,512]{1,0:T(8,128)(2,1)S(1)}, bf16[128,512]{1,0:T(8,128)(2,1)S(1)}, u32[]{:S(2)}, u32[]{:S(2)}) collective-permute-start(bf16[128,512]{1,0:T(8,128)(2,1)S(1)} %get-tuple-element.655), channel_id=1, source_target_pairs={{0,8},{4,12},{8,0},{12,4},{1,9},{5,13},{9,1},{13,5},{2,10},{6,14},... | collective-permute-start | bytes 393224 | tf_op jit(solution)/shard_map/ppermute | solution.py:58
  25.3 7.7 %collective-permute-start.6 = (bf16[128,512]{1,0:T(8,128)(2,1)S(1)}, bf16[128,512]{1,0:T(8,128)(2,1)S(1)}, u32[]{:S(2)}, u32[]{:S(2)}) collective-permute-start(bf16[128,512]{1,0:T(8,128)(2,1)S(1)} %get-tuple-element.652), channel_id=1, source_target_pairs={{0,12},{4,8},{8,4},{12,0},{1,13},{5,9},{9,5},{13,1},{2,14},{6,10},... | collective-permute-start | bytes 393224 | tf_op jit(solution)/shard_map/ppermute | solution.py:58
  25.7 8.0 %collective-permute-start.3 = (bf16[1,272,512]{2,1,0:T(8,128)(2,1)S(1)}, bf16[1,272,512]{2,1,0:T(8,128)(2,1)S(1)}, u32[]{:S(2)}, u32[]{:S(2)}) collective-permute-start(bf16[1,272,512]{2,1,0:T(8,128)(2,1)S(1)} %get-tuple-element.287), channel_id=1, source_target_pairs={{0,3},{1,2},{2,1},{3,0},{4,7},{5,6},{6,5},{7,4},{8,11},{9,10},{10,... | collective-permute-start | bytes 835592 | tf_op jit(solution)/shard_map/ppermute | solution.py:58
  33.7 13.7 %collective-permute-start.10 = (bf16[2,2,16,2176]{3,2,1,0:T(8,128)(2,1)S(1)}, bf16[2,2,16,2176]{3,2,1,0:T(8,128)(2,1)S(1)}, u32[]{:S(2)}, u32[]{:S(2)}) collective-permute-start(bf16[2,2,16,2176]{3,2,1,0:T(8,128)(2,1)S(1)} %pad_maximum_fusion.9), channel_id=1, source_target_pairs={{0,4},{4,0},{8,12},{12,8},{1,5},{5,1},{9,13},{13,9},{2,6},{6,2},{1... | collective-permute-start | bytes 835592 | tf_op jit(solution)/shard_map/ppermute | solution.py:58
  35.2 12.2 %collective-permute-start.8 = (bf16[2,2,16,2176]{3,2,1,0:T(8,128)(2,1)S(1)}, bf16[2,2,16,2176]{3,2,1,0:T(8,128)(2,1)S(1)}, u32[]{:S(2)}, u32[]{:S(2)}) collective-permute-start(bf16[2,2,16,2176]{3,2,1,0:T(8,128)(2,1)S(1)} %pad_maximum_fusion.9), channel_id=1, source_target_pairs={{0,12},{4,8},{8,4},{12,0},{1,13},{5,9},{9,5},{13,1},{2,14},{6,10},... | collective-permute-start | bytes 835592 | tf_op jit(solution)/shard_map/ppermute | solution.py:58
  36.8 11.9 %collective-permute-start.9 = (bf16[2,2,16,2176]{3,2,1,0:T(8,128)(2,1)S(1)}, bf16[2,2,16,2176]{3,2,1,0:T(8,128)(2,1)S(1)}, u32[]{:S(2)}, u32[]{:S(2)}) collective-permute-start(bf16[2,2,16,2176]{3,2,1,0:T(8,128)(2,1)S(1)} %pad_maximum_fusion.9), channel_id=1, source_target_pairs={{0,8},{4,12},{8,0},{12,4},{1,9},{5,13},{9,1},{13,5},{2,10},{6,14},... | collective-permute-start | bytes 835592 | tf_op jit(solution)/shard_map/ppermute | solution.py:58
  49.0 2.8 collective-permute-start.11
  54.0 19.0 %collective-permute-start.15 = (bf16[4,64,512]{2,1,0:T(8,128)(2,1)S(1)}, bf16[4,64,512]{2,1,0:T(8,128)(2,1)S(1)}, u32[]{:S(2)}, u32[]{:S(2)}) collective-permute-start(bf16[4,64,512]{2,1,0:T(8,128)(2,1)S(1)} %slice.83), channel_id=1, source_target_pairs={{0,16},{16,0},{1,17},{17,1},{2,18},{18,2},{3,19},{19,3},{4,20},{20... | collective-permute-start | bytes 786440 | tf_op jit(solution)/shard_map/ppermute | solution.py:58
  54.3 18.9 %collective-permute-start.12 = (bf16[1,272,512]{2,1,0:T(8,128)(2,1)S(1)}, bf16[1,272,512]{2,1,0:T(8,128)(2,1)S(1)}, u32[]{:S(2)}, u32[]{:S(2)}) collective-permute-start(bf16[1,272,512]{2,1,0:T(8,128)(2,1)S(1)} %copy-done.11), channel_id=1, source_target_pairs={{0,1},{1,0},{2,3},{3,2},{4,5},{5,4},{6,7},{7,6},{8,9},{9,8},{10,11... | collective-permute-start | bytes 835592 | tf_op jit(solution)/shard_map/ppermute | solution.py:58
  54.3 18.8 %collective-permute-start.13 = (bf16[1,272,512]{2,1,0:T(8,128)(2,1)S(1)}, bf16[1,272,512]{2,1,0:T(8,128)(2,1)S(1)}, u32[]{:S(2)}, u32[]{:S(2)}) collective-permute-start(bf16[1,272,512]{2,1,0:T(8,128)(2,1)S(1)} %get-tuple-element.337), channel_id=1, source_target_pairs={{0,2},{1,3},{2,0},{3,1},{4,6},{5,7},{6,4},{7,5},{8,10},{9,11},{10,... | collective-permute-start | bytes 835592 | tf_op jit(solution)/shard_map/ppermute | solution.py:58
  56.6 16.6 %collective-permute-start.14 = (bf16[1,272,512]{2,1,0:T(8,128)(2,1)S(1)}, bf16[1,272,512]{2,1,0:T(8,128)(2,1)S(1)}, u32[]{:S(2)}, u32[]{:S(2)}) collective-permute-start(bf16[1,272,512]{2,1,0:T(8,128)(2,1)S(1)} %get-tuple-element.338), channel_id=1, source_target_pairs={{0,3},{1,2},{2,1},{3,0},{4,7},{5,6},{6,5},{7,4},{8,11},{9,10},{10,... | collective-permute-start | bytes 835592 | tf_op jit(solution)/shard_map/ppermute | solution.py:58
  73.2 18.8 %collective-permute-start.17 = (bf16[4,64,512]{2,1,0:T(8,128)(2,1)S(1)}, bf16[4,64,512]{2,1,0:T(8,128)(2,1)S(1)}, u32[]{:S(2)}, u32[]{:S(2)}) collective-permute-start(bf16[4,64,512]{2,1,0:T(8,128)(2,1)S(1)} %get-tuple-element.369), channel_id=1, source_target_pairs={{0,16},{16,0},{1,17},{17,1},{2,18},{18,2},{3,19},{19,3},{4,20},{20... | collective-permute-start | bytes 786440 | tf_op jit(solution)/shard_map/ppermute | solution.py:58
  76.0 16.1 %collective-permute-start.16 = (bf16[2,4,64,512]{3,2,1,0:T(8,128)(2,1)S(1)}, bf16[2,4,64,512]{3,2,1,0:T(8,128)(2,1)S(1)}, u32[]{:S(2)}, u32[]{:S(2)}) collective-permute-start(bf16[2,4,64,512]{3,2,1,0:T(8,128)(2,1)S(1)} %pad_maximum_fusion.7), channel_id=1, source_target_pairs={{0,2},{1,3},{2,0},{3,1},{4,6},{5,7},{6,4},{7,5},{8,10},{9,11},{10,... | collective-permute-start | bytes 1572872 | tf_op jit(solution)/shard_map/ppermute | solution.py:58
  93.1 19.8 %collective-permute-start.18 = (bf16[2,128,512]{2,1,0:T(8,128)(2,1)S(1)}, bf16[2,128,512]{2,1,0:T(8,128)(2,1)S(1)}, u32[]{:S(2)}, u32[]{:S(2)}) collective-permute-start(bf16[2,128,512]{2,1,0:T(8,128)(2,1)S(1)} %copy-done.43), channel_id=1, source_target_pairs={{0,1},{1,0},{2,3},{3,2},{4,5},{5,4},{6,7},{7,6},{8,9},{9,8},{10,11... | collective-permute-start | bytes 786440 | tf_op jit(solution)/shard_map/ppermute | solution.py:58
  93.1 21.1 %collective-permute-start.19 = (bf16[2,128,512]{2,1,0:T(8,128)(2,1)}, bf16[2,128,512]{2,1,0:T(8,128)(2,1)S(1)}, u32[]{:S(2)}, u32[]{:S(2)}) collective-permute-start(bf16[2,128,512]{2,1,0:T(8,128)(2,1)} %get-tuple-element.378), channel_id=1, source_target_pairs={{0,2},{1,3},{2,0},{3,1},{4,6},{5,7},{6,4},{7,5},{8,10},{9,11},{10,... | collective-permute-start | bytes 786440 | tf_op jit(solution)/shard_map/ppermute | solution.py:58
  93.4 21.4 %collective-permute-start.20 = (bf16[2,128,512]{2,1,0:T(8,128)(2,1)}, bf16[2,128,512]{2,1,0:T(8,128)(2,1)}, u32[]{:S(2)}, u32[]{:S(2)}) collective-permute-start(bf16[2,128,512]{2,1,0:T(8,128)(2,1)} %get-tuple-element.379), channel_id=1, source_target_pairs={{0,3},{1,2},{2,1},{3,0},{4,7},{5,6},{6,5},{7,4},{8,11},{9,10},{10,... | collective-permute-start | bytes 786440 | tf_op jit(solution)/shard_map/ppermute | solution.py:58
  112.1 10.7 %collective-permute-start.21 = (bf16[2,128,512]{2,1,0:T(8,128)(2,1)}, bf16[2,128,512]{2,1,0:T(8,128)(2,1)S(1)}, u32[]{:S(2)}, u32[]{:S(2)}) collective-permute-start(bf16[2,128,512]{2,1,0:T(8,128)(2,1)} %get-tuple-element.393), channel_id=1, source_target_pairs={{0,1},{1,0},{2,3},{3,2},{4,5},{5,4},{6,7},{7,6},{8,9},{9,8},{10,11... | collective-permute-start | bytes 786440 | tf_op jit(solution)/shard_map/ppermute | solution.py:58
  112.4 10.4 %collective-permute-start.22 = (bf16[2,128,512]{2,1,0:T(8,128)(2,1)}, bf16[2,128,512]{2,1,0:T(8,128)(2,1)S(1)}, u32[]{:S(2)}, u32[]{:S(2)}) collective-permute-start(bf16[2,128,512]{2,1,0:T(8,128)(2,1)} %get-tuple-element.394), channel_id=1, source_target_pairs={{0,2},{1,3},{2,0},{3,1},{4,6},{5,7},{6,4},{7,5},{8,10},{9,11},{10,... | collective-permute-start | bytes 786440 | tf_op jit(solution)/shard_map/ppermute | solution.py:58
  112.9 13.1 %collective-permute-start.23 = (bf16[2,128,512]{2,1,0:T(8,128)(2,1)}, bf16[2,128,512]{2,1,0:T(8,128)(2,1)S(1)}, u32[]{:S(2)}, u32[]{:S(2)}) collective-permute-start(bf16[2,128,512]{2,1,0:T(8,128)(2,1)} %get-tuple-element.395), channel_id=1, source_target_pairs={{0,3},{1,2},{2,1},{3,0},{4,7},{5,6},{6,5},{7,4},{8,11},{9,10},{10,... | collective-permute-start | bytes 786440 | tf_op jit(solution)/shard_map/ppermute | solution.py:58
  114.2 33.6 %collective-permute-start.29 = (bf16[16,64,512]{2,1,0:T(8,128)(2,1)S(1)}, bf16[16,64,512]{2,1,0:T(8,128)(2,1)S(1)}, u32[]{:S(2)}, u32[]{:S(2)}) collective-permute-start(bf16[16,64,512]{2,1,0:T(8,128)(2,1)S(1)} %bitcast.165), channel_id=1, source_target_pairs={{0,1},{1,0},{2,3},{3,2},{4,5},{5,4},{6,7},{7,6},{8,9},{9,8},{10,11... | collective-permute-start | bytes 3145736 | tf_op jit(solution)/shard_map/ppermute | solution.py:58
  126.7 14.4 %collective-permute-start.27 = (bf16[2,4,64,512]{3,2,1,0:T(8,128)(2,1)S(1)}, bf16[2,4,64,512]{3,2,1,0:T(8,128)(2,1)S(1)}, u32[]{:S(2)}, u32[]{:S(2)}) collective-permute-start(bf16[2,4,64,512]{3,2,1,0:T(8,128)(2,1)S(1)} %pad_maximum_fusion.8), channel_id=1, source_target_pairs={{0,2},{1,3},{2,0},{3,1},{4,6},{5,7},{6,4},{7,5},{8,10},{9,11},{10,... | collective-permute-start | bytes 1572872 | tf_op jit(solution)/shard_map/ppermute | solution.py:58
  127.0 14.2 %collective-permute-start.24 = (bf16[128,1152]{1,0:T(8,128)(2,1)}, bf16[128,1152]{1,0:T(8,128)(2,1)S(1)}, u32[]{:S(2)}, u32[]{:S(2)}) collective-permute-start(bf16[128,1152]{1,0:T(8,128)(2,1)} %get-tuple-element.408), channel_id=1, source_target_pairs={{0,4},{4,0},{8,12},{12,8},{1,5},{5,1},{9,13},{13,9},{2,6},{6,2},{1... | collective-permute-start | bytes 884744 | tf_op jit(solution)/shard_map/ppermute | solution.py:58
  128.5 12.7 %collective-permute-start.25 = (bf16[128,1152]{1,0:T(8,128)(2,1)}, bf16[128,1152]{1,0:T(8,128)(2,1)}, u32[]{:S(2)}, u32[]{:S(2)}) collective-permute-start(bf16[128,1152]{1,0:T(8,128)(2,1)} %get-tuple-element.409), channel_id=1, source_target_pairs={{0,8},{4,12},{8,0},{12,4},{1,9},{5,13},{9,1},{13,5},{2,10},{6,14},... | collective-permute-start | bytes 884744 | tf_op jit(solution)/shard_map/ppermute | solution.py:58
  130.1 13.9 %collective-permute-start.26 = (bf16[128,1152]{1,0:T(8,128)(2,1)}, bf16[128,1152]{1,0:T(8,128)(2,1)}, u32[]{:S(2)}, u32[]{:S(2)}) collective-permute-start(bf16[128,1152]{1,0:T(8,128)(2,1)} %get-tuple-element.410), channel_id=1, source_target_pairs={{0,12},{4,8},{8,4},{12,0},{1,13},{5,9},{9,5},{13,1},{2,14},{6,10},... | collective-permute-start | bytes 884744 | tf_op jit(solution)/shard_map/ppermute | solution.py:58
  144.1 3.6 %collective-permute-start.30 = (bf16[16,64,512]{2,1,0:T(8,128)(2,1)S(1)}, bf16[16,64,512]{2,1,0:T(8,128)(2,1)}, u32[]{:S(2)}, u32[]{:S(2)}) collective-permute-start(bf16[16,64,512]{2,1,0:T(8,128)(2,1)S(1)} %bitcast.168), channel_id=1, source_target_pairs={{0,1},{1,0},{2,3},{3,2},{4,5},{5,4},{6,7},{7,6},{8,9},{9,8},{10,11... | collective-permute-start | bytes 3145736 | tf_op jit(solution)/shard_map/ppermute | solution.py:58
  144.2 12.5 %collective-permute-start.28 = (bf16[128,1152]{1,0:T(8,128)(2,1)}, bf16[128,1152]{1,0:T(8,128)(2,1)}, u32[]{:S(2)}, u32[]{:S(2)}) collective-permute-start(bf16[128,1152]{1,0:T(8,128)(2,1)} %get-tuple-element.413), channel_id=1, source_target_pairs={{0,4},{4,0},{8,12},{12,8},{1,5},{5,1},{9,13},{13,9},{2,6},{6,2},{1... | collective-permute-start | bytes 884744 | tf_op jit(solution)/shard_map/ppermute | solution.py:58
  145.8 14.5 %collective-permute-start.31 = (bf16[128,1152]{1,0:T(8,128)(2,1)S(1)}, bf16[128,1152]{1,0:T(8,128)(2,1)}, u32[]{:S(2)}, u32[]{:S(2)}) collective-permute-start(bf16[128,1152]{1,0:T(8,128)(2,1)S(1)} %copy-done.18), channel_id=1, source_target_pairs={{0,8},{4,12},{8,0},{12,4},{1,9},{5,13},{9,1},{13,5},{2,10},{6,14},... | collective-permute-start | bytes 884744 | tf_op jit(solution)/shard_map/ppermute | solution.py:58
  147.3 14.7 %collective-permute-start.32 = (bf16[128,1152]{1,0:T(8,128)(2,1)S(1)}, bf16[128,1152]{1,0:T(8,128)(2,1)}, u32[]{:S(2)}, u32[]{:S(2)}) collective-permute-start(bf16[128,1152]{1,0:T(8,128)(2,1)S(1)} %copy-done.17), channel_id=1, source_target_pairs={{0,12},{4,8},{8,4},{12,0},{1,13},{5,9},{9,5},{13,1},{2,14},{6,10},... | collective-permute-start | bytes 884744 | tf_op jit(solution)/shard_map/ppermute | solution.py:58
  156.7 15.3 %collective-permute-start.33 = (bf16[128,1152]{1,0:T(8,128)(2,1)}, bf16[128,1152]{1,0:T(8,128)(2,1)S(1)}, u32[]{:S(2)}, u32[]{:S(2)}) collective-permute-start(bf16[128,1152]{1,0:T(8,128)(2,1)} %get-tuple-element.433.refs_1_), channel_id=1, source_target_pairs={{0,4},{4,0},{8,12},{12,8},{1,5},{5,1},{9,13},{13,9},{2,6},{6,2},{1... | collective-permute-start | bytes 884744 | tf_op jit(solution)/shard_map/ppermute | solution.py:58
  158.2 13.8 %collective-permute-start.34 = (bf16[128,1152]{1,0:T(8,128)(2,1)}, bf16[128,1152]{1,0:T(8,128)(2,1)S(1)}, u32[]{:S(2)}, u32[]{:S(2)}) collective-permute-start(bf16[128,1152]{1,0:T(8,128)(2,1)} %get-tuple-element.433.refs_1_), channel_id=1, source_target_pairs={{0,8},{4,12},{8,0},{12,4},{1,9},{5,13},{9,1},{13,5},{2,10},{6,14},... | collective-permute-start | bytes 884744 | tf_op jit(solution)/shard_map/ppermute | solution.py:58
  159.8 14.0 %collective-permute-start.35 = (bf16[128,1152]{1,0:T(8,128)(2,1)}, bf16[128,1152]{1,0:T(8,128)(2,1)S(1)}, u32[]{:S(2)}, u32[]{:S(2)}) collective-permute-start(bf16[128,1152]{1,0:T(8,128)(2,1)} %get-tuple-element.433.refs_1_), channel_id=1, source_target_pairs={{0,12},{4,8},{8,4},{12,0},{1,13},{5,9},{9,5},{13,1},{2,14},{6,10},... | collective-permute-start | bytes 884744 | tf_op jit(solution)/shard_map/ppermute | solution.py:58
  173.8 14.1 %collective-permute-start.39 = (bf16[16,128,512]{2,1,0:T(8,128)(2,1)}, bf16[16,128,512]{2,1,0:T(8,128)(2,1)}, u32[]{:S(2)}, u32[]{:S(2)}) collective-permute-start(bf16[16,128,512]{2,1,0:T(8,128)(2,1)} %get-tuple-element.445), channel_id=1, source_target_pairs={{0,1},{1,0},{2,3},{3,2},{4,5},{5,4},{6,7},{7,6},{8,9},{9,8},{10,11... | collective-permute-start | bytes 6291464 | tf_op jit(solution)/shard_map/ppermute | solution.py:58
  173.8 19.5 %collective-permute-start.36 = (bf16[128,1152]{1,0:T(8,128)(2,1)}, bf16[128,1152]{1,0:T(8,128)(2,1)S(1)}, u32[]{:S(2)}, u32[]{:S(2)}) collective-permute-start(bf16[128,1152]{1,0:T(8,128)(2,1)} %get-tuple-element.446.refs_1_), channel_id=1, source_target_pairs={{0,4},{4,0},{8,12},{12,8},{1,5},{5,1},{9,13},{13,9},{2,6},{6,2},{1... | collective-permute-start | bytes 884744 | tf_op jit(solution)/shard_map/ppermute | solution.py:58
  175.3 18.1 %collective-permute-start.37 = (bf16[128,1152]{1,0:T(8,128)(2,1)}, bf16[128,1152]{1,0:T(8,128)(2,1)S(1)}, u32[]{:S(2)}, u32[]{:S(2)}) collective-permute-start(bf16[128,1152]{1,0:T(8,128)(2,1)} %get-tuple-element.446.refs_1_), channel_id=1, source_target_pairs={{0,8},{4,12},{8,0},{12,4},{1,9},{5,13},{9,1},{13,5},{2,10},{6,14},... | collective-permute-start | bytes 884744 | tf_op jit(solution)/shard_map/ppermute | solution.py:58
  176.9 16.5 %collective-permute-start.38 = (bf16[128,1152]{1,0:T(8,128)(2,1)}, bf16[128,1152]{1,0:T(8,128)(2,1)S(1)}, u32[]{:S(2)}, u32[]{:S(2)}) collective-permute-start(bf16[128,1152]{1,0:T(8,128)(2,1)} %get-tuple-element.446.refs_1_), channel_id=1, source_target_pairs={{0,12},{4,8},{8,4},{12,0},{1,13},{5,9},{9,5},{13,1},{2,14},{6,10},... | collective-permute-start | bytes 884744 | tf_op jit(solution)/shard_map/ppermute | solution.py:58
  187.8 19.7 %collective-permute-start.40 = (bf16[2,128,512]{2,1,0:T(8,128)(2,1)}, bf16[2,128,512]{2,1,0:T(8,128)(2,1)S(1)}, u32[]{:S(2)}, u32[]{:S(2)}) collective-permute-start(bf16[2,128,512]{2,1,0:T(8,128)(2,1)} %get-tuple-element.459), channel_id=1, source_target_pairs={{0,1},{1,0},{2,3},{3,2},{4,5},{5,4},{6,7},{7,6},{8,9},{9,8},{10,11... | collective-permute-start | bytes 786440 | tf_op jit(solution)/shard_map/ppermute | solution.py:58
  187.9 19.6 %collective-permute-start.41 = (bf16[2,128,512]{2,1,0:T(8,128)(2,1)}, bf16[2,128,512]{2,1,0:T(8,128)(2,1)S(1)}, u32[]{:S(2)}, u32[]{:S(2)}) collective-permute-start(bf16[2,128,512]{2,1,0:T(8,128)(2,1)} %get-tuple-element.460), channel_id=1, source_target_pairs={{0,2},{1,3},{2,0},{3,1},{4,6},{5,7},{6,4},{7,5},{8,10},{9,11},{10,... | collective-permute-start | bytes 786440 | tf_op jit(solution)/shard_map/ppermute | solution.py:58
  193.3 14.2 %collective-permute-start.42 = (bf16[2,128,512]{2,1,0:T(8,128)(2,1)}, bf16[2,128,512]{2,1,0:T(8,128)(2,1)}, u32[]{:S(2)}, u32[]{:S(2)}) collective-permute-start(bf16[2,128,512]{2,1,0:T(8,128)(2,1)} %get-tuple-element.461), channel_id=1, source_target_pairs={{0,3},{1,2},{2,1},{3,0},{4,7},{5,6},{6,5},{7,4},{8,11},{9,10},{10,... | collective-permute-start | bytes 786440 | tf_op jit(solution)/shard_map/ppermute | solution.py:58
  205.3 2.1 collective-permute-start.43
  205.8 9.4 %collective-permute-start.44 = (bf16[2,128,512]{2,1,0:T(8,128)(2,1)}, bf16[2,128,512]{2,1,0:T(8,128)(2,1)S(1)}, u32[]{:S(2)}, u32[]{:S(2)}) collective-permute-start(bf16[2,128,512]{2,1,0:T(8,128)(2,1)} %get-tuple-element.464), channel_id=1, source_target_pairs={{0,2},{1,3},{2,0},{3,1},{4,6},{5,7},{6,4},{7,5},{8,10},{9,11},{10,... | collective-permute-start | bytes 786440 | tf_op jit(solution)/shard_map/ppermute | solution.py:58
  207.5 11.8 %collective-permute-start.45 = (bf16[2,128,512]{2,1,0:T(8,128)(2,1)}, bf16[2,128,512]{2,1,0:T(8,128)(2,1)S(1)}, u32[]{:S(2)}, u32[]{:S(2)}) collective-permute-start(bf16[2,128,512]{2,1,0:T(8,128)(2,1)} %get-tuple-element.465), channel_id=1, source_target_pairs={{0,3},{1,2},{2,1},{3,0},{4,7},{5,6},{6,5},{7,4},{8,11},{9,10},{10,... | collective-permute-start | bytes 786440 | tf_op jit(solution)/shard_map/ppermute | solution.py:58
  220.0 31.0 %collective-permute-start.47 = (bf16[2,4,128,512]{3,2,1,0:T(8,128)(2,1)}, bf16[2,4,128,512]{3,2,1,0:T(8,128)(2,1)S(1)}, u32[]{:S(2)}, u32[]{:S(2)}) collective-permute-start(bf16[2,4,128,512]{3,2,1,0:T(8,128)(2,1)} %fusion.2), channel_id=1, source_target_pairs={{0,2},{1,3},{2,0},{3,1},{4,6},{5,7},{6,4},{7,5},{8,10},{9,11},{10,... | collective-permute-start | bytes 3145736 | tf_op jit(solution)/shard_map/ppermute | solution.py:58
  221.6 29.4 %collective-permute-start.46 = (bf16[16,16,640]{2,1,0:T(8,128)(2,1)}, bf16[16,16,640]{2,1,0:T(8,128)(2,1)S(1)}, u32[]{:S(2)}, u32[]{:S(2)}) collective-permute-start(bf16[16,16,640]{2,1,0:T(8,128)(2,1)} %get-tuple-element.489), channel_id=1, source_target_pairs={{0,1},{1,0},{2,3},{3,2},{4,5},{5,4},{6,7},{7,6},{8,9},{9,8},{10,11... | collective-permute-start | bytes 983048 | tf_op jit(solution)/shard_map/ppermute | solution.py:58
  251.9 32.2 %collective-permute-start.51 = (bf16[4,128,512]{2,1,0:T(8,128)(2,1)S(1)}, bf16[4,128,512]{2,1,0:T(8,128)(2,1)S(1)}, u32[]{:S(2)}, u32[]{:S(2)}) collective-permute-start(bf16[4,128,512]{2,1,0:T(8,128)(2,1)S(1)} %fusion.3), channel_id=1, source_target_pairs={{0,16},{16,0},{1,17},{17,1},{2,18},{18,2},{3,19},{19,3},{4,20},{20... | collective-permute-start | bytes 1572872 | tf_op jit(solution)/shard_map/ppermute | solution.py:58
  252.2 31.9 %collective-permute-start.48 = (bf16[1,256,512]{2,1,0:T(8,128)(2,1)}, bf16[1,256,512]{2,1,0:T(8,128)(2,1)S(1)}, u32[]{:S(2)}, u32[]{:S(2)}) collective-permute-start(bf16[1,256,512]{2,1,0:T(8,128)(2,1)} %get-tuple-element.507), channel_id=1, source_target_pairs={{0,1},{1,0},{2,3},{3,2},{4,5},{5,4},{6,7},{7,6},{8,9},{9,8},{10,11... | collective-permute-start | bytes 786440 | tf_op jit(solution)/shard_map/ppermute | solution.py:58
  252.3 31.8 %collective-permute-start.49 = (bf16[1,256,512]{2,1,0:T(8,128)(2,1)}, bf16[1,256,512]{2,1,0:T(8,128)(2,1)}, u32[]{:S(2)}, u32[]{:S(2)}) collective-permute-start(bf16[1,256,512]{2,1,0:T(8,128)(2,1)} %get-tuple-element.508), channel_id=1, source_target_pairs={{0,2},{1,3},{2,0},{3,1},{4,6},{5,7},{6,4},{7,5},{8,10},{9,11},{10,... | collective-permute-start | bytes 786440 | tf_op jit(solution)/shard_map/ppermute | solution.py:58
  253.0 31.1 %collective-permute-start.50 = (bf16[1,256,512]{2,1,0:T(8,128)(2,1)}, bf16[1,256,512]{2,1,0:T(8,128)(2,1)}, u32[]{:S(2)}, u32[]{:S(2)}) collective-permute-start(bf16[1,256,512]{2,1,0:T(8,128)(2,1)} %get-tuple-element.509), channel_id=1, source_target_pairs={{0,3},{1,2},{2,1},{3,0},{4,7},{5,6},{6,5},{7,4},{8,11},{9,10},{10,... | collective-permute-start | bytes 786440 | tf_op jit(solution)/shard_map/ppermute | solution.py:58
  285.0 10.0 %collective-permute-start.54 = (bf16[16,16,1536]{2,1,0:T(8,128)(2,1)}, bf16[16,16,1536]{2,1,0:T(8,128)(2,1)S(1)}, u32[]{:S(2)}, u32[]{:S(2)}) collective-permute-start(bf16[16,16,1536]{2,1,0:T(8,128)(2,1)} %get-tuple-element.520), channel_id=1, source_target_pairs={{0,1},{1,0},{2,3},{3,2},{4,5},{5,4},{6,7},{7,6},{8,9},{9,8},{10,11... | collective-permute-start | bytes 2359304 | tf_op jit(solution)/shard_map/ppermute | solution.py:58
  285.3 2.5 collective-permute-start.52
  285.5 8.8 %collective-permute-start.53 = (bf16[1,256,512]{2,1,0:T(8,128)(2,1)}, bf16[1,256,512]{2,1,0:T(8,128)(2,1)S(1)}, u32[]{:S(2)}, u32[]{:S(2)}) collective-permute-start(bf16[1,256,512]{2,1,0:T(8,128)(2,1)} %get-tuple-element.518), channel_id=1, source_target_pairs={{0,2},{1,3},{2,0},{3,1},{4,6},{5,7},{6,4},{7,5},{8,10},{9,11},{10,... | collective-permute-start | bytes 786440 | tf_op jit(solution)/shard_map/ppermute | solution.py:58
  295.5 11.5 %collective-permute-start.56 = (bf16[2,2,16,2176]{3,2,1,0:T(8,128)(2,1)S(1)}, bf16[2,2,16,2176]{3,2,1,0:T(8,128)(2,1)S(1)}, u32[]{:S(2)}, u32[]{:S(2)}) collective-permute-start(bf16[2,2,16,2176]{3,2,1,0:T(8,128)(2,1)S(1)} %get-tuple-element.611), channel_id=1, source_target_pairs={{0,4},{4,0},{8,12},{12,8},{1,5},{5,1},{9,13},{13,9},{2,6},{6,2},{1... | collective-permute-start | bytes 835592 | tf_op jit(solution)/shard_map/ppermute | solution.py:199
  297.1 9.8 %collective-permute-start.57 = (bf16[2,2,16,2176]{3,2,1,0:T(8,128)(2,1)S(1)}, bf16[2,2,16,2176]{3,2,1,0:T(8,128)(2,1)S(1)}, u32[]{:S(2)}, u32[]{:S(2)}) collective-permute-start(bf16[2,2,16,2176]{3,2,1,0:T(8,128)(2,1)S(1)} %get-tuple-element.612), channel_id=1, source_target_pairs={{0,8},{4,12},{8,0},{12,4},{1,9},{5,13},{9,1},{13,5},{2,10},{6,14},... | collective-permute-start | bytes 835592 | tf_op jit(solution)/shard_map/ppermute | solution.py:199
  298.6 12.1 %collective-permute-start.58 = (bf16[2,2,16,2176]{3,2,1,0:T(8,128)(2,1)S(1)}, bf16[2,2,16,2176]{3,2,1,0:T(8,128)(2,1)S(1)}, u32[]{:S(2)}, u32[]{:S(2)}) collective-permute-start(bf16[2,2,16,2176]{3,2,1,0:T(8,128)(2,1)S(1)} %get-tuple-element.610), channel_id=1, source_target_pairs={{0,12},{4,8},{8,4},{12,0},{1,13},{5,9},{9,5},{13,1},{2,14},{6,10},... | collective-permute-start | bytes 835592 | tf_op jit(solution)/shard_map/ppermute | solution.py:199
  299.0 7.9 %collective-permute-start.55 = (bf16[1,256,512]{2,1,0:T(8,128)(2,1)S(1)}, bf16[1,256,512]{2,1,0:T(8,128)(2,1)S(1)}, u32[]{:S(2)}, u32[]{:S(2)}) collective-permute-start(bf16[1,256,512]{2,1,0:T(8,128)(2,1)S(1)} %copy-done.37), channel_id=1, source_target_pairs={{0,3},{1,2},{2,1},{3,0},{4,7},{5,6},{6,5},{7,4},{8,11},{9,10},{10,... | collective-permute-start | bytes 786440 | tf_op jit(solution)/shard_map/ppermute | solution.py:58
  310.9 13.8 %collective-permute-start.62 = (bf16[16,2176]{1,0:T(8,128)(2,1)S(1)}, bf16[16,2176]{1,0:T(8,128)(2,1)S(1)}, u32[]{:S(2)}, u32[]{:S(2)}) collective-permute-start(bf16[16,2176]{1,0:T(8,128)(2,1)S(1)} %get-tuple-element.644), channel_id=1, source_target_pairs={{0,2},{1,3},{2,0},{3,1},{16,18},{17,19},{18,16},{19,17},{4,6},{5,7... | collective-permute-start | bytes 208904 | tf_op jit(solution)/shard_map/ppermute | solution.py:199
  311.7 14.5 %collective-permute-start.63 = (bf16[16,2176]{1,0:T(8,128)(2,1)S(1)}, bf16[16,2176]{1,0:T(8,128)(2,1)S(1)}, u32[]{:S(2)}, u32[]{:S(2)}) collective-permute-start(bf16[16,2176]{1,0:T(8,128)(2,1)S(1)} %get-tuple-element.643), channel_id=1, source_target_pairs={{0,16},{1,17},{2,18},{3,19},{16,0},{17,1},{18,2},{19,3},{4,20},{5,... | collective-permute-start | bytes 208904 | tf_op jit(solution)/shard_map/ppermute | solution.py:199
  314.2 16.7 %collective-permute-start.59 = (bf16[128,512]{1,0:T(8,128)(2,1)S(1)}, bf16[128,512]{1,0:T(8,128)(2,1)S(1)}, u32[]{:S(2)}, u32[]{:S(2)}) collective-permute-start(bf16[128,512]{1,0:T(8,128)(2,1)S(1)} %get-tuple-element.631), channel_id=1, source_target_pairs={{0,4},{4,0},{8,12},{12,8},{1,5},{5,1},{9,13},{13,9},{2,6},{6,2},{1... | collective-permute-start | bytes 393224 | tf_op jit(solution)/shard_map/ppermute | solution.py:58
  315.8 15.1 %collective-permute-start.60 = (bf16[128,512]{1,0:T(8,128)(2,1)S(1)}, bf16[128,512]{1,0:T(8,128)(2,1)S(1)}, u32[]{:S(2)}, u32[]{:S(2)}) collective-permute-start(bf16[128,512]{1,0:T(8,128)(2,1)S(1)} %get-tuple-element.630), channel_id=1, source_target_pairs={{0,8},{4,12},{8,0},{12,4},{1,9},{5,13},{9,1},{13,5},{2,10},{6,14},... | collective-permute-start | bytes 393224 | tf_op jit(solution)/shard_map/ppermute | solution.py:58
  317.4 13.5 %collective-permute-start.61 = (bf16[128,512]{1,0:T(8,128)(2,1)S(1)}, bf16[128,512]{1,0:T(8,128)(2,1)S(1)}, u32[]{:S(2)}, u32[]{:S(2)}) collective-permute-start(bf16[128,512]{1,0:T(8,128)(2,1)S(1)} %get-tuple-element.629), channel_id=1, source_target_pairs={{0,12},{4,8},{8,4},{12,0},{1,13},{5,9},{9,5},{13,1},{2,14},{6,10},... | collective-permute-start | bytes 393224 | tf_op jit(solution)/shard_map/ppermute | solution.py:58
  324.7 6.2 %collective-permute-start.64 = (bf16[16,2176]{1,0:T(8,128)(2,1)S(1)}, bf16[16,2176]{1,0:T(8,128)(2,1)S(1)}, u32[]{:S(2)}, u32[]{:S(2)}) collective-permute-start(bf16[16,2176]{1,0:T(8,128)(2,1)S(1)} %get-tuple-element.642), channel_id=1, source_target_pairs={{0,18},{1,19},{2,16},{3,17},{16,2},{17,3},{18,0},{19,1},{4,22},{5,... | collective-permute-start | bytes 208904 | tf_op jit(solution)/shard_map/ppermute | solution.py:199
  (46 other events, 273.3 us)

commit v4 on v3

--- a/solution.py
+++ b/solution.py
@@ -14,7 +14,6 @@
 BLOCK = 256
 LANES = 128
 MARKS = 16
-VMEM_LIMIT = 60 * 1024 * 1024
 
 LOG2E = math.log2(math.e)
 LN2 = math.log(2.0)
@@ -167,7 +166,7 @@
         self.exchange()
         self.combine()
 
-    def at_once(self, axes):
+    def cut(self, axes):
         bits = [bit for bit in self.left if bit[0] in axes]
         self.order = [bit for bit in self.order if bit not in bits]
         depth = self.left.index(bits[0])
@@ -176,28 +175,33 @@
         self.left = [bit for bit in self.left if bit not in bits]
         shape = self.value.shape
         value = self.value.reshape(shape[:depth] + (2 ** len(bits),) + shape[depth + len(bits) :])
-        place, names = 0, []
+        place = 0
         for axis, size, mask in bits:
             place = 2 * place + ((lax.axis_index(axis) & mask) != 0).astype(jnp.int32)
-            if axis not in names:
-                names.append(axis)
-        total = [lax.dynamic_index_in_dim(value, place, depth, keepdims=False)]
-        sizes = [size for axis, size in self.sizes if axis in names]
+        parts = [
+            lax.dynamic_index_in_dim(value, place ^ j, depth, keepdims=False)
+            for j in range(2 ** len(bits))
+        ]
+        self.value = [parts[0]] + [part.astype(bf16) for part in parts[1:]]
+        self.link = bits
+
+    def send(self):
+        bits = self.link
+        sizes = [(axis, size) for axis, size in self.sizes if axis in [bit[0] for bit in bits]]
+        names = tuple(axis for axis, _ in sizes)
         for j in range(1, 2 ** len(bits)):
-            piece = lax.dynamic_index_in_dim(value, place ^ j, depth, keepdims=False)
             masks = {axis: 0 for axis in names}
             for i, (axis, _, mask) in enumerate(bits):
                 if j >> (len(bits) - 1 - i) & 1:
                     masks[axis] |= mask
             pairs = []
-            for source in range(math.prod(sizes)):
+            for source in range(math.prod(size for _, size in sizes)):
                 target, rest, unit = 0, source, 1
-                for axis, size in reversed(list(zip(names, sizes))):
+                for axis, size in reversed(sizes):
                     target += ((rest % size) ^ masks[axis]) * unit
                     rest, unit = rest // size, unit * size
                 pairs.append((source, target))
-            total.append(lax.ppermute(piece.astype(bf16), tuple(names), pairs))
-        self.value = total
+            self.value[j] = lax.ppermute(self.value[j], names, pairs)
 
 
 hold = lax.optimization_barrier
@@ -210,7 +214,12 @@
     return values
 
 
-def call(kernel, name, grid, in_specs, outs, scratch, args, micros, aliases=None):
+def call(kernel, name, grid, in_specs, outs, scratch, args, micros, aliases=None, room=10):
+    def full(shape):
+        return pl.BlockSpec(shape, lambda *_: (0,) * len(shape))
+
+    in_specs = [spec or full(arg.shape) for spec, arg in zip(in_specs, args[1:], strict=True)]
+    outs = [(spec or full(shape), shape, dtype) for spec, shape, dtype in outs]
     return pl.pallas_call(
         kernel,
         grid_spec=pltpu.PrefetchScalarGridSpec(
@@ -222,7 +231,7 @@
         ),
         out_shape=[jax.ShapeDtypeStruct(shape, dtype) for _, shape, dtype in outs],
         input_output_aliases=aliases or {},
-        compiler_params=pltpu.CompilerParams(vmem_limit_bytes=VMEM_LIMIT),
+        compiler_params=pltpu.CompilerParams(vmem_limit_bytes=room << 20),
         cost_estimate=pl.CostEstimate(
             flops=int(micros * 1e9), bytes_accessed=1 << 20, transcendentals=0
         ),
@@ -425,6 +434,7 @@
         (me, *x_slots, weights, weights, *old),
         12,
         {3 + slots + i: i for i in range(len(old))},
+        room=26,
     )
     return result
 
@@ -448,6 +458,7 @@
         attend_scratch(length, piece, parts),
         (me, segment_rows, q_t, k, v_t),
         28 / parts,
+        room=16,
     )
     return result[:slots], result[slots:]
 
@@ -635,18 +646,18 @@
             *([before] if row else []),
         ),
         28,
+        room=60,
     )
     return result[:slot_count], result[slot_count:]
 
 
-def middle_of(att_refs, inputs_ref, w_out, me):
-    rows, piece, width = att_refs[0].shape
-    attended = jnp.concatenate([ref[...] for ref in att_refs], axis=0)
-    attended = attended.reshape(-1, width)
-    origin = jnp.concatenate(
-        [inputs_ref[pl.ds((me ^ j) * rows, rows)] for j in range(len(att_refs))], axis=0
-    ).reshape(-1, width)
-    return attended, origin.astype(f32) + dot(attended, w_out)
+def tokens_of(refs, span):
+    return jnp.concatenate([ref[:, span] for ref in refs], axis=0).reshape(-1, refs[0].shape[-1])
+
+
+def rows_of(ref, me, rows, slot_count, span):
+    parts = [ref[pl.ds((me ^ j) * rows, rows), span] for j in range(slot_count)]
+    return jnp.concatenate(parts, axis=0).reshape(-1, ref.shape[-1])
 
 
 def diagonal(piece):
@@ -655,73 +666,62 @@
     return place == lane % piece, lane // piece, lane
 
 
-def mix_kernel(slot_count, experts, *refs):
+def mix_kernel(slot_count, experts, piece, *refs):
     me_ref = refs[0]
     att_refs = refs[1 : 1 + slot_count]
     inputs_ref, cot_ref, w_out_ref, gain_ref, control_ref = refs[1 + slot_count : 6 + slot_count]
-    rest = refs[6 + slot_count :]
-    pay_refs = rest[:experts]
-    second_ref, middle_ref = rest[experts:]
-    rows, piece, width = att_refs[0].shape
+    pay_refs = refs[6 + slot_count :]
+    rows, positions, width = att_refs[0].shape
     tokens = rows * slot_count
     me = me_ref[0]
-    _, middle = middle_of(att_refs, inputs_ref, w_out_ref[...], me)
-    normed, _ = normalize(middle)
-    second = (normed * gain_ref[...]).astype(bf16)
-    second_ref[...] = second.reshape(tokens, piece, width)
-    middle_ref[...] = middle.reshape(tokens, piece, width)
-    grad = jnp.concatenate(
-        [cot_ref[pl.ds((me ^ j) * rows, rows)] for j in range(slot_count)], axis=0
-    ).reshape(-1, width)
-    logits = dot(second, control_ref[...], NT).reshape(tokens, piece, LANES)
-    top = jnp.max(logits, axis=0)
-    weights = jnp.exp(logits - top)
-    total = jnp.sum(weights, axis=0)
-    log_total = top + jnp.log(total)
     own, _, lane = diagonal(piece)
-    weights = jnp.where(own, weights * (1.0 / total), 0.0)
-    spread_out = weights.reshape(-1, LANES).astype(bf16)
-    mixed = dot(spread_out, second, TN).astype(bf16)
-    grad_results = dot(spread_out, grad, TN).astype(bf16)
-    a, b, c = split3(log_total)
-    for e in range(experts):
-        mine = slice(e * piece, (e + 1) * piece)
-        first = slice(e * piece, e * piece + 1)
-        stats = jnp.where(lane == 0, a[:, first], jnp.where(lane == 1, b[:, first], c[:, first]))
-        pay_refs[e][:, :width] = mixed[mine]
-        pay_refs[e][:, width : 2 * width] = grad_results[mine]
-        pay_refs[e][:, 2 * width :] = stats.astype(bf16)
+    w_out = w_out_ref[...]
+    for sub in range(positions // piece):
+        span = slice(sub * piece, (sub + 1) * piece)
+        added = dot(tokens_of(att_refs, span), w_out)
+        second = []
+        for token in range(tokens):
+            row = (me ^ (token // rows)) * rows + token % rows
+            middle = inputs_ref[row, span].astype(f32) + added[token * piece : (token + 1) * piece]
+            normed, _ = normalize(middle)
+            second.append((normed * gain_ref[...]).astype(bf16))
+        second = jnp.concatenate(second, axis=0)
+        grad = rows_of(cot_ref, me, rows, slot_count, span)
+        logits = dot(second, control_ref[...], NT).reshape(tokens, piece, LANES)
+        top = jnp.max(logits, axis=0)
+        weights = jnp.exp(logits - top)
+        total = jnp.sum(weights, axis=0)
+        log_total = top + jnp.log(total)
+        weights = jnp.where(own, weights * (1.0 / total), 0.0)
+        spread_out = weights.reshape(-1, LANES).astype(bf16)
+        mixed = dot(spread_out, second, TN).astype(bf16)
+        grad_results = dot(spread_out, grad, TN).astype(bf16)
+        a, b, c = split3(log_total)
+        for e in range(experts):
+            mine = slice(e * piece, (e + 1) * piece)
+            first = slice(e * piece, e * piece + 1)
+            stats = jnp.where(lane == 0, a[:, first], jnp.where(lane == 1, b[:, first], c[:, first]))
+            pay_refs[e][span, :width] = mixed[mine]
+            pay_refs[e][span, width : 2 * width] = grad_results[mine]
+            pay_refs[e][span, 2 * width :] = stats.astype(bf16)
 
 
 def mix(me, part, att_slots, inputs, cotangent, w_out, gain, control, experts):
     slot_count = len(att_slots)
     rows, positions, width = att_slots[0].shape
     tokens = rows * slot_count
-    piece = LANES // experts
-    steps = positions // piece
-    span = pl.BlockSpec((tokens, piece, width), lambda b, me: (0, b, 0))
-    shifted = pl.BlockSpec((tokens, piece, width), lambda b, me: (0, part * steps + b, 0))
-    pay = (
-        pl.BlockSpec((piece, 2 * width + LANES), lambda b, me: (b, 0)),
-        (positions, 2 * width + LANES),
-        bf16,
-    )
-    result = call(
-        functools.partial(mix_kernel, slot_count, experts),
+    half = pl.BlockSpec((tokens, positions, width), lambda b, me: (0, part, 0))
+    pay = (None, (positions, 2 * width + LANES), bf16)
+    return call(
+        functools.partial(mix_kernel, slot_count, experts, LANES // experts),
         "mix",
-        (steps,),
-        [pl.BlockSpec((rows, piece, width), lambda b, me: (0, b, 0))] * slot_count
-        + [shifted, shifted, fourth(width), whole(1, width), whole(LANES, width)],
-        [pay] * experts
-        + [
-            (span, (tokens, positions, width), bf16),
-            (span, (tokens, positions, width), f32),
-        ],
+        (1,),
+        [None] * slot_count + [half, half, fourth(width), None, None],
+        [pay] * experts,
         [],
         (me, *att_slots, inputs, cotangent, w_out, gain, control),
-        positions * 12 / 256,
+        positions * 8 / 256,
     )
-    return result[:experts], result[experts], result[experts + 1]
 
 
 def expert_kernel(part, parts, tiled, slot_count, *refs):
@@ -897,6 +897,7 @@
         scratch,
         (me, *pay_slots, *weights, *earlier),
         7,
+        room=18,
     )
     more = list(result[1:])
     if last and not tiled:
@@ -911,171 +912,173 @@
     return result[0], more
 
 
-def unmix_kernel(slot_count, experts, part, last, *refs):
+def unmix_kernel(slot_count, experts, piece, part, last, *refs):
     me_ref = refs[0]
     ret_refs = refs[1 : 1 + experts]
     att_refs = refs[1 + experts : 1 + experts + slot_count]
     rest = refs[1 + experts + slot_count :]
-    second_ref, middle_ref, cot_ref, w_out_ref, gain_ref, control_ref = rest[:6]
-    rest = rest[6:]
+    inputs_ref, cot_ref, w_out_ref, gain_ref, control_ref = rest[:5]
+    rest = rest[5:]
     if part:
-        old_out_ref, old_control_ref, old_gain_ref = rest[2:5]
-        rest = rest[5:]
+        old_out_ref, old_control_ref, old_gain_ref = rest[1:4]
+        rest = rest[4:]
     out_ref, grad_middle_ref = rest[:2]
     back_refs = rest[2 : 2 + slot_count]
     rest = rest[2 + slot_count :]
     if last:
-        keep_ref, send_ref, grad_out_ref, grad_control_ref, grad_gain_ref, small = rest
+        keep_ref, send_ref, middle_scratch, small = rest
     else:
-        grad_out_ref, grad_control_ref, grad_gain_ref = rest
-    rows, piece, width = att_refs[0].shape
+        grad_out_ref, grad_control_ref, grad_gain_ref, middle_scratch = rest
+    rows, positions, width = att_refs[0].shape
     tokens = rows * slot_count
     me = me_ref[0]
 
-    @pl.when(pl.program_id(0) == 0)
-    def _():
-        if part:
-            grad_out_ref[...] = old_out_ref[...]
-            grad_control_ref[...] = old_control_ref[...]
-            grad_gain_ref[...] = old_gain_ref[...]
-        else:
-            grad_out_ref[...] = jnp.zeros_like(grad_out_ref)
-            grad_control_ref[...] = jnp.zeros_like(grad_control_ref)
-            grad_gain_ref[...] = jnp.zeros_like(grad_gain_ref)
-
-    second = second_ref[...].reshape(-1, width)
-    middle = middle_ref[...].reshape(-1, width)
-    cot = jnp.concatenate(
-        [cot_ref[pl.ds((me ^ j) * rows, rows)] for j in range(slot_count)], axis=0
-    ).reshape(-1, width)
     own, group, _ = diagonal(piece)
-    log_total = jnp.zeros((piece, LANES), f32)
-    inner = jnp.zeros((piece, LANES), f32)
-    for e in range(experts):
-        stats = ret_refs[e][:, 2 * width :].astype(f32)
-        mine = group == e
-        log_total = jnp.where(mine, stats[:, 0:1] + stats[:, 1:2] + stats[:, 2:3], log_total)
-        inner = jnp.where(mine, stats[:, 3:4] + stats[:, 4:5] + stats[:, 5:6], inner)
-    results = jnp.concatenate([ref[:, :width] for ref in ret_refs], axis=0)
-    back = jnp.concatenate([ref[:, width : 2 * width] for ref in ret_refs], axis=0)
     control = control_ref[...]
-    logits = dot(second, control, NT).reshape(tokens, piece, LANES)
-    weights = jnp.where(own, jnp.exp(logits - log_total), 0.0)
-    low = weights.reshape(-1, LANES).astype(bf16)
-    output = (middle + dot(low, results).astype(bf16).astype(f32)).astype(bf16)
-    grad_weights = (dot(cot, results, NT) + dot(second, back, NT)).reshape(tokens, piece, LANES)
-    grad_logits = (weights * (grad_weights - inner)).reshape(-1, LANES).astype(bf16)
-    grad_second = dot(low, back) + dot(grad_logits, control)
-    grad_second = grad_second.astype(bf16).astype(f32)
-    grad_control_ref[...] += dot(grad_logits, second, TN)
-    normed, scaled = normalize(middle)
-    product = (grad_second * normed).reshape(-1, 8, width)
-    grad_gain_ref[...] += jnp.sum(product, axis=0)
-    grad_middle = cot.astype(f32) + norm_back(grad_second * gain_ref[...], normed, scaled)
-    grad_middle = grad_middle.astype(bf16)
-    grad_attended = dot(grad_middle, w_out_ref[...], NT).astype(bf16)
-    output = output.reshape(tokens, piece, width)
-    grad_attended = grad_attended.reshape(tokens, piece, width)
-    grad_middle_ref[...] = grad_middle.reshape(tokens, piece, width)
-    for j in range(slot_count):
-        mine = slice(j * rows, (j + 1) * rows)
-        out_ref[pl.ds((me ^ j) * rows, rows)] = output[mine]
-        back_refs[j][...] = grad_attended[mine]
-    attended = jnp.concatenate([ref[...] for ref in att_refs], axis=0).reshape(-1, width)
-    grad_out_ref[...] += dot(attended, grad_middle, TN)
-
+    w_out = w_out_ref[...]
+    grad_out, grad_control, grad_gain = 0.0, 0.0, 0.0
+    if part:
+        grad_out, grad_control = old_out_ref[...], old_control_ref[...]
+        grad_gain = old_gain_ref[...]
+    for sub in range(positions // piece):
+        span = slice(sub * piece, (sub + 1) * piece)
+        attended = tokens_of(att_refs, span)
+        added = dot(attended, w_out)
+        second = []
+        for token in range(tokens):
+            row = (me ^ (token // rows)) * rows + token % rows
+            middle = inputs_ref[row, span].astype(f32) + added[token * piece : (token + 1) * piece]
+            middle_scratch[token] = middle
+            normed, _ = normalize(middle)
+            second.append((normed * gain_ref[...]).astype(bf16))
+        second = jnp.concatenate(second, axis=0)
+        cot = rows_of(cot_ref, me, rows, slot_count, span)
+        log_total = jnp.zeros((piece, LANES), f32)
+        inner = jnp.zeros((piece, LANES), f32)
+        for e in range(experts):
+            stats = ret_refs[e][span, 2 * width :].astype(f32)
+            mine = group == e
+            log_total = jnp.where(mine, stats[:, 0:1] + stats[:, 1:2] + stats[:, 2:3], log_total)
+            inner = jnp.where(mine, stats[:, 3:4] + stats[:, 4:5] + stats[:, 5:6], inner)
+        results = jnp.concatenate([ref[span, :width] for ref in ret_refs], axis=0)
+        back = jnp.concatenate([ref[span, width : 2 * width] for ref in ret_refs], axis=0)
+        logits = dot(second, control, NT).reshape(tokens, piece, LANES)
+        weights = jnp.where(own, jnp.exp(logits - log_total), 0.0)
+        low = weights.reshape(-1, LANES).astype(bf16)
+        spread = dot(low, results)
+        grad_weights = (dot(cot, results, NT) + dot(second, back, NT)).reshape(tokens, piece, LANES)
+        grad_logits = (weights * (grad_weights - inner)).reshape(-1, LANES).astype(bf16)
+        grad_second = dot(low, back) + dot(grad_logits, control)
+        grad_control = grad_control + dot(grad_logits, second, TN)
+        grad_middles = []
+        for token in range(tokens):
+            row = (me ^ (token // rows)) * rows + token % rows
+            mine = slice(token * piece, (token + 1) * piece)
+            middle = middle_scratch[token]
+            out_ref[row, span] = (middle + spread[mine].astype(bf16).astype(f32)).astype(bf16)
+            grad = grad_second[mine].astype(bf16).astype(f32)
+            normed, scaled = normalize(middle)
+            grad_gain = grad_gain + jnp.sum((grad * normed).reshape(-1, 8, width), axis=0)
+            grad_middle = norm_back(grad * gain_ref[...], normed, scaled)
+            grad_middle = (cot_ref[row, span].astype(f32) + grad_middle).astype(bf16)
+            grad_middle_ref[token, span] = grad_middle
+            grad_middles.append(grad_middle)
+        grad_middle = jnp.concatenate(grad_middles, axis=0)
+        grad_attended = dot(grad_middle, w_out, NT).astype(bf16)
+        grad_attended = grad_attended.reshape(tokens, piece, width)
+        for j in range(slot_count):
+            back_refs[j][:, span] = grad_attended[j * rows : (j + 1) * rows]
+        grad_out = grad_out + dot(attended, grad_middle, TN)
     if last:
-
-        @pl.when(pl.program_id(0) == pl.num_programs(0) - 1)
-        def _():
-            small[...] = jnp.zeros_like(small)
-            small[0:1] = jnp.sum(grad_gain_ref[...], axis=0, keepdims=True)
-            for e in range(experts):
-                total = grad_control_ref[e * piece : (e + 1) * piece]
-                place = pl.ds(1 + (me_ref[1] ^ e), 1)
-                small[place] = jnp.sum(total, axis=0, keepdims=True)
-            blocks, lines = keep_ref.shape[:2]
-            for columns, value in (
-                (slice(0, width), grad_out_ref[...]),
-                (slice(width, width + LANES), small[...].T),
-            ):
-                keep, send = by_core(me, value.reshape(blocks, 2, lines, -1))
-                keep_ref[:, :, columns] = keep
-                send_ref[:, :, columns] = send.astype(bf16)
+        small[...] = jnp.zeros_like(small)
+        small[0:1] = jnp.sum(grad_gain, axis=0, keepdims=True)
+        for e in range(experts):
+            total = grad_control[e * piece : (e + 1) * piece]
+            small[pl.ds(1 + (me_ref[1] ^ e), 1)] = jnp.sum(total, axis=0, keepdims=True)
+        blocks, lines = keep_ref.shape[:2]
+        for columns, value in (
+            (slice(0, width), grad_out),
+            (slice(width, width + LANES), small[...].T),
+        ):
+            keep, send = by_core(me, value.reshape(blocks, 2, lines, -1))
+            keep_ref[:, :, columns] = keep
+            send_ref[:, :, columns] = send.astype(bf16)
+    else:
+        grad_control_ref[...] = grad_control
+        grad_gain_ref[...] = grad_gain
+        grad_out_ref[...] = grad_out
 
 
 def unmix(
-    me, part, last, shards, ret_slots, att_slots, second, middle, cotangent, w_out, gain, control, before
+    me, part, last, shards, ret_slots, att_slots, inputs, cotangent, w_out, gain, control, before
 ):
     slot_count, experts = len(att_slots), len(ret_slots)
     rows, positions, width = att_slots[0].shape
     tokens = rows * slot_count
-    piece = LANES // experts
-    steps = positions // piece
-    span = pl.BlockSpec((tokens, piece, width), lambda b, me: (0, b, 0))
-    shifted = pl.BlockSpec((tokens, piece, width), lambda b, me: (0, part * steps + b, 0))
-    slot = pl.BlockSpec((rows, piece, width), lambda b, me: (0, b, 0))
-    full = (shifted, cotangent.shape, bf16)
-    sums = [
-        (whole(width, width), (width, width), f32),
-        (whole(LANES, width), (LANES, width), f32),
-        (whole(8, width), (8, width), f32),
-    ]
-    count = 1 + experts + slot_count + 6
-    scratch = []
-    made = sums
+    half = pl.BlockSpec((tokens, positions, width), lambda b, me: (0, part, 0))
+    count = 1 + experts + slot_count + 5
     if last:
-        half = (shards // 2, width // shards, width + LANES)
-        made = [(whole(*half), half, f32), (whole(*half), half, bf16)]
-        scratch = [(shape, dtype) for _, shape, dtype in sums] + [((LANES, width), f32)]
+        kept = (shards // 2, width // shards, width + LANES)
+        made = [(None, kept, f32), (None, kept, bf16)]
+    else:
+        made = [
+            (None, (width, width), f32),
+            (None, (LANES, width), f32),
+            (None, (8, width), f32),
+        ]
     result = call(
-        functools.partial(unmix_kernel, slot_count, experts, part, last),
+        functools.partial(unmix_kernel, slot_count, experts, LANES // experts, part, last),
         "unmix",
-        (steps,),
-        [pl.BlockSpec((piece, 2 * width + LANES), lambda b, me: (b, 0))] * experts
-        + [slot] * slot_count
-        + [span, span, shifted, fourth(width), whole(1, width), whole(LANES, width)]
-        + ([pl.BlockSpec(memory_space=pl.ANY)] * 2 + [spec for spec, _, _ in sums] if part else []),
-        [full, full] + [(slot, (rows, positions, width), bf16)] * slot_count + made,
-        scratch,
-        (me, *ret_slots, *att_slots, second, middle, cotangent, w_out, gain, control, *before),
-        positions * 17 / 256,
-        {count: 0, count + 1: 1} if part else None,
+        (1,),
+        [None] * (experts + slot_count)
+        + [half, half, fourth(width), None, None]
+        + ([pl.BlockSpec(memory_space=pl.ANY)] + [None] * 3 if part else []),
+        [(half, cotangent.shape, bf16), (None, (tokens, positions, width), bf16)]
+        + [(None, (rows, positions, width), bf16)] * slot_count
+        + made,
+        [((tokens, LANES // experts, width), f32)] + ([((LANES, width), f32)] if last else []),
+        (me, *ret_slots, *att_slots, inputs, cotangent, w_out, gain, control, *before),
+        positions * 12 / 256,
+        {count: 0} if part else None,
+        room=10 if part else 58,
     )
     do_slots = result[2 : 2 + slot_count]
-    return do_slots, result[:2] + result[2 + slot_count :]
-
-
-def finish_kernel(slot_count, row_count, *refs):
+    return do_slots, result[1], [result[0], *result[2 + slot_count :]]
+
+
+def finish_kernel(slot_count, row_count, parts, *refs):
     me_ref = refs[0]
     gf_refs = refs[1 : 1 + slot_count * row_count]
-    inputs_ref, grad_middle_ref, gain_ref, out_ref = refs[1 + slot_count * row_count :]
+    rest = refs[1 + slot_count * row_count :]
+    inputs_ref, grad_middle_refs, (gain_ref, out_ref) = rest[0], rest[1 : 1 + parts], rest[1 + parts :]
     me = me_ref[0]
-    for j in range(slot_count):
-        for row in range(row_count):
-            place = (me ^ j) * row_count + row
-            normed, scaled = normalize(inputs_ref[place].astype(f32))
-            incoming = gf_refs[row * slot_count + j][0].astype(f32) * gain_ref[...]
-            grad = norm_back(incoming, normed, scaled)
-            grad = grad + grad_middle_ref[j * row_count + row].astype(f32)
-            out_ref[place] = grad.astype(bf16)
-
-
-def finish(me, gf_rows, inputs, grad_middle, gain):
-    slot_count, row_count = len(gf_rows[0]), len(gf_rows)
-    tokens, positions, width = inputs.shape
     piece = 64
-    span = pl.BlockSpec((tokens, piece, width), lambda b, me: (0, b, 0))
-    slot = pl.BlockSpec((1, piece, width), lambda b, me: (0, b, 0))
+    positions = out_ref.shape[1]
+    some = positions // parts
+    for start in range(0, positions, piece):
+        span = slice(start, start + piece)
+        inner = slice(start % some, start % some + piece)
+        for j in range(slot_count):
+            for row in range(row_count):
+                place = (me ^ j) * row_count + row
+                normed, scaled = normalize(inputs_ref[place, span].astype(f32))
+                incoming = gf_refs[row * slot_count + j][0, span].astype(f32) * gain_ref[...]
+                grad = norm_back(incoming, normed, scaled)
+                middle = grad_middle_refs[start // some][j * row_count + row, inner]
+                out_ref[place, span] = (grad + middle.astype(f32)).astype(bf16)
+
+
+def finish(me, gf_rows, inputs, grad_middles, gain):
+    slot_count, row_count, parts = len(gf_rows[0]), len(gf_rows), len(grad_middles)
     return call(
-        functools.partial(finish_kernel, slot_count, row_count),
+        functools.partial(finish_kernel, slot_count, row_count, parts),
         "finish",
-        (positions // piece,),
-        [slot] * (slot_count * row_count) + [span, span, whole(1, width)],
-        [(span, (tokens, positions, width), bf16)],
+        (1,),
+        [None] * (slot_count * row_count + 2 + parts),
+        [(None, inputs.shape, bf16)],
         [],
-        (me, *[gf for row in gf_rows for gf in row], inputs, grad_middle, gain),
-        6,
+        (me, *[gf for row in gf_rows for gf in row], inputs, *grad_middles, gain),
+        4,
     )[0]
 
 
@@ -1104,15 +1107,15 @@
 
     parts = 2 if positions % BLOCK == 0 else 1
 
-    def row_parts(array):
-        return [
-            lax.dynamic_slice_in_dim(array, (seq_me ^ j) * rows, rows, axis=0) for j in range(slots)
-        ]
-
     marks = segments.astype(bf16)[:, None, :]
     marks = jnp.pad(marks, ((0, 0), (0, MARKS - 1), (0, width - positions)))
-    x_parts = row_parts(jnp.concatenate([inputs, marks], axis=1))
-    x_parts = [[x[row : row + 1] for x in x_parts] for row in range(rows)]
+
+    def row_part(row, j):
+        index = (seq_me ^ j) * rows + row
+        parts = [lax.dynamic_slice_in_dim(array, index, 1, axis=0) for array in (inputs, marks)]
+        return jnp.concatenate(parts, axis=1)
+
+    x_parts = [[row_part(row, j) for j in range(slots)] for row in range(rows)]
     x_rows = [[x_parts[0][0]]]
 
     def send_some(slots_of, done, first, last):
@@ -1176,22 +1179,18 @@
         )
         att_parts.append(swap_slots(att, "seq"))
         kept.append(more)
-    pay_parts, second_parts, middle_parts = [], [], []
+    pay_parts = []
     for part in range(parts):
-        pay, second, middle = mix(
+        pay = mix(
             me, part, att_parts[part], inputs, cotangent, packed, gain_two, control, experts
         )
         if part + 1 < parts:
-            pay, second, middle, att_parts[part + 1] = together(
-                (pay, second, middle, att_parts[part + 1]), halves[1]
-            )
+            pay, att_parts[part + 1] = together((pay, att_parts[part + 1]), halves[1])
         if part == 0:
             halves[1].steps("seq")
         if part == parts - 1:
-            pay, second, middle, pay_parts = together((pay, second, middle, pay_parts), halves[1])
+            pay, pay_parts = together((pay, pay_parts), halves[1])
         pay_parts.append(swap_slots(pay, "gi"))
-        second_parts.append(second)
-        middle_parts.append(middle)
     halves = [half.value.reshape(-1, *half.value.shape[-2:]) for half in halves]
     halves = [(half, partner(half, "seq", slots, 1)) for half in halves]
     ret_parts, earlier = [], []
@@ -1212,30 +1211,30 @@
     def to_bits(keep, other):
         return (keep.astype(f32) + other.astype(f32)).reshape(*bits, *keep.shape[1:])
 
-    do_parts, before = [], []
+    do_parts, grad_middles, before = [], [], []
     for part in range(parts):
         last = part == parts - 1
         if last:
             sum_expert = Halving(to_bits(kept_grad, received), owners, ("seq", "gq"), 1)
             sum_expert.prepare()
             ret_parts[part], before = together((ret_parts[part], before), sum_expert)
-        do, before = unmix(
+        do, grad_middle, before = unmix(
             me,
             part,
             last,
             groups * members * slots,
             ret_parts[part],
             att_parts[part],
-            second_parts[part],
-            middle_parts[part],
+            inputs,
             cotangent,
             packed,
             gain_two,
             control,
             before,
         )
+        grad_middles.append(grad_middle)
         do_parts.append(swap_slots(do, "seq"))
-    output, grad_middle, keep_out, send_out = before
+    output, keep_out, send_out = before
     every_bit = [2] * len(bits_of(place))
     do_parts, send_out = together((do_parts, send_out), sum_expert)
     sum_expert.exchange()
@@ -1273,22 +1272,25 @@
     send_some(gf_slots, gf_rows[-1], 1, slots // 2 + 1)
     keep, send = grad_in
     received = partner(send, "seq", slots, 1)
-    gf_rows, gf_slots, received = hold((gf_rows, gf_slots, received))
+    sum_expert.combine()
+    sums = sum_expert.finish()
+    columns = [p if j == 0 else p.astype(bf16) for j, p in enumerate(member_parts(sums))]
+    columns = swap_slots(columns, "gi")
+    gf_rows, gf_slots, received, columns = hold((gf_rows, gf_slots, received, columns))
     send_some(gf_slots, gf_rows[-1], slots // 2 + 1, slots)
     total = keep + received.astype(f32)
     total = jnp.concatenate([total, keep_out + received_out.astype(f32)], axis=-1)
     total = total.reshape(*every_bit[1:], *total.shape[1:])
     sum_in = Halving(total, place, ("gi", "gq", "seq"))
-    sum_in.at_once(("gi",))
-    gf_rows = together(gf_rows, sum_in, sum_expert)
+    sum_in.cut(("gi",))
+    sum_in.send()
+    gf_rows = together(gf_rows, sum_in)
     sum_in.combine()
-    sum_in.at_once(("gq", "seq"))
-    sum_expert.combine()
-    sums = sum_expert.finish()
-    columns = [p if j == 0 else p.astype(bf16) for j, p in enumerate(member_parts(sums))]
-    columns = swap_slots(columns, "gi")
-    grad_inputs = finish(me, gf_rows, inputs, grad_middle, gain_one)
-    grad_inputs, columns = together((grad_inputs, columns), sum_in)
+    sum_in.cut(("gq", "seq"))
+    gf_rows = together(gf_rows, sum_in)
+    sum_in.send()
+    grad_inputs = finish(me, gf_rows, inputs, grad_middles, gain_one)
+    grad_inputs = together(grad_inputs, sum_in)
     sum_in.combine()
     columns = natural(columns, member)
     columns = jnp.stack([c.astype(f32) for c in columns])

time: 342 us -> 341 us (level)
  Pallas kernels: 168 us -> 143 us
  local copies, waits for them, and re-layouts: 14.6 us -> 27 us
  other arithmetic: 15 us -> 22 us
  waiting for transfers between devices: 77.3 us -> 82.6 us
    pallas_call x12, Pallas kernels: 168 us -> 143 us  [call(): pl.pallas_call(kernel, grid_spec=pltpu.PrefetchScalarGridSpec(num_scalar_...]
    unnamed x93 -> x143, local copies, waits for them, and re-layouts: 8.43 us -> 14.8 us
    ppermute x59, waiting for transfers between devices: 68.8 us -> 72.2 us  [partner(): return lax.ppermute(value, axis, [(i, i ^ mask) for i in range(size)])]
  transfers between devices with their start and end apart: 65 -> 65, of which waited for: 21 -> 23; matrix products, arithmetic and copies ran while one was open for 3% -> 7% of each run, Pallas kernels for 50% -> 43%
where the time goes in v4:
time: 341 us; the launch traced here: 335 us
  Pallas kernels  143 us (42%)
  waiting for transfers between devices  82.6 us (24%)
  starting transfers between devices  58.5 us (17%)
  local copies, waits for them, and re-layouts  27 us (8%)
  other arithmetic  22 us (6%)
    pallas_call x12, Pallas kernels, call(): pl.pallas_call(kernel, grid_spec=pltpu.PrefetchScalarGridSpec(num_scalar_...  143 us
    ppermute x59, waiting for transfers between devices, partner(): return lax.ppermute(value, axis, [(i, i ^ mask) for i in range(size)])  72.2 us
    ppermute x59, starting transfers between devices, partner(): return lax.ppermute(value, axis, [(i, i ^ mask) for i in range(size)])  50.4 us
    unnamed x143, local copies, waits for them, and re-layouts  14.8 us
    ppermute x6, waiting for transfers between devices, send(): self.value[j] = lax.ppermute(self.value[j], names, pairs)  10.4 us
    ppermute x6, starting transfers between devices, send(): self.value[j] = lax.ppermute(self.value[j], names, pairs)  8.16 us
  transfers between devices with their start and end apart: 65, of which 23 were waited for; matrix products, arithmetic and copies ran while one was open for 7% of the time, Pallas kernels for 43%

profile of v4, /device:TPU:0, one launch (start us, length us, event | category | flops | bytes accessed | tf_op | source)
XLA Modules:
  0.0 335.4 jit_solution(3613232196389003769)
XLA Ops:
  3.8 3.0 collective-permute-start.2
  7.6 1.7 constant_dynamic-slice_fusion
  12.6 7.5 %collective-permute-done.1.refs_3_ = bf16[1,272,512]{2,1,0:T(8,128)(2,1)S(1)} collective-permute-done((bf16[1,272,512]{2,1,0:T(8,128)(2,1)}, bf16[1,272,512]{2,1,0:T(8,128)(2,1)S(1)}, u32[]{:S(2)}, u32[]{:S(2)}) %collective-permute-start.1) | collective-permute-done | bytes 278560 | tf_op jit(solution)/shard_map/ppermute | solution.py:57
  20.1 2.6 collective-permute-start.7
  22.9 2.6 collective-permute-start.6
  26.4 3.0 collective-permute-done.7
  29.5 2.0 collective-permute-done.6
  31.5 1.9 collective-permute-done.5
  35.1 1.5 collective-permute-start.10
  36.6 1.6 collective-permute-start.9
  39.5 4.3 %collective-permute-done.10 = bf16[2,2,16,2176]{3,2,1,0:T(8,128)(2,1)S(1)} collective-permute-done((bf16[2,2,16,2176]{3,2,1,0:T(8,128)(2,1)S(1)}, bf16[2,2,16,2176]{3,2,1,0:T(8,128)(2,1)S(1)}, u32[]{:S(2)}, u32[]{:S(2)}) %collective-permute-start.10) | collective-permute-done | bytes 278560 | tf_op jit(solution)/shard_map/ppermute | solution.py:57
  43.8 2.4 collective-permute-done.9
  46.2 3.8 %collective-permute-done.8 = bf16[2,2,16,2176]{3,2,1,0:T(8,128)(2,1)S(1)} collective-permute-done((bf16[2,2,16,2176]{3,2,1,0:T(8,128)(2,1)S(1)}, bf16[2,2,16,2176]{3,2,1,0:T(8,128)(2,1)S(1)}, u32[]{:S(2)}, u32[]{:S(2)}) %collective-permute-start.8) | collective-permute-done | bytes 278560 | tf_op jit(solution)/shard_map/ppermute | solution.py:57
  50.5 2.8 collective-permute-done.11
  53.3 1.4 select_bitcast_fusion.1
  55.9 1.7 copy.126
  59.0 2.3 collective-permute-start.13
  62.4 10.3 %attend_first.2 = (bf16[2,128,512]{2,1,0:T(8,128)(2,1)S(1)}, bf16[2,128,512]{2,1,0:T(8,128)(2,1)S(1)}, bf16[2,128,512]{2,1,0:T(8,128)(2,1)S(1)}, bf16[2,128,512]...) custom-call(s32[2]{0:T(128)S(1)} %pad_add_fusion.refs_0_, ...), custom_call_target="tpu_custom_call" | custom-call | flops 12000000000 | bytes 1048576 | tf_op jit(solution)/shard_map/attend_first/pallas_call | solution.py:223
  72.7 1.5 fusion.25
  74.5 2.8 collective-permute-start.17
  77.3 1.7 collective-permute-start.16
  79.0 10.0 %attend_first.3 = (bf16[2,128,512]{2,1,0:T(8,128)(2,1)S(1)}, bf16[2,128,512]{2,1,0:T(8,128)(2,1)S(1)}, bf16[2,128,512]{2,1,0:T(8,128)(2,1)S(1)}, bf16[2,128,512]...) custom-call(s32[2]{0:T(128)S(1)} %pad_add_fusion.refs_0_, ...), custom_call_target="tpu_custom_call", output_to_operand_aliasing={{0}: (7, {}), {1}: (8, {}), {2}: (9, {}), {3}: (10, {}), {4... | custom-call | flops 12000000000 | bytes 1048576 | tf_op jit(solution)/shard_map/attend_first/pallas_call | solution.py:223
  89.1 1.4 copy-done.45
  90.5 1.3 copy-done.46
  94.3 1.5 collective-permute-start.20
  95.8 14.7 %attend_next.1 = (bf16[2,128,512]{2,1,0:T(8,128)(2,1)S(1)}, bf16[2,128,512]{2,1,0:T(8,128)(2,1)S(1)}, bf16[2,128,512]{2,1,0:T(8,128)(2,1)S(1)}, bf16[2,128,512]{...) custom-call(s32[2]{0:T(128)S(1)} %pad_add_fusion.refs_0_, ...), custom_call_target="tpu_custom_call" | custom-call | flops 14000000000 | bytes 1048576 | tf_op jit(solution)/shard_map/attend_next/pallas_call | solution.py:223
  113.4 4.3 %mix.2 = (bf16[128,1152]{1,0:T(8,128)(2,1)S(1)}, bf16[128,1152]{1,0:T(8,128)(2,1)S(1)}, bf16[128,1152]{1,0:T(8,128)(2,1)S(1)}, bf16[128,1152]{1,0:T(8,128)(2,1)S(1)}) custom-call(s32[2]{0:T(128)S(1)} %pad_add_fusion.refs_0_, bf16[2,128,512]{2,1,0:T(8,128)(2,1)S(1)} %get-tuple-element.381.refs_1_.refs_5_, ...), custom_call_target="tpu_custom_call" | custom-call | flops 4000000000 | bytes 1048576 | tf_op jit(solution)/shard_map/mix/pallas_call | solution.py:223
  117.7 3.3 collective-permute-done.22.refs_3_.refs_7_
  121.0 4.1 %collective-permute-done.23.refs_4_.refs_8_ = bf16[2,128,512]{2,1,0:T(8,128)(2,1)S(1)} collective-permute-done((bf16[2,128,512]{2,1,0:T(8,128)(2,1)S(1)}, bf16[2,128,512]{2,1,0:T(8,128)(2,1)S(1)}, u32[]{:S(2)}, u32[]{:S(2)}) %collective-permute-start.23) | collective-permute-done | bytes 262176 | tf_op jit(solution)/shard_map/ppermute | solution.py:57
  125.9 1.5 collective-permute-start.24
  127.4 1.6 collective-permute-start.25
  129.4 4.3 %mix.3 = (bf16[128,1152]{1,0:T(8,128)(2,1)S(1)}, bf16[128,1152]{1,0:T(8,128)(2,1)S(1)}, bf16[128,1152]{1,0:T(8,128)(2,1)S(1)}, bf16[128,1152]{1,0:T(8,128)(2,1)S(1)}) custom-call(s32[2]{0:T(128)S(1)} %pad_add_fusion.refs_0_, bf16[2,128,512]{2,1,0:T(8,128)(2,1)S(1)} %get-tuple-element.396.refs_1_.refs_5_, ...), custom_call_target="tpu_custom_call" | custom-call | flops 4000000000 | bytes 1048576 | tf_op jit(solution)/shard_map/mix/pallas_call | solution.py:223
  133.7 5.8 %collective-permute-done.27 = bf16[2,4,64,512]{3,2,1,0:T(8,128)(2,1)S(1)} collective-permute-done((bf16[2,4,64,512]{3,2,1,0:T(8,128)(2,1)S(1)}, bf16[2,4,64,512]{3,2,1,0:T(8,128)(2,1)S(1)}, u32[]{:S(2)}, u32[]{:S(2)}) %collective-permute-start.27) | collective-permute-done | bytes 524320 | tf_op jit(solution)/shard_map/ppermute | solution.py:57
  139.8 2.7 collective-permute-done.26.refs_4_
  142.6 1.6 collective-permute-start.28
  144.2 1.6 collective-permute-start.31
  146.2 5.0 %expert.2 = (bf16[128,1152]{1,0:T(8,128)(2,1)S(1)}, bf16[128,512]{1,0:T(8,128)(2,1)S(1)}, bf16[128,512]{1,0:T(8,128)(2,1)S(1)}, bf16[128,2048]{1,0:T(8,128)(2,1)S(1)}, bf16[128,2048]{1,0:T(8,128)(2,1)S(1)}) custom-call(s32[2]{0:T(128)S(1)} %pad_add_fusion.refs_0_, bf16[128,1152]{1,0:T(8,128)(2,1)S(1)} %get-tuple-element.411.refs_1_, ...), custom_call_target="tpu_custom_call" | custom-call | flops 7000000000 | bytes 1048576 | tf_op jit(solution)/shard_map/expert/pallas_call | solution.py:223
  152.1 2.5 collective-permute-start.35
  155.6 4.9 %collective-permute-done.32.refs_4_ = bf16[128,1152]{1,0:T(8,128)(2,1)S(1)} collective-permute-done((bf16[128,1152]{1,0:T(8,128)(2,1)S(1)}, bf16[128,1152]{1,0:T(8,128)(2,1)S(1)}, u32[]{:S(2)}, u32[]{:S(2)}) %collective-permute-start.32) | collective-permute-done | bytes 294944 | tf_op jit(solution)/shard_map/ppermute | solution.py:57
  160.4 7.6 %expert.3 = (bf16[128,1152]{1,0:T(8,128)(2,1)S(1)}, bf16[16,128,512]{2,1,0:T(8,128)(2,1)S(1)}, bf16[16,128,512]{2,1,0:T(8,128)(2,1)}) custom-call(s32[2]{0:T(128)S(1)} %pad_add_fusion.refs_0_, bf16[128,1152]{1,0:T(8,128)(2,1)S(1)} %get-tuple-element.409.refs_1_, bf16[128,1152]{1,0:T(8,128)(2,1)S(1)} %collective-permute-done.28.refs_2_, ...), custom_call_target="tpu_custom_call" | custom-call | flops 7000000000 | bytes 1048576 | tf_op jit(solution)/shard_map/expert/pallas_call | solution.py:223
  168.1 4.2 %collective-permute-done.34.refs_3_ = bf16[128,1152]{1,0:T(8,128)(2,1)S(1)} collective-permute-done((bf16[128,1152]{1,0:T(8,128)(2,1)S(1)}, bf16[128,1152]{1,0:T(8,128)(2,1)S(1)}, u32[]{:S(2)}, u32[]{:S(2)}) %collective-permute-start.34) | collective-permute-done | bytes 294944 | tf_op jit(solution)/shard_map/ppermute | solution.py:57
  173.7 1.7 collective-permute-start.38
  175.9 1.3 collective-permute-start.36
  177.2 11.8 %unmix.2 = (bf16[8,256,512]{2,1,0:T(8,128)(2,1)}, bf16[8,128,512]{2,1,0:T(8,128)(2,1)}, bf16[2,128,512]{2,1,0:T(8,128)(2,1)}, bf16[2,128,512]{2,1,0:T(8,128)(2,1...) custom-call(s32[2]{0:T(128)} %copy-done.31, ...), custom_call_target="tpu_custom_call" | custom-call | flops 6000000000 | bytes 1048576 | tf_op jit(solution)/shard_map/unmix/pallas_call | solution.py:223
  189.1 1.7 collective-permute-start.41
  190.8 2.4 convert_add_fusion
  194.4 1.6 dynamic-slice_bitcast_fusion
  197.4 8.8 %unmix.3 = (bf16[8,256,512]{2,1,0:T(8,128)(2,1)}, bf16[8,128,512]{2,1,0:T(8,128)(2,1)S(1)}, bf16[2,128,512]{2,1,0:T(8,128)(2,1)S(1)}, bf16[2,128,512]{2,1,0:T(8,...) custom-call(s32[2]{0:T(128)S(1)} %copy-done.32, ...), custom_call_target="tpu_custom_call", output_to_operand_aliasing={{0}: (14, {})} | custom-call | flops 6000000000 | bytes 1048576 | tf_op jit(solution)/shard_map/unmix/pallas_call | solution.py:223
  209.9 7.6 %collective-permute-done.44.refs_11_ = bf16[2,128,512]{2,1,0:T(8,128)(2,1)S(1)} collective-permute-done((bf16[2,128,512]{2,1,0:T(8,128)(2,1)}, bf16[2,128,512]{2,1,0:T(8,128)(2,1)S(1)}, u32[]{:S(2)}, u32[]{:S(2)}) %collective-permute-start.44) | collective-permute-done | bytes 262176 | tf_op jit(solution)/shard_map/ppermute | solution.py:57
  217.5 4.5 %collective-permute-done.45.refs_12_ = bf16[2,128,512]{2,1,0:T(8,128)(2,1)S(1)} collective-permute-done((bf16[2,128,512]{2,1,0:T(8,128)(2,1)}, bf16[2,128,512]{2,1,0:T(8,128)(2,1)S(1)}, u32[]{:S(2)}, u32[]{:S(2)}) %collective-permute-start.45) | collective-permute-done | bytes 262176 | tf_op jit(solution)/shard_map/ppermute | solution.py:57
  223.6 29.3 %attend_back.2 = (bf16[1,256,512]{2,1,0:T(8,128)(2,1)}, bf16[1,256,512]{2,1,0:T(8,128)(2,1)}, bf16[1,256,512]{2,1,0:T(8,128)(2,1)}, bf16[1,256,512]{2,1,0:T(8,128)(2,1)}, f32[512,1536]{1,0:T(8,128)}) custom-call(s32[2]{0:T(128)} %copy-done.31, bf16[1,272,512]{2,1,0:T(8,128)(2,1)} %copy-done.6, bf16[1,272,512]{2,1,0:T(8,128)(2,1)} %copy-done.15, ...), custom_call_target="tpu_custom_call" | custom-call | flops 28000000000 | bytes 1048576 | tf_op jit(solution)/shard_map/attend_back/pallas_call | solution.py:223
  253.0 1.7 convert_add_fusion.1
  254.9 1.6 collective-permute-start.49
  257.1 29.8 %attend_back.3 = (bf16[1,256,512]{2,1,0:T(8,128)(2,1)}, bf16[1,256,512]{2,1,0:T(8,128)(2,1)}, bf16[1,256,512]{2,1,0:T(8,128)(2,1)}, bf16[1,256,512]{2,1,0:T(8,12...) custom-call(s32[2]{0:T(128)} %copy-done.31, bf16[1,272,512]{2,1,0:T(8,128)(2,1)} %copy-done.5, ...), custom_call_target="tpu_custom_call" | custom-call | flops 28000000000 | bytes 1048576 | tf_op jit(solution)/shard_map/attend_back/pallas_call | solution.py:223
  289.6 1.8 collective-permute-start.57
  291.4 1.5 collective-permute-start.53
  293.4 2.9 collective-permute-done.57
  299.0 2.2 collective-permute-done.55
  301.4 1.8 convert_add_fusion.2
  303.4 2.4 collective-permute-start.61
  309.5 3.4 %collective-permute-done.61 = bf16[2,2,16,2176]{3,2,1,0:T(8,128)(2,1)S(1)} collective-permute-done((bf16[2,2,16,2176]{3,2,1,0:T(8,128)(2,1)S(1)}, bf16[2,2,16,2176]{3,2,1,0:T(8,128)(2,1)S(1)}, u32[]{:S(2)}, u32[]{:S(2)}) %collective-permute-start.61) | collective-permute-done | bytes 278560 | tf_op jit(solution)/shard_map/ppermute | solution.py:204
  312.9 7.0 %collective-permute-done.59 = bf16[2,2,16,2176]{3,2,1,0:T(8,128)(2,1)S(1)} collective-permute-done((bf16[2,2,16,2176]{3,2,1,0:T(8,128)(2,1)S(1)}, bf16[2,2,16,2176]{3,2,1,0:T(8,128)(2,1)S(1)}, u32[]{:S(2)}, u32[]{:S(2)}) %collective-permute-start.59) | collective-permute-done | bytes 278560 | tf_op jit(solution)/shard_map/ppermute | solution.py:204
  321.3 2.6 collective-permute-start.63
  324.6 7.3 %finish.1 = bf16[8,256,512]{2,1,0:T(8,128)(2,1)} custom-call(s32[2]{0:T(128)S(1)} %copy-done.33, bf16[1,256,512]{2,1,0:T(8,128)(2,1)S(1)} %copy-done.38, bf16[1,256,512]{2,1,0:T(8,128)(2,1)S(1)} %collective-permute-done.48.refs_2_, bf16[1,256,512]{2,1,0:T(8,128)(2,1)S(1)} %collective-permute-done.49.refs_3_, ...), custom_call_target="tpu_custom_call" | custom-call | flops 4000000000 | bytes 1048576 | tf_op jit(solution)/shard_map/finish/pallas_call | solution.py:223
  (298 shorter events, 50.4 us)
Async XLA Ops:
  3.8 8.7 %collective-permute-start.2 = (bf16[16,2176]{1,0:T(8,128)(2,1)S(1)}, bf16[16,2176]{1,0:T(8,128)(2,1)S(1)}, u32[]{:S(2)}, u32[]{:S(2)}) collective-permute-start(bf16[16,2176]{1,0:T(8,128)(2,1)S(1)} %fusion.21), channel_id=1, source_target_pairs={{0,2},{1,3},{2,0},{3,1},{4,6},{5,7},{6,4},{7,5},{8,10},{9,11},{10,... | collective-permute-start | bytes 208904 | tf_op jit(solution)/shard_map/ppermute | solution.py:57
  10.1 2.5 collective-permute-start
  10.8 9.3 %collective-permute-start.1 = (bf16[1,272,512]{2,1,0:T(8,128)(2,1)}, bf16[1,272,512]{2,1,0:T(8,128)(2,1)S(1)}, u32[]{:S(2)}, u32[]{:S(2)}) collective-permute-start(bf16[1,272,512]{2,1,0:T(8,128)(2,1)} %pad_maximum_fusion.11), channel_id=1, source_target_pairs={{0,2},{1,3},{2,0},{3,1},{4,6},{5,7},{6,4},{7,5},{8,10},{9,11},{10,... | collective-permute-start | bytes 835592 | tf_op jit(solution)/shard_map/ppermute | solution.py:57
  20.1 9.3 %collective-permute-start.7 = (bf16[2,16,2176]{2,1,0:T(8,128)(2,1)S(1)}, bf16[2,16,2176]{2,1,0:T(8,128)(2,1)S(1)}, u32[]{:S(2)}, u32[]{:S(2)}) collective-permute-start(bf16[2,16,2176]{2,1,0:T(8,128)(2,1)S(1)} %pad_maximum_fusion.18), channel_id=1, source_target_pairs={{0,16},{16,0},{1,17},{17,1},{2,18},{18,2},{3,19},{19,3},{4,20},{20... | collective-permute-start | bytes 417800 | tf_op jit(solution)/shard_map/ppermute | solution.py:57
  22.9 8.6 %collective-permute-start.6 = (bf16[128,512]{1,0:T(8,128)(2,1)S(1)}, bf16[128,512]{1,0:T(8,128)(2,1)S(1)}, u32[]{:S(2)}, u32[]{:S(2)}) collective-permute-start(bf16[128,512]{1,0:T(8,128)(2,1)S(1)} %get-tuple-element.654), channel_id=1, source_target_pairs={{0,12},{4,8},{8,4},{12,0},{1,13},{5,9},{9,5},{13,1},{2,14},{6,10},... | collective-permute-start | bytes 393224 | tf_op jit(solution)/shard_map/ppermute | solution.py:57
  25.4 6.1 %collective-permute-start.4 = (bf16[128,512]{1,0:T(8,128)(2,1)S(1)}, bf16[128,512]{1,0:T(8,128)(2,1)S(1)}, u32[]{:S(2)}, u32[]{:S(2)}) collective-permute-start(bf16[128,512]{1,0:T(8,128)(2,1)S(1)} %get-tuple-element.656), channel_id=1, source_target_pairs={{0,4},{4,0},{8,12},{12,8},{1,5},{5,1},{9,13},{13,9},{2,6},{6,2},{1... | collective-permute-start | bytes 393224 | tf_op jit(solution)/shard_map/ppermute | solution.py:57
  26.0 7.4 %collective-permute-start.5 = (bf16[128,512]{1,0:T(8,128)(2,1)S(1)}, bf16[128,512]{1,0:T(8,128)(2,1)S(1)}, u32[]{:S(2)}, u32[]{:S(2)}) collective-permute-start(bf16[128,512]{1,0:T(8,128)(2,1)S(1)} %get-tuple-element.657), channel_id=1, source_target_pairs={{0,8},{4,12},{8,0},{12,4},{1,9},{5,13},{9,1},{13,5},{2,10},{6,14},... | collective-permute-start | bytes 393224 | tf_op jit(solution)/shard_map/ppermute | solution.py:57
  26.4 8.0 %collective-permute-start.3 = (bf16[1,272,512]{2,1,0:T(8,128)(2,1)S(1)}, bf16[1,272,512]{2,1,0:T(8,128)(2,1)S(1)}, u32[]{:S(2)}, u32[]{:S(2)}) collective-permute-start(bf16[1,272,512]{2,1,0:T(8,128)(2,1)S(1)} %get-tuple-element.288), channel_id=1, source_target_pairs={{0,3},{1,2},{2,1},{3,0},{4,7},{5,6},{6,5},{7,4},{8,11},{9,10},{10,... | collective-permute-start | bytes 835592 | tf_op jit(solution)/shard_map/ppermute | solution.py:57
  35.1 8.7 %collective-permute-start.10 = (bf16[2,2,16,2176]{3,2,1,0:T(8,128)(2,1)S(1)}, bf16[2,2,16,2176]{3,2,1,0:T(8,128)(2,1)S(1)}, u32[]{:S(2)}, u32[]{:S(2)}) collective-permute-start(bf16[2,2,16,2176]{3,2,1,0:T(8,128)(2,1)S(1)} %pad_maximum_fusion.17), channel_id=1, source_target_pairs={{0,4},{4,0},{8,12},{12,8},{1,5},{5,1},{9,13},{13,9},{2,6},{6,2},{1... | collective-permute-start | bytes 835592 | tf_op jit(solution)/shard_map/ppermute | solution.py:57
  36.6 9.6 %collective-permute-start.9 = (bf16[2,2,16,2176]{3,2,1,0:T(8,128)(2,1)S(1)}, bf16[2,2,16,2176]{3,2,1,0:T(8,128)(2,1)S(1)}, u32[]{:S(2)}, u32[]{:S(2)}) collective-permute-start(bf16[2,2,16,2176]{3,2,1,0:T(8,128)(2,1)S(1)} %pad_maximum_fusion.17), channel_id=1, source_target_pairs={{0,8},{4,12},{8,0},{12,4},{1,9},{5,13},{9,1},{13,5},{2,10},{6,14},... | collective-permute-start | bytes 835592 | tf_op jit(solution)/shard_map/ppermute | solution.py:57
  38.2 11.8 %collective-permute-start.8 = (bf16[2,2,16,2176]{3,2,1,0:T(8,128)(2,1)S(1)}, bf16[2,2,16,2176]{3,2,1,0:T(8,128)(2,1)S(1)}, u32[]{:S(2)}, u32[]{:S(2)}) collective-permute-start(bf16[2,2,16,2176]{3,2,1,0:T(8,128)(2,1)S(1)} %pad_maximum_fusion.17), channel_id=1, source_target_pairs={{0,12},{4,8},{8,4},{12,0},{1,13},{5,9},{9,5},{13,1},{2,14},{6,10},... | collective-permute-start | bytes 835592 | tf_op jit(solution)/shard_map/ppermute | solution.py:57
  50.3 3.0 collective-permute-start.11
  58.7 15.6 %collective-permute-start.15 = (bf16[4,64,512]{2,1,0:T(8,128)(2,1)S(1)}, bf16[4,64,512]{2,1,0:T(8,128)(2,1)S(1)}, u32[]{:S(2)}, u32[]{:S(2)}) collective-permute-start(bf16[4,64,512]{2,1,0:T(8,128)(2,1)S(1)} %slice.51), channel_id=1, source_target_pairs={{0,16},{16,0},{1,17},{17,1},{2,18},{18,2},{3,19},{19,3},{4,20},{20... | collective-permute-start | bytes 786440 | tf_op jit(solution)/shard_map/ppermute | solution.py:57
  58.9 15.5 %collective-permute-start.12 = (bf16[1,272,512]{2,1,0:T(8,128)(2,1)}, bf16[1,272,512]{2,1,0:T(8,128)(2,1)S(1)}, u32[]{:S(2)}, u32[]{:S(2)}) collective-permute-start(bf16[1,272,512]{2,1,0:T(8,128)(2,1)} %get-tuple-element.337), channel_id=1, source_target_pairs={{0,1},{1,0},{2,3},{3,2},{4,5},{5,4},{6,7},{7,6},{8,9},{9,8},{10,11... | collective-permute-start | bytes 835592 | tf_op jit(solution)/shard_map/ppermute | solution.py:57
  59.0 15.5 %collective-permute-start.13 = (bf16[1,272,512]{2,1,0:T(8,128)(2,1)}, bf16[1,272,512]{2,1,0:T(8,128)(2,1)S(1)}, u32[]{:S(2)}, u32[]{:S(2)}) collective-permute-start(bf16[1,272,512]{2,1,0:T(8,128)(2,1)} %get-tuple-element.338), channel_id=1, source_target_pairs={{0,2},{1,3},{2,0},{3,1},{4,6},{5,7},{6,4},{7,5},{8,10},{9,11},{10,... | collective-permute-start | bytes 835592 | tf_op jit(solution)/shard_map/ppermute | solution.py:57
  61.3 13.2 %collective-permute-start.14 = (bf16[1,272,512]{2,1,0:T(8,128)(2,1)}, bf16[1,272,512]{2,1,0:T(8,128)(2,1)S(1)}, u32[]{:S(2)}, u32[]{:S(2)}) collective-permute-start(bf16[1,272,512]{2,1,0:T(8,128)(2,1)} %get-tuple-element.339), channel_id=1, source_target_pairs={{0,3},{1,2},{2,1},{3,0},{4,7},{5,6},{6,5},{7,4},{8,11},{9,10},{10,... | collective-permute-start | bytes 835592 | tf_op jit(solution)/shard_map/ppermute | solution.py:57
  74.5 18.9 %collective-permute-start.17 = (bf16[4,64,512]{2,1,0:T(8,128)(2,1)S(1)}, bf16[4,64,512]{2,1,0:T(8,128)(2,1)S(1)}, u32[]{:S(2)}, u32[]{:S(2)}) collective-permute-start(bf16[4,64,512]{2,1,0:T(8,128)(2,1)S(1)} %get-tuple-element.370), channel_id=1, source_target_pairs={{0,16},{16,0},{1,17},{17,1},{2,18},{18,2},{3,19},{19,3},{4,20},{20... | collective-permute-start | bytes 786440 | tf_op jit(solution)/shard_map/ppermute | solution.py:57
  77.3 16.3 %collective-permute-start.16 = (bf16[2,4,64,512]{3,2,1,0:T(8,128)(2,1)S(1)}, bf16[2,4,64,512]{3,2,1,0:T(8,128)(2,1)S(1)}, u32[]{:S(2)}, u32[]{:S(2)}) collective-permute-start(bf16[2,4,64,512]{3,2,1,0:T(8,128)(2,1)S(1)} %pad_maximum_fusion.7), channel_id=1, source_target_pairs={{0,2},{1,3},{2,0},{3,1},{4,6},{5,7},{6,4},{7,5},{8,10},{9,11},{10,... | collective-permute-start | bytes 1572872 | tf_op jit(solution)/shard_map/ppermute | solution.py:57
  93.9 18.3 %collective-permute-start.18 = (bf16[2,128,512]{2,1,0:T(8,128)(2,1)S(1)}, bf16[2,128,512]{2,1,0:T(8,128)(2,1)S(1)}, u32[]{:S(2)}, u32[]{:S(2)}) collective-permute-start(bf16[2,128,512]{2,1,0:T(8,128)(2,1)S(1)} %get-tuple-element.378), channel_id=1, source_target_pairs={{0,1},{1,0},{2,3},{3,2},{4,5},{5,4},{6,7},{7,6},{8,9},{9,8},{10,11... | collective-permute-start | bytes 786440 | tf_op jit(solution)/shard_map/ppermute | solution.py:57
  93.9 19.4 %collective-permute-start.19 = (bf16[2,128,512]{2,1,0:T(8,128)(2,1)S(1)}, bf16[2,128,512]{2,1,0:T(8,128)(2,1)S(1)}, u32[]{:S(2)}, u32[]{:S(2)}) collective-permute-start(bf16[2,128,512]{2,1,0:T(8,128)(2,1)S(1)} %get-tuple-element.379), channel_id=1, source_target_pairs={{0,2},{1,3},{2,0},{3,1},{4,6},{5,7},{6,4},{7,5},{8,10},{9,11},{10,... | collective-permute-start | bytes 786440 | tf_op jit(solution)/shard_map/ppermute | solution.py:57
  94.3 19.0 %collective-permute-start.20 = (bf16[2,128,512]{2,1,0:T(8,128)(2,1)S(1)}, bf16[2,128,512]{2,1,0:T(8,128)(2,1)S(1)}, u32[]{:S(2)}, u32[]{:S(2)}) collective-permute-start(bf16[2,128,512]{2,1,0:T(8,128)(2,1)S(1)} %get-tuple-element.380), channel_id=1, source_target_pairs={{0,3},{1,2},{2,1},{3,0},{4,7},{5,6},{6,5},{7,4},{8,11},{9,10},{10,... | collective-permute-start | bytes 786440 | tf_op jit(solution)/shard_map/ppermute | solution.py:57
  111.5 6.2 %collective-permute-start.21 = (bf16[2,128,512]{2,1,0:T(8,128)(2,1)S(1)}, bf16[2,128,512]{2,1,0:T(8,128)(2,1)S(1)}, u32[]{:S(2)}, u32[]{:S(2)}) collective-permute-start(bf16[2,128,512]{2,1,0:T(8,128)(2,1)S(1)} %get-tuple-element.392), channel_id=1, source_target_pairs={{0,1},{1,0},{2,3},{3,2},{4,5},{5,4},{6,7},{7,6},{8,9},{9,8},{10,11... | collective-permute-start | bytes 786440 | tf_op jit(solution)/shard_map/ppermute | solution.py:57
  111.8 9.2 %collective-permute-start.22 = (bf16[2,128,512]{2,1,0:T(8,128)(2,1)S(1)}, bf16[2,128,512]{2,1,0:T(8,128)(2,1)S(1)}, u32[]{:S(2)}, u32[]{:S(2)}) collective-permute-start(bf16[2,128,512]{2,1,0:T(8,128)(2,1)S(1)} %get-tuple-element.393), channel_id=1, source_target_pairs={{0,2},{1,3},{2,0},{3,1},{4,6},{5,7},{6,4},{7,5},{8,10},{9,11},{10,... | collective-permute-start | bytes 786440 | tf_op jit(solution)/shard_map/ppermute | solution.py:57
  112.2 12.9 %collective-permute-start.23 = (bf16[2,128,512]{2,1,0:T(8,128)(2,1)S(1)}, bf16[2,128,512]{2,1,0:T(8,128)(2,1)S(1)}, u32[]{:S(2)}, u32[]{:S(2)}) collective-permute-start(bf16[2,128,512]{2,1,0:T(8,128)(2,1)S(1)} %get-tuple-element.394), channel_id=1, source_target_pairs={{0,3},{1,2},{2,1},{3,0},{4,7},{5,6},{6,5},{7,4},{8,11},{9,10},{10,... | collective-permute-start | bytes 786440 | tf_op jit(solution)/shard_map/ppermute | solution.py:57
  125.1 14.4 %collective-permute-start.27 = (bf16[2,4,64,512]{3,2,1,0:T(8,128)(2,1)S(1)}, bf16[2,4,64,512]{3,2,1,0:T(8,128)(2,1)S(1)}, u32[]{:S(2)}, u32[]{:S(2)}) collective-permute-start(bf16[2,4,64,512]{3,2,1,0:T(8,128)(2,1)S(1)} %pad_maximum_fusion.8), channel_id=1, source_target_pairs={{0,2},{1,3},{2,0},{3,1},{4,6},{5,7},{6,4},{7,5},{8,10},{9,11},{10,... | collective-permute-start | bytes 1572872 | tf_op jit(solution)/shard_map/ppermute | solution.py:57
  125.5 20.7 %collective-permute-start.29 = (bf16[16,64,512]{2,1,0:T(8,128)(2,1)S(1)}, bf16[16,64,512]{2,1,0:T(8,128)(2,1)S(1)}, u32[]{:S(2)}, u32[]{:S(2)}) collective-permute-start(bf16[16,64,512]{2,1,0:T(8,128)(2,1)S(1)} %bitcast.155), channel_id=1, source_target_pairs={{0,1},{1,0},{2,3},{3,2},{4,5},{5,4},{6,7},{7,6},{8,9},{9,8},{10,11... | collective-permute-start | bytes 3145736 | tf_op jit(solution)/shard_map/ppermute | solution.py:57
  125.9 13.9 %collective-permute-start.24 = (bf16[128,1152]{1,0:T(8,128)(2,1)S(1)}, bf16[128,1152]{1,0:T(8,128)(2,1)S(1)}, u32[]{:S(2)}, u32[]{:S(2)}) collective-permute-start(bf16[128,1152]{1,0:T(8,128)(2,1)S(1)} %get-tuple-element.405), channel_id=1, source_target_pairs={{0,4},{4,0},{8,12},{12,8},{1,5},{5,1},{9,13},{13,9},{2,6},{6,2},{1... | collective-permute-start | bytes 884744 | tf_op jit(solution)/shard_map/ppermute | solution.py:57
  127.4 12.4 %collective-permute-start.25 = (bf16[128,1152]{1,0:T(8,128)(2,1)S(1)}, bf16[128,1152]{1,0:T(8,128)(2,1)S(1)}, u32[]{:S(2)}, u32[]{:S(2)}) collective-permute-start(bf16[128,1152]{1,0:T(8,128)(2,1)S(1)} %get-tuple-element.406), channel_id=1, source_target_pairs={{0,8},{4,12},{8,0},{12,4},{1,9},{5,13},{9,1},{13,5},{2,10},{6,14},... | collective-permute-start | bytes 884744 | tf_op jit(solution)/shard_map/ppermute | solution.py:57
  128.9 13.5 %collective-permute-start.26 = (bf16[128,1152]{1,0:T(8,128)(2,1)S(1)}, bf16[128,1152]{1,0:T(8,128)(2,1)S(1)}, u32[]{:S(2)}, u32[]{:S(2)}) collective-permute-start(bf16[128,1152]{1,0:T(8,128)(2,1)S(1)} %get-tuple-element.407), channel_id=1, source_target_pairs={{0,12},{4,8},{8,4},{12,0},{1,13},{5,9},{9,5},{13,1},{2,14},{6,10},... | collective-permute-start | bytes 884744 | tf_op jit(solution)/shard_map/ppermute | solution.py:57
  142.6 3.6 %collective-permute-start.30 = (bf16[16,64,512]{2,1,0:T(8,128)(2,1)S(1)}, bf16[16,64,512]{2,1,0:T(8,128)(2,1)S(1)}, u32[]{:S(2)}, u32[]{:S(2)}) collective-permute-start(bf16[16,64,512]{2,1,0:T(8,128)(2,1)S(1)} %bitcast.158), channel_id=1, source_target_pairs={{0,1},{1,0},{2,3},{3,2},{4,5},{5,4},{6,7},{7,6},{8,9},{9,8},{10,11... | collective-permute-start | bytes 3145736 | tf_op jit(solution)/shard_map/ppermute | solution.py:57
  142.6 9.4 %collective-permute-start.28 = (bf16[128,1152]{1,0:T(8,128)(2,1)S(1)}, bf16[128,1152]{1,0:T(8,128)(2,1)S(1)}, u32[]{:S(2)}, u32[]{:S(2)}) collective-permute-start(bf16[128,1152]{1,0:T(8,128)(2,1)S(1)} %get-tuple-element.410), channel_id=1, source_target_pairs={{0,4},{4,0},{8,12},{12,8},{1,5},{5,1},{9,13},{13,9},{2,6},{6,2},{1... | collective-permute-start | bytes 884744 | tf_op jit(solution)/shard_map/ppermute | solution.py:57
  144.2 11.4 %collective-permute-start.31 = (bf16[128,1152]{1,0:T(8,128)(2,1)S(1)}, bf16[128,1152]{1,0:T(8,128)(2,1)S(1)}, u32[]{:S(2)}, u32[]{:S(2)}) collective-permute-start(bf16[128,1152]{1,0:T(8,128)(2,1)S(1)} %get-tuple-element.419), channel_id=1, source_target_pairs={{0,8},{4,12},{8,0},{12,4},{1,9},{5,13},{9,1},{13,5},{2,10},{6,14},... | collective-permute-start | bytes 884744 | tf_op jit(solution)/shard_map/ppermute | solution.py:57
  145.8 14.7 %collective-permute-start.32 = (bf16[128,1152]{1,0:T(8,128)(2,1)S(1)}, bf16[128,1152]{1,0:T(8,128)(2,1)S(1)}, u32[]{:S(2)}, u32[]{:S(2)}) collective-permute-start(bf16[128,1152]{1,0:T(8,128)(2,1)S(1)} %get-tuple-element.420), channel_id=1, source_target_pairs={{0,12},{4,8},{8,4},{12,0},{1,13},{5,9},{9,5},{13,1},{2,14},{6,10},... | collective-permute-start | bytes 884744 | tf_op jit(solution)/shard_map/ppermute | solution.py:57
  152.1 16.0 %collective-permute-start.35 = (bf16[128,1152]{1,0:T(8,128)(2,1)S(1)}, bf16[128,1152]{1,0:T(8,128)(2,1)S(1)}, u32[]{:S(2)}, u32[]{:S(2)}) collective-permute-start(bf16[128,1152]{1,0:T(8,128)(2,1)S(1)} %get-tuple-element.430.refs_1_), channel_id=1, source_target_pairs={{0,12},{4,8},{8,4},{12,0},{1,13},{5,9},{9,5},{13,1},{2,14},{6,10},... | collective-permute-start | bytes 884744 | tf_op jit(solution)/shard_map/ppermute | solution.py:57
  154.6 17.7 %collective-permute-start.34 = (bf16[128,1152]{1,0:T(8,128)(2,1)S(1)}, bf16[128,1152]{1,0:T(8,128)(2,1)S(1)}, u32[]{:S(2)}, u32[]{:S(2)}) collective-permute-start(bf16[128,1152]{1,0:T(8,128)(2,1)S(1)} %get-tuple-element.430.refs_1_), channel_id=1, source_target_pairs={{0,8},{4,12},{8,0},{12,4},{1,9},{5,13},{9,1},{13,5},{2,10},{6,14},... | collective-permute-start | bytes 884744 | tf_op jit(solution)/shard_map/ppermute | solution.py:57
  155.0 17.3 %collective-permute-start.33 = (bf16[128,1152]{1,0:T(8,128)(2,1)S(1)}, bf16[128,1152]{1,0:T(8,128)(2,1)S(1)}, u32[]{:S(2)}, u32[]{:S(2)}) collective-permute-start(bf16[128,1152]{1,0:T(8,128)(2,1)S(1)} %get-tuple-element.430.refs_1_), channel_id=1, source_target_pairs={{0,4},{4,0},{8,12},{12,8},{1,5},{5,1},{9,13},{13,9},{2,6},{6,2},{1... | collective-permute-start | bytes 884744 | tf_op jit(solution)/shard_map/ppermute | solution.py:57
  173.7 15.4 %collective-permute-start.39 = (bf16[16,128,512]{2,1,0:T(8,128)(2,1)}, bf16[16,128,512]{2,1,0:T(8,128)(2,1)}, u32[]{:S(2)}, u32[]{:S(2)}) collective-permute-start(bf16[16,128,512]{2,1,0:T(8,128)(2,1)} %get-tuple-element.439), channel_id=1, source_target_pairs={{0,1},{1,0},{2,3},{3,2},{4,5},{5,4},{6,7},{7,6},{8,9},{9,8},{10,11... | collective-permute-start | bytes 6291464 | tf_op jit(solution)/shard_map/ppermute | solution.py:57
  173.7 22.3 %collective-permute-start.38 = (bf16[128,1152]{1,0:T(8,128)(2,1)S(1)}, bf16[128,1152]{1,0:T(8,128)(2,1)S(1)}, u32[]{:S(2)}, u32[]{:S(2)}) collective-permute-start(bf16[128,1152]{1,0:T(8,128)(2,1)S(1)} %get-tuple-element.440.refs_1_), channel_id=1, source_target_pairs={{0,12},{4,8},{8,4},{12,0},{1,13},{5,9},{9,5},{13,1},{2,14},{6,10},... | collective-permute-start | bytes 884744 | tf_op jit(solution)/shard_map/ppermute | solution.py:57
  175.5 20.7 %collective-permute-start.37 = (bf16[128,1152]{1,0:T(8,128)(2,1)S(1)}, bf16[128,1152]{1,0:T(8,128)(2,1)S(1)}, u32[]{:S(2)}, u32[]{:S(2)}) collective-permute-start(bf16[128,1152]{1,0:T(8,128)(2,1)S(1)} %get-tuple-element.440.refs_1_), channel_id=1, source_target_pairs={{0,8},{4,12},{8,0},{12,4},{1,9},{5,13},{9,1},{13,5},{2,10},{6,14},... | collective-permute-start | bytes 884744 | tf_op jit(solution)/shard_map/ppermute | solution.py:57
  175.9 20.2 %collective-permute-start.36 = (bf16[128,1152]{1,0:T(8,128)(2,1)S(1)}, bf16[128,1152]{1,0:T(8,128)(2,1)S(1)}, u32[]{:S(2)}, u32[]{:S(2)}) collective-permute-start(bf16[128,1152]{1,0:T(8,128)(2,1)S(1)} %get-tuple-element.440.refs_1_), channel_id=1, source_target_pairs={{0,4},{4,0},{8,12},{12,8},{1,5},{5,1},{9,13},{13,9},{2,6},{6,2},{1... | collective-permute-start | bytes 884744 | tf_op jit(solution)/shard_map/ppermute | solution.py:57
  189.1 19.8 %collective-permute-start.40 = (bf16[2,128,512]{2,1,0:T(8,128)(2,1)}, bf16[2,128,512]{2,1,0:T(8,128)(2,1)}, u32[]{:S(2)}, u32[]{:S(2)}) collective-permute-start(bf16[2,128,512]{2,1,0:T(8,128)(2,1)} %get-tuple-element.450), channel_id=1, source_target_pairs={{0,1},{1,0},{2,3},{3,2},{4,5},{5,4},{6,7},{7,6},{8,9},{9,8},{10,11... | collective-permute-start | bytes 786440 | tf_op jit(solution)/shard_map/ppermute | solution.py:57
  189.1 20.8 %collective-permute-start.41 = (bf16[2,128,512]{2,1,0:T(8,128)(2,1)}, bf16[2,128,512]{2,1,0:T(8,128)(2,1)}, u32[]{:S(2)}, u32[]{:S(2)}) collective-permute-start(bf16[2,128,512]{2,1,0:T(8,128)(2,1)} %get-tuple-element.451), channel_id=1, source_target_pairs={{0,2},{1,3},{2,0},{3,1},{4,6},{5,7},{6,4},{7,5},{8,10},{9,11},{10,... | collective-permute-start | bytes 786440 | tf_op jit(solution)/shard_map/ppermute | solution.py:57
  196.0 13.8 %collective-permute-start.42 = (bf16[2,128,512]{2,1,0:T(8,128)(2,1)}, bf16[2,128,512]{2,1,0:T(8,128)(2,1)}, u32[]{:S(2)}, u32[]{:S(2)}) collective-permute-start(bf16[2,128,512]{2,1,0:T(8,128)(2,1)} %get-tuple-element.452), channel_id=1, source_target_pairs={{0,3},{1,2},{2,1},{3,0},{4,7},{5,6},{6,5},{7,4},{8,11},{9,10},{10,... | collective-permute-start | bytes 786440 | tf_op jit(solution)/shard_map/ppermute | solution.py:57
  208.2 9.3 %collective-permute-start.44 = (bf16[2,128,512]{2,1,0:T(8,128)(2,1)}, bf16[2,128,512]{2,1,0:T(8,128)(2,1)S(1)}, u32[]{:S(2)}, u32[]{:S(2)}) collective-permute-start(bf16[2,128,512]{2,1,0:T(8,128)(2,1)} %get-tuple-element.455), channel_id=1, source_target_pairs={{0,2},{1,3},{2,0},{3,1},{4,6},{5,7},{6,4},{7,5},{8,10},{9,11},{10,... | collective-permute-start | bytes 786440 | tf_op jit(solution)/shard_map/ppermute | solution.py:57
  208.9 13.1 %collective-permute-start.45 = (bf16[2,128,512]{2,1,0:T(8,128)(2,1)}, bf16[2,128,512]{2,1,0:T(8,128)(2,1)S(1)}, u32[]{:S(2)}, u32[]{:S(2)}) collective-permute-start(bf16[2,128,512]{2,1,0:T(8,128)(2,1)} %get-tuple-element.456), channel_id=1, source_target_pairs={{0,3},{1,2},{2,1},{3,0},{4,7},{5,6},{6,5},{7,4},{8,11},{9,10},{10,... | collective-permute-start | bytes 786440 | tf_op jit(solution)/shard_map/ppermute | solution.py:57
  222.7 30.3 %collective-permute-start.46 = (bf16[16,16,640]{2,1,0:T(8,128)(2,1)S(1)}, bf16[16,16,640]{2,1,0:T(8,128)(2,1)S(1)}, u32[]{:S(2)}, u32[]{:S(2)}) collective-permute-start(bf16[16,16,640]{2,1,0:T(8,128)(2,1)S(1)} %get-tuple-element.480), channel_id=1, source_target_pairs={{0,1},{1,0},{2,3},{3,2},{4,5},{5,4},{6,7},{7,6},{8,9},{9,8},{10,11... | collective-permute-start | bytes 983048 | tf_op jit(solution)/shard_map/ppermute | solution.py:57
  223.1 29.9 %collective-permute-start.47 = (bf16[2,4,128,512]{3,2,1,0:T(8,128)(2,1)}, bf16[2,4,128,512]{3,2,1,0:T(8,128)(2,1)}, u32[]{:S(2)}, u32[]{:S(2)}) collective-permute-start(bf16[2,4,128,512]{3,2,1,0:T(8,128)(2,1)} %fusion), channel_id=1, source_target_pairs={{0,2},{1,3},{2,0},{3,1},{4,6},{5,7},{6,4},{7,5},{8,10},{9,11},{10,... | collective-permute-start | bytes 3145736 | tf_op jit(solution)/shard_map/ppermute | solution.py:57
  254.8 32.1 %collective-permute-start.48 = (bf16[1,256,512]{2,1,0:T(8,128)(2,1)}, bf16[1,256,512]{2,1,0:T(8,128)(2,1)S(1)}, u32[]{:S(2)}, u32[]{:S(2)}) collective-permute-start(bf16[1,256,512]{2,1,0:T(8,128)(2,1)} %get-tuple-element.498), channel_id=1, source_target_pairs={{0,1},{1,0},{2,3},{3,2},{4,5},{5,4},{6,7},{7,6},{8,9},{9,8},{10,11... | collective-permute-start | bytes 786440 | tf_op jit(solution)/shard_map/ppermute | solution.py:57
  254.9 32.1 %collective-permute-start.49 = (bf16[1,256,512]{2,1,0:T(8,128)(2,1)}, bf16[1,256,512]{2,1,0:T(8,128)(2,1)S(1)}, u32[]{:S(2)}, u32[]{:S(2)}) collective-permute-start(bf16[1,256,512]{2,1,0:T(8,128)(2,1)} %get-tuple-element.499), channel_id=1, source_target_pairs={{0,2},{1,3},{2,0},{3,1},{4,6},{5,7},{6,4},{7,5},{8,10},{9,11},{10,... | collective-permute-start | bytes 786440 | tf_op jit(solution)/shard_map/ppermute | solution.py:57
  256.5 30.5 %collective-permute-start.50 = (bf16[1,256,512]{2,1,0:T(8,128)(2,1)S(1)}, bf16[1,256,512]{2,1,0:T(8,128)(2,1)S(1)}, u32[]{:S(2)}, u32[]{:S(2)}) collective-permute-start(bf16[1,256,512]{2,1,0:T(8,128)(2,1)S(1)} %copy-done.69), channel_id=1, source_target_pairs={{0,3},{1,2},{2,1},{3,0},{4,7},{5,6},{6,5},{7,4},{8,11},{9,10},{10,... | collective-permute-start | bytes 786440 | tf_op jit(solution)/shard_map/ppermute | solution.py:57
  256.8 30.2 %collective-permute-start.51 = (bf16[4,128,512]{2,1,0:T(8,128)(2,1)S(1)}, bf16[4,128,512]{2,1,0:T(8,128)(2,1)S(1)}, u32[]{:S(2)}, u32[]{:S(2)}) collective-permute-start(bf16[4,128,512]{2,1,0:T(8,128)(2,1)S(1)} %fusion.1), channel_id=1, source_target_pairs={{0,16},{16,0},{1,17},{17,1},{2,18},{18,2},{3,19},{19,3},{4,20},{20... | collective-permute-start | bytes 1572872 | tf_op jit(solution)/shard_map/ppermute | solution.py:57
  287.0 14.3 %collective-permute-start.54 = (bf16[16,16,1536]{2,1,0:T(8,128)(2,1)}, bf16[16,16,1536]{2,1,0:T(8,128)(2,1)}, u32[]{:S(2)}, u32[]{:S(2)}) collective-permute-start(bf16[16,16,1536]{2,1,0:T(8,128)(2,1)} %get-tuple-element.511), channel_id=1, source_target_pairs={{0,1},{1,0},{2,3},{3,2},{4,5},{5,4},{6,7},{7,6},{8,9},{9,8},{10,11... | collective-permute-start | bytes 2359304 | tf_op jit(solution)/shard_map/ppermute | solution.py:57
  289.6 6.7 %collective-permute-start.57 = (bf16[128,512]{1,0:T(8,128)(2,1)S(1)}, bf16[128,512]{1,0:T(8,128)(2,1)S(1)}, u32[]{:S(2)}, u32[]{:S(2)}) collective-permute-start(bf16[128,512]{1,0:T(8,128)(2,1)S(1)} %get-tuple-element.631), channel_id=1, source_target_pairs={{0,12},{4,8},{8,4},{12,0},{1,13},{5,9},{9,5},{13,1},{2,14},{6,10},... | collective-permute-start | bytes 393224 | tf_op jit(solution)/shard_map/ppermute | solution.py:57
  291.4 9.8 %collective-permute-start.52 = (bf16[1,256,512]{2,1,0:T(8,128)(2,1)}, bf16[1,256,512]{2,1,0:T(8,128)(2,1)S(1)}, u32[]{:S(2)}, u32[]{:S(2)}) collective-permute-start(bf16[1,256,512]{2,1,0:T(8,128)(2,1)} %get-tuple-element.508), channel_id=1, source_target_pairs={{0,1},{1,0},{2,3},{3,2},{4,5},{5,4},{6,7},{7,6},{8,9},{9,8},{10,11... | collective-permute-start | bytes 786440 | tf_op jit(solution)/shard_map/ppermute | solution.py:57
  291.4 9.8 %collective-permute-start.53 = (bf16[1,256,512]{2,1,0:T(8,128)(2,1)}, bf16[1,256,512]{2,1,0:T(8,128)(2,1)S(1)}, u32[]{:S(2)}, u32[]{:S(2)}) collective-permute-start(bf16[1,256,512]{2,1,0:T(8,128)(2,1)} %get-tuple-element.509), channel_id=1, source_target_pairs={{0,2},{1,3},{2,0},{3,1},{4,6},{5,7},{6,4},{7,5},{8,10},{9,11},{10,... | collective-permute-start | bytes 786440 | tf_op jit(solution)/shard_map/ppermute | solution.py:57
  293.0 6.1 %collective-permute-start.56 = (bf16[128,512]{1,0:T(8,128)(2,1)S(1)}, bf16[128,512]{1,0:T(8,128)(2,1)S(1)}, u32[]{:S(2)}, u32[]{:S(2)}) collective-permute-start(bf16[128,512]{1,0:T(8,128)(2,1)S(1)} %get-tuple-element.632), channel_id=1, source_target_pairs={{0,8},{4,12},{8,0},{12,4},{1,9},{5,13},{9,1},{13,5},{2,10},{6,14},... | collective-permute-start | bytes 393224 | tf_op jit(solution)/shard_map/ppermute | solution.py:57
  296.3 5.0 %collective-permute-start.55 = (bf16[128,512]{1,0:T(8,128)(2,1)S(1)}, bf16[128,512]{1,0:T(8,128)(2,1)S(1)}, u32[]{:S(2)}, u32[]{:S(2)}) collective-permute-start(bf16[128,512]{1,0:T(8,128)(2,1)S(1)} %get-tuple-element.633), channel_id=1, source_target_pairs={{0,4},{4,0},{8,12},{12,8},{1,5},{5,1},{9,13},{13,9},{2,6},{6,2},{1... | collective-permute-start | bytes 393224 | tf_op jit(solution)/shard_map/ppermute | solution.py:57
  301.3 8.2 %collective-permute-start.58 = (bf16[1,256,512]{2,1,0:T(8,128)(2,1)S(1)}, bf16[1,256,512]{2,1,0:T(8,128)(2,1)S(1)}, u32[]{:S(2)}, u32[]{:S(2)}) collective-permute-start(bf16[1,256,512]{2,1,0:T(8,128)(2,1)S(1)} %copy-done.65), channel_id=1, source_target_pairs={{0,3},{1,2},{2,1},{3,0},{4,7},{5,6},{6,5},{7,4},{8,11},{9,10},{10,... | collective-permute-start | bytes 786440 | tf_op jit(solution)/shard_map/ppermute | solution.py:57
  303.4 9.5 %collective-permute-start.61 = (bf16[2,2,16,2176]{3,2,1,0:T(8,128)(2,1)S(1)}, bf16[2,2,16,2176]{3,2,1,0:T(8,128)(2,1)S(1)}, u32[]{:S(2)}, u32[]{:S(2)}) collective-permute-start(bf16[2,2,16,2176]{3,2,1,0:T(8,128)(2,1)S(1)} %get-tuple-element.612), channel_id=1, source_target_pairs={{0,12},{4,8},{8,4},{12,0},{1,13},{5,9},{9,5},{13,1},{2,14},{6,10},... | collective-permute-start | bytes 835592 | tf_op jit(solution)/shard_map/ppermute | solution.py:204
  305.8 14.0 %collective-permute-start.59 = (bf16[2,2,16,2176]{3,2,1,0:T(8,128)(2,1)S(1)}, bf16[2,2,16,2176]{3,2,1,0:T(8,128)(2,1)S(1)}, u32[]{:S(2)}, u32[]{:S(2)}) collective-permute-start(bf16[2,2,16,2176]{3,2,1,0:T(8,128)(2,1)S(1)} %get-tuple-element.613), channel_id=1, source_target_pairs={{0,4},{4,0},{8,12},{12,8},{1,5},{5,1},{9,13},{13,9},{2,6},{6,2},{1... | collective-permute-start | bytes 835592 | tf_op jit(solution)/shard_map/ppermute | solution.py:204
  307.1 12.7 %collective-permute-start.60 = (bf16[2,2,16,2176]{3,2,1,0:T(8,128)(2,1)S(1)}, bf16[2,2,16,2176]{3,2,1,0:T(8,128)(2,1)S(1)}, u32[]{:S(2)}, u32[]{:S(2)}) collective-permute-start(bf16[2,2,16,2176]{3,2,1,0:T(8,128)(2,1)S(1)} %get-tuple-element.614), channel_id=1, source_target_pairs={{0,8},{4,12},{8,0},{12,4},{1,9},{5,13},{9,1},{13,5},{2,10},{6,14},... | collective-permute-start | bytes 835592 | tf_op jit(solution)/shard_map/ppermute | solution.py:204
  320.1 11.8 %collective-permute-start.62 = (bf16[16,2176]{1,0:T(8,128)(2,1)S(1)}, bf16[16,2176]{1,0:T(8,128)(2,1)S(1)}, u32[]{:S(2)}, u32[]{:S(2)}) collective-permute-start(bf16[16,2176]{1,0:T(8,128)(2,1)S(1)} %get-tuple-element.549), channel_id=1, source_target_pairs={{0,2},{1,3},{2,0},{3,1},{16,18},{17,19},{18,16},{19,17},{4,6},{5,7... | collective-permute-start | bytes 208904 | tf_op jit(solution)/shard_map/ppermute | solution.py:204
  321.3 10.6 %collective-permute-start.63 = (bf16[16,2176]{1,0:T(8,128)(2,1)S(1)}, bf16[16,2176]{1,0:T(8,128)(2,1)S(1)}, u32[]{:S(2)}, u32[]{:S(2)}) collective-permute-start(bf16[16,2176]{1,0:T(8,128)(2,1)S(1)} %get-tuple-element.550), channel_id=1, source_target_pairs={{0,16},{1,17},{2,18},{3,19},{16,0},{17,1},{18,2},{19,3},{4,20},{5,... | collective-permute-start | bytes 208904 | tf_op jit(solution)/shard_map/ppermute | solution.py:204
  323.9 8.0 %collective-permute-start.64 = (bf16[16,2176]{1,0:T(8,128)(2,1)S(1)}, bf16[16,2176]{1,0:T(8,128)(2,1)S(1)}, u32[]{:S(2)}, u32[]{:S(2)}) collective-permute-start(bf16[16,2176]{1,0:T(8,128)(2,1)S(1)} %get-tuple-element.551), channel_id=1, source_target_pairs={{0,18},{1,19},{2,16},{3,17},{16,2},{17,3},{18,0},{19,1},{4,22},{5,... | collective-permute-start | bytes 208904 | tf_op jit(solution)/shard_map/ppermute | solution.py:204
  (71 other events, 1003.9 us)

commit v5 on v4

--- a/solution.py
+++ b/solution.py
@@ -133,9 +133,14 @@
         self.have += bits
 
 
+def total_of(terms):
+    return functools.reduce(jnp.add, [term.astype(f32) for term in terms])
+
+
 class Halving(Steps):
     def __init__(self, value, sizes, order, inner=0):
-        super().__init__(value, sizes, order)
+        super().__init__(None, sizes, order)
+        self.terms = value if isinstance(value, list) else [value]
         self.sizes = sizes
         self.left = [bit for bit in bits_of(sizes) if bit in self.order]
         self.inner = inner
@@ -147,18 +152,28 @@
         axis, size, mask = bit
         depth += self.inner if axis == "seq" else 0
         high = ((lax.axis_index(axis) & mask) != 0).astype(jnp.int32)
-        keep = lax.dynamic_index_in_dim(self.value, high, depth, keepdims=False)
-        send = lax.dynamic_index_in_dim(self.value, 1 - high, depth, keepdims=False)
-        self.value = (keep, send.astype(bf16))
+        keep, send = [
+            [lax.dynamic_index_in_dim(term, at, depth, keepdims=False) for term in self.terms]
+            for at in (high, 1 - high)
+        ]
+        self.terms = keep
+        self.value = total_of(send).astype(bf16)
         self.link = bit
 
     def exchange(self):
         axis, size, mask = self.link
-        keep, send = self.value
-        self.value = (keep, partner(send, axis, size, mask))
+        self.value = partner(self.value, axis, size, mask)
 
     def combine(self):
-        self.value = functools.reduce(jnp.add, [part.astype(f32) for part in self.value])
+        if isinstance(self.value, list):
+            self.terms = self.value
+        else:
+            self.terms = self.terms + [self.value]
+        self.value = None
+
+    def finish(self):
+        super().finish()
+        return total_of(self.terms)
 
     def step(self, bit):
         self.order.insert(0, bit)
@@ -173,8 +188,9 @@
         if self.inner or bits != self.left[depth : depth + len(bits)]:
             raise NotImplementedError
         self.left = [bit for bit in self.left if bit not in bits]
-        shape = self.value.shape
-        value = self.value.reshape(shape[:depth] + (2 ** len(bits),) + shape[depth + len(bits) :])
+        value = total_of(self.terms)
+        shape = value.shape
+        value = value.reshape(shape[:depth] + (2 ** len(bits),) + shape[depth + len(bits) :])
         place = 0
         for axis, size, mask in bits:
             place = 2 * place + ((lax.axis_index(axis) & mask) != 0).astype(jnp.int32)
@@ -343,8 +359,8 @@
     vector_ref, w_ref = refs[1 + slots : 3 + slots]
     rest = refs[3 + slots + old :]
     att_refs = rest[:slots]
-    seg_ref, qt_ref, k_ref, v_ref, q_ref, vt_ref, ot_ref, lse_ref = rest[slots : slots + 8]
-    w_t, *aux = rest[slots + 8 :]
+    seg_ref, qt_ref, k_ref, v_ref, q_ref, vt_ref, ot_ref, lse_ref, rows_ref = rest[slots : slots + 9]
+    w_t, *aux = rest[slots + 9 :]
     width = w_ref.shape[0]
     piece = x_refs[0].shape[1] - MARKS
     me = me_ref[0]
@@ -353,7 +369,8 @@
     w_t[:width] = w_ref[:, :width].T
     w_t[width:] = w_ref[:, 2 * width :].T
     aux[2][...] = causal_bias(piece if parts > 1 else LANES)
-    gain = vector_ref[...].astype(f32).T[0:1]
+    rows_ref[...] = vector_ref[...].astype(f32).T
+    gain = rows_ref[0:1]
     for j in range(slots):
         place = pl.ds(pl.multiple_of((me ^ j) * piece, piece), piece)
         marks = x_refs[j][0, piece:].astype(f32)
@@ -417,6 +434,7 @@
         + [
             (this(width, slots * some), (rows, width, slots * some), bf16),
             (this(HEADS, slots * some), (rows, HEADS, slots * some), f32),
+            (whole(LANES, width), (LANES, width), f32),
         ]
     )
     result = call(
@@ -1040,7 +1058,7 @@
         (me, *ret_slots, *att_slots, inputs, cotangent, w_out, gain, control, *before),
         positions * 12 / 256,
         {count: 0} if part else None,
-        room=10 if part else 58,
+        room=58,
     )
     do_slots = result[2 : 2 + slot_count]
     return do_slots, result[1], [result[0], *result[2 + slot_count :]]
@@ -1126,7 +1144,6 @@
     small = jnp.pad(jnp.transpose(small), ((0, 0), (0, LANES - 2 - experts)))
     packed = jnp.concatenate([w_qkv, w_out, small], axis=1).astype(bf16)
     packed = Doubling(packed, place, ("seq", "gq", "core"))
-    send_some(x_parts[0], x_rows[0], 1, slots // 2 + 1)
     packed.steps("seq")
     x_rows, x_parts, w_expand, w_shrink = together((x_rows, x_parts, w_expand, w_shrink), packed)
 
@@ -1135,11 +1152,12 @@
             lax.dynamic_index_in_dim(array, member ^ j, 0, keepdims=False) for j in range(members)
         ]
 
-    send_some(x_parts[0], x_rows[0], slots // 2 + 1, slots)
+    send_some(x_parts[0], x_rows[0], 1, slots // 2 + 1)
     weights = member_parts(pack_expert(w_expand.astype(bf16), w_shrink.astype(bf16)))
     weights = swap_slots(weights, "gi")
     packed.steps("gq")
     x_rows, x_parts, weights = together((x_rows, x_parts, weights), packed)
+    send_some(x_parts[0], x_rows[0], slots // 2 + 1, slots)
     packed.at_once("gi")
     weights = jnp.stack(natural(weights, member))
     x_rows, x_parts, weights = together((x_rows, x_parts, weights), packed)
@@ -1155,6 +1173,13 @@
     old = []
     for row in range(rows):
         old = attend_first(me, row, rows, x_rows[row], packed, parts, old)
+        if row == 0:
+            vectors = old[-1]
+            gains = [vectors[0:1], vectors[1:2]]
+            control = natural([vectors[2 + e : 3 + e] for e in range(experts)], member)
+            control = jnp.concatenate(
+                [jnp.broadcast_to(c, (LANES // experts, width)) for c in control], axis=0
+            ).astype(bf16)
         if row + 1 < rows:
             x_rows.append(swap_slots(x_parts[row + 1], "seq"))
             old, x_rows[row + 1] = together((old, x_rows[row + 1]), *halves)
@@ -1162,21 +1187,12 @@
             halves[0].steps("seq")
             halves[1].steps("gq")
         if row == rows - 1:
-            old = together(old, *halves)
-    vectors = jnp.transpose(packed[:, 4 * width :])
-    gain_one = vectors[0:1].astype(f32)
-    gain_two = vectors[1:2].astype(f32)
-    control = natural([vectors[2 + e : 3 + e] for e in range(experts)], member)
-    control = jnp.concatenate(
-        [jnp.broadcast_to(c, (LANES // experts, width)) for c in control], axis=0
-    )
-    att, projected, kept = old[:slots], old[slots : slots + 6], old[slots + 6 :]
+            old, (gain_one, gain_two), control = together((old, gains, control), *halves)
+    att, projected, kept = old[:slots], old[slots : slots + 6], old[slots + 6 : slots + 8]
     att_parts, kept = [swap_slots(att, "seq")], [kept]
     for part in range(1, parts):
         att, more = attend_next(me, part, parts, projected, slots)
-        more, att_parts[-1], gain_one, gain_two, control = hold(
-            (more, att_parts[-1], gain_one, gain_two, control)
-        )
+        more, att_parts[-1] = hold((more, att_parts[-1]))
         att_parts.append(swap_slots(att, "seq"))
         kept.append(more)
     pay_parts = []
@@ -1208,8 +1224,8 @@
     bits = [2] * len(bits_of((("gq", groups),)))
     bits += [members] + [2] * (len(bits_of((("seq", slots),))) - 1)
 
-    def to_bits(keep, other):
-        return (keep.astype(f32) + other.astype(f32)).reshape(*bits, *keep.shape[1:])
+    def to_bits(*terms):
+        return [term.reshape(*bits, *term.shape[1:]) for term in terms]
 
     do_parts, grad_middles, before = [], [], []
     for part in range(parts):

time: 341 us -> 333 us (0.977)
  local copies, waits for them, and re-layouts: 27 us -> 18.8 us
    convert_element_type x0 -> x2, other arithmetic: none -> 4.52 us  [prepare(): self.value = total_of(send).astype(bf16)]
    add x5 -> x3, other arithmetic: 5.35 us -> 1.66 us  [total_of(): return functools.reduce(jnp.add, [term.astype(f32) for term in terms])]
    unnamed x143 -> x130, local copies, waits for them, and re-layouts: 14.8 us -> 11.3 us
  transfers between devices with their start and end apart: 65 -> 65, of which waited for: 23 -> 23; matrix products, arithmetic and copies ran while one was open for 7% -> 5% of each run, Pallas kernels for 43% -> 45%
where the time goes in v5:
time: 333 us; the launch traced here: 328 us
  Pallas kernels  146 us (44%)
  waiting for transfers between devices  80.2 us (24%)
  starting transfers between devices  61.3 us (18%)
  other arithmetic  19 us (6%)
  local copies, waits for them, and re-layouts  18.8 us (6%)
    pallas_call x12, Pallas kernels, call(): pl.pallas_call(kernel, grid_spec=pltpu.PrefetchScalarGridSpec(num_scalar_...  146 us
    ppermute x59, waiting for transfers between devices, partner(): return lax.ppermute(value, axis, [(i, i ^ mask) for i in range(size)])  70.9 us
    ppermute x59, starting transfers between devices, partner(): return lax.ppermute(value, axis, [(i, i ^ mask) for i in range(size)])  53.3 us
    unnamed x130, local copies, waits for them, and re-layouts  11.3 us
    ppermute x6, waiting for transfers between devices, send(): self.value[j] = lax.ppermute(self.value[j], names, pairs)  9.26 us
    ppermute x6, starting transfers between devices, send(): self.value[j] = lax.ppermute(self.value[j], names, pairs)  8.01 us
  transfers between devices with their start and end apart: 65, of which 23 were waited for; matrix products, arithmetic and copies ran while one was open for 5% of the time, Pallas kernels for 45%

profile of v5, /device:TPU:0, one launch (start us, length us, event | category | flops | bytes accessed | tf_op | source)
XLA Modules:
  0.0 327.7 jit_solution(16515987938256876349)
XLA Ops:
  3.8 3.0 collective-permute-start
  7.6 1.7 constant_dynamic-slice_fusion
  11.0 2.7 collective-permute-start.6
  13.9 2.6 collective-permute-start.5
  17.4 2.8 collective-permute-done.6
  20.7 1.6 collective-permute-done.5
  22.4 1.8 collective-permute-done.4
  24.2 3.4 %collective-permute-done.2.refs_3_ = bf16[1,272,512]{2,1,0:T(8,128)(2,1)S(1)} collective-permute-done((bf16[1,272,512]{2,1,0:T(8,128)(2,1)S(1)}, bf16[1,272,512]{2,1,0:T(8,128)(2,1)S(1)}, u32[]{:S(2)}, u32[]{:S(2)}) %collective-permute-start.2) | collective-permute-done | bytes 278560 | tf_op jit(solution)/shard_map/ppermute | solution.py:57
  28.4 2.5 collective-permute-start.9
  32.0 2.1 collective-permute-done.10
  34.1 4.4 %collective-permute-done.9 = bf16[2,2,16,2176]{3,2,1,0:T(8,128)(2,1)S(1)} collective-permute-done((bf16[2,2,16,2176]{3,2,1,0:T(8,128)(2,1)S(1)}, bf16[2,2,16,2176]{3,2,1,0:T(8,128)(2,1)S(1)}, u32[]{:S(2)}, u32[]{:S(2)}) %collective-permute-start.9) | collective-permute-done | bytes 278560 | tf_op jit(solution)/shard_map/ppermute | solution.py:57
  38.5 4.1 %collective-permute-done.8 = bf16[2,2,16,2176]{3,2,1,0:T(8,128)(2,1)S(1)} collective-permute-done((bf16[2,2,16,2176]{3,2,1,0:T(8,128)(2,1)S(1)}, bf16[2,2,16,2176]{3,2,1,0:T(8,128)(2,1)S(1)}, u32[]{:S(2)}, u32[]{:S(2)}) %collective-permute-start.8) | collective-permute-done | bytes 278560 | tf_op jit(solution)/shard_map/ppermute | solution.py:57
  43.7 2.7 collective-permute-done.11
  47.6 3.4 %collective-permute-start.15 = (bf16[4,64,512]{2,1,0:T(8,128)(2,1)S(1)}, bf16[4,64,512]{2,1,0:T(8,128)(2,1)S(1)}, u32[]{:S(2)}, u32[]{:S(2)}) collective-permute-start(bf16[4,64,512]{2,1,0:T(8,128)(2,1)S(1)} %slice.48), channel_id=1, source_target_pairs={{0,16},{16,0},{1,17},{17,1},{2,18},{18,2},{3,19},{19,3},{4,20},{20... | collective-permute-start | bytes 786440 | tf_op jit(solution)/shard_map/ppermute | solution.py:57
  51.6 1.3 collective-permute-start.14
  52.9 10.4 %attend_first.2 = (bf16[2,128,512]{2,1,0:T(8,128)(2,1)S(1)}, bf16[2,128,512]{2,1,0:T(8,128)(2,1)S(1)}, bf16[2,128,512]{2,1,0:T(8,128)(2,1)S(1)}, bf16[2,128,512]...) custom-call(s32[2]{0:T(128)S(1)} %pad_add_fusion.refs_0_, ...), custom_call_target="tpu_custom_call" | custom-call | flops 12000000000 | bytes 1048576 | tf_op jit(solution)/shard_map/attend_first/pallas_call | solution.py:239
  64.2 1.4 collective-permute-done.14.refs_4_
  66.1 10.2 %attend_first.3 = (bf16[2,128,512]{2,1,0:T(8,128)(2,1)S(1)}, bf16[2,128,512]{2,1,0:T(8,128)(2,1)S(1)}, bf16[2,128,512]{2,1,0:T(8,128)(2,1)S(1)}, bf16[2,128,512]...) custom-call(s32[2]{0:T(128)S(1)} %pad_add_fusion.refs_0_, ...), custom_call_target="tpu_custom_call", output_to_operand_aliasing={{0}: (7, {}), {1}: (8, {}), {2}: (9, {}), {3}: (10, {}), {4... | custom-call | flops 12000000000 | bytes 1048576 | tf_op jit(solution)/shard_map/attend_first/pallas_call | solution.py:239
  76.3 1.3 copy-done.34
  77.6 1.3 copy-done.35
  81.0 1.6 collective-permute-start.19
  82.9 14.7 %attend_next.1 = (bf16[2,128,512]{2,1,0:T(8,128)(2,1)S(1)}, bf16[2,128,512]{2,1,0:T(8,128)(2,1)S(1)}, bf16[2,128,512]{2,1,0:T(8,128)(2,1)S(1)}, bf16[2,128,512]{...) custom-call(s32[2]{0:T(128)S(1)} %pad_add_fusion.refs_0_, ...), custom_call_target="tpu_custom_call" | custom-call | flops 14000000000 | bytes 1048576 | tf_op jit(solution)/shard_map/attend_next/pallas_call | solution.py:239
  98.9 1.6 collective-permute-start.22
  100.5 4.3 %mix.2 = (bf16[128,1152]{1,0:T(8,128)(2,1)S(1)}, bf16[128,1152]{1,0:T(8,128)(2,1)S(1)}, bf16[128,1152]{1,0:T(8,128)(2,1)S(1)}, bf16[128,1152]{1,0:T(8,128)(2,1)S(1)}) custom-call(s32[2]{0:T(128)S(1)} %pad_add_fusion.refs_0_, bf16[2,128,512]{2,1,0:T(8,128)(2,1)S(1)} %get-tuple-element.380.refs_1_.refs_5_, ...), custom_call_target="tpu_custom_call" | custom-call | flops 4000000000 | bytes 1048576 | tf_op jit(solution)/shard_map/mix/pallas_call | solution.py:239
  104.9 3.2 collective-permute-done.22.refs_3_.refs_7_
  108.0 4.1 %collective-permute-done.23.refs_4_.refs_8_ = bf16[2,128,512]{2,1,0:T(8,128)(2,1)S(1)} collective-permute-done((bf16[2,128,512]{2,1,0:T(8,128)(2,1)S(1)}, bf16[2,128,512]{2,1,0:T(8,128)(2,1)S(1)}, u32[]{:S(2)}, u32[]{:S(2)}) %collective-permute-start.23) | collective-permute-done | bytes 262176 | tf_op jit(solution)/shard_map/ppermute | solution.py:57
  112.1 1.5 collective-permute-start.27
  114.1 1.5 collective-permute-start.24
  115.6 2.0 collective-permute-start.25
  117.6 4.3 %mix.3 = (bf16[128,1152]{1,0:T(8,128)(2,1)S(1)}, bf16[128,1152]{1,0:T(8,128)(2,1)S(1)}, bf16[128,1152]{1,0:T(8,128)(2,1)S(1)}, bf16[128,1152]{1,0:T(8,128)(2,1)S(1)}) custom-call(s32[2]{0:T(128)S(1)} %pad_add_fusion.refs_0_, bf16[2,128,512]{2,1,0:T(8,128)(2,1)S(1)} %get-tuple-element.395.refs_1_.refs_5_, ...), custom_call_target="tpu_custom_call" | custom-call | flops 4000000000 | bytes 1048576 | tf_op jit(solution)/shard_map/mix/pallas_call | solution.py:239
  121.9 4.6 %collective-permute-done.27 = bf16[2,4,64,512]{3,2,1,0:T(8,128)(2,1)S(1)} collective-permute-done((bf16[2,4,64,512]{3,2,1,0:T(8,128)(2,1)S(1)}, bf16[2,4,64,512]{3,2,1,0:T(8,128)(2,1)S(1)}, u32[]{:S(2)}, u32[]{:S(2)}) %collective-permute-start.27) | collective-permute-done | bytes 524320 | tf_op jit(solution)/shard_map/ppermute | solution.py:57
  126.7 4.2 %collective-permute-done.26.refs_4_ = bf16[128,1152]{1,0:T(8,128)(2,1)S(1)} collective-permute-done((bf16[128,1152]{1,0:T(8,128)(2,1)S(1)}, bf16[128,1152]{1,0:T(8,128)(2,1)S(1)}, u32[]{:S(2)}, u32[]{:S(2)}) %collective-permute-start.26) | collective-permute-done | bytes 294944 | tf_op jit(solution)/shard_map/ppermute | solution.py:57
  131.1 1.5 collective-permute-start.28
  132.6 1.7 collective-permute-start.31
  134.7 5.0 %expert.2 = (bf16[128,1152]{1,0:T(8,128)(2,1)S(1)}, bf16[128,512]{1,0:T(8,128)(2,1)S(1)}, bf16[128,512]{1,0:T(8,128)(2,1)S(1)}, bf16[128,2048]{1,0:T(8,128)(2,1)S(1)}, bf16[128,2048]{1,0:T(8,128)(2,1)S(1)}) custom-call(s32[2]{0:T(128)S(1)} %pad_add_fusion.refs_0_, bf16[128,1152]{1,0:T(8,128)(2,1)S(1)} %get-tuple-element.410.refs_1_, ...), custom_call_target="tpu_custom_call" | custom-call | flops 7000000000 | bytes 1048576 | tf_op jit(solution)/shard_map/expert/pallas_call | solution.py:239
  140.5 2.7 collective-permute-start.35
  144.0 4.9 %collective-permute-done.32.refs_4_ = bf16[128,1152]{1,0:T(8,128)(2,1)S(1)} collective-permute-done((bf16[128,1152]{1,0:T(8,128)(2,1)S(1)}, bf16[128,1152]{1,0:T(8,128)(2,1)S(1)}, u32[]{:S(2)}, u32[]{:S(2)}) %collective-permute-start.32) | collective-permute-done | bytes 294944 | tf_op jit(solution)/shard_map/ppermute | solution.py:57
  148.9 7.5 %expert.3 = (bf16[128,1152]{1,0:T(8,128)(2,1)S(1)}, bf16[16,128,512]{2,1,0:T(8,128)(2,1)S(1)}, bf16[16,128,512]{2,1,0:T(8,128)(2,1)}) custom-call(s32[2]{0:T(128)S(1)} %pad_add_fusion.refs_0_, bf16[128,1152]{1,0:T(8,128)(2,1)S(1)} %get-tuple-element.408.refs_1_, bf16[128,1152]{1,0:T(8,128)(2,1)S(1)} %collective-permute-done.28.refs_2_, ...), custom_call_target="tpu_custom_call" | custom-call | flops 7000000000 | bytes 1048576 | tf_op jit(solution)/shard_map/expert/pallas_call | solution.py:239
  156.5 4.2 %collective-permute-done.34.refs_3_ = bf16[128,1152]{1,0:T(8,128)(2,1)S(1)} collective-permute-done((bf16[128,1152]{1,0:T(8,128)(2,1)S(1)}, bf16[128,1152]{1,0:T(8,128)(2,1)S(1)}, u32[]{:S(2)}, u32[]{:S(2)}) %collective-permute-start.34) | collective-permute-done | bytes 294944 | tf_op jit(solution)/shard_map/ppermute | solution.py:57
  161.5 2.5 collective-permute-start.38
  165.0 11.8 %unmix.2 = (bf16[8,256,512]{2,1,0:T(8,128)(2,1)}, bf16[8,128,512]{2,1,0:T(8,128)(2,1)}, bf16[2,128,512]{2,1,0:T(8,128)(2,1)}, bf16[2,128,512]{2,1,0:T(8,128)(2,1...) custom-call(s32[2]{0:T(128)} %copy-done.24, ...), custom_call_target="tpu_custom_call" | custom-call | flops 6000000000 | bytes 1048576 | tf_op jit(solution)/shard_map/unmix/pallas_call | solution.py:239
  177.5 2.5 fusion
  180.0 1.2 collective-permute-start.42
  182.1 12.1 %unmix.3 = (bf16[8,256,512]{2,1,0:T(8,128)(2,1)}, bf16[8,128,512]{2,1,0:T(8,128)(2,1)}, bf16[2,128,512]{2,1,0:T(8,128)(2,1)}, bf16[2,128,512]{2,1,0:T(8,128)(2,1...) custom-call(s32[2]{0:T(128)} %copy-done.24, ...), custom_call_target="tpu_custom_call", output_to_operand_aliasing={{0}: (14, {})} | custom-call | flops 6000000000 | bytes 1048576 | tf_op jit(solution)/shard_map/unmix/pallas_call | solution.py:239
  196.1 7.8 %collective-permute-done.44.refs_11_ = bf16[2,128,512]{2,1,0:T(8,128)(2,1)S(1)} collective-permute-done((bf16[2,128,512]{2,1,0:T(8,128)(2,1)}, bf16[2,128,512]{2,1,0:T(8,128)(2,1)S(1)}, u32[]{:S(2)}, u32[]{:S(2)}) %collective-permute-start.44) | collective-permute-done | bytes 262176 | tf_op jit(solution)/shard_map/ppermute | solution.py:57
  203.9 4.2 %collective-permute-done.45.refs_12_ = bf16[2,128,512]{2,1,0:T(8,128)(2,1)} collective-permute-done((bf16[2,128,512]{2,1,0:T(8,128)(2,1)}, bf16[2,128,512]{2,1,0:T(8,128)(2,1)}, u32[]{:S(2)}, u32[]{:S(2)}) %collective-permute-start.45) | collective-permute-done | bytes 262176 | tf_op jit(solution)/shard_map/ppermute | solution.py:57
  209.3 28.9 %attend_back.2 = (bf16[1,256,512]{2,1,0:T(8,128)(2,1)}, bf16[1,256,512]{2,1,0:T(8,128)(2,1)}, bf16[1,256,512]{2,1,0:T(8,128)(2,1)}, bf16[1,256,512]{2,1,0:T(8,128)(2,1)}, f32[512,1536]{1,0:T(8,128)}) custom-call(s32[2]{0:T(128)} %copy-done.24, bf16[1,272,512]{2,1,0:T(8,128)(2,1)} %copy-done.4, bf16[1,272,512]{2,1,0:T(8,128)(2,1)} %copy-done.11, ...), custom_call_target="tpu_custom_call" | custom-call | flops 28000000000 | bytes 1048576 | tf_op jit(solution)/shard_map/attend_back/pallas_call | solution.py:239
  239.2 2.0 fusion.2
  241.3 1.5 collective-permute-start.49
  243.1 2.7 collective-permute-start.51
  245.8 30.1 %attend_back.3 = (bf16[1,256,512]{2,1,0:T(8,128)(2,1)}, bf16[1,256,512]{2,1,0:T(8,128)(2,1)}, bf16[1,256,512]{2,1,0:T(8,128)(2,1)}, bf16[1,256,512]{2,1,0:T(8,12...) custom-call(s32[2]{0:T(128)} %copy-done.24, bf16[1,272,512]{2,1,0:T(8,128)(2,1)} %copy-done.3, ...), custom_call_target="tpu_custom_call" | custom-call | flops 28000000000 | bytes 1048576 | tf_op jit(solution)/shard_map/attend_back/pallas_call | solution.py:239
  276.0 1.5 fusion.1
  279.3 2.5 collective-permute-start.57
  282.8 3.8 %collective-permute-done.57 = bf16[128,512]{1,0:T(8,128)(2,1)} collective-permute-done((bf16[128,512]{1,0:T(8,128)(2,1)S(1)}, bf16[128,512]{1,0:T(8,128)(2,1)}, u32[]{:S(2)}, u32[]{:S(2)}) %collective-permute-start.57) | collective-permute-done | bytes 131104 | tf_op jit(solution)/shard_map/ppermute | solution.py:57
  286.6 1.5 collective-permute-start.53
  290.1 4.1 %collective-permute-done.53.refs_7_ = bf16[1,256,512]{2,1,0:T(8,128)(2,1)S(1)} collective-permute-done((bf16[1,256,512]{2,1,0:T(8,128)(2,1)}, bf16[1,256,512]{2,1,0:T(8,128)(2,1)S(1)}, u32[]{:S(2)}, u32[]{:S(2)}) %collective-permute-start.53) | collective-permute-done | bytes 262176 | tf_op jit(solution)/shard_map/ppermute | solution.py:57
  294.3 1.3 convert_add_fusion
  295.9 2.6 collective-permute-start.61
  299.4 1.0 fusion.6
  303.0 2.9 collective-permute-done.61
  305.9 6.4 %collective-permute-done.59 = bf16[2,2,16,2176]{3,2,1,0:T(8,128)(2,1)S(1)} collective-permute-done((bf16[2,2,16,2176]{3,2,1,0:T(8,128)(2,1)S(1)}, bf16[2,2,16,2176]{3,2,1,0:T(8,128)(2,1)S(1)}, u32[]{:S(2)}, u32[]{:S(2)}) %collective-permute-start.59) | collective-permute-done | bytes 278560 | tf_op jit(solution)/shard_map/ppermute | solution.py:220
  312.5 1.3 collective-permute-start.62
  314.0 3.0 collective-permute-start.64
  317.0 7.3 %finish.1 = bf16[8,256,512]{2,1,0:T(8,128)(2,1)} custom-call(s32[2]{0:T(128)S(1)} %copy-done.25, bf16[1,256,512]{2,1,0:T(8,128)(2,1)S(1)} %copy-done.28, bf16[1,256,512]{2,1,0:T(8,128)(2,1)S(1)} %collective-permute-done.48.refs_2_, bf16[1,256,512]{2,1,0:T(8,128)(2,1)S(1)} %collective-permute-done.49.refs_3_, ...), custom_call_target="tpu_custom_call" | custom-call | flops 4000000000 | bytes 1048576 | tf_op jit(solution)/shard_map/finish/pallas_call | solution.py:239
  (279 shorter events, 39.9 us)
Async XLA Ops:
  3.8 7.2 %collective-permute-start = (bf16[16,2176]{1,0:T(8,128)(2,1)S(1)}, bf16[16,2176]{1,0:T(8,128)(2,1)S(1)}, u32[]{:S(2)}, u32[]{:S(2)}) collective-permute-start(bf16[16,2176]{1,0:T(8,128)(2,1)S(1)} %fusion.22), channel_id=1, source_target_pairs={{0,2},{1,3},{2,0},{3,1},{4,6},{5,7},{6,4},{7,5},{8,10},{9,11},{10,... | collective-permute-start | bytes 208904 | tf_op jit(solution)/shard_map/ppermute | solution.py:57
  11.0 9.2 %collective-permute-start.6 = (bf16[2,16,2176]{2,1,0:T(8,128)(2,1)S(1)}, bf16[2,16,2176]{2,1,0:T(8,128)(2,1)S(1)}, u32[]{:S(2)}, u32[]{:S(2)}) collective-permute-start(bf16[2,16,2176]{2,1,0:T(8,128)(2,1)S(1)} %pad_maximum_fusion.18), channel_id=1, source_target_pairs={{0,16},{16,0},{1,17},{17,1},{2,18},{18,2},{3,19},{19,3},{4,20},{20... | collective-permute-start | bytes 417800 | tf_op jit(solution)/shard_map/ppermute | solution.py:57
  13.9 8.5 %collective-permute-start.5 = (bf16[128,512]{1,0:T(8,128)(2,1)S(1)}, bf16[128,512]{1,0:T(8,128)(2,1)S(1)}, u32[]{:S(2)}, u32[]{:S(2)}) collective-permute-start(bf16[128,512]{1,0:T(8,128)(2,1)S(1)} %get-tuple-element.648), channel_id=1, source_target_pairs={{0,12},{4,8},{8,4},{12,0},{1,13},{5,9},{9,5},{13,1},{2,14},{6,10},... | collective-permute-start | bytes 393224 | tf_op jit(solution)/shard_map/ppermute | solution.py:57
  16.4 6.0 %collective-permute-start.3 = (bf16[128,512]{1,0:T(8,128)(2,1)S(1)}, bf16[128,512]{1,0:T(8,128)(2,1)S(1)}, u32[]{:S(2)}, u32[]{:S(2)}) collective-permute-start(bf16[128,512]{1,0:T(8,128)(2,1)S(1)} %get-tuple-element.650), channel_id=1, source_target_pairs={{0,4},{4,0},{8,12},{12,8},{1,5},{5,1},{9,13},{13,9},{2,6},{6,2},{1... | collective-permute-start | bytes 393224 | tf_op jit(solution)/shard_map/ppermute | solution.py:57
  17.0 7.2 %collective-permute-start.4 = (bf16[128,512]{1,0:T(8,128)(2,1)S(1)}, bf16[128,512]{1,0:T(8,128)(2,1)S(1)}, u32[]{:S(2)}, u32[]{:S(2)}) collective-permute-start(bf16[128,512]{1,0:T(8,128)(2,1)S(1)} %get-tuple-element.651), channel_id=1, source_target_pairs={{0,8},{4,12},{8,0},{12,4},{1,9},{5,13},{9,1},{13,5},{2,10},{6,14},... | collective-permute-start | bytes 393224 | tf_op jit(solution)/shard_map/ppermute | solution.py:57
  17.4 6.8 %collective-permute-start.1 = (bf16[1,272,512]{2,1,0:T(8,128)(2,1)S(1)}, bf16[1,272,512]{2,1,0:T(8,128)(2,1)S(1)}, u32[]{:S(2)}, u32[]{:S(2)}) collective-permute-start(bf16[1,272,512]{2,1,0:T(8,128)(2,1)S(1)} %get-tuple-element.283), channel_id=1, source_target_pairs={{0,1},{1,0},{2,3},{3,2},{4,5},{5,4},{6,7},{7,6},{8,9},{9,8},{10,11... | collective-permute-start | bytes 835592 | tf_op jit(solution)/shard_map/ppermute | solution.py:57
  20.2 7.3 %collective-permute-start.2 = (bf16[1,272,512]{2,1,0:T(8,128)(2,1)S(1)}, bf16[1,272,512]{2,1,0:T(8,128)(2,1)S(1)}, u32[]{:S(2)}, u32[]{:S(2)}) collective-permute-start(bf16[1,272,512]{2,1,0:T(8,128)(2,1)S(1)} %get-tuple-element.284), channel_id=1, source_target_pairs={{0,2},{1,3},{2,0},{3,1},{4,6},{5,7},{6,4},{7,5},{8,10},{9,11},{10,... | collective-permute-start | bytes 835592 | tf_op jit(solution)/shard_map/ppermute | solution.py:57
  27.6 6.5 %collective-permute-start.10 = (bf16[2,2,16,2176]{3,2,1,0:T(8,128)(2,1)S(1)}, bf16[2,2,16,2176]{3,2,1,0:T(8,128)(2,1)S(1)}, u32[]{:S(2)}, u32[]{:S(2)}) collective-permute-start(bf16[2,2,16,2176]{3,2,1,0:T(8,128)(2,1)S(1)} %pad_maximum_fusion.17), channel_id=1, source_target_pairs={{0,4},{4,0},{8,12},{12,8},{1,5},{5,1},{9,13},{13,9},{2,6},{6,2},{1... | collective-permute-start | bytes 835592 | tf_op jit(solution)/shard_map/ppermute | solution.py:57
  28.4 10.0 %collective-permute-start.9 = (bf16[2,2,16,2176]{3,2,1,0:T(8,128)(2,1)S(1)}, bf16[2,2,16,2176]{3,2,1,0:T(8,128)(2,1)S(1)}, u32[]{:S(2)}, u32[]{:S(2)}) collective-permute-start(bf16[2,2,16,2176]{3,2,1,0:T(8,128)(2,1)S(1)} %pad_maximum_fusion.17), channel_id=1, source_target_pairs={{0,8},{4,12},{8,0},{12,4},{1,9},{5,13},{9,1},{13,5},{2,10},{6,14},... | collective-permute-start | bytes 835592 | tf_op jit(solution)/shard_map/ppermute | solution.py:57
  30.9 11.7 %collective-permute-start.8 = (bf16[2,2,16,2176]{3,2,1,0:T(8,128)(2,1)S(1)}, bf16[2,2,16,2176]{3,2,1,0:T(8,128)(2,1)S(1)}, u32[]{:S(2)}, u32[]{:S(2)}) collective-permute-start(bf16[2,2,16,2176]{3,2,1,0:T(8,128)(2,1)S(1)} %pad_maximum_fusion.17), channel_id=1, source_target_pairs={{0,12},{4,8},{8,4},{12,0},{1,13},{5,9},{9,5},{13,1},{2,14},{6,10},... | collective-permute-start | bytes 835592 | tf_op jit(solution)/shard_map/ppermute | solution.py:57
  31.1 11.8 %collective-permute-start.7 = (bf16[1,272,512]{2,1,0:T(8,128)(2,1)S(1)}, bf16[1,272,512]{2,1,0:T(8,128)(2,1)S(1)}, u32[]{:S(2)}, u32[]{:S(2)}) collective-permute-start(bf16[1,272,512]{2,1,0:T(8,128)(2,1)S(1)} %get-tuple-element.296), channel_id=1, source_target_pairs={{0,3},{1,2},{2,1},{3,0},{4,7},{5,6},{6,5},{7,4},{8,11},{9,10},{10,... | collective-permute-start | bytes 835592 | tf_op jit(solution)/shard_map/ppermute | solution.py:57
  43.6 2.8 collective-permute-start.11
  47.6 16.4 %collective-permute-start.15 = (bf16[4,64,512]{2,1,0:T(8,128)(2,1)S(1)}, bf16[4,64,512]{2,1,0:T(8,128)(2,1)S(1)}, u32[]{:S(2)}, u32[]{:S(2)}) collective-permute-start(bf16[4,64,512]{2,1,0:T(8,128)(2,1)S(1)} %slice.48), channel_id=1, source_target_pairs={{0,16},{16,0},{1,17},{17,1},{2,18},{18,2},{3,19},{19,3},{4,20},{20... | collective-permute-start | bytes 786440 | tf_op jit(solution)/shard_map/ppermute | solution.py:57
  51.0 13.2 %collective-permute-start.12 = (bf16[1,272,512]{2,1,0:T(8,128)(2,1)S(1)}, bf16[1,272,512]{2,1,0:T(8,128)(2,1)S(1)}, u32[]{:S(2)}, u32[]{:S(2)}) collective-permute-start(bf16[1,272,512]{2,1,0:T(8,128)(2,1)S(1)} %copy-done.52), channel_id=1, source_target_pairs={{0,1},{1,0},{2,3},{3,2},{4,5},{5,4},{6,7},{7,6},{8,9},{9,8},{10,11... | collective-permute-start | bytes 835592 | tf_op jit(solution)/shard_map/ppermute | solution.py:57
  51.0 13.2 %collective-permute-start.13 = (bf16[1,272,512]{2,1,0:T(8,128)(2,1)S(1)}, bf16[1,272,512]{2,1,0:T(8,128)(2,1)S(1)}, u32[]{:S(2)}, u32[]{:S(2)}) collective-permute-start(bf16[1,272,512]{2,1,0:T(8,128)(2,1)S(1)} %copy-done.51), channel_id=1, source_target_pairs={{0,2},{1,3},{2,0},{3,1},{4,6},{5,7},{6,4},{7,5},{8,10},{9,11},{10,... | collective-permute-start | bytes 835592 | tf_op jit(solution)/shard_map/ppermute | solution.py:57
  51.6 14.0 %collective-permute-start.14 = (bf16[1,272,512]{2,1,0:T(8,128)(2,1)S(1)}, bf16[1,272,512]{2,1,0:T(8,128)(2,1)S(1)}, u32[]{:S(2)}, u32[]{:S(2)}) collective-permute-start(bf16[1,272,512]{2,1,0:T(8,128)(2,1)S(1)} %copy-done.50), channel_id=1, source_target_pairs={{0,3},{1,2},{2,1},{3,0},{4,7},{5,6},{6,5},{7,4},{8,11},{9,10},{10,... | collective-permute-start | bytes 835592 | tf_op jit(solution)/shard_map/ppermute | solution.py:57
  65.6 15.0 %collective-permute-start.17 = (bf16[4,64,512]{2,1,0:T(8,128)(2,1)S(1)}, bf16[4,64,512]{2,1,0:T(8,128)(2,1)S(1)}, u32[]{:S(2)}, u32[]{:S(2)}) collective-permute-start(bf16[4,64,512]{2,1,0:T(8,128)(2,1)S(1)} %get-tuple-element.369), channel_id=1, source_target_pairs={{0,16},{16,0},{1,17},{17,1},{2,18},{18,2},{3,19},{19,3},{4,20},{20... | collective-permute-start | bytes 786440 | tf_op jit(solution)/shard_map/ppermute | solution.py:57
  65.6 15.1 %collective-permute-start.16 = (bf16[2,4,64,512]{3,2,1,0:T(8,128)(2,1)S(1)}, bf16[2,4,64,512]{3,2,1,0:T(8,128)(2,1)S(1)}, u32[]{:S(2)}, u32[]{:S(2)}) collective-permute-start(bf16[2,4,64,512]{3,2,1,0:T(8,128)(2,1)S(1)} %pad_maximum_fusion.7), channel_id=1, source_target_pairs={{0,2},{1,3},{2,0},{3,1},{4,6},{5,7},{6,4},{7,5},{8,10},{9,11},{10,... | collective-permute-start | bytes 1572872 | tf_op jit(solution)/shard_map/ppermute | solution.py:57
  81.0 19.5 %collective-permute-start.18 = (bf16[2,128,512]{2,1,0:T(8,128)(2,1)S(1)}, bf16[2,128,512]{2,1,0:T(8,128)(2,1)S(1)}, u32[]{:S(2)}, u32[]{:S(2)}) collective-permute-start(bf16[2,128,512]{2,1,0:T(8,128)(2,1)S(1)} %get-tuple-element.377), channel_id=1, source_target_pairs={{0,1},{1,0},{2,3},{3,2},{4,5},{5,4},{6,7},{7,6},{8,9},{9,8},{10,11... | collective-permute-start | bytes 786440 | tf_op jit(solution)/shard_map/ppermute | solution.py:57
  81.0 19.4 %collective-permute-start.19 = (bf16[2,128,512]{2,1,0:T(8,128)(2,1)S(1)}, bf16[2,128,512]{2,1,0:T(8,128)(2,1)S(1)}, u32[]{:S(2)}, u32[]{:S(2)}) collective-permute-start(bf16[2,128,512]{2,1,0:T(8,128)(2,1)S(1)} %get-tuple-element.378), channel_id=1, source_target_pairs={{0,2},{1,3},{2,0},{3,1},{4,6},{5,7},{6,4},{7,5},{8,10},{9,11},{10,... | collective-permute-start | bytes 786440 | tf_op jit(solution)/shard_map/ppermute | solution.py:57
  82.6 17.9 %collective-permute-start.20 = (bf16[2,128,512]{2,1,0:T(8,128)(2,1)S(1)}, bf16[2,128,512]{2,1,0:T(8,128)(2,1)S(1)}, u32[]{:S(2)}, u32[]{:S(2)}) collective-permute-start(bf16[2,128,512]{2,1,0:T(8,128)(2,1)S(1)} %get-tuple-element.379), channel_id=1, source_target_pairs={{0,3},{1,2},{2,1},{3,0},{4,7},{5,6},{6,5},{7,4},{8,11},{9,10},{10,... | collective-permute-start | bytes 786440 | tf_op jit(solution)/shard_map/ppermute | solution.py:57
  98.5 6.3 %collective-permute-start.21 = (bf16[2,128,512]{2,1,0:T(8,128)(2,1)S(1)}, bf16[2,128,512]{2,1,0:T(8,128)(2,1)S(1)}, u32[]{:S(2)}, u32[]{:S(2)}) collective-permute-start(bf16[2,128,512]{2,1,0:T(8,128)(2,1)S(1)} %get-tuple-element.391), channel_id=1, source_target_pairs={{0,1},{1,0},{2,3},{3,2},{4,5},{5,4},{6,7},{7,6},{8,9},{9,8},{10,11... | collective-permute-start | bytes 786440 | tf_op jit(solution)/shard_map/ppermute | solution.py:57
  98.9 9.2 %collective-permute-start.22 = (bf16[2,128,512]{2,1,0:T(8,128)(2,1)S(1)}, bf16[2,128,512]{2,1,0:T(8,128)(2,1)S(1)}, u32[]{:S(2)}, u32[]{:S(2)}) collective-permute-start(bf16[2,128,512]{2,1,0:T(8,128)(2,1)S(1)} %get-tuple-element.392), channel_id=1, source_target_pairs={{0,2},{1,3},{2,0},{3,1},{4,6},{5,7},{6,4},{7,5},{8,10},{9,11},{10,... | collective-permute-start | bytes 786440 | tf_op jit(solution)/shard_map/ppermute | solution.py:57
  100.4 11.6 %collective-permute-start.23 = (bf16[2,128,512]{2,1,0:T(8,128)(2,1)S(1)}, bf16[2,128,512]{2,1,0:T(8,128)(2,1)S(1)}, u32[]{:S(2)}, u32[]{:S(2)}) collective-permute-start(bf16[2,128,512]{2,1,0:T(8,128)(2,1)S(1)} %get-tuple-element.393), channel_id=1, source_target_pairs={{0,3},{1,2},{2,1},{3,0},{4,7},{5,6},{6,5},{7,4},{8,11},{9,10},{10,... | collective-permute-start | bytes 786440 | tf_op jit(solution)/shard_map/ppermute | solution.py:57
  112.1 14.4 %collective-permute-start.27 = (bf16[2,4,64,512]{3,2,1,0:T(8,128)(2,1)S(1)}, bf16[2,4,64,512]{3,2,1,0:T(8,128)(2,1)S(1)}, u32[]{:S(2)}, u32[]{:S(2)}) collective-permute-start(bf16[2,4,64,512]{3,2,1,0:T(8,128)(2,1)S(1)} %pad_maximum_fusion.8), channel_id=1, source_target_pairs={{0,2},{1,3},{2,0},{3,1},{4,6},{5,7},{6,4},{7,5},{8,10},{9,11},{10,... | collective-permute-start | bytes 1572872 | tf_op jit(solution)/shard_map/ppermute | solution.py:57
  113.7 21.0 %collective-permute-start.29 = (bf16[16,64,512]{2,1,0:T(8,128)(2,1)S(1)}, bf16[16,64,512]{2,1,0:T(8,128)(2,1)S(1)}, u32[]{:S(2)}, u32[]{:S(2)}) collective-permute-start(bf16[16,64,512]{2,1,0:T(8,128)(2,1)S(1)} %bitcast.171), channel_id=1, source_target_pairs={{0,1},{1,0},{2,3},{3,2},{4,5},{5,4},{6,7},{7,6},{8,9},{9,8},{10,11... | collective-permute-start | bytes 3145736 | tf_op jit(solution)/shard_map/ppermute | solution.py:57
  114.1 12.6 %collective-permute-start.24 = (bf16[128,1152]{1,0:T(8,128)(2,1)S(1)}, bf16[128,1152]{1,0:T(8,128)(2,1)S(1)}, u32[]{:S(2)}, u32[]{:S(2)}) collective-permute-start(bf16[128,1152]{1,0:T(8,128)(2,1)S(1)} %get-tuple-element.404), channel_id=1, source_target_pairs={{0,4},{4,0},{8,12},{12,8},{1,5},{5,1},{9,13},{13,9},{2,6},{6,2},{1... | collective-permute-start | bytes 884744 | tf_op jit(solution)/shard_map/ppermute | solution.py:57
  115.6 11.1 %collective-permute-start.25 = (bf16[128,1152]{1,0:T(8,128)(2,1)S(1)}, bf16[128,1152]{1,0:T(8,128)(2,1)S(1)}, u32[]{:S(2)}, u32[]{:S(2)}) collective-permute-start(bf16[128,1152]{1,0:T(8,128)(2,1)S(1)} %get-tuple-element.405), channel_id=1, source_target_pairs={{0,8},{4,12},{8,0},{12,4},{1,9},{5,13},{9,1},{13,5},{2,10},{6,14},... | collective-permute-start | bytes 884744 | tf_op jit(solution)/shard_map/ppermute | solution.py:57
  117.6 13.3 %collective-permute-start.26 = (bf16[128,1152]{1,0:T(8,128)(2,1)S(1)}, bf16[128,1152]{1,0:T(8,128)(2,1)S(1)}, u32[]{:S(2)}, u32[]{:S(2)}) collective-permute-start(bf16[128,1152]{1,0:T(8,128)(2,1)S(1)} %get-tuple-element.406), channel_id=1, source_target_pairs={{0,12},{4,8},{8,4},{12,0},{1,13},{5,9},{9,5},{13,1},{2,14},{6,10},... | collective-permute-start | bytes 884744 | tf_op jit(solution)/shard_map/ppermute | solution.py:57
  131.0 3.6 %collective-permute-start.30 = (bf16[16,64,512]{2,1,0:T(8,128)(2,1)S(1)}, bf16[16,64,512]{2,1,0:T(8,128)(2,1)S(1)}, u32[]{:S(2)}, u32[]{:S(2)}) collective-permute-start(bf16[16,64,512]{2,1,0:T(8,128)(2,1)S(1)} %bitcast.174), channel_id=1, source_target_pairs={{0,1},{1,0},{2,3},{3,2},{4,5},{5,4},{6,7},{7,6},{8,9},{9,8},{10,11... | collective-permute-start | bytes 3145736 | tf_op jit(solution)/shard_map/ppermute | solution.py:57
  131.1 9.4 %collective-permute-start.28 = (bf16[128,1152]{1,0:T(8,128)(2,1)S(1)}, bf16[128,1152]{1,0:T(8,128)(2,1)S(1)}, u32[]{:S(2)}, u32[]{:S(2)}) collective-permute-start(bf16[128,1152]{1,0:T(8,128)(2,1)S(1)} %get-tuple-element.409), channel_id=1, source_target_pairs={{0,4},{4,0},{8,12},{12,8},{1,5},{5,1},{9,13},{13,9},{2,6},{6,2},{1... | collective-permute-start | bytes 884744 | tf_op jit(solution)/shard_map/ppermute | solution.py:57
  132.6 11.4 %collective-permute-start.31 = (bf16[128,1152]{1,0:T(8,128)(2,1)S(1)}, bf16[128,1152]{1,0:T(8,128)(2,1)S(1)}, u32[]{:S(2)}, u32[]{:S(2)}) collective-permute-start(bf16[128,1152]{1,0:T(8,128)(2,1)S(1)} %get-tuple-element.418), channel_id=1, source_target_pairs={{0,8},{4,12},{8,0},{12,4},{1,9},{5,13},{9,1},{13,5},{2,10},{6,14},... | collective-permute-start | bytes 884744 | tf_op jit(solution)/shard_map/ppermute | solution.py:57
  134.4 14.5 %collective-permute-start.32 = (bf16[128,1152]{1,0:T(8,128)(2,1)S(1)}, bf16[128,1152]{1,0:T(8,128)(2,1)S(1)}, u32[]{:S(2)}, u32[]{:S(2)}) collective-permute-start(bf16[128,1152]{1,0:T(8,128)(2,1)S(1)} %get-tuple-element.419), channel_id=1, source_target_pairs={{0,12},{4,8},{8,4},{12,0},{1,13},{5,9},{9,5},{13,1},{2,14},{6,10},... | collective-permute-start | bytes 884744 | tf_op jit(solution)/shard_map/ppermute | solution.py:57
  140.5 16.0 %collective-permute-start.35 = (bf16[128,1152]{1,0:T(8,128)(2,1)S(1)}, bf16[128,1152]{1,0:T(8,128)(2,1)S(1)}, u32[]{:S(2)}, u32[]{:S(2)}) collective-permute-start(bf16[128,1152]{1,0:T(8,128)(2,1)S(1)} %get-tuple-element.429.refs_1_), channel_id=1, source_target_pairs={{0,12},{4,8},{8,4},{12,0},{1,13},{5,9},{9,5},{13,1},{2,14},{6,10},... | collective-permute-start | bytes 884744 | tf_op jit(solution)/shard_map/ppermute | solution.py:57
  143.2 17.5 %collective-permute-start.34 = (bf16[128,1152]{1,0:T(8,128)(2,1)S(1)}, bf16[128,1152]{1,0:T(8,128)(2,1)S(1)}, u32[]{:S(2)}, u32[]{:S(2)}) collective-permute-start(bf16[128,1152]{1,0:T(8,128)(2,1)S(1)} %get-tuple-element.429.refs_1_), channel_id=1, source_target_pairs={{0,8},{4,12},{8,0},{12,4},{1,9},{5,13},{9,1},{13,5},{2,10},{6,14},... | collective-permute-start | bytes 884744 | tf_op jit(solution)/shard_map/ppermute | solution.py:57
  143.5 17.3 %collective-permute-start.33 = (bf16[128,1152]{1,0:T(8,128)(2,1)S(1)}, bf16[128,1152]{1,0:T(8,128)(2,1)S(1)}, u32[]{:S(2)}, u32[]{:S(2)}) collective-permute-start(bf16[128,1152]{1,0:T(8,128)(2,1)S(1)} %get-tuple-element.429.refs_1_), channel_id=1, source_target_pairs={{0,4},{4,0},{8,12},{12,8},{1,5},{5,1},{9,13},{13,9},{2,6},{6,2},{1... | collective-permute-start | bytes 884744 | tf_op jit(solution)/shard_map/ppermute | solution.py:57
  161.5 15.4 %collective-permute-start.39 = (bf16[16,128,512]{2,1,0:T(8,128)(2,1)}, bf16[16,128,512]{2,1,0:T(8,128)(2,1)}, u32[]{:S(2)}, u32[]{:S(2)}) collective-permute-start(bf16[16,128,512]{2,1,0:T(8,128)(2,1)} %get-tuple-element.438), channel_id=1, source_target_pairs={{0,1},{1,0},{2,3},{3,2},{4,5},{5,4},{6,7},{7,6},{8,9},{9,8},{10,11... | collective-permute-start | bytes 6291464 | tf_op jit(solution)/shard_map/ppermute | solution.py:57
  161.5 18.5 %collective-permute-start.38 = (bf16[128,1152]{1,0:T(8,128)(2,1)S(1)}, bf16[128,1152]{1,0:T(8,128)(2,1)S(1)}, u32[]{:S(2)}, u32[]{:S(2)}) collective-permute-start(bf16[128,1152]{1,0:T(8,128)(2,1)S(1)} %get-tuple-element.439.refs_1_), channel_id=1, source_target_pairs={{0,12},{4,8},{8,4},{12,0},{1,13},{5,9},{9,5},{13,1},{2,14},{6,10},... | collective-permute-start | bytes 884744 | tf_op jit(solution)/shard_map/ppermute | solution.py:57
  164.0 17.2 %collective-permute-start.37 = (bf16[128,1152]{1,0:T(8,128)(2,1)S(1)}, bf16[128,1152]{1,0:T(8,128)(2,1)S(1)}, u32[]{:S(2)}, u32[]{:S(2)}) collective-permute-start(bf16[128,1152]{1,0:T(8,128)(2,1)S(1)} %get-tuple-element.439.refs_1_), channel_id=1, source_target_pairs={{0,8},{4,12},{8,0},{12,4},{1,9},{5,13},{9,1},{13,5},{2,10},{6,14},... | collective-permute-start | bytes 884744 | tf_op jit(solution)/shard_map/ppermute | solution.py:57
  164.3 16.9 %collective-permute-start.36 = (bf16[128,1152]{1,0:T(8,128)(2,1)S(1)}, bf16[128,1152]{1,0:T(8,128)(2,1)S(1)}, u32[]{:S(2)}, u32[]{:S(2)}) collective-permute-start(bf16[128,1152]{1,0:T(8,128)(2,1)S(1)} %get-tuple-element.439.refs_1_), channel_id=1, source_target_pairs={{0,4},{4,0},{8,12},{12,8},{1,5},{5,1},{9,13},{13,9},{2,6},{6,2},{1... | collective-permute-start | bytes 884744 | tf_op jit(solution)/shard_map/ppermute | solution.py:57
  176.8 18.3 %collective-permute-start.40 = (bf16[2,128,512]{2,1,0:T(8,128)(2,1)}, bf16[2,128,512]{2,1,0:T(8,128)(2,1)S(1)}, u32[]{:S(2)}, u32[]{:S(2)}) collective-permute-start(bf16[2,128,512]{2,1,0:T(8,128)(2,1)} %get-tuple-element.449), channel_id=1, source_target_pairs={{0,1},{1,0},{2,3},{3,2},{4,5},{5,4},{6,7},{7,6},{8,9},{9,8},{10,11... | collective-permute-start | bytes 786440 | tf_op jit(solution)/shard_map/ppermute | solution.py:57
  176.9 19.2 %collective-permute-start.41 = (bf16[2,128,512]{2,1,0:T(8,128)(2,1)}, bf16[2,128,512]{2,1,0:T(8,128)(2,1)S(1)}, u32[]{:S(2)}, u32[]{:S(2)}) collective-permute-start(bf16[2,128,512]{2,1,0:T(8,128)(2,1)} %get-tuple-element.450), channel_id=1, source_target_pairs={{0,2},{1,3},{2,0},{3,1},{4,6},{5,7},{6,4},{7,5},{8,10},{9,11},{10,... | collective-permute-start | bytes 786440 | tf_op jit(solution)/shard_map/ppermute | solution.py:57
  180.0 16.1 %collective-permute-start.42 = (bf16[2,128,512]{2,1,0:T(8,128)(2,1)}, bf16[2,128,512]{2,1,0:T(8,128)(2,1)}, u32[]{:S(2)}, u32[]{:S(2)}) collective-permute-start(bf16[2,128,512]{2,1,0:T(8,128)(2,1)} %get-tuple-element.451), channel_id=1, source_target_pairs={{0,3},{1,2},{2,1},{3,0},{4,7},{5,6},{6,5},{7,4},{8,11},{9,10},{10,... | collective-permute-start | bytes 786440 | tf_op jit(solution)/shard_map/ppermute | solution.py:57
  194.6 9.4 %collective-permute-start.44 = (bf16[2,128,512]{2,1,0:T(8,128)(2,1)}, bf16[2,128,512]{2,1,0:T(8,128)(2,1)S(1)}, u32[]{:S(2)}, u32[]{:S(2)}) collective-permute-start(bf16[2,128,512]{2,1,0:T(8,128)(2,1)} %get-tuple-element.454), channel_id=1, source_target_pairs={{0,2},{1,3},{2,0},{3,1},{4,6},{5,7},{6,4},{7,5},{8,10},{9,11},{10,... | collective-permute-start | bytes 786440 | tf_op jit(solution)/shard_map/ppermute | solution.py:57
  195.1 13.0 %collective-permute-start.45 = (bf16[2,128,512]{2,1,0:T(8,128)(2,1)}, bf16[2,128,512]{2,1,0:T(8,128)(2,1)}, u32[]{:S(2)}, u32[]{:S(2)}) collective-permute-start(bf16[2,128,512]{2,1,0:T(8,128)(2,1)} %get-tuple-element.455), channel_id=1, source_target_pairs={{0,3},{1,2},{2,1},{3,0},{4,7},{5,6},{6,5},{7,4},{8,11},{9,10},{10,... | collective-permute-start | bytes 786440 | tf_op jit(solution)/shard_map/ppermute | solution.py:57
  208.1 30.1 %collective-permute-start.46 = (bf16[16,16,640]{2,1,0:T(8,128)(2,1)}, bf16[16,16,640]{2,1,0:T(8,128)(2,1)S(1)}, u32[]{:S(2)}, u32[]{:S(2)}) collective-permute-start(bf16[16,16,640]{2,1,0:T(8,128)(2,1)} %get-tuple-element.478), channel_id=1, source_target_pairs={{0,1},{1,0},{2,3},{3,2},{4,5},{5,4},{6,7},{7,6},{8,9},{9,8},{10,11... | collective-permute-start | bytes 983048 | tf_op jit(solution)/shard_map/ppermute | solution.py:57
  208.7 29.5 %collective-permute-start.47 = (bf16[2,4,128,512]{3,2,1,0:T(8,128)(2,1)}, bf16[2,4,128,512]{3,2,1,0:T(8,128)(2,1)S(1)}, u32[]{:S(2)}, u32[]{:S(2)}) collective-permute-start(bf16[2,4,128,512]{3,2,1,0:T(8,128)(2,1)} %fusion), channel_id=1, source_target_pairs={{0,2},{1,3},{2,0},{3,1},{4,6},{5,7},{6,4},{7,5},{8,10},{9,11},{10,... | collective-permute-start | bytes 3145736 | tf_op jit(solution)/shard_map/ppermute | solution.py:57
  241.3 34.6 %collective-permute-start.48 = (bf16[1,256,512]{2,1,0:T(8,128)(2,1)}, bf16[1,256,512]{2,1,0:T(8,128)(2,1)S(1)}, u32[]{:S(2)}, u32[]{:S(2)}) collective-permute-start(bf16[1,256,512]{2,1,0:T(8,128)(2,1)} %get-tuple-element.494), channel_id=1, source_target_pairs={{0,1},{1,0},{2,3},{3,2},{4,5},{5,4},{6,7},{7,6},{8,9},{9,8},{10,11... | collective-permute-start | bytes 786440 | tf_op jit(solution)/shard_map/ppermute | solution.py:57
  241.3 34.6 %collective-permute-start.49 = (bf16[1,256,512]{2,1,0:T(8,128)(2,1)}, bf16[1,256,512]{2,1,0:T(8,128)(2,1)S(1)}, u32[]{:S(2)}, u32[]{:S(2)}) collective-permute-start(bf16[1,256,512]{2,1,0:T(8,128)(2,1)} %get-tuple-element.495), channel_id=1, source_target_pairs={{0,2},{1,3},{2,0},{3,1},{4,6},{5,7},{6,4},{7,5},{8,10},{9,11},{10,... | collective-permute-start | bytes 786440 | tf_op jit(solution)/shard_map/ppermute | solution.py:57
  242.8 33.2 %collective-permute-start.50 = (bf16[1,256,512]{2,1,0:T(8,128)(2,1)}, bf16[1,256,512]{2,1,0:T(8,128)(2,1)S(1)}, u32[]{:S(2)}, u32[]{:S(2)}) collective-permute-start(bf16[1,256,512]{2,1,0:T(8,128)(2,1)} %get-tuple-element.496), channel_id=1, source_target_pairs={{0,3},{1,2},{2,1},{3,0},{4,7},{5,6},{6,5},{7,4},{8,11},{9,10},{10,... | collective-permute-start | bytes 786440 | tf_op jit(solution)/shard_map/ppermute | solution.py:57
  243.1 32.8 %collective-permute-start.51 = (bf16[4,128,512]{2,1,0:T(8,128)(2,1)}, bf16[4,128,512]{2,1,0:T(8,128)(2,1)S(1)}, u32[]{:S(2)}, u32[]{:S(2)}) collective-permute-start(bf16[4,128,512]{2,1,0:T(8,128)(2,1)} %fusion.2), channel_id=1, source_target_pairs={{0,16},{16,0},{1,17},{17,1},{2,18},{18,2},{3,19},{19,3},{4,20},{20... | collective-permute-start | bytes 1572872 | tf_op jit(solution)/shard_map/ppermute | solution.py:57
  276.0 18.3 %collective-permute-start.54 = (bf16[16,16,1536]{2,1,0:T(8,128)(2,1)}, bf16[16,16,1536]{2,1,0:T(8,128)(2,1)}, u32[]{:S(2)}, u32[]{:S(2)}) collective-permute-start(bf16[16,16,1536]{2,1,0:T(8,128)(2,1)} %get-tuple-element.506), channel_id=1, source_target_pairs={{0,1},{1,0},{2,3},{3,2},{4,5},{5,4},{6,7},{7,6},{8,9},{9,8},{10,11... | collective-permute-start | bytes 2359304 | tf_op jit(solution)/shard_map/ppermute | solution.py:57
  279.3 7.3 %collective-permute-start.57 = (bf16[128,512]{1,0:T(8,128)(2,1)S(1)}, bf16[128,512]{1,0:T(8,128)(2,1)}, u32[]{:S(2)}, u32[]{:S(2)}) collective-permute-start(bf16[128,512]{1,0:T(8,128)(2,1)S(1)} %get-tuple-element.625), channel_id=1, source_target_pairs={{0,12},{4,8},{8,4},{12,0},{1,13},{5,9},{9,5},{13,1},{2,14},{6,10},... | collective-permute-start | bytes 393224 | tf_op jit(solution)/shard_map/ppermute | solution.py:57
  281.8 8.3 %collective-permute-start.56 = (bf16[128,512]{1,0:T(8,128)(2,1)}, bf16[128,512]{1,0:T(8,128)(2,1)S(1)}, u32[]{:S(2)}, u32[]{:S(2)}) collective-permute-start(bf16[128,512]{1,0:T(8,128)(2,1)} %get-tuple-element.626), channel_id=1, source_target_pairs={{0,8},{4,12},{8,0},{12,4},{1,9},{5,13},{9,1},{13,5},{2,10},{6,14},... | collective-permute-start | bytes 393224 | tf_op jit(solution)/shard_map/ppermute | solution.py:57
  282.1 8.0 %collective-permute-start.55 = (bf16[128,512]{1,0:T(8,128)(2,1)}, bf16[128,512]{1,0:T(8,128)(2,1)S(1)}, u32[]{:S(2)}, u32[]{:S(2)}) collective-permute-start(bf16[128,512]{1,0:T(8,128)(2,1)} %get-tuple-element.627), channel_id=1, source_target_pairs={{0,4},{4,0},{8,12},{12,8},{1,5},{5,1},{9,13},{13,9},{2,6},{6,2},{1... | collective-permute-start | bytes 393224 | tf_op jit(solution)/shard_map/ppermute | solution.py:57
  282.8 7.3 %collective-permute-start.52 = (bf16[1,256,512]{2,1,0:T(8,128)(2,1)}, bf16[1,256,512]{2,1,0:T(8,128)(2,1)S(1)}, u32[]{:S(2)}, u32[]{:S(2)}) collective-permute-start(bf16[1,256,512]{2,1,0:T(8,128)(2,1)} %get-tuple-element.503), channel_id=1, source_target_pairs={{0,1},{1,0},{2,3},{3,2},{4,5},{5,4},{6,7},{7,6},{8,9},{9,8},{10,11... | collective-permute-start | bytes 786440 | tf_op jit(solution)/shard_map/ppermute | solution.py:57
  286.6 7.6 %collective-permute-start.53 = (bf16[1,256,512]{2,1,0:T(8,128)(2,1)}, bf16[1,256,512]{2,1,0:T(8,128)(2,1)S(1)}, u32[]{:S(2)}, u32[]{:S(2)}) collective-permute-start(bf16[1,256,512]{2,1,0:T(8,128)(2,1)} %get-tuple-element.504), channel_id=1, source_target_pairs={{0,2},{1,3},{2,0},{3,1},{4,6},{5,7},{6,4},{7,5},{8,10},{9,11},{10,... | collective-permute-start | bytes 786440 | tf_op jit(solution)/shard_map/ppermute | solution.py:57
  294.2 8.8 %collective-permute-start.58 = (bf16[1,256,512]{2,1,0:T(8,128)(2,1)}, bf16[1,256,512]{2,1,0:T(8,128)(2,1)S(1)}, u32[]{:S(2)}, u32[]{:S(2)}) collective-permute-start(bf16[1,256,512]{2,1,0:T(8,128)(2,1)} %get-tuple-element.515), channel_id=1, source_target_pairs={{0,3},{1,2},{2,1},{3,0},{4,7},{5,6},{6,5},{7,4},{8,11},{9,10},{10,... | collective-permute-start | bytes 786440 | tf_op jit(solution)/shard_map/ppermute | solution.py:57
  295.9 10.0 %collective-permute-start.61 = (bf16[2,2,16,2176]{3,2,1,0:T(8,128)(2,1)S(1)}, bf16[2,2,16,2176]{3,2,1,0:T(8,128)(2,1)S(1)}, u32[]{:S(2)}, u32[]{:S(2)}) collective-permute-start(bf16[2,2,16,2176]{3,2,1,0:T(8,128)(2,1)S(1)} %get-tuple-element.606), channel_id=1, source_target_pairs={{0,12},{4,8},{8,4},{12,0},{1,13},{5,9},{9,5},{13,1},{2,14},{6,10},... | collective-permute-start | bytes 835592 | tf_op jit(solution)/shard_map/ppermute | solution.py:220
  298.5 13.8 %collective-permute-start.59 = (bf16[2,2,16,2176]{3,2,1,0:T(8,128)(2,1)S(1)}, bf16[2,2,16,2176]{3,2,1,0:T(8,128)(2,1)S(1)}, u32[]{:S(2)}, u32[]{:S(2)}) collective-permute-start(bf16[2,2,16,2176]{3,2,1,0:T(8,128)(2,1)S(1)} %get-tuple-element.607), channel_id=1, source_target_pairs={{0,4},{4,0},{8,12},{12,8},{1,5},{5,1},{9,13},{13,9},{2,6},{6,2},{1... | collective-permute-start | bytes 835592 | tf_op jit(solution)/shard_map/ppermute | solution.py:220
  299.1 13.2 %collective-permute-start.60 = (bf16[2,2,16,2176]{3,2,1,0:T(8,128)(2,1)S(1)}, bf16[2,2,16,2176]{3,2,1,0:T(8,128)(2,1)S(1)}, u32[]{:S(2)}, u32[]{:S(2)}) collective-permute-start(bf16[2,2,16,2176]{3,2,1,0:T(8,128)(2,1)S(1)} %get-tuple-element.608), channel_id=1, source_target_pairs={{0,8},{4,12},{8,0},{12,4},{1,9},{5,13},{9,1},{13,5},{2,10},{6,14},... | collective-permute-start | bytes 835592 | tf_op jit(solution)/shard_map/ppermute | solution.py:220
  312.5 11.8 %collective-permute-start.62 = (bf16[16,2176]{1,0:T(8,128)(2,1)S(1)}, bf16[16,2176]{1,0:T(8,128)(2,1)S(1)}, u32[]{:S(2)}, u32[]{:S(2)}) collective-permute-start(bf16[16,2176]{1,0:T(8,128)(2,1)S(1)} %get-tuple-element.543), channel_id=1, source_target_pairs={{0,2},{1,3},{2,0},{3,1},{16,18},{17,19},{18,16},{19,17},{4,6},{5,7... | collective-permute-start | bytes 208904 | tf_op jit(solution)/shard_map/ppermute | solution.py:220
  313.7 10.5 %collective-permute-start.63 = (bf16[16,2176]{1,0:T(8,128)(2,1)S(1)}, bf16[16,2176]{1,0:T(8,128)(2,1)S(1)}, u32[]{:S(2)}, u32[]{:S(2)}) collective-permute-start(bf16[16,2176]{1,0:T(8,128)(2,1)S(1)} %get-tuple-element.544), channel_id=1, source_target_pairs={{0,16},{1,17},{2,18},{3,19},{16,0},{17,1},{18,2},{19,3},{4,20},{5,... | collective-permute-start | bytes 208904 | tf_op jit(solution)/shard_map/ppermute | solution.py:220
  314.0 10.3 %collective-permute-start.64 = (bf16[16,2176]{1,0:T(8,128)(2,1)S(1)}, bf16[16,2176]{1,0:T(8,128)(2,1)S(1)}, u32[]{:S(2)}, u32[]{:S(2)}) collective-permute-start(bf16[16,2176]{1,0:T(8,128)(2,1)S(1)} %get-tuple-element.545), channel_id=1, source_target_pairs={{0,18},{1,19},{2,16},{3,17},{16,2},{17,3},{18,0},{19,1},{4,22},{5,... | collective-permute-start | bytes 208904 | tf_op jit(solution)/shard_map/ppermute | solution.py:220
  (65 other events, 906.4 us)

commit v6 on v5

--- a/solution.py
+++ b/solution.py
@@ -1300,13 +1300,11 @@
     sum_in = Halving(total, place, ("gi", "gq", "seq"))
     sum_in.cut(("gi",))
     sum_in.send()
-    gf_rows = together(gf_rows, sum_in)
+    grad_inputs = finish(me, gf_rows, inputs, grad_middles, gain_one)
+    grad_inputs = together(grad_inputs, sum_in)
     sum_in.combine()
     sum_in.cut(("gq", "seq"))
-    gf_rows = together(gf_rows, sum_in)
     sum_in.send()
-    grad_inputs = finish(me, gf_rows, inputs, grad_middles, gain_one)
-    grad_inputs = together(grad_inputs, sum_in)
     sum_in.combine()
     columns = natural(columns, member)
     columns = jnp.stack([c.astype(f32) for c in columns])

time: 333 us -> 331 us (level)
    unnamed x130 -> x122, local copies, waits for them, and re-layouts: 11.3 us -> 10.2 us
  transfers between devices with their start and end apart: 65 -> 65, of which waited for: 23 -> 24; matrix products, arithmetic and copies ran while one was open for 5% -> 5% of each run, Pallas kernels for 45% -> 45%
where the time goes in v6:
time: 331 us; the launch traced here: 325 us
  Pallas kernels  146 us (44%)
  waiting for transfers between devices  79 us (24%)
  starting transfers between devices  61.4 us (19%)
  other arithmetic  18.5 us (6%)
  local copies, waits for them, and re-layouts  17.6 us (5%)
    pallas_call x12, Pallas kernels, call(): pl.pallas_call(kernel, grid_spec=pltpu.PrefetchScalarGridSpec(num_scalar_...  146 us
    ppermute x59, waiting for transfers between devices, partner(): return lax.ppermute(value, axis, [(i, i ^ mask) for i in range(size)])  72.4 us
    ppermute x59, starting transfers between devices, partner(): return lax.ppermute(value, axis, [(i, i ^ mask) for i in range(size)])  53.4 us
    unnamed x122, local copies, waits for them, and re-layouts  10.2 us
    ppermute x6, starting transfers between devices, send(): self.value[j] = lax.ppermute(self.value[j], names, pairs)  8.07 us
    ppermute x6, waiting for transfers between devices, send(): self.value[j] = lax.ppermute(self.value[j], names, pairs)  6.64 us
  transfers between devices with their start and end apart: 65, of which 24 were waited for; matrix products, arithmetic and copies ran while one was open for 5% of the time, Pallas kernels for 45%

profile of v6, /device:TPU:0, one launch (start us, length us, event | category | flops | bytes accessed | tf_op | source)
XLA Modules:
  0.0 325.2 jit_solution(6175731876806351310)
XLA Ops:
  3.8 3.0 collective-permute-start
  7.6 1.7 constant_dynamic-slice_fusion
  11.0 2.7 collective-permute-start.6
  13.9 2.6 collective-permute-start.5
  17.4 2.8 collective-permute-done.6
  20.7 1.6 collective-permute-done.5
  22.4 1.8 collective-permute-done.4
  24.2 3.4 %collective-permute-done.2.refs_3_ = bf16[1,272,512]{2,1,0:T(8,128)(2,1)S(1)} collective-permute-done((bf16[1,272,512]{2,1,0:T(8,128)(2,1)S(1)}, bf16[1,272,512]{2,1,0:T(8,128)(2,1)S(1)}, u32[]{:S(2)}, u32[]{:S(2)}) %collective-permute-start.2) | collective-permute-done | bytes 278560 | tf_op jit(solution)/shard_map/ppermute | solution.py:57
  28.4 2.5 collective-permute-start.9
  32.0 2.1 collective-permute-done.10
  34.1 4.4 %collective-permute-done.9 = bf16[2,2,16,2176]{3,2,1,0:T(8,128)(2,1)S(1)} collective-permute-done((bf16[2,2,16,2176]{3,2,1,0:T(8,128)(2,1)S(1)}, bf16[2,2,16,2176]{3,2,1,0:T(8,128)(2,1)S(1)}, u32[]{:S(2)}, u32[]{:S(2)}) %collective-permute-start.9) | collective-permute-done | bytes 278560 | tf_op jit(solution)/shard_map/ppermute | solution.py:57
  38.5 4.1 %collective-permute-done.8 = bf16[2,2,16,2176]{3,2,1,0:T(8,128)(2,1)S(1)} collective-permute-done((bf16[2,2,16,2176]{3,2,1,0:T(8,128)(2,1)S(1)}, bf16[2,2,16,2176]{3,2,1,0:T(8,128)(2,1)S(1)}, u32[]{:S(2)}, u32[]{:S(2)}) %collective-permute-start.8) | collective-permute-done | bytes 278560 | tf_op jit(solution)/shard_map/ppermute | solution.py:57
  43.7 2.7 collective-permute-done.11
  47.6 3.4 %collective-permute-start.15 = (bf16[4,64,512]{2,1,0:T(8,128)(2,1)S(1)}, bf16[4,64,512]{2,1,0:T(8,128)(2,1)S(1)}, u32[]{:S(2)}, u32[]{:S(2)}) collective-permute-start(bf16[4,64,512]{2,1,0:T(8,128)(2,1)S(1)} %slice.48), channel_id=1, source_target_pairs={{0,16},{16,0},{1,17},{17,1},{2,18},{18,2},{3,19},{19,3},{4,20},{20... | collective-permute-start | bytes 786440 | tf_op jit(solution)/shard_map/ppermute | solution.py:57
  51.6 1.3 collective-permute-start.14
  52.9 10.4 %attend_first.2 = (bf16[2,128,512]{2,1,0:T(8,128)(2,1)S(1)}, bf16[2,128,512]{2,1,0:T(8,128)(2,1)S(1)}, bf16[2,128,512]{2,1,0:T(8,128)(2,1)S(1)}, bf16[2,128,512]...) custom-call(s32[2]{0:T(128)S(1)} %pad_add_fusion.refs_0_, ...), custom_call_target="tpu_custom_call" | custom-call | flops 12000000000 | bytes 1048576 | tf_op jit(solution)/shard_map/attend_first/pallas_call | solution.py:239
  64.2 1.4 collective-permute-done.14.refs_4_
  66.1 10.2 %attend_first.3 = (bf16[2,128,512]{2,1,0:T(8,128)(2,1)S(1)}, bf16[2,128,512]{2,1,0:T(8,128)(2,1)S(1)}, bf16[2,128,512]{2,1,0:T(8,128)(2,1)S(1)}, bf16[2,128,512]...) custom-call(s32[2]{0:T(128)S(1)} %pad_add_fusion.refs_0_, ...), custom_call_target="tpu_custom_call", output_to_operand_aliasing={{0}: (7, {}), {1}: (8, {}), {2}: (9, {}), {3}: (10, {}), {4... | custom-call | flops 12000000000 | bytes 1048576 | tf_op jit(solution)/shard_map/attend_first/pallas_call | solution.py:239
  76.3 1.3 copy-done.34
  77.6 1.3 copy-done.35
  81.0 1.6 collective-permute-start.19
  82.9 14.6 %attend_next.1 = (bf16[2,128,512]{2,1,0:T(8,128)(2,1)S(1)}, bf16[2,128,512]{2,1,0:T(8,128)(2,1)S(1)}, bf16[2,128,512]{2,1,0:T(8,128)(2,1)S(1)}, bf16[2,128,512]{...) custom-call(s32[2]{0:T(128)S(1)} %pad_add_fusion.refs_0_, ...), custom_call_target="tpu_custom_call" | custom-call | flops 14000000000 | bytes 1048576 | tf_op jit(solution)/shard_map/attend_next/pallas_call | solution.py:239
  98.8 1.5 collective-permute-start.22
  100.4 4.3 %mix.2 = (bf16[128,1152]{1,0:T(8,128)(2,1)S(1)}, bf16[128,1152]{1,0:T(8,128)(2,1)S(1)}, bf16[128,1152]{1,0:T(8,128)(2,1)S(1)}, bf16[128,1152]{1,0:T(8,128)(2,1)S(1)}) custom-call(s32[2]{0:T(128)S(1)} %pad_add_fusion.refs_0_, bf16[2,128,512]{2,1,0:T(8,128)(2,1)S(1)} %get-tuple-element.356.refs_1_.refs_5_, ...), custom_call_target="tpu_custom_call" | custom-call | flops 4000000000 | bytes 1048576 | tf_op jit(solution)/shard_map/mix/pallas_call | solution.py:239
  104.7 3.2 collective-permute-done.22.refs_3_.refs_7_
  107.9 4.1 %collective-permute-done.23.refs_4_.refs_8_ = bf16[2,128,512]{2,1,0:T(8,128)(2,1)S(1)} collective-permute-done((bf16[2,128,512]{2,1,0:T(8,128)(2,1)S(1)}, bf16[2,128,512]{2,1,0:T(8,128)(2,1)S(1)}, u32[]{:S(2)}, u32[]{:S(2)}) %collective-permute-start.23) | collective-permute-done | bytes 262176 | tf_op jit(solution)/shard_map/ppermute | solution.py:57
  112.0 1.5 collective-permute-start.27
  114.0 1.5 collective-permute-start.24
  115.5 2.0 collective-permute-start.25
  117.5 4.3 %mix.3 = (bf16[128,1152]{1,0:T(8,128)(2,1)S(1)}, bf16[128,1152]{1,0:T(8,128)(2,1)S(1)}, bf16[128,1152]{1,0:T(8,128)(2,1)S(1)}, bf16[128,1152]{1,0:T(8,128)(2,1)S(1)}) custom-call(s32[2]{0:T(128)S(1)} %pad_add_fusion.refs_0_, bf16[2,128,512]{2,1,0:T(8,128)(2,1)S(1)} %get-tuple-element.371.refs_1_.refs_5_, ...), custom_call_target="tpu_custom_call" | custom-call | flops 4000000000 | bytes 1048576 | tf_op jit(solution)/shard_map/mix/pallas_call | solution.py:239
  121.8 4.6 %collective-permute-done.27 = bf16[2,4,64,512]{3,2,1,0:T(8,128)(2,1)S(1)} collective-permute-done((bf16[2,4,64,512]{3,2,1,0:T(8,128)(2,1)S(1)}, bf16[2,4,64,512]{3,2,1,0:T(8,128)(2,1)S(1)}, u32[]{:S(2)}, u32[]{:S(2)}) %collective-permute-start.27) | collective-permute-done | bytes 524320 | tf_op jit(solution)/shard_map/ppermute | solution.py:57
  126.6 4.1 %collective-permute-done.26.refs_4_ = bf16[128,1152]{1,0:T(8,128)(2,1)S(1)} collective-permute-done((bf16[128,1152]{1,0:T(8,128)(2,1)S(1)}, bf16[128,1152]{1,0:T(8,128)(2,1)S(1)}, u32[]{:S(2)}, u32[]{:S(2)}) %collective-permute-start.26) | collective-permute-done | bytes 294944 | tf_op jit(solution)/shard_map/ppermute | solution.py:57
  130.9 1.6 collective-permute-start.28
  132.5 1.7 collective-permute-start.31
  134.5 5.0 %expert.2 = (bf16[128,1152]{1,0:T(8,128)(2,1)S(1)}, bf16[128,512]{1,0:T(8,128)(2,1)S(1)}, bf16[128,512]{1,0:T(8,128)(2,1)S(1)}, bf16[128,2048]{1,0:T(8,128)(2,1)S(1)}, bf16[128,2048]{1,0:T(8,128)(2,1)S(1)}) custom-call(s32[2]{0:T(128)S(1)} %pad_add_fusion.refs_0_, bf16[128,1152]{1,0:T(8,128)(2,1)S(1)} %get-tuple-element.386.refs_1_, ...), custom_call_target="tpu_custom_call" | custom-call | flops 7000000000 | bytes 1048576 | tf_op jit(solution)/shard_map/expert/pallas_call | solution.py:239
  140.4 2.7 collective-permute-start.35
  143.9 4.9 %collective-permute-done.32.refs_4_ = bf16[128,1152]{1,0:T(8,128)(2,1)S(1)} collective-permute-done((bf16[128,1152]{1,0:T(8,128)(2,1)S(1)}, bf16[128,1152]{1,0:T(8,128)(2,1)S(1)}, u32[]{:S(2)}, u32[]{:S(2)}) %collective-permute-start.32) | collective-permute-done | bytes 294944 | tf_op jit(solution)/shard_map/ppermute | solution.py:57
  148.7 7.6 %expert.3 = (bf16[128,1152]{1,0:T(8,128)(2,1)S(1)}, bf16[16,128,512]{2,1,0:T(8,128)(2,1)S(1)}, bf16[16,128,512]{2,1,0:T(8,128)(2,1)}) custom-call(s32[2]{0:T(128)S(1)} %pad_add_fusion.refs_0_, bf16[128,1152]{1,0:T(8,128)(2,1)S(1)} %get-tuple-element.384.refs_1_, bf16[128,1152]{1,0:T(8,128)(2,1)S(1)} %collective-permute-done.28.refs_2_, ...), custom_call_target="tpu_custom_call" | custom-call | flops 7000000000 | bytes 1048576 | tf_op jit(solution)/shard_map/expert/pallas_call | solution.py:239
  156.4 4.2 %collective-permute-done.34.refs_3_ = bf16[128,1152]{1,0:T(8,128)(2,1)S(1)} collective-permute-done((bf16[128,1152]{1,0:T(8,128)(2,1)S(1)}, bf16[128,1152]{1,0:T(8,128)(2,1)S(1)}, u32[]{:S(2)}, u32[]{:S(2)}) %collective-permute-start.34) | collective-permute-done | bytes 294944 | tf_op jit(solution)/shard_map/ppermute | solution.py:57
  161.4 2.5 collective-permute-start.38
  164.9 11.8 %unmix.2 = (bf16[8,256,512]{2,1,0:T(8,128)(2,1)}, bf16[8,128,512]{2,1,0:T(8,128)(2,1)}, bf16[2,128,512]{2,1,0:T(8,128)(2,1)}, bf16[2,128,512]{2,1,0:T(8,128)(2,1...) custom-call(s32[2]{0:T(128)} %copy-done.24, ...), custom_call_target="tpu_custom_call" | custom-call | flops 6000000000 | bytes 1048576 | tf_op jit(solution)/shard_map/unmix/pallas_call | solution.py:239
  177.4 1.5 fusion
  179.0 1.3 collective-permute-start.42
  181.1 12.2 %unmix.3 = (bf16[8,256,512]{2,1,0:T(8,128)(2,1)}, bf16[8,128,512]{2,1,0:T(8,128)(2,1)}, bf16[2,128,512]{2,1,0:T(8,128)(2,1)}, bf16[2,128,512]{2,1,0:T(8,128)(2,1...) custom-call(s32[2]{0:T(128)} %copy-done.24, ...), custom_call_target="tpu_custom_call", output_to_operand_aliasing={{0}: (14, {})} | custom-call | flops 6000000000 | bytes 1048576 | tf_op jit(solution)/shard_map/unmix/pallas_call | solution.py:239
  195.2 7.9 %collective-permute-done.44.refs_11_ = bf16[2,128,512]{2,1,0:T(8,128)(2,1)} collective-permute-done((bf16[2,128,512]{2,1,0:T(8,128)(2,1)}, bf16[2,128,512]{2,1,0:T(8,128)(2,1)}, u32[]{:S(2)}, u32[]{:S(2)}) %collective-permute-start.44) | collective-permute-done | bytes 262176 | tf_op jit(solution)/shard_map/ppermute | solution.py:57
  203.1 4.1 %collective-permute-done.45.refs_12_ = bf16[2,128,512]{2,1,0:T(8,128)(2,1)} collective-permute-done((bf16[2,128,512]{2,1,0:T(8,128)(2,1)}, bf16[2,128,512]{2,1,0:T(8,128)(2,1)}, u32[]{:S(2)}, u32[]{:S(2)}) %collective-permute-start.45) | collective-permute-done | bytes 262176 | tf_op jit(solution)/shard_map/ppermute | solution.py:57
  208.4 28.9 %attend_back.2 = (bf16[1,256,512]{2,1,0:T(8,128)(2,1)}, bf16[1,256,512]{2,1,0:T(8,128)(2,1)}, bf16[1,256,512]{2,1,0:T(8,128)(2,1)}, bf16[1,256,512]{2,1,0:T(8,128)(2,1)}, f32[512,1536]{1,0:T(8,128)}) custom-call(s32[2]{0:T(128)} %copy-done.24, bf16[1,272,512]{2,1,0:T(8,128)(2,1)} %copy-done.4, bf16[1,272,512]{2,1,0:T(8,128)(2,1)} %copy-done.11, ...), custom_call_target="tpu_custom_call" | custom-call | flops 28000000000 | bytes 1048576 | tf_op jit(solution)/shard_map/attend_back/pallas_call | solution.py:239
  237.3 2.3 fusion.2
  239.6 1.5 collective-permute-start.49
  241.5 2.7 collective-permute-start.51
  244.2 29.9 %attend_back.3 = (bf16[1,256,512]{2,1,0:T(8,128)(2,1)}, bf16[1,256,512]{2,1,0:T(8,128)(2,1)}, bf16[1,256,512]{2,1,0:T(8,128)(2,1)}, bf16[1,256,512]{2,1,0:T(8,12...) custom-call(s32[2]{0:T(128)} %copy-done.24, bf16[1,272,512]{2,1,0:T(8,128)(2,1)} %copy-done.3, ...), custom_call_target="tpu_custom_call" | custom-call | flops 28000000000 | bytes 1048576 | tf_op jit(solution)/shard_map/attend_back/pallas_call | solution.py:239
  274.2 1.5 fusion.1
  277.5 2.5 collective-permute-start.57
  281.0 3.8 %collective-permute-done.57 = bf16[128,512]{1,0:T(8,128)(2,1)} collective-permute-done((bf16[128,512]{1,0:T(8,128)(2,1)S(1)}, bf16[128,512]{1,0:T(8,128)(2,1)}, u32[]{:S(2)}, u32[]{:S(2)}) %collective-permute-start.57) | collective-permute-done | bytes 131104 | tf_op jit(solution)/shard_map/ppermute | solution.py:57
  284.8 1.5 collective-permute-start.53
  288.3 4.1 %collective-permute-done.53.refs_7_ = bf16[1,256,512]{2,1,0:T(8,128)(2,1)S(1)} collective-permute-done((bf16[1,256,512]{2,1,0:T(8,128)(2,1)}, bf16[1,256,512]{2,1,0:T(8,128)(2,1)S(1)}, u32[]{:S(2)}, u32[]{:S(2)}) %collective-permute-start.53) | collective-permute-done | bytes 262176 | tf_op jit(solution)/shard_map/ppermute | solution.py:57
  292.4 1.3 convert_add_fusion
  294.0 2.6 collective-permute-start.61
  299.1 2.1 collective-permute-done.58.refs_8_
  301.2 7.3 %finish.1 = bf16[8,256,512]{2,1,0:T(8,128)(2,1)} custom-call(s32[2]{0:T(128)S(1)} %copy-done.25, bf16[1,256,512]{2,1,0:T(8,128)(2,1)S(1)} %copy-done.28, bf16[1,256,512]{2,1,0:T(8,128)(2,1)S(1)} %collective-permute-done.48.refs_2_, bf16[1,256,512]{2,1,0:T(8,128)(2,1)S(1)} %collective-permute-done.49.refs_3_, ...), custom_call_target="tpu_custom_call" | custom-call | flops 4000000000 | bytes 1048576 | tf_op jit(solution)/shard_map/finish/pallas_call | solution.py:239
  308.5 2.0 collective-permute-done.59
  310.7 1.3 collective-permute-start.62
  312.4 2.7 collective-permute-start.63
  316.8 4.5 %collective-permute-done.64 = bf16[16,2176]{1,0:T(8,128)(2,1)S(1)} collective-permute-done((bf16[16,2176]{1,0:T(8,128)(2,1)S(1)}, bf16[16,2176]{1,0:T(8,128)(2,1)S(1)}, u32[]{:S(2)}, u32[]{:S(2)}) %collective-permute-start.64) | collective-permute-done | bytes 69664 | tf_op jit(solution)/shard_map/ppermute | solution.py:220
  (270 shorter events, 39.9 us)
Async XLA Ops:
  3.8 7.2 %collective-permute-start = (bf16[16,2176]{1,0:T(8,128)(2,1)S(1)}, bf16[16,2176]{1,0:T(8,128)(2,1)S(1)}, u32[]{:S(2)}, u32[]{:S(2)}) collective-permute-start(bf16[16,2176]{1,0:T(8,128)(2,1)S(1)} %fusion.24), channel_id=1, source_target_pairs={{0,2},{1,3},{2,0},{3,1},{4,6},{5,7},{6,4},{7,5},{8,10},{9,11},{10,... | collective-permute-start | bytes 208904 | tf_op jit(solution)/shard_map/ppermute | solution.py:57
  11.0 9.2 %collective-permute-start.6 = (bf16[2,16,2176]{2,1,0:T(8,128)(2,1)S(1)}, bf16[2,16,2176]{2,1,0:T(8,128)(2,1)S(1)}, u32[]{:S(2)}, u32[]{:S(2)}) collective-permute-start(bf16[2,16,2176]{2,1,0:T(8,128)(2,1)S(1)} %pad_maximum_fusion.18), channel_id=1, source_target_pairs={{0,16},{16,0},{1,17},{17,1},{2,18},{18,2},{3,19},{19,3},{4,20},{20... | collective-permute-start | bytes 417800 | tf_op jit(solution)/shard_map/ppermute | solution.py:57
  13.9 8.5 %collective-permute-start.5 = (bf16[128,512]{1,0:T(8,128)(2,1)S(1)}, bf16[128,512]{1,0:T(8,128)(2,1)S(1)}, u32[]{:S(2)}, u32[]{:S(2)}) collective-permute-start(bf16[128,512]{1,0:T(8,128)(2,1)S(1)} %get-tuple-element.600), channel_id=1, source_target_pairs={{0,12},{4,8},{8,4},{12,0},{1,13},{5,9},{9,5},{13,1},{2,14},{6,10},... | collective-permute-start | bytes 393224 | tf_op jit(solution)/shard_map/ppermute | solution.py:57
  16.4 6.0 %collective-permute-start.3 = (bf16[128,512]{1,0:T(8,128)(2,1)S(1)}, bf16[128,512]{1,0:T(8,128)(2,1)S(1)}, u32[]{:S(2)}, u32[]{:S(2)}) collective-permute-start(bf16[128,512]{1,0:T(8,128)(2,1)S(1)} %get-tuple-element.602), channel_id=1, source_target_pairs={{0,4},{4,0},{8,12},{12,8},{1,5},{5,1},{9,13},{13,9},{2,6},{6,2},{1... | collective-permute-start | bytes 393224 | tf_op jit(solution)/shard_map/ppermute | solution.py:57
  17.0 7.2 %collective-permute-start.4 = (bf16[128,512]{1,0:T(8,128)(2,1)S(1)}, bf16[128,512]{1,0:T(8,128)(2,1)S(1)}, u32[]{:S(2)}, u32[]{:S(2)}) collective-permute-start(bf16[128,512]{1,0:T(8,128)(2,1)S(1)} %get-tuple-element.603), channel_id=1, source_target_pairs={{0,8},{4,12},{8,0},{12,4},{1,9},{5,13},{9,1},{13,5},{2,10},{6,14},... | collective-permute-start | bytes 393224 | tf_op jit(solution)/shard_map/ppermute | solution.py:57
  17.4 6.8 %collective-permute-start.1 = (bf16[1,272,512]{2,1,0:T(8,128)(2,1)S(1)}, bf16[1,272,512]{2,1,0:T(8,128)(2,1)S(1)}, u32[]{:S(2)}, u32[]{:S(2)}) collective-permute-start(bf16[1,272,512]{2,1,0:T(8,128)(2,1)S(1)} %get-tuple-element.259), channel_id=1, source_target_pairs={{0,1},{1,0},{2,3},{3,2},{4,5},{5,4},{6,7},{7,6},{8,9},{9,8},{10,11... | collective-permute-start | bytes 835592 | tf_op jit(solution)/shard_map/ppermute | solution.py:57
  20.2 7.3 %collective-permute-start.2 = (bf16[1,272,512]{2,1,0:T(8,128)(2,1)S(1)}, bf16[1,272,512]{2,1,0:T(8,128)(2,1)S(1)}, u32[]{:S(2)}, u32[]{:S(2)}) collective-permute-start(bf16[1,272,512]{2,1,0:T(8,128)(2,1)S(1)} %get-tuple-element.260), channel_id=1, source_target_pairs={{0,2},{1,3},{2,0},{3,1},{4,6},{5,7},{6,4},{7,5},{8,10},{9,11},{10,... | collective-permute-start | bytes 835592 | tf_op jit(solution)/shard_map/ppermute | solution.py:57
  27.6 6.5 %collective-permute-start.10 = (bf16[2,2,16,2176]{3,2,1,0:T(8,128)(2,1)S(1)}, bf16[2,2,16,2176]{3,2,1,0:T(8,128)(2,1)S(1)}, u32[]{:S(2)}, u32[]{:S(2)}) collective-permute-start(bf16[2,2,16,2176]{3,2,1,0:T(8,128)(2,1)S(1)} %pad_maximum_fusion.17), channel_id=1, source_target_pairs={{0,4},{4,0},{8,12},{12,8},{1,5},{5,1},{9,13},{13,9},{2,6},{6,2},{1... | collective-permute-start | bytes 835592 | tf_op jit(solution)/shard_map/ppermute | solution.py:57
  28.4 10.0 %collective-permute-start.9 = (bf16[2,2,16,2176]{3,2,1,0:T(8,128)(2,1)S(1)}, bf16[2,2,16,2176]{3,2,1,0:T(8,128)(2,1)S(1)}, u32[]{:S(2)}, u32[]{:S(2)}) collective-permute-start(bf16[2,2,16,2176]{3,2,1,0:T(8,128)(2,1)S(1)} %pad_maximum_fusion.17), channel_id=1, source_target_pairs={{0,8},{4,12},{8,0},{12,4},{1,9},{5,13},{9,1},{13,5},{2,10},{6,14},... | collective-permute-start | bytes 835592 | tf_op jit(solution)/shard_map/ppermute | solution.py:57
  30.9 11.7 %collective-permute-start.8 = (bf16[2,2,16,2176]{3,2,1,0:T(8,128)(2,1)S(1)}, bf16[2,2,16,2176]{3,2,1,0:T(8,128)(2,1)S(1)}, u32[]{:S(2)}, u32[]{:S(2)}) collective-permute-start(bf16[2,2,16,2176]{3,2,1,0:T(8,128)(2,1)S(1)} %pad_maximum_fusion.17), channel_id=1, source_target_pairs={{0,12},{4,8},{8,4},{12,0},{1,13},{5,9},{9,5},{13,1},{2,14},{6,10},... | collective-permute-start | bytes 835592 | tf_op jit(solution)/shard_map/ppermute | solution.py:57
  31.1 11.8 %collective-permute-start.7 = (bf16[1,272,512]{2,1,0:T(8,128)(2,1)S(1)}, bf16[1,272,512]{2,1,0:T(8,128)(2,1)S(1)}, u32[]{:S(2)}, u32[]{:S(2)}) collective-permute-start(bf16[1,272,512]{2,1,0:T(8,128)(2,1)S(1)} %get-tuple-element.272), channel_id=1, source_target_pairs={{0,3},{1,2},{2,1},{3,0},{4,7},{5,6},{6,5},{7,4},{8,11},{9,10},{10,... | collective-permute-start | bytes 835592 | tf_op jit(solution)/shard_map/ppermute | solution.py:57
  43.6 2.8 collective-permute-start.11
  47.6 16.4 %collective-permute-start.15 = (bf16[4,64,512]{2,1,0:T(8,128)(2,1)S(1)}, bf16[4,64,512]{2,1,0:T(8,128)(2,1)S(1)}, u32[]{:S(2)}, u32[]{:S(2)}) collective-permute-start(bf16[4,64,512]{2,1,0:T(8,128)(2,1)S(1)} %slice.48), channel_id=1, source_target_pairs={{0,16},{16,0},{1,17},{17,1},{2,18},{18,2},{3,19},{19,3},{4,20},{20... | collective-permute-start | bytes 786440 | tf_op jit(solution)/shard_map/ppermute | solution.py:57
  51.0 13.1 %collective-permute-start.12 = (bf16[1,272,512]{2,1,0:T(8,128)(2,1)S(1)}, bf16[1,272,512]{2,1,0:T(8,128)(2,1)S(1)}, u32[]{:S(2)}, u32[]{:S(2)}) collective-permute-start(bf16[1,272,512]{2,1,0:T(8,128)(2,1)S(1)} %copy-done.51), channel_id=1, source_target_pairs={{0,1},{1,0},{2,3},{3,2},{4,5},{5,4},{6,7},{7,6},{8,9},{9,8},{10,11... | collective-permute-start | bytes 835592 | tf_op jit(solution)/shard_map/ppermute | solution.py:57
  51.0 13.1 %collective-permute-start.13 = (bf16[1,272,512]{2,1,0:T(8,128)(2,1)S(1)}, bf16[1,272,512]{2,1,0:T(8,128)(2,1)S(1)}, u32[]{:S(2)}, u32[]{:S(2)}) collective-permute-start(bf16[1,272,512]{2,1,0:T(8,128)(2,1)S(1)} %copy-done.50), channel_id=1, source_target_pairs={{0,2},{1,3},{2,0},{3,1},{4,6},{5,7},{6,4},{7,5},{8,10},{9,11},{10,... | collective-permute-start | bytes 835592 | tf_op jit(solution)/shard_map/ppermute | solution.py:57
  51.6 14.0 %collective-permute-start.14 = (bf16[1,272,512]{2,1,0:T(8,128)(2,1)S(1)}, bf16[1,272,512]{2,1,0:T(8,128)(2,1)S(1)}, u32[]{:S(2)}, u32[]{:S(2)}) collective-permute-start(bf16[1,272,512]{2,1,0:T(8,128)(2,1)S(1)} %copy-done.49), channel_id=1, source_target_pairs={{0,3},{1,2},{2,1},{3,0},{4,7},{5,6},{6,5},{7,4},{8,11},{9,10},{10,... | collective-permute-start | bytes 835592 | tf_op jit(solution)/shard_map/ppermute | solution.py:57
  65.6 15.0 %collective-permute-start.17 = (bf16[4,64,512]{2,1,0:T(8,128)(2,1)S(1)}, bf16[4,64,512]{2,1,0:T(8,128)(2,1)S(1)}, u32[]{:S(2)}, u32[]{:S(2)}) collective-permute-start(bf16[4,64,512]{2,1,0:T(8,128)(2,1)S(1)} %get-tuple-element.345), channel_id=1, source_target_pairs={{0,16},{16,0},{1,17},{17,1},{2,18},{18,2},{3,19},{19,3},{4,20},{20... | collective-permute-start | bytes 786440 | tf_op jit(solution)/shard_map/ppermute | solution.py:57
  65.6 15.1 %collective-permute-start.16 = (bf16[2,4,64,512]{3,2,1,0:T(8,128)(2,1)S(1)}, bf16[2,4,64,512]{3,2,1,0:T(8,128)(2,1)S(1)}, u32[]{:S(2)}, u32[]{:S(2)}) collective-permute-start(bf16[2,4,64,512]{3,2,1,0:T(8,128)(2,1)S(1)} %pad_maximum_fusion.7), channel_id=1, source_target_pairs={{0,2},{1,3},{2,0},{3,1},{4,6},{5,7},{6,4},{7,5},{8,10},{9,11},{10,... | collective-permute-start | bytes 1572872 | tf_op jit(solution)/shard_map/ppermute | solution.py:57
  80.9 19.4 %collective-permute-start.18 = (bf16[2,128,512]{2,1,0:T(8,128)(2,1)S(1)}, bf16[2,128,512]{2,1,0:T(8,128)(2,1)S(1)}, u32[]{:S(2)}, u32[]{:S(2)}) collective-permute-start(bf16[2,128,512]{2,1,0:T(8,128)(2,1)S(1)} %get-tuple-element.353), channel_id=1, source_target_pairs={{0,1},{1,0},{2,3},{3,2},{4,5},{5,4},{6,7},{7,6},{8,9},{9,8},{10,11... | collective-permute-start | bytes 786440 | tf_op jit(solution)/shard_map/ppermute | solution.py:57
  81.0 19.3 %collective-permute-start.19 = (bf16[2,128,512]{2,1,0:T(8,128)(2,1)S(1)}, bf16[2,128,512]{2,1,0:T(8,128)(2,1)S(1)}, u32[]{:S(2)}, u32[]{:S(2)}) collective-permute-start(bf16[2,128,512]{2,1,0:T(8,128)(2,1)S(1)} %get-tuple-element.354), channel_id=1, source_target_pairs={{0,2},{1,3},{2,0},{3,1},{4,6},{5,7},{6,4},{7,5},{8,10},{9,11},{10,... | collective-permute-start | bytes 786440 | tf_op jit(solution)/shard_map/ppermute | solution.py:57
  82.6 17.8 %collective-permute-start.20 = (bf16[2,128,512]{2,1,0:T(8,128)(2,1)S(1)}, bf16[2,128,512]{2,1,0:T(8,128)(2,1)S(1)}, u32[]{:S(2)}, u32[]{:S(2)}) collective-permute-start(bf16[2,128,512]{2,1,0:T(8,128)(2,1)S(1)} %get-tuple-element.355), channel_id=1, source_target_pairs={{0,3},{1,2},{2,1},{3,0},{4,7},{5,6},{6,5},{7,4},{8,11},{9,10},{10,... | collective-permute-start | bytes 786440 | tf_op jit(solution)/shard_map/ppermute | solution.py:57
  98.4 6.3 %collective-permute-start.21 = (bf16[2,128,512]{2,1,0:T(8,128)(2,1)S(1)}, bf16[2,128,512]{2,1,0:T(8,128)(2,1)S(1)}, u32[]{:S(2)}, u32[]{:S(2)}) collective-permute-start(bf16[2,128,512]{2,1,0:T(8,128)(2,1)S(1)} %get-tuple-element.367), channel_id=1, source_target_pairs={{0,1},{1,0},{2,3},{3,2},{4,5},{5,4},{6,7},{7,6},{8,9},{9,8},{10,11... | collective-permute-start | bytes 786440 | tf_op jit(solution)/shard_map/ppermute | solution.py:57
  98.8 9.2 %collective-permute-start.22 = (bf16[2,128,512]{2,1,0:T(8,128)(2,1)S(1)}, bf16[2,128,512]{2,1,0:T(8,128)(2,1)S(1)}, u32[]{:S(2)}, u32[]{:S(2)}) collective-permute-start(bf16[2,128,512]{2,1,0:T(8,128)(2,1)S(1)} %get-tuple-element.368), channel_id=1, source_target_pairs={{0,2},{1,3},{2,0},{3,1},{4,6},{5,7},{6,4},{7,5},{8,10},{9,11},{10,... | collective-permute-start | bytes 786440 | tf_op jit(solution)/shard_map/ppermute | solution.py:57
  100.3 11.7 %collective-permute-start.23 = (bf16[2,128,512]{2,1,0:T(8,128)(2,1)S(1)}, bf16[2,128,512]{2,1,0:T(8,128)(2,1)S(1)}, u32[]{:S(2)}, u32[]{:S(2)}) collective-permute-start(bf16[2,128,512]{2,1,0:T(8,128)(2,1)S(1)} %get-tuple-element.369), channel_id=1, source_target_pairs={{0,3},{1,2},{2,1},{3,0},{4,7},{5,6},{6,5},{7,4},{8,11},{9,10},{10,... | collective-permute-start | bytes 786440 | tf_op jit(solution)/shard_map/ppermute | solution.py:57
  112.0 14.4 %collective-permute-start.27 = (bf16[2,4,64,512]{3,2,1,0:T(8,128)(2,1)S(1)}, bf16[2,4,64,512]{3,2,1,0:T(8,128)(2,1)S(1)}, u32[]{:S(2)}, u32[]{:S(2)}) collective-permute-start(bf16[2,4,64,512]{3,2,1,0:T(8,128)(2,1)S(1)} %pad_maximum_fusion.8), channel_id=1, source_target_pairs={{0,2},{1,3},{2,0},{3,1},{4,6},{5,7},{6,4},{7,5},{8,10},{9,11},{10,... | collective-permute-start | bytes 1572872 | tf_op jit(solution)/shard_map/ppermute | solution.py:57
  113.6 20.9 %collective-permute-start.29 = (bf16[16,64,512]{2,1,0:T(8,128)(2,1)S(1)}, bf16[16,64,512]{2,1,0:T(8,128)(2,1)S(1)}, u32[]{:S(2)}, u32[]{:S(2)}) collective-permute-start(bf16[16,64,512]{2,1,0:T(8,128)(2,1)S(1)} %bitcast.175), channel_id=1, source_target_pairs={{0,1},{1,0},{2,3},{3,2},{4,5},{5,4},{6,7},{7,6},{8,9},{9,8},{10,11... | collective-permute-start | bytes 3145736 | tf_op jit(solution)/shard_map/ppermute | solution.py:57
  114.0 12.6 %collective-permute-start.24 = (bf16[128,1152]{1,0:T(8,128)(2,1)S(1)}, bf16[128,1152]{1,0:T(8,128)(2,1)S(1)}, u32[]{:S(2)}, u32[]{:S(2)}) collective-permute-start(bf16[128,1152]{1,0:T(8,128)(2,1)S(1)} %get-tuple-element.380), channel_id=1, source_target_pairs={{0,4},{4,0},{8,12},{12,8},{1,5},{5,1},{9,13},{13,9},{2,6},{6,2},{1... | collective-permute-start | bytes 884744 | tf_op jit(solution)/shard_map/ppermute | solution.py:57
  115.5 11.2 %collective-permute-start.25 = (bf16[128,1152]{1,0:T(8,128)(2,1)S(1)}, bf16[128,1152]{1,0:T(8,128)(2,1)S(1)}, u32[]{:S(2)}, u32[]{:S(2)}) collective-permute-start(bf16[128,1152]{1,0:T(8,128)(2,1)S(1)} %get-tuple-element.381), channel_id=1, source_target_pairs={{0,8},{4,12},{8,0},{12,4},{1,9},{5,13},{9,1},{13,5},{2,10},{6,14},... | collective-permute-start | bytes 884744 | tf_op jit(solution)/shard_map/ppermute | solution.py:57
  117.5 13.3 %collective-permute-start.26 = (bf16[128,1152]{1,0:T(8,128)(2,1)S(1)}, bf16[128,1152]{1,0:T(8,128)(2,1)S(1)}, u32[]{:S(2)}, u32[]{:S(2)}) collective-permute-start(bf16[128,1152]{1,0:T(8,128)(2,1)S(1)} %get-tuple-element.382), channel_id=1, source_target_pairs={{0,12},{4,8},{8,4},{12,0},{1,13},{5,9},{9,5},{13,1},{2,14},{6,10},... | collective-permute-start | bytes 884744 | tf_op jit(solution)/shard_map/ppermute | solution.py:57
  130.9 3.6 %collective-permute-start.30 = (bf16[16,64,512]{2,1,0:T(8,128)(2,1)S(1)}, bf16[16,64,512]{2,1,0:T(8,128)(2,1)S(1)}, u32[]{:S(2)}, u32[]{:S(2)}) collective-permute-start(bf16[16,64,512]{2,1,0:T(8,128)(2,1)S(1)} %bitcast.178), channel_id=1, source_target_pairs={{0,1},{1,0},{2,3},{3,2},{4,5},{5,4},{6,7},{7,6},{8,9},{9,8},{10,11... | collective-permute-start | bytes 3145736 | tf_op jit(solution)/shard_map/ppermute | solution.py:57
  130.9 9.4 %collective-permute-start.28 = (bf16[128,1152]{1,0:T(8,128)(2,1)S(1)}, bf16[128,1152]{1,0:T(8,128)(2,1)S(1)}, u32[]{:S(2)}, u32[]{:S(2)}) collective-permute-start(bf16[128,1152]{1,0:T(8,128)(2,1)S(1)} %get-tuple-element.385), channel_id=1, source_target_pairs={{0,4},{4,0},{8,12},{12,8},{1,5},{5,1},{9,13},{13,9},{2,6},{6,2},{1... | collective-permute-start | bytes 884744 | tf_op jit(solution)/shard_map/ppermute | solution.py:57
  132.5 11.4 %collective-permute-start.31 = (bf16[128,1152]{1,0:T(8,128)(2,1)S(1)}, bf16[128,1152]{1,0:T(8,128)(2,1)S(1)}, u32[]{:S(2)}, u32[]{:S(2)}) collective-permute-start(bf16[128,1152]{1,0:T(8,128)(2,1)S(1)} %get-tuple-element.394), channel_id=1, source_target_pairs={{0,8},{4,12},{8,0},{12,4},{1,9},{5,13},{9,1},{13,5},{2,10},{6,14},... | collective-permute-start | bytes 884744 | tf_op jit(solution)/shard_map/ppermute | solution.py:57
  134.3 14.5 %collective-permute-start.32 = (bf16[128,1152]{1,0:T(8,128)(2,1)S(1)}, bf16[128,1152]{1,0:T(8,128)(2,1)S(1)}, u32[]{:S(2)}, u32[]{:S(2)}) collective-permute-start(bf16[128,1152]{1,0:T(8,128)(2,1)S(1)} %get-tuple-element.395), channel_id=1, source_target_pairs={{0,12},{4,8},{8,4},{12,0},{1,13},{5,9},{9,5},{13,1},{2,14},{6,10},... | collective-permute-start | bytes 884744 | tf_op jit(solution)/shard_map/ppermute | solution.py:57
  140.4 16.0 %collective-permute-start.35 = (bf16[128,1152]{1,0:T(8,128)(2,1)S(1)}, bf16[128,1152]{1,0:T(8,128)(2,1)S(1)}, u32[]{:S(2)}, u32[]{:S(2)}) collective-permute-start(bf16[128,1152]{1,0:T(8,128)(2,1)S(1)} %get-tuple-element.405.refs_1_), channel_id=1, source_target_pairs={{0,12},{4,8},{8,4},{12,0},{1,13},{5,9},{9,5},{13,1},{2,14},{6,10},... | collective-permute-start | bytes 884744 | tf_op jit(solution)/shard_map/ppermute | solution.py:57
  143.0 17.5 %collective-permute-start.34 = (bf16[128,1152]{1,0:T(8,128)(2,1)S(1)}, bf16[128,1152]{1,0:T(8,128)(2,1)S(1)}, u32[]{:S(2)}, u32[]{:S(2)}) collective-permute-start(bf16[128,1152]{1,0:T(8,128)(2,1)S(1)} %get-tuple-element.405.refs_1_), channel_id=1, source_target_pairs={{0,8},{4,12},{8,0},{12,4},{1,9},{5,13},{9,1},{13,5},{2,10},{6,14},... | collective-permute-start | bytes 884744 | tf_op jit(solution)/shard_map/ppermute | solution.py:57
  143.3 17.3 %collective-permute-start.33 = (bf16[128,1152]{1,0:T(8,128)(2,1)S(1)}, bf16[128,1152]{1,0:T(8,128)(2,1)S(1)}, u32[]{:S(2)}, u32[]{:S(2)}) collective-permute-start(bf16[128,1152]{1,0:T(8,128)(2,1)S(1)} %get-tuple-element.405.refs_1_), channel_id=1, source_target_pairs={{0,4},{4,0},{8,12},{12,8},{1,5},{5,1},{9,13},{13,9},{2,6},{6,2},{1... | collective-permute-start | bytes 884744 | tf_op jit(solution)/shard_map/ppermute | solution.py:57
  161.4 15.4 %collective-permute-start.39 = (bf16[16,128,512]{2,1,0:T(8,128)(2,1)}, bf16[16,128,512]{2,1,0:T(8,128)(2,1)}, u32[]{:S(2)}, u32[]{:S(2)}) collective-permute-start(bf16[16,128,512]{2,1,0:T(8,128)(2,1)} %get-tuple-element.414), channel_id=1, source_target_pairs={{0,1},{1,0},{2,3},{3,2},{4,5},{5,4},{6,7},{7,6},{8,9},{9,8},{10,11... | collective-permute-start | bytes 6291464 | tf_op jit(solution)/shard_map/ppermute | solution.py:57
  161.4 17.5 %collective-permute-start.38 = (bf16[128,1152]{1,0:T(8,128)(2,1)S(1)}, bf16[128,1152]{1,0:T(8,128)(2,1)S(1)}, u32[]{:S(2)}, u32[]{:S(2)}) collective-permute-start(bf16[128,1152]{1,0:T(8,128)(2,1)S(1)} %get-tuple-element.415.refs_1_), channel_id=1, source_target_pairs={{0,12},{4,8},{8,4},{12,0},{1,13},{5,9},{9,5},{13,1},{2,14},{6,10},... | collective-permute-start | bytes 884744 | tf_op jit(solution)/shard_map/ppermute | solution.py:57
  163.9 16.3 %collective-permute-start.37 = (bf16[128,1152]{1,0:T(8,128)(2,1)S(1)}, bf16[128,1152]{1,0:T(8,128)(2,1)S(1)}, u32[]{:S(2)}, u32[]{:S(2)}) collective-permute-start(bf16[128,1152]{1,0:T(8,128)(2,1)S(1)} %get-tuple-element.415.refs_1_), channel_id=1, source_target_pairs={{0,8},{4,12},{8,0},{12,4},{1,9},{5,13},{9,1},{13,5},{2,10},{6,14},... | collective-permute-start | bytes 884744 | tf_op jit(solution)/shard_map/ppermute | solution.py:57
  164.2 16.1 %collective-permute-start.36 = (bf16[128,1152]{1,0:T(8,128)(2,1)S(1)}, bf16[128,1152]{1,0:T(8,128)(2,1)S(1)}, u32[]{:S(2)}, u32[]{:S(2)}) collective-permute-start(bf16[128,1152]{1,0:T(8,128)(2,1)S(1)} %get-tuple-element.415.refs_1_), channel_id=1, source_target_pairs={{0,4},{4,0},{8,12},{12,8},{1,5},{5,1},{9,13},{13,9},{2,6},{6,2},{1... | collective-permute-start | bytes 884744 | tf_op jit(solution)/shard_map/ppermute | solution.py:57
  176.7 17.5 %collective-permute-start.40 = (bf16[2,128,512]{2,1,0:T(8,128)(2,1)}, bf16[2,128,512]{2,1,0:T(8,128)(2,1)}, u32[]{:S(2)}, u32[]{:S(2)}) collective-permute-start(bf16[2,128,512]{2,1,0:T(8,128)(2,1)} %get-tuple-element.425), channel_id=1, source_target_pairs={{0,1},{1,0},{2,3},{3,2},{4,5},{5,4},{6,7},{7,6},{8,9},{9,8},{10,11... | collective-permute-start | bytes 786440 | tf_op jit(solution)/shard_map/ppermute | solution.py:57
  176.8 18.4 %collective-permute-start.41 = (bf16[2,128,512]{2,1,0:T(8,128)(2,1)}, bf16[2,128,512]{2,1,0:T(8,128)(2,1)}, u32[]{:S(2)}, u32[]{:S(2)}) collective-permute-start(bf16[2,128,512]{2,1,0:T(8,128)(2,1)} %get-tuple-element.426), channel_id=1, source_target_pairs={{0,2},{1,3},{2,0},{3,1},{4,6},{5,7},{6,4},{7,5},{8,10},{9,11},{10,... | collective-permute-start | bytes 786440 | tf_op jit(solution)/shard_map/ppermute | solution.py:57
  179.0 16.2 %collective-permute-start.42 = (bf16[2,128,512]{2,1,0:T(8,128)(2,1)}, bf16[2,128,512]{2,1,0:T(8,128)(2,1)}, u32[]{:S(2)}, u32[]{:S(2)}) collective-permute-start(bf16[2,128,512]{2,1,0:T(8,128)(2,1)} %get-tuple-element.427), channel_id=1, source_target_pairs={{0,3},{1,2},{2,1},{3,0},{4,7},{5,6},{6,5},{7,4},{8,11},{9,10},{10,... | collective-permute-start | bytes 786440 | tf_op jit(solution)/shard_map/ppermute | solution.py:57
  193.7 9.5 %collective-permute-start.44 = (bf16[2,128,512]{2,1,0:T(8,128)(2,1)}, bf16[2,128,512]{2,1,0:T(8,128)(2,1)}, u32[]{:S(2)}, u32[]{:S(2)}) collective-permute-start(bf16[2,128,512]{2,1,0:T(8,128)(2,1)} %get-tuple-element.430), channel_id=1, source_target_pairs={{0,2},{1,3},{2,0},{3,1},{4,6},{5,7},{6,4},{7,5},{8,10},{9,11},{10,... | collective-permute-start | bytes 786440 | tf_op jit(solution)/shard_map/ppermute | solution.py:57
  194.2 13.0 %collective-permute-start.45 = (bf16[2,128,512]{2,1,0:T(8,128)(2,1)}, bf16[2,128,512]{2,1,0:T(8,128)(2,1)}, u32[]{:S(2)}, u32[]{:S(2)}) collective-permute-start(bf16[2,128,512]{2,1,0:T(8,128)(2,1)} %get-tuple-element.431), channel_id=1, source_target_pairs={{0,3},{1,2},{2,1},{3,0},{4,7},{5,6},{6,5},{7,4},{8,11},{9,10},{10,... | collective-permute-start | bytes 786440 | tf_op jit(solution)/shard_map/ppermute | solution.py:57
  207.2 30.1 %collective-permute-start.46 = (bf16[16,16,640]{2,1,0:T(8,128)(2,1)}, bf16[16,16,640]{2,1,0:T(8,128)(2,1)S(1)}, u32[]{:S(2)}, u32[]{:S(2)}) collective-permute-start(bf16[16,16,640]{2,1,0:T(8,128)(2,1)} %get-tuple-element.454), channel_id=1, source_target_pairs={{0,1},{1,0},{2,3},{3,2},{4,5},{5,4},{6,7},{7,6},{8,9},{9,8},{10,11... | collective-permute-start | bytes 983048 | tf_op jit(solution)/shard_map/ppermute | solution.py:57
  207.8 29.5 %collective-permute-start.47 = (bf16[2,4,128,512]{3,2,1,0:T(8,128)(2,1)S(1)}, bf16[2,4,128,512]{3,2,1,0:T(8,128)(2,1)}, u32[]{:S(2)}, u32[]{:S(2)}) collective-permute-start(bf16[2,4,128,512]{3,2,1,0:T(8,128)(2,1)S(1)} %fusion), channel_id=1, source_target_pairs={{0,2},{1,3},{2,0},{3,1},{4,6},{5,7},{6,4},{7,5},{8,10},{9,11},{10,... | collective-permute-start | bytes 3145736 | tf_op jit(solution)/shard_map/ppermute | solution.py:57
  239.6 34.5 %collective-permute-start.48 = (bf16[1,256,512]{2,1,0:T(8,128)(2,1)}, bf16[1,256,512]{2,1,0:T(8,128)(2,1)S(1)}, u32[]{:S(2)}, u32[]{:S(2)}) collective-permute-start(bf16[1,256,512]{2,1,0:T(8,128)(2,1)} %get-tuple-element.470), channel_id=1, source_target_pairs={{0,1},{1,0},{2,3},{3,2},{4,5},{5,4},{6,7},{7,6},{8,9},{9,8},{10,11... | collective-permute-start | bytes 786440 | tf_op jit(solution)/shard_map/ppermute | solution.py:57
  239.6 34.5 %collective-permute-start.49 = (bf16[1,256,512]{2,1,0:T(8,128)(2,1)}, bf16[1,256,512]{2,1,0:T(8,128)(2,1)S(1)}, u32[]{:S(2)}, u32[]{:S(2)}) collective-permute-start(bf16[1,256,512]{2,1,0:T(8,128)(2,1)} %get-tuple-element.471), channel_id=1, source_target_pairs={{0,2},{1,3},{2,0},{3,1},{4,6},{5,7},{6,4},{7,5},{8,10},{9,11},{10,... | collective-permute-start | bytes 786440 | tf_op jit(solution)/shard_map/ppermute | solution.py:57
  241.1 33.0 %collective-permute-start.50 = (bf16[1,256,512]{2,1,0:T(8,128)(2,1)}, bf16[1,256,512]{2,1,0:T(8,128)(2,1)S(1)}, u32[]{:S(2)}, u32[]{:S(2)}) collective-permute-start(bf16[1,256,512]{2,1,0:T(8,128)(2,1)} %get-tuple-element.472), channel_id=1, source_target_pairs={{0,3},{1,2},{2,1},{3,0},{4,7},{5,6},{6,5},{7,4},{8,11},{9,10},{10,... | collective-permute-start | bytes 786440 | tf_op jit(solution)/shard_map/ppermute | solution.py:57
  241.5 32.6 %collective-permute-start.51 = (bf16[4,128,512]{2,1,0:T(8,128)(2,1)}, bf16[4,128,512]{2,1,0:T(8,128)(2,1)S(1)}, u32[]{:S(2)}, u32[]{:S(2)}) collective-permute-start(bf16[4,128,512]{2,1,0:T(8,128)(2,1)} %fusion.2), channel_id=1, source_target_pairs={{0,16},{16,0},{1,17},{17,1},{2,18},{18,2},{3,19},{19,3},{4,20},{20... | collective-permute-start | bytes 1572872 | tf_op jit(solution)/shard_map/ppermute | solution.py:57
  274.1 18.3 %collective-permute-start.54 = (bf16[16,16,1536]{2,1,0:T(8,128)(2,1)}, bf16[16,16,1536]{2,1,0:T(8,128)(2,1)}, u32[]{:S(2)}, u32[]{:S(2)}) collective-permute-start(bf16[16,16,1536]{2,1,0:T(8,128)(2,1)} %get-tuple-element.482), channel_id=1, source_target_pairs={{0,1},{1,0},{2,3},{3,2},{4,5},{5,4},{6,7},{7,6},{8,9},{9,8},{10,11... | collective-permute-start | bytes 2359304 | tf_op jit(solution)/shard_map/ppermute | solution.py:57
  277.5 7.3 %collective-permute-start.57 = (bf16[128,512]{1,0:T(8,128)(2,1)S(1)}, bf16[128,512]{1,0:T(8,128)(2,1)}, u32[]{:S(2)}, u32[]{:S(2)}) collective-permute-start(bf16[128,512]{1,0:T(8,128)(2,1)S(1)} %get-tuple-element.577), channel_id=1, source_target_pairs={{0,12},{4,8},{8,4},{12,0},{1,13},{5,9},{9,5},{13,1},{2,14},{6,10},... | collective-permute-start | bytes 393224 | tf_op jit(solution)/shard_map/ppermute | solution.py:57
  280.0 8.3 %collective-permute-start.56 = (bf16[128,512]{1,0:T(8,128)(2,1)}, bf16[128,512]{1,0:T(8,128)(2,1)S(1)}, u32[]{:S(2)}, u32[]{:S(2)}) collective-permute-start(bf16[128,512]{1,0:T(8,128)(2,1)} %get-tuple-element.578), channel_id=1, source_target_pairs={{0,8},{4,12},{8,0},{12,4},{1,9},{5,13},{9,1},{13,5},{2,10},{6,14},... | collective-permute-start | bytes 393224 | tf_op jit(solution)/shard_map/ppermute | solution.py:57
  280.3 8.0 %collective-permute-start.55 = (bf16[128,512]{1,0:T(8,128)(2,1)}, bf16[128,512]{1,0:T(8,128)(2,1)S(1)}, u32[]{:S(2)}, u32[]{:S(2)}) collective-permute-start(bf16[128,512]{1,0:T(8,128)(2,1)} %get-tuple-element.579), channel_id=1, source_target_pairs={{0,4},{4,0},{8,12},{12,8},{1,5},{5,1},{9,13},{13,9},{2,6},{6,2},{1... | collective-permute-start | bytes 393224 | tf_op jit(solution)/shard_map/ppermute | solution.py:57
  281.0 7.4 %collective-permute-start.52 = (bf16[1,256,512]{2,1,0:T(8,128)(2,1)}, bf16[1,256,512]{2,1,0:T(8,128)(2,1)S(1)}, u32[]{:S(2)}, u32[]{:S(2)}) collective-permute-start(bf16[1,256,512]{2,1,0:T(8,128)(2,1)} %get-tuple-element.479), channel_id=1, source_target_pairs={{0,1},{1,0},{2,3},{3,2},{4,5},{5,4},{6,7},{7,6},{8,9},{9,8},{10,11... | collective-permute-start | bytes 786440 | tf_op jit(solution)/shard_map/ppermute | solution.py:57
  284.8 7.6 %collective-permute-start.53 = (bf16[1,256,512]{2,1,0:T(8,128)(2,1)}, bf16[1,256,512]{2,1,0:T(8,128)(2,1)S(1)}, u32[]{:S(2)}, u32[]{:S(2)}) collective-permute-start(bf16[1,256,512]{2,1,0:T(8,128)(2,1)} %get-tuple-element.480), channel_id=1, source_target_pairs={{0,2},{1,3},{2,0},{3,1},{4,6},{5,7},{6,4},{7,5},{8,10},{9,11},{10,... | collective-permute-start | bytes 786440 | tf_op jit(solution)/shard_map/ppermute | solution.py:57
  292.4 8.8 %collective-permute-start.58 = (bf16[1,256,512]{2,1,0:T(8,128)(2,1)}, bf16[1,256,512]{2,1,0:T(8,128)(2,1)S(1)}, u32[]{:S(2)}, u32[]{:S(2)}) collective-permute-start(bf16[1,256,512]{2,1,0:T(8,128)(2,1)} %get-tuple-element.491), channel_id=1, source_target_pairs={{0,3},{1,2},{2,1},{3,0},{4,7},{5,6},{6,5},{7,4},{8,11},{9,10},{10,... | collective-permute-start | bytes 786440 | tf_op jit(solution)/shard_map/ppermute | solution.py:57
  294.0 14.5 %collective-permute-start.61 = (bf16[2,2,16,2176]{3,2,1,0:T(8,128)(2,1)S(1)}, bf16[2,2,16,2176]{3,2,1,0:T(8,128)(2,1)S(1)}, u32[]{:S(2)}, u32[]{:S(2)}) collective-permute-start(bf16[2,2,16,2176]{3,2,1,0:T(8,128)(2,1)S(1)} %get-tuple-element.558), channel_id=1, source_target_pairs={{0,12},{4,8},{8,4},{12,0},{1,13},{5,9},{9,5},{13,1},{2,14},{6,10},... | collective-permute-start | bytes 835592 | tf_op jit(solution)/shard_map/ppermute | solution.py:220
  296.6 13.8 %collective-permute-start.59 = (bf16[2,2,16,2176]{3,2,1,0:T(8,128)(2,1)S(1)}, bf16[2,2,16,2176]{3,2,1,0:T(8,128)(2,1)S(1)}, u32[]{:S(2)}, u32[]{:S(2)}) collective-permute-start(bf16[2,2,16,2176]{3,2,1,0:T(8,128)(2,1)S(1)} %get-tuple-element.559), channel_id=1, source_target_pairs={{0,4},{4,0},{8,12},{12,8},{1,5},{5,1},{9,13},{13,9},{2,6},{6,2},{1... | collective-permute-start | bytes 835592 | tf_op jit(solution)/shard_map/ppermute | solution.py:220
  297.3 13.1 %collective-permute-start.60 = (bf16[2,2,16,2176]{3,2,1,0:T(8,128)(2,1)S(1)}, bf16[2,2,16,2176]{3,2,1,0:T(8,128)(2,1)S(1)}, u32[]{:S(2)}, u32[]{:S(2)}) collective-permute-start(bf16[2,2,16,2176]{3,2,1,0:T(8,128)(2,1)S(1)} %get-tuple-element.560), channel_id=1, source_target_pairs={{0,8},{4,12},{8,0},{12,4},{1,9},{5,13},{9,1},{13,5},{2,10},{6,14},... | collective-permute-start | bytes 835592 | tf_op jit(solution)/shard_map/ppermute | solution.py:220
  310.7 6.2 %collective-permute-start.62 = (bf16[16,2176]{1,0:T(8,128)(2,1)S(1)}, bf16[16,2176]{1,0:T(8,128)(2,1)S(1)}, u32[]{:S(2)}, u32[]{:S(2)}) collective-permute-start(bf16[16,2176]{1,0:T(8,128)(2,1)S(1)} %get-tuple-element.590), channel_id=1, source_target_pairs={{0,2},{1,3},{2,0},{3,1},{16,18},{17,19},{18,16},{19,17},{4,6},{5,7... | collective-permute-start | bytes 208904 | tf_op jit(solution)/shard_map/ppermute | solution.py:220
  311.9 9.4 %collective-permute-start.64 = (bf16[16,2176]{1,0:T(8,128)(2,1)S(1)}, bf16[16,2176]{1,0:T(8,128)(2,1)S(1)}, u32[]{:S(2)}, u32[]{:S(2)}) collective-permute-start(bf16[16,2176]{1,0:T(8,128)(2,1)S(1)} %get-tuple-element.591), channel_id=1, source_target_pairs={{0,18},{1,19},{2,16},{3,17},{16,2},{17,3},{18,0},{19,1},{4,22},{5,... | collective-permute-start | bytes 208904 | tf_op jit(solution)/shard_map/ppermute | solution.py:220
  312.4 9.1 %collective-permute-start.63 = (bf16[16,2176]{1,0:T(8,128)(2,1)S(1)}, bf16[16,2176]{1,0:T(8,128)(2,1)S(1)}, u32[]{:S(2)}, u32[]{:S(2)}) collective-permute-start(bf16[16,2176]{1,0:T(8,128)(2,1)S(1)} %get-tuple-element.592), channel_id=1, source_target_pairs={{0,16},{1,17},{2,18},{3,19},{16,0},{17,1},{18,2},{19,3},{4,20},{5,... | collective-permute-start | bytes 208904 | tf_op jit(solution)/shard_map/ppermute | solution.py:220
  (61 other events, 793.6 us)

commit v7 on v6

--- a/solution.py
+++ b/solution.py
@@ -1292,7 +1292,7 @@
     sums = sum_expert.finish()
     columns = [p if j == 0 else p.astype(bf16) for j, p in enumerate(member_parts(sums))]
     columns = swap_slots(columns, "gi")
-    gf_rows, gf_slots, received, columns = hold((gf_rows, gf_slots, received, columns))
+    gf_rows, gf_slots, received = hold((gf_rows, gf_slots, received))
     send_some(gf_slots, gf_rows[-1], slots // 2 + 1, slots)
     total = keep + received.astype(f32)
     total = jnp.concatenate([total, keep_out + received_out.astype(f32)], axis=-1)
@@ -1301,7 +1301,7 @@
     sum_in.cut(("gi",))
     sum_in.send()
     grad_inputs = finish(me, gf_rows, inputs, grad_middles, gain_one)
-    grad_inputs = together(grad_inputs, sum_in)
+    grad_inputs, columns = together((grad_inputs, columns), sum_in)
     sum_in.combine()
     sum_in.cut(("gq", "seq"))
     sum_in.send()

time: 331 us -> 323 us (0.976)
  waiting for transfers between devices: 79 us -> 72.5 us
    ppermute x59, waiting for transfers between devices: 72.4 us -> 67.2 us  [partner(): return lax.ppermute(value, axis, [(i, i ^ mask) for i in range(size)])]
    unnamed x122 -> x130, local copies, waits for them, and re-layouts: 10.2 us -> 9.62 us
  transfers between devices with their start and end apart: 65 -> 65, of which waited for: 24 -> 23; matrix products, arithmetic and copies ran while one was open for 5% -> 5% of each run, Pallas kernels for 45% -> 46%
where the time goes in v7:
time: 323 us; the launch traced here: 318 us
  Pallas kernels  146 us (45%)
  waiting for transfers between devices  72.5 us (22%)
  starting transfers between devices  64.1 us (20%)
  other arithmetic  17.4 us (5%)
  local copies, waits for them, and re-layouts  15.4 us (5%)
    pallas_call x12, Pallas kernels, call(): pl.pallas_call(kernel, grid_spec=pltpu.PrefetchScalarGridSpec(num_scalar_...  146 us
    ppermute x59, waiting for transfers between devices, partner(): return lax.ppermute(value, axis, [(i, i ^ mask) for i in range(size)])  67.2 us
    ppermute x59, starting transfers between devices, partner(): return lax.ppermute(value, axis, [(i, i ^ mask) for i in range(size)])  54.6 us
    unnamed x130, local copies, waits for them, and re-layouts  9.62 us
    ppermute x6, starting transfers between devices, send(): self.value[j] = lax.ppermute(self.value[j], names, pairs)  9.47 us
  transfers between devices with their start and end apart: 65, of which 23 were waited for; matrix products, arithmetic and copies ran while one was open for 5% of the time, Pallas kernels for 46%

profile of v7, /device:TPU:0, one launch (start us, length us, event | category | flops | bytes accessed | tf_op | source)
XLA Modules:
  0.0 318.0 jit_solution(5578392375651913945)
XLA Ops:
  3.8 3.0 collective-permute-start
  7.6 1.7 constant_dynamic-slice_fusion
  11.0 2.7 collective-permute-start.6
  13.9 2.6 collective-permute-start.5
  17.4 2.8 collective-permute-done.6
  20.7 1.6 collective-permute-done.5
  22.4 1.8 collective-permute-done.4
  24.2 3.4 %collective-permute-done.2.refs_3_ = bf16[1,272,512]{2,1,0:T(8,128)(2,1)S(1)} collective-permute-done((bf16[1,272,512]{2,1,0:T(8,128)(2,1)S(1)}, bf16[1,272,512]{2,1,0:T(8,128)(2,1)S(1)}, u32[]{:S(2)}, u32[]{:S(2)}) %collective-permute-start.2) | collective-permute-done | bytes 278560 | tf_op jit(solution)/shard_map/ppermute | solution.py:57
  28.4 2.5 collective-permute-start.9
  32.0 2.1 collective-permute-done.10
  34.1 4.4 %collective-permute-done.9 = bf16[2,2,16,2176]{3,2,1,0:T(8,128)(2,1)S(1)} collective-permute-done((bf16[2,2,16,2176]{3,2,1,0:T(8,128)(2,1)S(1)}, bf16[2,2,16,2176]{3,2,1,0:T(8,128)(2,1)S(1)}, u32[]{:S(2)}, u32[]{:S(2)}) %collective-permute-start.9) | collective-permute-done | bytes 278560 | tf_op jit(solution)/shard_map/ppermute | solution.py:57
  38.5 4.1 %collective-permute-done.8 = bf16[2,2,16,2176]{3,2,1,0:T(8,128)(2,1)S(1)} collective-permute-done((bf16[2,2,16,2176]{3,2,1,0:T(8,128)(2,1)S(1)}, bf16[2,2,16,2176]{3,2,1,0:T(8,128)(2,1)S(1)}, u32[]{:S(2)}, u32[]{:S(2)}) %collective-permute-start.8) | collective-permute-done | bytes 278560 | tf_op jit(solution)/shard_map/ppermute | solution.py:57
  43.7 2.7 collective-permute-done.11
  47.7 3.4 %collective-permute-start.15 = (bf16[4,64,512]{2,1,0:T(8,128)(2,1)S(1)}, bf16[4,64,512]{2,1,0:T(8,128)(2,1)S(1)}, u32[]{:S(2)}, u32[]{:S(2)}) collective-permute-start(bf16[4,64,512]{2,1,0:T(8,128)(2,1)S(1)} %slice.48), channel_id=1, source_target_pairs={{0,16},{16,0},{1,17},{17,1},{2,18},{18,2},{3,19},{19,3},{4,20},{20... | collective-permute-start | bytes 786440 | tf_op jit(solution)/shard_map/ppermute | solution.py:57
  51.6 1.3 collective-permute-start.14
  52.9 10.4 %attend_first.2 = (bf16[2,128,512]{2,1,0:T(8,128)(2,1)S(1)}, bf16[2,128,512]{2,1,0:T(8,128)(2,1)S(1)}, bf16[2,128,512]{2,1,0:T(8,128)(2,1)S(1)}, bf16[2,128,512]...) custom-call(s32[2]{0:T(128)S(1)} %pad_add_fusion.refs_0_, ...), custom_call_target="tpu_custom_call" | custom-call | flops 12000000000 | bytes 1048576 | tf_op jit(solution)/shard_map/attend_first/pallas_call | solution.py:239
  64.2 1.4 collective-permute-done.14.refs_4_
  66.1 10.2 %attend_first.3 = (bf16[2,128,512]{2,1,0:T(8,128)(2,1)S(1)}, bf16[2,128,512]{2,1,0:T(8,128)(2,1)S(1)}, bf16[2,128,512]{2,1,0:T(8,128)(2,1)S(1)}, bf16[2,128,512]...) custom-call(s32[2]{0:T(128)S(1)} %pad_add_fusion.refs_0_, ...), custom_call_target="tpu_custom_call", output_to_operand_aliasing={{0}: (7, {}), {1}: (8, {}), {2}: (9, {}), {3}: (10, {}), {4... | custom-call | flops 12000000000 | bytes 1048576 | tf_op jit(solution)/shard_map/attend_first/pallas_call | solution.py:239
  76.3 1.3 copy-done.34
  77.7 1.3 copy-done.35
  79.0 1.0 copy-done.36
  81.1 1.6 collective-permute-start.19
  82.9 14.6 %attend_next.1 = (bf16[2,128,512]{2,1,0:T(8,128)(2,1)S(1)}, bf16[2,128,512]{2,1,0:T(8,128)(2,1)S(1)}, bf16[2,128,512]{2,1,0:T(8,128)(2,1)S(1)}, bf16[2,128,512]{...) custom-call(s32[2]{0:T(128)S(1)} %pad_add_fusion.refs_0_, ...), custom_call_target="tpu_custom_call" | custom-call | flops 14000000000 | bytes 1048576 | tf_op jit(solution)/shard_map/attend_next/pallas_call | solution.py:239
  98.8 1.6 collective-permute-start.22
  100.5 4.3 %mix.2 = (bf16[128,1152]{1,0:T(8,128)(2,1)S(1)}, bf16[128,1152]{1,0:T(8,128)(2,1)S(1)}, bf16[128,1152]{1,0:T(8,128)(2,1)S(1)}, bf16[128,1152]{1,0:T(8,128)(2,1)S(1)}) custom-call(s32[2]{0:T(128)S(1)} %pad_add_fusion.refs_0_, bf16[2,128,512]{2,1,0:T(8,128)(2,1)S(1)} %get-tuple-element.356.refs_1_.refs_5_, ...), custom_call_target="tpu_custom_call" | custom-call | flops 4000000000 | bytes 1048576 | tf_op jit(solution)/shard_map/mix/pallas_call | solution.py:239
  104.8 3.2 collective-permute-done.22.refs_3_.refs_7_
  108.0 4.1 %collective-permute-done.23.refs_4_.refs_8_ = bf16[2,128,512]{2,1,0:T(8,128)(2,1)S(1)} collective-permute-done((bf16[2,128,512]{2,1,0:T(8,128)(2,1)S(1)}, bf16[2,128,512]{2,1,0:T(8,128)(2,1)S(1)}, u32[]{:S(2)}, u32[]{:S(2)}) %collective-permute-start.23) | collective-permute-done | bytes 262176 | tf_op jit(solution)/shard_map/ppermute | solution.py:57
  112.1 1.5 collective-permute-start.27
  114.1 1.5 collective-permute-start.24
  115.6 2.0 collective-permute-start.25
  117.6 4.3 %mix.3 = (bf16[128,1152]{1,0:T(8,128)(2,1)S(1)}, bf16[128,1152]{1,0:T(8,128)(2,1)S(1)}, bf16[128,1152]{1,0:T(8,128)(2,1)S(1)}, bf16[128,1152]{1,0:T(8,128)(2,1)S(1)}) custom-call(s32[2]{0:T(128)S(1)} %pad_add_fusion.refs_0_, bf16[2,128,512]{2,1,0:T(8,128)(2,1)S(1)} %get-tuple-element.371.refs_1_.refs_5_, ...), custom_call_target="tpu_custom_call" | custom-call | flops 4000000000 | bytes 1048576 | tf_op jit(solution)/shard_map/mix/pallas_call | solution.py:239
  121.9 4.6 %collective-permute-done.27 = bf16[2,4,64,512]{3,2,1,0:T(8,128)(2,1)S(1)} collective-permute-done((bf16[2,4,64,512]{3,2,1,0:T(8,128)(2,1)S(1)}, bf16[2,4,64,512]{3,2,1,0:T(8,128)(2,1)S(1)}, u32[]{:S(2)}, u32[]{:S(2)}) %collective-permute-start.27) | collective-permute-done | bytes 524320 | tf_op jit(solution)/shard_map/ppermute | solution.py:57
  126.7 4.2 %collective-permute-done.26.refs_4_ = bf16[128,1152]{1,0:T(8,128)(2,1)S(1)} collective-permute-done((bf16[128,1152]{1,0:T(8,128)(2,1)S(1)}, bf16[128,1152]{1,0:T(8,128)(2,1)S(1)}, u32[]{:S(2)}, u32[]{:S(2)}) %collective-permute-start.26) | collective-permute-done | bytes 294944 | tf_op jit(solution)/shard_map/ppermute | solution.py:57
  131.0 1.6 collective-permute-start.28
  132.6 1.7 collective-permute-start.31
  134.6 5.0 %expert.2 = (bf16[128,1152]{1,0:T(8,128)(2,1)S(1)}, bf16[128,512]{1,0:T(8,128)(2,1)S(1)}, bf16[128,512]{1,0:T(8,128)(2,1)S(1)}, bf16[128,2048]{1,0:T(8,128)(2,1)S(1)}, bf16[128,2048]{1,0:T(8,128)(2,1)S(1)}) custom-call(s32[2]{0:T(128)S(1)} %pad_add_fusion.refs_0_, bf16[128,1152]{1,0:T(8,128)(2,1)S(1)} %get-tuple-element.386.refs_1_, ...), custom_call_target="tpu_custom_call" | custom-call | flops 7000000000 | bytes 1048576 | tf_op jit(solution)/shard_map/expert/pallas_call | solution.py:239
  140.5 2.7 collective-permute-start.35
  143.9 4.9 %collective-permute-done.32.refs_4_ = bf16[128,1152]{1,0:T(8,128)(2,1)S(1)} collective-permute-done((bf16[128,1152]{1,0:T(8,128)(2,1)S(1)}, bf16[128,1152]{1,0:T(8,128)(2,1)S(1)}, u32[]{:S(2)}, u32[]{:S(2)}) %collective-permute-start.32) | collective-permute-done | bytes 294944 | tf_op jit(solution)/shard_map/ppermute | solution.py:57
  148.8 7.6 %expert.3 = (bf16[128,1152]{1,0:T(8,128)(2,1)S(1)}, bf16[16,128,512]{2,1,0:T(8,128)(2,1)S(1)}, bf16[16,128,512]{2,1,0:T(8,128)(2,1)}) custom-call(s32[2]{0:T(128)S(1)} %pad_add_fusion.refs_0_, bf16[128,1152]{1,0:T(8,128)(2,1)S(1)} %get-tuple-element.384.refs_1_, bf16[128,1152]{1,0:T(8,128)(2,1)S(1)} %collective-permute-done.28.refs_2_, ...), custom_call_target="tpu_custom_call" | custom-call | flops 7000000000 | bytes 1048576 | tf_op jit(solution)/shard_map/expert/pallas_call | solution.py:239
  156.5 4.2 %collective-permute-done.34.refs_3_ = bf16[128,1152]{1,0:T(8,128)(2,1)S(1)} collective-permute-done((bf16[128,1152]{1,0:T(8,128)(2,1)S(1)}, bf16[128,1152]{1,0:T(8,128)(2,1)S(1)}, u32[]{:S(2)}, u32[]{:S(2)}) %collective-permute-start.34) | collective-permute-done | bytes 294944 | tf_op jit(solution)/shard_map/ppermute | solution.py:57
  160.8 2.5 collective-permute-start.38
  164.3 11.8 %unmix.2 = (bf16[8,256,512]{2,1,0:T(8,128)(2,1)}, bf16[8,128,512]{2,1,0:T(8,128)(2,1)}, bf16[2,128,512]{2,1,0:T(8,128)(2,1)}, bf16[2,128,512]{2,1,0:T(8,128)(2,1...) custom-call(s32[2]{0:T(128)} %copy-done.24, ...), custom_call_target="tpu_custom_call" | custom-call | flops 6000000000 | bytes 1048576 | tf_op jit(solution)/shard_map/unmix/pallas_call | solution.py:239
  176.9 2.5 fusion
  179.3 1.2 collective-permute-start.42
  181.5 12.1 %unmix.3 = (bf16[8,256,512]{2,1,0:T(8,128)(2,1)}, bf16[8,128,512]{2,1,0:T(8,128)(2,1)}, bf16[2,128,512]{2,1,0:T(8,128)(2,1)}, bf16[2,128,512]{2,1,0:T(8,128)(2,1...) custom-call(s32[2]{0:T(128)} %copy-done.24, ...), custom_call_target="tpu_custom_call", output_to_operand_aliasing={{0}: (14, {})} | custom-call | flops 6000000000 | bytes 1048576 | tf_op jit(solution)/shard_map/unmix/pallas_call | solution.py:239
  195.5 7.9 %collective-permute-done.44.refs_11_ = bf16[2,128,512]{2,1,0:T(8,128)(2,1)} collective-permute-done((bf16[2,128,512]{2,1,0:T(8,128)(2,1)}, bf16[2,128,512]{2,1,0:T(8,128)(2,1)}, u32[]{:S(2)}, u32[]{:S(2)}) %collective-permute-start.44) | collective-permute-done | bytes 262176 | tf_op jit(solution)/shard_map/ppermute | solution.py:57
  203.4 4.1 %collective-permute-done.45.refs_12_ = bf16[2,128,512]{2,1,0:T(8,128)(2,1)} collective-permute-done((bf16[2,128,512]{2,1,0:T(8,128)(2,1)}, bf16[2,128,512]{2,1,0:T(8,128)(2,1)}, u32[]{:S(2)}, u32[]{:S(2)}) %collective-permute-start.45) | collective-permute-done | bytes 262176 | tf_op jit(solution)/shard_map/ppermute | solution.py:57
  208.7 28.9 %attend_back.2 = (bf16[1,256,512]{2,1,0:T(8,128)(2,1)}, bf16[1,256,512]{2,1,0:T(8,128)(2,1)}, bf16[1,256,512]{2,1,0:T(8,128)(2,1)}, bf16[1,256,512]{2,1,0:T(8,128)(2,1)}, f32[512,1536]{1,0:T(8,128)}) custom-call(s32[2]{0:T(128)} %copy-done.24, bf16[1,272,512]{2,1,0:T(8,128)(2,1)} %copy-done.4, bf16[1,272,512]{2,1,0:T(8,128)(2,1)} %copy-done.11, ...), custom_call_target="tpu_custom_call" | custom-call | flops 28000000000 | bytes 1048576 | tf_op jit(solution)/shard_map/attend_back/pallas_call | solution.py:239
  238.7 1.2 fusion.2
  240.0 1.5 collective-permute-start.49
  241.9 2.7 collective-permute-start.51
  244.6 29.9 %attend_back.3 = (bf16[1,256,512]{2,1,0:T(8,128)(2,1)}, bf16[1,256,512]{2,1,0:T(8,128)(2,1)}, bf16[1,256,512]{2,1,0:T(8,128)(2,1)}, bf16[1,256,512]{2,1,0:T(8,12...) custom-call(s32[2]{0:T(128)} %copy-done.24, bf16[1,272,512]{2,1,0:T(8,128)(2,1)} %copy-done.3, ...), custom_call_target="tpu_custom_call" | custom-call | flops 28000000000 | bytes 1048576 | tf_op jit(solution)/shard_map/attend_back/pallas_call | solution.py:239
  274.7 1.0 convert_add_fusion.3
  276.2 1.5 collective-permute-start.53
  277.7 1.6 fusion.1
  279.4 2.5 collective-permute-start.58
  283.1 1.7 collective-permute-done.53.refs_7_
  285.1 1.4 convert_add_fusion
  286.9 2.5 collective-permute-start.61
  290.1 3.2 %collective-permute-done.55.refs_8_ = bf16[1,256,512]{2,1,0:T(8,128)(2,1)S(1)} collective-permute-done((bf16[1,256,512]{2,1,0:T(8,128)(2,1)S(1)}, bf16[1,256,512]{2,1,0:T(8,128)(2,1)S(1)}, u32[]{:S(2)}, u32[]{:S(2)}) %collective-permute-start.55) | collective-permute-done | bytes 262176 | tf_op jit(solution)/shard_map/ppermute | solution.py:57
  293.3 1.7 collective-permute-start.60
  295.1 7.3 %finish.1 = bf16[8,256,512]{2,1,0:T(8,128)(2,1)} custom-call(s32[2]{0:T(128)S(1)} %copy-done.25, bf16[1,256,512]{2,1,0:T(8,128)(2,1)S(1)} %copy-done.28, bf16[1,256,512]{2,1,0:T(8,128)(2,1)S(1)} %collective-permute-done.48.refs_2_, bf16[1,256,512]{2,1,0:T(8,128)(2,1)S(1)} %collective-permute-done.49.refs_3_, ...), custom_call_target="tpu_custom_call" | custom-call | flops 4000000000 | bytes 1048576 | tf_op jit(solution)/shard_map/finish/pallas_call | solution.py:239
  305.3 2.6 collective-permute-start.63
  309.9 3.9 %collective-permute-done.64 = bf16[16,2176]{1,0:T(8,128)(2,1)S(1)} collective-permute-done((bf16[16,2176]{1,0:T(8,128)(2,1)S(1)}, bf16[16,2176]{1,0:T(8,128)(2,1)S(1)}, u32[]{:S(2)}, u32[]{:S(2)}) %collective-permute-start.64) | collective-permute-done | bytes 69664 | tf_op jit(solution)/shard_map/ppermute | solution.py:220
  (278 shorter events, 38.0 us)
Async XLA Ops:
  3.8 7.2 %collective-permute-start = (bf16[16,2176]{1,0:T(8,128)(2,1)S(1)}, bf16[16,2176]{1,0:T(8,128)(2,1)S(1)}, u32[]{:S(2)}, u32[]{:S(2)}) collective-permute-start(bf16[16,2176]{1,0:T(8,128)(2,1)S(1)} %fusion.24), channel_id=1, source_target_pairs={{0,2},{1,3},{2,0},{3,1},{4,6},{5,7},{6,4},{7,5},{8,10},{9,11},{10,... | collective-permute-start | bytes 208904 | tf_op jit(solution)/shard_map/ppermute | solution.py:57
  11.0 9.2 %collective-permute-start.6 = (bf16[2,16,2176]{2,1,0:T(8,128)(2,1)S(1)}, bf16[2,16,2176]{2,1,0:T(8,128)(2,1)S(1)}, u32[]{:S(2)}, u32[]{:S(2)}) collective-permute-start(bf16[2,16,2176]{2,1,0:T(8,128)(2,1)S(1)} %pad_maximum_fusion.18), channel_id=1, source_target_pairs={{0,16},{16,0},{1,17},{17,1},{2,18},{18,2},{3,19},{19,3},{4,20},{20... | collective-permute-start | bytes 417800 | tf_op jit(solution)/shard_map/ppermute | solution.py:57
  13.9 8.5 %collective-permute-start.5 = (bf16[128,512]{1,0:T(8,128)(2,1)S(1)}, bf16[128,512]{1,0:T(8,128)(2,1)S(1)}, u32[]{:S(2)}, u32[]{:S(2)}) collective-permute-start(bf16[128,512]{1,0:T(8,128)(2,1)S(1)} %get-tuple-element.600), channel_id=1, source_target_pairs={{0,12},{4,8},{8,4},{12,0},{1,13},{5,9},{9,5},{13,1},{2,14},{6,10},... | collective-permute-start | bytes 393224 | tf_op jit(solution)/shard_map/ppermute | solution.py:57
  16.4 6.0 %collective-permute-start.3 = (bf16[128,512]{1,0:T(8,128)(2,1)S(1)}, bf16[128,512]{1,0:T(8,128)(2,1)S(1)}, u32[]{:S(2)}, u32[]{:S(2)}) collective-permute-start(bf16[128,512]{1,0:T(8,128)(2,1)S(1)} %get-tuple-element.602), channel_id=1, source_target_pairs={{0,4},{4,0},{8,12},{12,8},{1,5},{5,1},{9,13},{13,9},{2,6},{6,2},{1... | collective-permute-start | bytes 393224 | tf_op jit(solution)/shard_map/ppermute | solution.py:57
  17.0 7.2 %collective-permute-start.4 = (bf16[128,512]{1,0:T(8,128)(2,1)S(1)}, bf16[128,512]{1,0:T(8,128)(2,1)S(1)}, u32[]{:S(2)}, u32[]{:S(2)}) collective-permute-start(bf16[128,512]{1,0:T(8,128)(2,1)S(1)} %get-tuple-element.603), channel_id=1, source_target_pairs={{0,8},{4,12},{8,0},{12,4},{1,9},{5,13},{9,1},{13,5},{2,10},{6,14},... | collective-permute-start | bytes 393224 | tf_op jit(solution)/shard_map/ppermute | solution.py:57
  17.4 6.8 %collective-permute-start.1 = (bf16[1,272,512]{2,1,0:T(8,128)(2,1)S(1)}, bf16[1,272,512]{2,1,0:T(8,128)(2,1)S(1)}, u32[]{:S(2)}, u32[]{:S(2)}) collective-permute-start(bf16[1,272,512]{2,1,0:T(8,128)(2,1)S(1)} %get-tuple-element.259), channel_id=1, source_target_pairs={{0,1},{1,0},{2,3},{3,2},{4,5},{5,4},{6,7},{7,6},{8,9},{9,8},{10,11... | collective-permute-start | bytes 835592 | tf_op jit(solution)/shard_map/ppermute | solution.py:57
  20.2 7.3 %collective-permute-start.2 = (bf16[1,272,512]{2,1,0:T(8,128)(2,1)S(1)}, bf16[1,272,512]{2,1,0:T(8,128)(2,1)S(1)}, u32[]{:S(2)}, u32[]{:S(2)}) collective-permute-start(bf16[1,272,512]{2,1,0:T(8,128)(2,1)S(1)} %get-tuple-element.260), channel_id=1, source_target_pairs={{0,2},{1,3},{2,0},{3,1},{4,6},{5,7},{6,4},{7,5},{8,10},{9,11},{10,... | collective-permute-start | bytes 835592 | tf_op jit(solution)/shard_map/ppermute | solution.py:57
  27.6 6.5 %collective-permute-start.10 = (bf16[2,2,16,2176]{3,2,1,0:T(8,128)(2,1)S(1)}, bf16[2,2,16,2176]{3,2,1,0:T(8,128)(2,1)S(1)}, u32[]{:S(2)}, u32[]{:S(2)}) collective-permute-start(bf16[2,2,16,2176]{3,2,1,0:T(8,128)(2,1)S(1)} %pad_maximum_fusion.17), channel_id=1, source_target_pairs={{0,4},{4,0},{8,12},{12,8},{1,5},{5,1},{9,13},{13,9},{2,6},{6,2},{1... | collective-permute-start | bytes 835592 | tf_op jit(solution)/shard_map/ppermute | solution.py:57
  28.4 10.0 %collective-permute-start.9 = (bf16[2,2,16,2176]{3,2,1,0:T(8,128)(2,1)S(1)}, bf16[2,2,16,2176]{3,2,1,0:T(8,128)(2,1)S(1)}, u32[]{:S(2)}, u32[]{:S(2)}) collective-permute-start(bf16[2,2,16,2176]{3,2,1,0:T(8,128)(2,1)S(1)} %pad_maximum_fusion.17), channel_id=1, source_target_pairs={{0,8},{4,12},{8,0},{12,4},{1,9},{5,13},{9,1},{13,5},{2,10},{6,14},... | collective-permute-start | bytes 835592 | tf_op jit(solution)/shard_map/ppermute | solution.py:57
  30.9 11.7 %collective-permute-start.8 = (bf16[2,2,16,2176]{3,2,1,0:T(8,128)(2,1)S(1)}, bf16[2,2,16,2176]{3,2,1,0:T(8,128)(2,1)S(1)}, u32[]{:S(2)}, u32[]{:S(2)}) collective-permute-start(bf16[2,2,16,2176]{3,2,1,0:T(8,128)(2,1)S(1)} %pad_maximum_fusion.17), channel_id=1, source_target_pairs={{0,12},{4,8},{8,4},{12,0},{1,13},{5,9},{9,5},{13,1},{2,14},{6,10},... | collective-permute-start | bytes 835592 | tf_op jit(solution)/shard_map/ppermute | solution.py:57
  31.1 11.8 %collective-permute-start.7 = (bf16[1,272,512]{2,1,0:T(8,128)(2,1)S(1)}, bf16[1,272,512]{2,1,0:T(8,128)(2,1)S(1)}, u32[]{:S(2)}, u32[]{:S(2)}) collective-permute-start(bf16[1,272,512]{2,1,0:T(8,128)(2,1)S(1)} %get-tuple-element.272), channel_id=1, source_target_pairs={{0,3},{1,2},{2,1},{3,0},{4,7},{5,6},{6,5},{7,4},{8,11},{9,10},{10,... | collective-permute-start | bytes 835592 | tf_op jit(solution)/shard_map/ppermute | solution.py:57
  43.6 2.8 collective-permute-start.11
  47.7 16.4 %collective-permute-start.15 = (bf16[4,64,512]{2,1,0:T(8,128)(2,1)S(1)}, bf16[4,64,512]{2,1,0:T(8,128)(2,1)S(1)}, u32[]{:S(2)}, u32[]{:S(2)}) collective-permute-start(bf16[4,64,512]{2,1,0:T(8,128)(2,1)S(1)} %slice.48), channel_id=1, source_target_pairs={{0,16},{16,0},{1,17},{17,1},{2,18},{18,2},{3,19},{19,3},{4,20},{20... | collective-permute-start | bytes 786440 | tf_op jit(solution)/shard_map/ppermute | solution.py:57
  51.0 13.1 %collective-permute-start.12 = (bf16[1,272,512]{2,1,0:T(8,128)(2,1)S(1)}, bf16[1,272,512]{2,1,0:T(8,128)(2,1)S(1)}, u32[]{:S(2)}, u32[]{:S(2)}) collective-permute-start(bf16[1,272,512]{2,1,0:T(8,128)(2,1)S(1)} %copy-done.51), channel_id=1, source_target_pairs={{0,1},{1,0},{2,3},{3,2},{4,5},{5,4},{6,7},{7,6},{8,9},{9,8},{10,11... | collective-permute-start | bytes 835592 | tf_op jit(solution)/shard_map/ppermute | solution.py:57
  51.0 13.1 %collective-permute-start.13 = (bf16[1,272,512]{2,1,0:T(8,128)(2,1)S(1)}, bf16[1,272,512]{2,1,0:T(8,128)(2,1)S(1)}, u32[]{:S(2)}, u32[]{:S(2)}) collective-permute-start(bf16[1,272,512]{2,1,0:T(8,128)(2,1)S(1)} %copy-done.50), channel_id=1, source_target_pairs={{0,2},{1,3},{2,0},{3,1},{4,6},{5,7},{6,4},{7,5},{8,10},{9,11},{10,... | collective-permute-start | bytes 835592 | tf_op jit(solution)/shard_map/ppermute | solution.py:57
  51.6 14.0 %collective-permute-start.14 = (bf16[1,272,512]{2,1,0:T(8,128)(2,1)S(1)}, bf16[1,272,512]{2,1,0:T(8,128)(2,1)S(1)}, u32[]{:S(2)}, u32[]{:S(2)}) collective-permute-start(bf16[1,272,512]{2,1,0:T(8,128)(2,1)S(1)} %copy-done.49), channel_id=1, source_target_pairs={{0,3},{1,2},{2,1},{3,0},{4,7},{5,6},{6,5},{7,4},{8,11},{9,10},{10,... | collective-permute-start | bytes 835592 | tf_op jit(solution)/shard_map/ppermute | solution.py:57
  65.6 15.0 %collective-permute-start.17 = (bf16[4,64,512]{2,1,0:T(8,128)(2,1)S(1)}, bf16[4,64,512]{2,1,0:T(8,128)(2,1)S(1)}, u32[]{:S(2)}, u32[]{:S(2)}) collective-permute-start(bf16[4,64,512]{2,1,0:T(8,128)(2,1)S(1)} %get-tuple-element.345), channel_id=1, source_target_pairs={{0,16},{16,0},{1,17},{17,1},{2,18},{18,2},{3,19},{19,3},{4,20},{20... | collective-permute-start | bytes 786440 | tf_op jit(solution)/shard_map/ppermute | solution.py:57
  65.6 15.1 %collective-permute-start.16 = (bf16[2,4,64,512]{3,2,1,0:T(8,128)(2,1)S(1)}, bf16[2,4,64,512]{3,2,1,0:T(8,128)(2,1)S(1)}, u32[]{:S(2)}, u32[]{:S(2)}) collective-permute-start(bf16[2,4,64,512]{3,2,1,0:T(8,128)(2,1)S(1)} %pad_maximum_fusion.7), channel_id=1, source_target_pairs={{0,2},{1,3},{2,0},{3,1},{4,6},{5,7},{6,4},{7,5},{8,10},{9,11},{10,... | collective-permute-start | bytes 1572872 | tf_op jit(solution)/shard_map/ppermute | solution.py:57
  81.0 19.4 %collective-permute-start.18 = (bf16[2,128,512]{2,1,0:T(8,128)(2,1)S(1)}, bf16[2,128,512]{2,1,0:T(8,128)(2,1)S(1)}, u32[]{:S(2)}, u32[]{:S(2)}) collective-permute-start(bf16[2,128,512]{2,1,0:T(8,128)(2,1)S(1)} %get-tuple-element.353), channel_id=1, source_target_pairs={{0,1},{1,0},{2,3},{3,2},{4,5},{5,4},{6,7},{7,6},{8,9},{9,8},{10,11... | collective-permute-start | bytes 786440 | tf_op jit(solution)/shard_map/ppermute | solution.py:57
  81.1 19.4 %collective-permute-start.19 = (bf16[2,128,512]{2,1,0:T(8,128)(2,1)S(1)}, bf16[2,128,512]{2,1,0:T(8,128)(2,1)S(1)}, u32[]{:S(2)}, u32[]{:S(2)}) collective-permute-start(bf16[2,128,512]{2,1,0:T(8,128)(2,1)S(1)} %get-tuple-element.354), channel_id=1, source_target_pairs={{0,2},{1,3},{2,0},{3,1},{4,6},{5,7},{6,4},{7,5},{8,10},{9,11},{10,... | collective-permute-start | bytes 786440 | tf_op jit(solution)/shard_map/ppermute | solution.py:57
  82.6 17.8 %collective-permute-start.20 = (bf16[2,128,512]{2,1,0:T(8,128)(2,1)S(1)}, bf16[2,128,512]{2,1,0:T(8,128)(2,1)S(1)}, u32[]{:S(2)}, u32[]{:S(2)}) collective-permute-start(bf16[2,128,512]{2,1,0:T(8,128)(2,1)S(1)} %get-tuple-element.355), channel_id=1, source_target_pairs={{0,3},{1,2},{2,1},{3,0},{4,7},{5,6},{6,5},{7,4},{8,11},{9,10},{10,... | collective-permute-start | bytes 786440 | tf_op jit(solution)/shard_map/ppermute | solution.py:57
  98.5 6.3 %collective-permute-start.21 = (bf16[2,128,512]{2,1,0:T(8,128)(2,1)S(1)}, bf16[2,128,512]{2,1,0:T(8,128)(2,1)S(1)}, u32[]{:S(2)}, u32[]{:S(2)}) collective-permute-start(bf16[2,128,512]{2,1,0:T(8,128)(2,1)S(1)} %get-tuple-element.367), channel_id=1, source_target_pairs={{0,1},{1,0},{2,3},{3,2},{4,5},{5,4},{6,7},{7,6},{8,9},{9,8},{10,11... | collective-permute-start | bytes 786440 | tf_op jit(solution)/shard_map/ppermute | solution.py:57
  98.8 9.2 %collective-permute-start.22 = (bf16[2,128,512]{2,1,0:T(8,128)(2,1)S(1)}, bf16[2,128,512]{2,1,0:T(8,128)(2,1)S(1)}, u32[]{:S(2)}, u32[]{:S(2)}) collective-permute-start(bf16[2,128,512]{2,1,0:T(8,128)(2,1)S(1)} %get-tuple-element.368), channel_id=1, source_target_pairs={{0,2},{1,3},{2,0},{3,1},{4,6},{5,7},{6,4},{7,5},{8,10},{9,11},{10,... | collective-permute-start | bytes 786440 | tf_op jit(solution)/shard_map/ppermute | solution.py:57
  100.4 11.7 %collective-permute-start.23 = (bf16[2,128,512]{2,1,0:T(8,128)(2,1)S(1)}, bf16[2,128,512]{2,1,0:T(8,128)(2,1)S(1)}, u32[]{:S(2)}, u32[]{:S(2)}) collective-permute-start(bf16[2,128,512]{2,1,0:T(8,128)(2,1)S(1)} %get-tuple-element.369), channel_id=1, source_target_pairs={{0,3},{1,2},{2,1},{3,0},{4,7},{5,6},{6,5},{7,4},{8,11},{9,10},{10,... | collective-permute-start | bytes 786440 | tf_op jit(solution)/shard_map/ppermute | solution.py:57
  112.1 14.4 %collective-permute-start.27 = (bf16[2,4,64,512]{3,2,1,0:T(8,128)(2,1)S(1)}, bf16[2,4,64,512]{3,2,1,0:T(8,128)(2,1)S(1)}, u32[]{:S(2)}, u32[]{:S(2)}) collective-permute-start(bf16[2,4,64,512]{3,2,1,0:T(8,128)(2,1)S(1)} %pad_maximum_fusion.8), channel_id=1, source_target_pairs={{0,2},{1,3},{2,0},{3,1},{4,6},{5,7},{6,4},{7,5},{8,10},{9,11},{10,... | collective-permute-start | bytes 1572872 | tf_op jit(solution)/shard_map/ppermute | solution.py:57
  113.6 21.0 %collective-permute-start.29 = (bf16[16,64,512]{2,1,0:T(8,128)(2,1)S(1)}, bf16[16,64,512]{2,1,0:T(8,128)(2,1)S(1)}, u32[]{:S(2)}, u32[]{:S(2)}) collective-permute-start(bf16[16,64,512]{2,1,0:T(8,128)(2,1)S(1)} %bitcast.175), channel_id=1, source_target_pairs={{0,1},{1,0},{2,3},{3,2},{4,5},{5,4},{6,7},{7,6},{8,9},{9,8},{10,11... | collective-permute-start | bytes 3145736 | tf_op jit(solution)/shard_map/ppermute | solution.py:57
  114.1 12.6 %collective-permute-start.24 = (bf16[128,1152]{1,0:T(8,128)(2,1)S(1)}, bf16[128,1152]{1,0:T(8,128)(2,1)S(1)}, u32[]{:S(2)}, u32[]{:S(2)}) collective-permute-start(bf16[128,1152]{1,0:T(8,128)(2,1)S(1)} %get-tuple-element.380), channel_id=1, source_target_pairs={{0,4},{4,0},{8,12},{12,8},{1,5},{5,1},{9,13},{13,9},{2,6},{6,2},{1... | collective-permute-start | bytes 884744 | tf_op jit(solution)/shard_map/ppermute | solution.py:57
  115.6 11.1 %collective-permute-start.25 = (bf16[128,1152]{1,0:T(8,128)(2,1)S(1)}, bf16[128,1152]{1,0:T(8,128)(2,1)S(1)}, u32[]{:S(2)}, u32[]{:S(2)}) collective-permute-start(bf16[128,1152]{1,0:T(8,128)(2,1)S(1)} %get-tuple-element.381), channel_id=1, source_target_pairs={{0,8},{4,12},{8,0},{12,4},{1,9},{5,13},{9,1},{13,5},{2,10},{6,14},... | collective-permute-start | bytes 884744 | tf_op jit(solution)/shard_map/ppermute | solution.py:57
  117.5 13.3 %collective-permute-start.26 = (bf16[128,1152]{1,0:T(8,128)(2,1)S(1)}, bf16[128,1152]{1,0:T(8,128)(2,1)S(1)}, u32[]{:S(2)}, u32[]{:S(2)}) collective-permute-start(bf16[128,1152]{1,0:T(8,128)(2,1)S(1)} %get-tuple-element.382), channel_id=1, source_target_pairs={{0,12},{4,8},{8,4},{12,0},{1,13},{5,9},{9,5},{13,1},{2,14},{6,10},... | collective-permute-start | bytes 884744 | tf_op jit(solution)/shard_map/ppermute | solution.py:57
  130.9 3.6 %collective-permute-start.30 = (bf16[16,64,512]{2,1,0:T(8,128)(2,1)S(1)}, bf16[16,64,512]{2,1,0:T(8,128)(2,1)S(1)}, u32[]{:S(2)}, u32[]{:S(2)}) collective-permute-start(bf16[16,64,512]{2,1,0:T(8,128)(2,1)S(1)} %bitcast.178), channel_id=1, source_target_pairs={{0,1},{1,0},{2,3},{3,2},{4,5},{5,4},{6,7},{7,6},{8,9},{9,8},{10,11... | collective-permute-start | bytes 3145736 | tf_op jit(solution)/shard_map/ppermute | solution.py:57
  131.0 9.4 %collective-permute-start.28 = (bf16[128,1152]{1,0:T(8,128)(2,1)S(1)}, bf16[128,1152]{1,0:T(8,128)(2,1)S(1)}, u32[]{:S(2)}, u32[]{:S(2)}) collective-permute-start(bf16[128,1152]{1,0:T(8,128)(2,1)S(1)} %get-tuple-element.385), channel_id=1, source_target_pairs={{0,4},{4,0},{8,12},{12,8},{1,5},{5,1},{9,13},{13,9},{2,6},{6,2},{1... | collective-permute-start | bytes 884744 | tf_op jit(solution)/shard_map/ppermute | solution.py:57
  132.6 11.4 %collective-permute-start.31 = (bf16[128,1152]{1,0:T(8,128)(2,1)S(1)}, bf16[128,1152]{1,0:T(8,128)(2,1)S(1)}, u32[]{:S(2)}, u32[]{:S(2)}) collective-permute-start(bf16[128,1152]{1,0:T(8,128)(2,1)S(1)} %get-tuple-element.394), channel_id=1, source_target_pairs={{0,8},{4,12},{8,0},{12,4},{1,9},{5,13},{9,1},{13,5},{2,10},{6,14},... | collective-permute-start | bytes 884744 | tf_op jit(solution)/shard_map/ppermute | solution.py:57
  134.3 14.5 %collective-permute-start.32 = (bf16[128,1152]{1,0:T(8,128)(2,1)S(1)}, bf16[128,1152]{1,0:T(8,128)(2,1)S(1)}, u32[]{:S(2)}, u32[]{:S(2)}) collective-permute-start(bf16[128,1152]{1,0:T(8,128)(2,1)S(1)} %get-tuple-element.395), channel_id=1, source_target_pairs={{0,12},{4,8},{8,4},{12,0},{1,13},{5,9},{9,5},{13,1},{2,14},{6,10},... | collective-permute-start | bytes 884744 | tf_op jit(solution)/shard_map/ppermute | solution.py:57
  140.5 16.0 %collective-permute-start.35 = (bf16[128,1152]{1,0:T(8,128)(2,1)S(1)}, bf16[128,1152]{1,0:T(8,128)(2,1)S(1)}, u32[]{:S(2)}, u32[]{:S(2)}) collective-permute-start(bf16[128,1152]{1,0:T(8,128)(2,1)S(1)} %get-tuple-element.405.refs_1_), channel_id=1, source_target_pairs={{0,12},{4,8},{8,4},{12,0},{1,13},{5,9},{9,5},{13,1},{2,14},{6,10},... | collective-permute-start | bytes 884744 | tf_op jit(solution)/shard_map/ppermute | solution.py:57
  143.1 17.5 %collective-permute-start.34 = (bf16[128,1152]{1,0:T(8,128)(2,1)S(1)}, bf16[128,1152]{1,0:T(8,128)(2,1)S(1)}, u32[]{:S(2)}, u32[]{:S(2)}) collective-permute-start(bf16[128,1152]{1,0:T(8,128)(2,1)S(1)} %get-tuple-element.405.refs_1_), channel_id=1, source_target_pairs={{0,8},{4,12},{8,0},{12,4},{1,9},{5,13},{9,1},{13,5},{2,10},{6,14},... | collective-permute-start | bytes 884744 | tf_op jit(solution)/shard_map/ppermute | solution.py:57
  143.4 17.3 %collective-permute-start.33 = (bf16[128,1152]{1,0:T(8,128)(2,1)S(1)}, bf16[128,1152]{1,0:T(8,128)(2,1)S(1)}, u32[]{:S(2)}, u32[]{:S(2)}) collective-permute-start(bf16[128,1152]{1,0:T(8,128)(2,1)S(1)} %get-tuple-element.405.refs_1_), channel_id=1, source_target_pairs={{0,4},{4,0},{8,12},{12,8},{1,5},{5,1},{9,13},{13,9},{2,6},{6,2},{1... | collective-permute-start | bytes 884744 | tf_op jit(solution)/shard_map/ppermute | solution.py:57
  160.7 15.6 %collective-permute-start.39 = (bf16[16,128,512]{2,1,0:T(8,128)(2,1)}, bf16[16,128,512]{2,1,0:T(8,128)(2,1)}, u32[]{:S(2)}, u32[]{:S(2)}) collective-permute-start(bf16[16,128,512]{2,1,0:T(8,128)(2,1)} %get-tuple-element.414), channel_id=1, source_target_pairs={{0,1},{1,0},{2,3},{3,2},{4,5},{5,4},{6,7},{7,6},{8,9},{9,8},{10,11... | collective-permute-start | bytes 6291464 | tf_op jit(solution)/shard_map/ppermute | solution.py:57
  160.8 18.6 %collective-permute-start.38 = (bf16[128,1152]{1,0:T(8,128)(2,1)S(1)}, bf16[128,1152]{1,0:T(8,128)(2,1)S(1)}, u32[]{:S(2)}, u32[]{:S(2)}) collective-permute-start(bf16[128,1152]{1,0:T(8,128)(2,1)S(1)} %get-tuple-element.415.refs_1_), channel_id=1, source_target_pairs={{0,12},{4,8},{8,4},{12,0},{1,13},{5,9},{9,5},{13,1},{2,14},{6,10},... | collective-permute-start | bytes 884744 | tf_op jit(solution)/shard_map/ppermute | solution.py:57
  163.3 17.3 %collective-permute-start.37 = (bf16[128,1152]{1,0:T(8,128)(2,1)S(1)}, bf16[128,1152]{1,0:T(8,128)(2,1)S(1)}, u32[]{:S(2)}, u32[]{:S(2)}) collective-permute-start(bf16[128,1152]{1,0:T(8,128)(2,1)S(1)} %get-tuple-element.415.refs_1_), channel_id=1, source_target_pairs={{0,8},{4,12},{8,0},{12,4},{1,9},{5,13},{9,1},{13,5},{2,10},{6,14},... | collective-permute-start | bytes 884744 | tf_op jit(solution)/shard_map/ppermute | solution.py:57
  163.6 17.0 %collective-permute-start.36 = (bf16[128,1152]{1,0:T(8,128)(2,1)S(1)}, bf16[128,1152]{1,0:T(8,128)(2,1)S(1)}, u32[]{:S(2)}, u32[]{:S(2)}) collective-permute-start(bf16[128,1152]{1,0:T(8,128)(2,1)S(1)} %get-tuple-element.415.refs_1_), channel_id=1, source_target_pairs={{0,4},{4,0},{8,12},{12,8},{1,5},{5,1},{9,13},{13,9},{2,6},{6,2},{1... | collective-permute-start | bytes 884744 | tf_op jit(solution)/shard_map/ppermute | solution.py:57
  176.2 18.3 %collective-permute-start.40 = (bf16[2,128,512]{2,1,0:T(8,128)(2,1)}, bf16[2,128,512]{2,1,0:T(8,128)(2,1)S(1)}, u32[]{:S(2)}, u32[]{:S(2)}) collective-permute-start(bf16[2,128,512]{2,1,0:T(8,128)(2,1)} %get-tuple-element.425), channel_id=1, source_target_pairs={{0,1},{1,0},{2,3},{3,2},{4,5},{5,4},{6,7},{7,6},{8,9},{9,8},{10,11... | collective-permute-start | bytes 786440 | tf_op jit(solution)/shard_map/ppermute | solution.py:57
  176.2 19.2 %collective-permute-start.41 = (bf16[2,128,512]{2,1,0:T(8,128)(2,1)}, bf16[2,128,512]{2,1,0:T(8,128)(2,1)S(1)}, u32[]{:S(2)}, u32[]{:S(2)}) collective-permute-start(bf16[2,128,512]{2,1,0:T(8,128)(2,1)} %get-tuple-element.426), channel_id=1, source_target_pairs={{0,2},{1,3},{2,0},{3,1},{4,6},{5,7},{6,4},{7,5},{8,10},{9,11},{10,... | collective-permute-start | bytes 786440 | tf_op jit(solution)/shard_map/ppermute | solution.py:57
  179.3 16.1 %collective-permute-start.42 = (bf16[2,128,512]{2,1,0:T(8,128)(2,1)}, bf16[2,128,512]{2,1,0:T(8,128)(2,1)S(1)}, u32[]{:S(2)}, u32[]{:S(2)}) collective-permute-start(bf16[2,128,512]{2,1,0:T(8,128)(2,1)} %get-tuple-element.427), channel_id=1, source_target_pairs={{0,3},{1,2},{2,1},{3,0},{4,7},{5,6},{6,5},{7,4},{8,11},{9,10},{10,... | collective-permute-start | bytes 786440 | tf_op jit(solution)/shard_map/ppermute | solution.py:57
  193.9 9.5 %collective-permute-start.44 = (bf16[2,128,512]{2,1,0:T(8,128)(2,1)}, bf16[2,128,512]{2,1,0:T(8,128)(2,1)}, u32[]{:S(2)}, u32[]{:S(2)}) collective-permute-start(bf16[2,128,512]{2,1,0:T(8,128)(2,1)} %get-tuple-element.430), channel_id=1, source_target_pairs={{0,2},{1,3},{2,0},{3,1},{4,6},{5,7},{6,4},{7,5},{8,10},{9,11},{10,... | collective-permute-start | bytes 786440 | tf_op jit(solution)/shard_map/ppermute | solution.py:57
  194.5 13.0 %collective-permute-start.45 = (bf16[2,128,512]{2,1,0:T(8,128)(2,1)}, bf16[2,128,512]{2,1,0:T(8,128)(2,1)}, u32[]{:S(2)}, u32[]{:S(2)}) collective-permute-start(bf16[2,128,512]{2,1,0:T(8,128)(2,1)} %get-tuple-element.431), channel_id=1, source_target_pairs={{0,3},{1,2},{2,1},{3,0},{4,7},{5,6},{6,5},{7,4},{8,11},{9,10},{10,... | collective-permute-start | bytes 786440 | tf_op jit(solution)/shard_map/ppermute | solution.py:57
  207.5 30.1 %collective-permute-start.46 = (bf16[16,16,640]{2,1,0:T(8,128)(2,1)}, bf16[16,16,640]{2,1,0:T(8,128)(2,1)S(1)}, u32[]{:S(2)}, u32[]{:S(2)}) collective-permute-start(bf16[16,16,640]{2,1,0:T(8,128)(2,1)} %get-tuple-element.454), channel_id=1, source_target_pairs={{0,1},{1,0},{2,3},{3,2},{4,5},{5,4},{6,7},{7,6},{8,9},{9,8},{10,11... | collective-permute-start | bytes 983048 | tf_op jit(solution)/shard_map/ppermute | solution.py:57
  208.1 29.5 %collective-permute-start.47 = (bf16[2,4,128,512]{3,2,1,0:T(8,128)(2,1)}, bf16[2,4,128,512]{3,2,1,0:T(8,128)(2,1)S(1)}, u32[]{:S(2)}, u32[]{:S(2)}) collective-permute-start(bf16[2,4,128,512]{3,2,1,0:T(8,128)(2,1)} %fusion), channel_id=1, source_target_pairs={{0,2},{1,3},{2,0},{3,1},{4,6},{5,7},{6,4},{7,5},{8,10},{9,11},{10,... | collective-permute-start | bytes 3145736 | tf_op jit(solution)/shard_map/ppermute | solution.py:57
  240.0 34.5 %collective-permute-start.48 = (bf16[1,256,512]{2,1,0:T(8,128)(2,1)}, bf16[1,256,512]{2,1,0:T(8,128)(2,1)S(1)}, u32[]{:S(2)}, u32[]{:S(2)}) collective-permute-start(bf16[1,256,512]{2,1,0:T(8,128)(2,1)} %get-tuple-element.470), channel_id=1, source_target_pairs={{0,1},{1,0},{2,3},{3,2},{4,5},{5,4},{6,7},{7,6},{8,9},{9,8},{10,11... | collective-permute-start | bytes 786440 | tf_op jit(solution)/shard_map/ppermute | solution.py:57
  240.0 34.5 %collective-permute-start.49 = (bf16[1,256,512]{2,1,0:T(8,128)(2,1)}, bf16[1,256,512]{2,1,0:T(8,128)(2,1)S(1)}, u32[]{:S(2)}, u32[]{:S(2)}) collective-permute-start(bf16[1,256,512]{2,1,0:T(8,128)(2,1)} %get-tuple-element.471), channel_id=1, source_target_pairs={{0,2},{1,3},{2,0},{3,1},{4,6},{5,7},{6,4},{7,5},{8,10},{9,11},{10,... | collective-permute-start | bytes 786440 | tf_op jit(solution)/shard_map/ppermute | solution.py:57
  241.6 32.9 %collective-permute-start.50 = (bf16[1,256,512]{2,1,0:T(8,128)(2,1)}, bf16[1,256,512]{2,1,0:T(8,128)(2,1)S(1)}, u32[]{:S(2)}, u32[]{:S(2)}) collective-permute-start(bf16[1,256,512]{2,1,0:T(8,128)(2,1)} %get-tuple-element.472), channel_id=1, source_target_pairs={{0,3},{1,2},{2,1},{3,0},{4,7},{5,6},{6,5},{7,4},{8,11},{9,10},{10,... | collective-permute-start | bytes 786440 | tf_op jit(solution)/shard_map/ppermute | solution.py:57
  241.9 32.6 %collective-permute-start.51 = (bf16[4,128,512]{2,1,0:T(8,128)(2,1)S(1)}, bf16[4,128,512]{2,1,0:T(8,128)(2,1)}, u32[]{:S(2)}, u32[]{:S(2)}) collective-permute-start(bf16[4,128,512]{2,1,0:T(8,128)(2,1)S(1)} %fusion.2), channel_id=1, source_target_pairs={{0,16},{16,0},{1,17},{17,1},{2,18},{18,2},{3,19},{19,3},{4,20},{20... | collective-permute-start | bytes 1572872 | tf_op jit(solution)/shard_map/ppermute | solution.py:57
  274.5 10.2 %collective-permute-start.54 = (bf16[16,16,1536]{2,1,0:T(8,128)(2,1)}, bf16[16,16,1536]{2,1,0:T(8,128)(2,1)}, u32[]{:S(2)}, u32[]{:S(2)}) collective-permute-start(bf16[16,16,1536]{2,1,0:T(8,128)(2,1)} %get-tuple-element.482), channel_id=1, source_target_pairs={{0,1},{1,0},{2,3},{3,2},{4,5},{5,4},{6,7},{7,6},{8,9},{9,8},{10,11... | collective-permute-start | bytes 2359304 | tf_op jit(solution)/shard_map/ppermute | solution.py:57
  275.8 6.5 %collective-permute-start.52 = (bf16[1,256,512]{2,1,0:T(8,128)(2,1)}, bf16[1,256,512]{2,1,0:T(8,128)(2,1)S(1)}, u32[]{:S(2)}, u32[]{:S(2)}) collective-permute-start(bf16[1,256,512]{2,1,0:T(8,128)(2,1)} %get-tuple-element.479), channel_id=1, source_target_pairs={{0,1},{1,0},{2,3},{3,2},{4,5},{5,4},{6,7},{7,6},{8,9},{9,8},{10,11... | collective-permute-start | bytes 786440 | tf_op jit(solution)/shard_map/ppermute | solution.py:57
  276.2 8.5 %collective-permute-start.53 = (bf16[1,256,512]{2,1,0:T(8,128)(2,1)}, bf16[1,256,512]{2,1,0:T(8,128)(2,1)S(1)}, u32[]{:S(2)}, u32[]{:S(2)}) collective-permute-start(bf16[1,256,512]{2,1,0:T(8,128)(2,1)} %get-tuple-element.480), channel_id=1, source_target_pairs={{0,2},{1,3},{2,0},{3,1},{4,6},{5,7},{6,4},{7,5},{8,10},{9,11},{10,... | collective-permute-start | bytes 786440 | tf_op jit(solution)/shard_map/ppermute | solution.py:57
  279.4 10.0 %collective-permute-start.58 = (bf16[128,512]{1,0:T(8,128)(2,1)S(1)}, bf16[128,512]{1,0:T(8,128)(2,1)S(1)}, u32[]{:S(2)}, u32[]{:S(2)}) collective-permute-start(bf16[128,512]{1,0:T(8,128)(2,1)S(1)} %get-tuple-element.577), channel_id=1, source_target_pairs={{0,12},{4,8},{8,4},{12,0},{1,13},{5,9},{9,5},{13,1},{2,14},{6,10},... | collective-permute-start | bytes 393224 | tf_op jit(solution)/shard_map/ppermute | solution.py:57
  281.9 20.5 %collective-permute-start.57 = (bf16[128,512]{1,0:T(8,128)(2,1)S(1)}, bf16[128,512]{1,0:T(8,128)(2,1)S(1)}, u32[]{:S(2)}, u32[]{:S(2)}) collective-permute-start(bf16[128,512]{1,0:T(8,128)(2,1)S(1)} %get-tuple-element.578), channel_id=1, source_target_pairs={{0,8},{4,12},{8,0},{12,4},{1,9},{5,13},{9,1},{13,5},{2,10},{6,14},... | collective-permute-start | bytes 393224 | tf_op jit(solution)/shard_map/ppermute | solution.py:57
  282.3 20.2 %collective-permute-start.56 = (bf16[128,512]{1,0:T(8,128)(2,1)S(1)}, bf16[128,512]{1,0:T(8,128)(2,1)S(1)}, u32[]{:S(2)}, u32[]{:S(2)}) collective-permute-start(bf16[128,512]{1,0:T(8,128)(2,1)S(1)} %get-tuple-element.579), channel_id=1, source_target_pairs={{0,4},{4,0},{8,12},{12,8},{1,5},{5,1},{9,13},{13,9},{2,6},{6,2},{1... | collective-permute-start | bytes 393224 | tf_op jit(solution)/shard_map/ppermute | solution.py:57
  284.8 8.6 %collective-permute-start.55 = (bf16[1,256,512]{2,1,0:T(8,128)(2,1)S(1)}, bf16[1,256,512]{2,1,0:T(8,128)(2,1)S(1)}, u32[]{:S(2)}, u32[]{:S(2)}) collective-permute-start(bf16[1,256,512]{2,1,0:T(8,128)(2,1)S(1)} %copy-done.59), channel_id=1, source_target_pairs={{0,3},{1,2},{2,1},{3,0},{4,7},{5,6},{6,5},{7,4},{8,11},{9,10},{10,... | collective-permute-start | bytes 786440 | tf_op jit(solution)/shard_map/ppermute | solution.py:57
  286.9 15.6 %collective-permute-start.61 = (bf16[2,2,16,2176]{3,2,1,0:T(8,128)(2,1)S(1)}, bf16[2,2,16,2176]{3,2,1,0:T(8,128)(2,1)S(1)}, u32[]{:S(2)}, u32[]{:S(2)}) collective-permute-start(bf16[2,2,16,2176]{3,2,1,0:T(8,128)(2,1)S(1)} %get-tuple-element.558), channel_id=1, source_target_pairs={{0,12},{4,8},{8,4},{12,0},{1,13},{5,9},{9,5},{13,1},{2,14},{6,10},... | collective-permute-start | bytes 835592 | tf_op jit(solution)/shard_map/ppermute | solution.py:220
  289.4 13.9 %collective-permute-start.59 = (bf16[2,2,16,2176]{3,2,1,0:T(8,128)(2,1)S(1)}, bf16[2,2,16,2176]{3,2,1,0:T(8,128)(2,1)S(1)}, u32[]{:S(2)}, u32[]{:S(2)}) collective-permute-start(bf16[2,2,16,2176]{3,2,1,0:T(8,128)(2,1)S(1)} %get-tuple-element.559), channel_id=1, source_target_pairs={{0,4},{4,0},{8,12},{12,8},{1,5},{5,1},{9,13},{13,9},{2,6},{6,2},{1... | collective-permute-start | bytes 835592 | tf_op jit(solution)/shard_map/ppermute | solution.py:220
  293.3 10.0 %collective-permute-start.60 = (bf16[2,2,16,2176]{3,2,1,0:T(8,128)(2,1)S(1)}, bf16[2,2,16,2176]{3,2,1,0:T(8,128)(2,1)S(1)}, u32[]{:S(2)}, u32[]{:S(2)}) collective-permute-start(bf16[2,2,16,2176]{3,2,1,0:T(8,128)(2,1)S(1)} %get-tuple-element.560), channel_id=1, source_target_pairs={{0,8},{4,12},{8,0},{12,4},{1,9},{5,13},{9,1},{13,5},{2,10},{6,14},... | collective-permute-start | bytes 835592 | tf_op jit(solution)/shard_map/ppermute | solution.py:220
  303.5 6.4 %collective-permute-start.62 = (bf16[16,2176]{1,0:T(8,128)(2,1)S(1)}, bf16[16,2176]{1,0:T(8,128)(2,1)S(1)}, u32[]{:S(2)}, u32[]{:S(2)}) collective-permute-start(bf16[16,2176]{1,0:T(8,128)(2,1)S(1)} %get-tuple-element.590), channel_id=1, source_target_pairs={{0,2},{1,3},{2,0},{3,1},{16,18},{17,19},{18,16},{19,17},{4,6},{5,7... | collective-permute-start | bytes 208904 | tf_op jit(solution)/shard_map/ppermute | solution.py:220
  304.4 9.4 %collective-permute-start.64 = (bf16[16,2176]{1,0:T(8,128)(2,1)S(1)}, bf16[16,2176]{1,0:T(8,128)(2,1)S(1)}, u32[]{:S(2)}, u32[]{:S(2)}) collective-permute-start(bf16[16,2176]{1,0:T(8,128)(2,1)S(1)} %get-tuple-element.591), channel_id=1, source_target_pairs={{0,18},{1,19},{2,16},{3,17},{16,2},{17,3},{18,0},{19,1},{4,22},{5,... | collective-permute-start | bytes 208904 | tf_op jit(solution)/shard_map/ppermute | solution.py:220
  305.3 9.0 %collective-permute-start.63 = (bf16[16,2176]{1,0:T(8,128)(2,1)S(1)}, bf16[16,2176]{1,0:T(8,128)(2,1)S(1)}, u32[]{:S(2)}, u32[]{:S(2)}) collective-permute-start(bf16[16,2176]{1,0:T(8,128)(2,1)S(1)} %get-tuple-element.592), channel_id=1, source_target_pairs={{0,16},{1,17},{2,18},{3,19},{16,0},{17,1},{18,2},{19,3},{4,20},{5,... | collective-permute-start | bytes 208904 | tf_op jit(solution)/shard_map/ppermute | solution.py:220
  (65 other events, 884.9 us)
